TPU v7x, 32 devices: a whole 2x2x4 slice. The times are simulated.
32 devices in a mesh: slab: 8 (over z, y), ray: 4 (over x, core).
Axes of the slice: x: 2, y: 2, z: 4, core: 2. Of those that a mesh axis runs over, the one named last changes fastest.
Arguments:
- ray_code: bfloat16 [2048, 128], P(('ray', 'slab')), may hold values from -4 to 4
- direction: int32 [2048], P('ray'), may hold values from 0 to 1
- target: float32 [3, 2048], P(None, 'ray'), may hold values from 0 to 1
- brick_code: bfloat16 [8, 1024, 128], P('slab'), may hold values from -4 to 4
- sample_code: bfloat16 [8, 64, 128], P('slab'), may hold values from -4 to 4
- w_hidden: bfloat16 [8, 128, 128], P('slab'), may hold values from -0.5 to 0.5
- b_hidden: float32 [8, 128], P('slab'), may hold values from -3 to 3
- w_out: bfloat16 [8, 4, 128], P('slab'), may hold values from -0.5 to 0.5
- b_out: float32 [8, 4], P('slab'), may hold values from -4 to 4
- brick_ids: int32 [8, 2, 2048], P('slab', None, 'ray'), may hold values from 0 to 1023
- occupancy: int32 [8, 2048], P('slab', 'ray'), may hold values from 0 to 2, as said below
Outputs:
- color: float32 [3, 2048], P(None, ('ray', 'slab'))
- grad_ray: float32 [2048, 128], P(('ray', 'slab'))
- grad_brick: float32 [8, 1024, 128], P('slab', 'ray')
- grad_sample: float32 [8, 64, 128], P('slab')
- grad_w_hidden: float32 [8, 128, 128], P('slab')
- grad_b_hidden: float32 [8, 128], P('slab')
- grad_w_out: float32 [8, 4, 128], P('slab')
- grad_b_out: float32 [8, 4], P('slab')
Inputs may be any that keep to these rules, and one draw needn't show every extreme that they name: Slots k >= occupancy[s, r] are padding and carry no density; every slab has a ray segment with 2 occupied slots. `brick_ids`: padded slots still name some brick of the slab's table.
All inputs are finite; a program needn't handle non-finite values.
Results may differ from a plain program's by a relative error of at most 0.008.
Values may be sent and summed in bfloat16 or wider, within the bound.
No kernel may reach another device: no remote copies, remote signals or barrier semaphores. Data moves between devices by JAX's collectives and lax.ppermute only.
A program may use at most 64 MiB of HBM per device.

v0:
```python
import jax
import jax.numpy as jnp
from jax import lax
from jax.sharding import PartitionSpec as P

step_length = 0.002


def shade_forward(
    brick_rows, sample_rows, ray_rows, slot_ids, occupied_count, hidden_w, hidden_b, out_w, out_b
):
    chosen = jnp.take(brick_rows, slot_ids.T, axis=0)
    summed = (
        chosen.astype(jnp.float32)[:, :, None, :]
        + sample_rows.astype(jnp.float32)[None, None, :, :]
        + ray_rows.astype(jnp.float32)[:, None, None, :]
    )
    inputs = summed.astype(jnp.bfloat16).reshape(-1, summed.shape[-1])
    preact = jnp.dot(inputs, hidden_w, preferred_element_type=jnp.float32) + hidden_b[None, :]
    hidden = jnp.maximum(preact, 0.0).astype(jnp.bfloat16)
    raw_out = (
        jnp.einsum("cd,nd->cn", out_w, hidden, preferred_element_type=jnp.float32) + out_b[:, None]
    )
    raw_out = raw_out.reshape(4, ray_rows.shape[0], -1)
    position = jnp.arange(raw_out.shape[2], dtype=jnp.int32) // sample_rows.shape[0]
    occupied = (position[None, :] < occupied_count[:, None]).astype(jnp.float32)
    return (inputs, preact, hidden, raw_out, occupied)


def render(raw_out, occupied):
    optical = step_length * jax.nn.softplus(raw_out[0]) * occupied
    entered = jnp.cumsum(optical, axis=-1) - optical
    weight = jnp.exp(-entered) * -jnp.expm1(-optical)
    shading = jax.nn.sigmoid(raw_out[1:])
    colors = jnp.sum(weight[None] * shading, axis=-1)
    through = jnp.exp(-jnp.sum(optical, axis=-1))
    return (optical, entered, weight, shading, colors, through)


def shade_backward(
    inputs, preact, hidden, raw_out, occupied, hidden_w, out_w, color_cot, trans_cot
):
    optical, entered, weight, shading, colors, through = render(raw_out, occupied)
    q_term = jnp.sum(shading * color_cot[:, :, None], axis=0)
    q_weight = q_term * weight
    after_sum = jnp.sum(q_weight, axis=-1, keepdims=True) - jnp.cumsum(q_weight, axis=-1)
    grad_optical = (
        q_term * jnp.exp(-(entered + optical)) - after_sum - (trans_cot * through)[:, None]
    )
    grad_density = step_length * grad_optical * occupied * jax.nn.sigmoid(raw_out[0])
    grad_shade = weight[None] * color_cot[:, :, None] * shading * (1.0 - shading)
    grad_raw = jnp.concatenate([grad_density[None], grad_shade], axis=0).reshape(4, -1)
    raw_rounded = grad_raw.astype(jnp.bfloat16)
    grad_hidden = jnp.einsum("cn,cd->nd", raw_rounded, out_w, preferred_element_type=jnp.float32)
    grad_pre = jnp.where(preact > 0.0, grad_hidden, 0.0).astype(jnp.bfloat16)
    grad_w_out = jnp.einsum("cn,nd->cd", raw_rounded, hidden, preferred_element_type=jnp.float32)
    grad_b_out = jnp.sum(grad_raw, axis=1)
    grad_w_hidden = jnp.einsum("nd,ne->de", inputs, grad_pre, preferred_element_type=jnp.float32)
    grad_b_hidden = jnp.sum(grad_pre.astype(jnp.float32), axis=0)
    grad_inputs = jnp.einsum("ne,de->nd", grad_pre, hidden_w, preferred_element_type=jnp.float32)
    return (grad_w_out, grad_b_out, grad_w_hidden, grad_b_hidden, grad_inputs)


def combine_pair(first, second, order_flag):
    first_color, first_trans = first
    second_color, second_trans = second
    first_ahead = first_color + first_trans[None] * second_color
    second_ahead = second_color + second_trans[None] * first_color
    return (jnp.where(order_flag[None], first_ahead, second_ahead), first_trans * second_trans)


def composite(seg_color, seg_trans, direction):
    forward = direction == 0
    backward = direction == 1
    start = (
        jnp.zeros(seg_color.shape[1:], jnp.float32),
        jnp.ones(seg_trans.shape[1:], jnp.float32),
    )

    def lower_step(totals, pieces):
        return (combine_pair(totals, pieces, forward), totals)

    def upper_step(totals, pieces):
        return (combine_pair(totals, pieces, backward), totals)

    ended, (low_color, low_trans) = lax.scan(lower_step, start, (seg_color, seg_trans))
    ended, (high_color, high_trans) = lax.scan(
        upper_step, start, (seg_color, seg_trans), reverse=True
    )
    return (low_color, low_trans, high_color, high_trans)


def body(
    ray_code,
    direction,
    target,
    brick_code,
    sample_code,
    w_hidden,
    b_hidden,
    w_out,
    b_out,
    brick_ids,
    occupancy,
):
    ray_rows_all = lax.all_gather(ray_code, "slab", axis=0, tiled=True)
    total_rays = ray_rows_all.shape[0]
    feature_width = ray_rows_all.shape[1]
    block_rays = min(total_rays, 128)
    count_blocks = total_rays // block_rays
    slots = brick_ids.shape[1]
    brick_rows = brick_code[0]
    sample_rows = sample_code[0]
    hidden_w = w_hidden[0]
    hidden_b = b_hidden[0]
    out_w = w_out[0]
    out_b = b_out[0]
    ray_blocks = ray_rows_all.reshape(count_blocks, block_rays, feature_width)
    id_blocks = brick_ids[0].reshape(slots, count_blocks, block_rays).transpose(1, 0, 2)
    occ_blocks = occupancy[0].reshape(count_blocks, block_rays)

    def forward_block(operands):
        ray_rows, slot_ids, occupied_count = operands
        inputs, preact, hidden, raw_out, occupied = shade_forward(
            brick_rows,
            sample_rows,
            ray_rows,
            slot_ids,
            occupied_count,
            hidden_w,
            hidden_b,
            out_w,
            out_b,
        )
        rendered = render(raw_out, occupied)
        return (rendered[4], rendered[5])

    colors_b, through_b = lax.map(forward_block, (ray_blocks, id_blocks, occ_blocks))
    seg_color = colors_b.transpose(1, 0, 2).reshape(3, total_rays)
    seg_trans = through_b.reshape(total_rays)
    slab_index = lax.axis_index("slab")
    forward = direction == 0
    all_color, all_trans = (
        lax.all_gather(seg_color[None], "slab", axis=0, tiled=True),
        lax.all_gather(seg_trans[None], "slab", axis=0, tiled=True),
    )
    low_all, low_t_all, high_all, high_t_all = composite(all_color, all_trans, direction)
    low_color = lax.dynamic_index_in_dim(low_all, slab_index, 0, keepdims=False)
    low_trans = lax.dynamic_index_in_dim(low_t_all, slab_index, 0, keepdims=False)
    high_color = lax.dynamic_index_in_dim(high_all, slab_index, 0, keepdims=False)
    high_trans = lax.dynamic_index_in_dim(high_t_all, slab_index, 0, keepdims=False)
    before_color = jnp.where(forward[None], low_color, high_color)
    before_trans = jnp.where(forward, low_trans, high_trans)
    after_color = jnp.where(forward[None], high_color, low_color)
    color_full = before_color + before_trans[None] * (seg_color + seg_trans[None] * after_color)
    residual_g = color_full - target
    cot_color = before_trans[None] * residual_g
    cot_trans = before_trans * jnp.sum(after_color * residual_g, axis=0)
    own_rays = total_rays // lax.axis_size("slab")
    color_own = lax.dynamic_slice_in_dim(color_full, slab_index * own_rays, own_rays, 1)
    color_blocks = cot_color.reshape(3, count_blocks, block_rays).transpose(1, 0, 2)
    trans_blocks = cot_trans.reshape(count_blocks, block_rays)
    brick_count = brick_rows.shape[0]
    sample_count = sample_rows.shape[0]

    def backward_block(totals, operands):
        ray_rows, slot_ids, occupied_count, block_color_cot, block_trans_cot = operands
        inputs, preact, hidden, raw_out, occupied = shade_forward(
            brick_rows,
            sample_rows,
            ray_rows,
            slot_ids,
            occupied_count,
            hidden_w,
            hidden_b,
            out_w,
            out_b,
        )
        grad_w_out, grad_b_out, grad_w_hidden, grad_b_hidden, grad_inputs = shade_backward(
            inputs,
            preact,
            hidden,
            raw_out,
            occupied,
            hidden_w,
            out_w,
            block_color_cot,
            block_trans_cot,
        )
        per_position = grad_inputs.reshape(block_rays, slots, sample_count, feature_width)
        per_slot = jnp.sum(per_position, axis=2)
        one_hot = (
            slot_ids.T.reshape(-1)[:, None] == jnp.arange(brick_count, dtype=jnp.int32)[None, :]
        ).astype(jnp.float32)
        brick_sum = jnp.einsum(
            "nb,nd->bd",
            one_hot,
            per_slot.reshape(-1, feature_width),
            precision=lax.Precision.HIGHEST,
        )
        totals = (
            totals[0] + grad_w_out,
            totals[1] + grad_b_out,
            totals[2] + grad_w_hidden,
            totals[3] + grad_b_hidden,
            totals[4] + jnp.sum(per_position, axis=(0, 1)),
            totals[5] + brick_sum,
        )
        return (totals, jnp.sum(per_slot, axis=1))

    start = (
        jnp.zeros((4, feature_width), jnp.float32),
        jnp.zeros((4,), jnp.float32),
        jnp.zeros((feature_width, feature_width), jnp.float32),
        jnp.zeros((feature_width,), jnp.float32),
        jnp.zeros((sample_count, feature_width), jnp.float32),
        jnp.zeros((brick_count, feature_width), jnp.float32),
    )
    totals, ray_grads = lax.scan(
        backward_block, start, (ray_blocks, id_blocks, occ_blocks, color_blocks, trans_blocks)
    )
    grad_ray = lax.psum_scatter(
        ray_grads.reshape(total_rays, feature_width), "slab", scatter_dimension=0, tiled=True
    )
    grad_brick = lax.psum_scatter(totals[5], "ray", scatter_dimension=0, tiled=True)
    summed = lax.psum((totals[4], totals[2], totals[3], totals[0], totals[1]), "ray")
    return (
        color_own,
        grad_ray,
        grad_brick[None],
        summed[0][None],
        summed[1][None],
        summed[2][None],
        summed[3][None],
        summed[4][None],
    )


def solution(mesh):
    in_specs = (
        P(("ray", "slab"), None),
        P("ray"),
        P(None, "ray"),
        P("slab", None, None),
        P("slab", None, None),
        P("slab", None, None),
        P("slab", None),
        P("slab", None, None),
        P("slab", None),
        P("slab", None, "ray"),
        P("slab", "ray"),
    )
    out_specs = (
        P(None, ("ray", "slab")),
        P(("ray", "slab"), None),
        P("slab", "ray", None),
        P("slab", None, None),
        P("slab", None, None),
        P("slab", None),
        P("slab", None, None),
        P("slab", None),
    )
    return jax.shard_map(body, mesh=mesh, in_specs=in_specs, out_specs=out_specs, check_vma=False)
```

profile of v0, /device:TPU:0, one launch (start us, length us, event | category | flops | bytes accessed | tf_op | source)
XLA Modules:
  0.0 382.1 jit_solution(2789575744425272322)
XLA Ops:
  8.9 32.5 %all_gather.9 = bf16[512,128]{1,0:T(8,128)(2,1)S(1)} all-gather(bf16[64,128]{1,0:T(8,128)(2,1)} %param.21), channel_id=1, replica_groups=mesh['slab'=8,'ray'=4] {'slab'}, dimensions={0}, use_global_device_ids=true | all-gather | bytes 147456 | tf_op jit(solution)/shard_map/all_gather | solution.py:106
  42.2 49.3 %while.77 = (s32[]{:T(128)}, f32[4,3,128]{2,1,0:T(4,128)S(1)}, f32[4,128]{1,0:T(4,128)S(1)}, s32[4,128]{1,0:T(4,128)}, s32[4,2,128]{1,2,0:T(8,128)S(1)}, /*index...) while((s32[]{:T(128)}, f32[4,3,128]{2,1,0:T(4,128)S(1)}, ...), condition=%wide.region_4.6_spmd, body=%wide.region_0.5_spmd.sunk | while | flops 568962176 | bytes 10918589 | solution.py:138
  48.9 4.7 %fusion.111 = f32[4,16384]{1,0:T(4,128)S(1)} fusion(bf16[4,128]{1,0:T(4,128)(2,1)} %get-tuple-element.1224, bf16[16384,128]{1,0:T(8,128)(2,1)} %bitcast.312, bf16[128,128]{1,0:T(8,128)(2,1)} %get-tuple-element.1222, f32[128]{0:T(128)} %bitcast.343, f32[4]{0:T(128)} %bitcast.348), kind=kOutput, calls=%fused_computation.20.clone.1 | convolution fusion | flops 560005120 | bytes 4490768 | tf_op jit(solution)/shard_map/while/body/eval_jaxpr/cd,nd->cn/dot_general | solution.py:22
  61.2 4.7 %fusion.111 = f32[4,16384]{1,0:T(4,128)S(1)} fusion(bf16[4,128]{1,0:T(4,128)(2,1)} %get-tuple-element.1224, bf16[16384,128]{1,0:T(8,128)(2,1)} %bitcast.312, bf16[128,128]{1,0:T(8,128)(2,1)} %get-tuple-element.1222, f32[128]{0:T(128)} %bitcast.343, f32[4]{0:T(128)} %bitcast.348), kind=kOutput, calls=%fused_computation.20.clone.1 | convolution fusion | flops 560005120 | bytes 4490768 | tf_op jit(solution)/shard_map/while/body/eval_jaxpr/cd,nd->cn/dot_general | solution.py:22
  73.6 4.7 %fusion.111 = f32[4,16384]{1,0:T(4,128)S(1)} fusion(bf16[4,128]{1,0:T(4,128)(2,1)} %get-tuple-element.1224, bf16[16384,128]{1,0:T(8,128)(2,1)} %bitcast.312, bf16[128,128]{1,0:T(8,128)(2,1)} %get-tuple-element.1222, f32[128]{0:T(128)} %bitcast.343, f32[4]{0:T(128)} %bitcast.348), kind=kOutput, calls=%fused_computation.20.clone.1 | convolution fusion | flops 560005120 | bytes 4490768 | tf_op jit(solution)/shard_map/while/body/eval_jaxpr/cd,nd->cn/dot_general | solution.py:22
  85.9 4.7 %fusion.111 = f32[4,16384]{1,0:T(4,128)S(1)} fusion(bf16[4,128]{1,0:T(4,128)(2,1)} %get-tuple-element.1224, bf16[16384,128]{1,0:T(8,128)(2,1)} %bitcast.312, bf16[128,128]{1,0:T(8,128)(2,1)} %get-tuple-element.1222, f32[128]{0:T(128)} %bitcast.343, f32[4]{0:T(128)} %bitcast.348), kind=kOutput, calls=%fused_computation.20.clone.1 | convolution fusion | flops 560005120 | bytes 4490768 | tf_op jit(solution)/shard_map/while/body/eval_jaxpr/cd,nd->cn/dot_general | solution.py:22
  91.5 26.0 %all-gather = f32[8,1,512]{2,1,0:T(1,128)S(1)} all-gather(f32[1,1,512]{2,1,0:T(1,128)S(1)} %bitcast.350), channel_id=1, replica_groups=mesh['slab'=8,'ray'=4] {'slab'}, dimensions={0}, use_global_device_ids=true | all-gather | bytes 18432 | tf_op jit(solution)/shard_map/all_gather | solution.py:145
  117.5 30.5 %all_gather.10 = f32[8,3,512]{2,1,0:T(4,128)S(1)} all-gather(f32[1,3,512]{2,1,0:T(4,128)S(1)} %bitcast.345), channel_id=1, replica_groups=mesh['slab'=8,'ray'=4] {'slab'}, dimensions={0}, use_global_device_ids=true | all-gather | bytes 55296 | tf_op jit(solution)/shard_map/all_gather | solution.py:144
  150.7 133.0 %while.80 = (s32[]{:T(128)}, f32[4,128]{1,0:T(4,128)S(1)}, f32[4]{0:T(128)S(1)}, f32[128,128]{1,0:T(8,128)S(1)}, f32[128]{0:T(128)S(1)}, /*index=5*/f32[64,128]{...) while((s32[]{:T(128)}, f32[4,128]{1,0:T(4,128)S(1)}, ...), condition=%wide.region_21.23_spmd.clone, body=%wide.region_10.22_spmd.clone.sunk | while | flops 2103940480 | bytes 183198816 | solution.py:219
  165.1 4.4 %fusion.138 = f32[4,128]{1,0:T(4,128)S(1)} fusion(f32[16384,128]{1,0:T(8,128)} %copy-done, f32[4,128]{1,0:T(4,128)S(1)} %get-tuple-element.1315, pred[]{:T(512)S(6)} %compare.19, f32[3,16384]{1,0:T(4,128)S(1)} %get-tuple-element.1174, f32[1,16384]{1,0:T(1,128)S(1)} %divide_multiply_fusion.2), kind=kOutput, calls=%fused_computation.59.clone.1 | convolution fusion | flops 21234688 | bytes 8654849 | tf_op jit(solution)/shard_map/while/body/eval_jaxpr/cn,nd->cd/dot_general | solution.py:56
  173.8 4.6 %bitcast_reduce_fusion.3 = (f32[128,128]{1,0:T(8,128)S(1)}, f32[128,2,128]{2,1,0:T(2,128)S(1)}, f32[16384,128]{1,0:T(8,128)}) fusion(bf16[16384,128]{1,0:T(8,128)(2,1)S(1)} %get-tuple-element.1179, bf16[128,128]{1,0:T(8,128)(2,1)S(1)} %copy-done.5), kind=kOutput, calls=%fused_computation.116.clone.1 | convolution fusion | flops 541016064 | bytes 12812288 | tf_op jit(solution)/shard_map/while/body/eval_jaxpr/ne,de->nd/dot_general | solution.py:60
  178.4 3.9 %reduce_sum.168 = f32[64,128]{1,0:T(8,128)S(1)} reduce(f32[128,2,64,128]{3,2,1,0:T(8,128)} %bitcast.310, f32[]{:T(128)} %constant.237.clone.1..sunk.1), dimensions={0,1}, to_apply=%region_18.19 | reduce | flops 2088960 | bytes 8421380 | tf_op jit(solution)/shard_map/while/body/eval_jaxpr/reduce_sum | solution.py:206
  198.4 4.4 %fusion.138 = f32[4,128]{1,0:T(4,128)S(1)} fusion(f32[16384,128]{1,0:T(8,128)} %copy-done, f32[4,128]{1,0:T(4,128)S(1)} %get-tuple-element.1315, pred[]{:T(512)S(6)} %compare.19, f32[3,16384]{1,0:T(4,128)S(1)} %get-tuple-element.1174, f32[1,16384]{1,0:T(1,128)S(1)} %divide_multiply_fusion.2), kind=kOutput, calls=%fused_computation.59.clone.1 | convolution fusion | flops 21234688 | bytes 8654849 | tf_op jit(solution)/shard_map/while/body/eval_jaxpr/cn,nd->cd/dot_general | solution.py:56
  207.0 4.6 %bitcast_reduce_fusion.3 = (f32[128,128]{1,0:T(8,128)S(1)}, f32[128,2,128]{2,1,0:T(2,128)S(1)}, f32[16384,128]{1,0:T(8,128)}) fusion(bf16[16384,128]{1,0:T(8,128)(2,1)S(1)} %get-tuple-element.1179, bf16[128,128]{1,0:T(8,128)(2,1)S(1)} %copy-done.5), kind=kOutput, calls=%fused_computation.116.clone.1 | convolution fusion | flops 541016064 | bytes 12812288 | tf_op jit(solution)/shard_map/while/body/eval_jaxpr/ne,de->nd/dot_general | solution.py:60
  231.6 4.4 %fusion.138 = f32[4,128]{1,0:T(4,128)S(1)} fusion(f32[16384,128]{1,0:T(8,128)} %copy-done, f32[4,128]{1,0:T(4,128)S(1)} %get-tuple-element.1315, pred[]{:T(512)S(6)} %compare.19, f32[3,16384]{1,0:T(4,128)S(1)} %get-tuple-element.1174, f32[1,16384]{1,0:T(1,128)S(1)} %divide_multiply_fusion.2), kind=kOutput, calls=%fused_computation.59.clone.1 | convolution fusion | flops 21234688 | bytes 8654849 | tf_op jit(solution)/shard_map/while/body/eval_jaxpr/cn,nd->cd/dot_general | solution.py:56
  240.2 4.6 %bitcast_reduce_fusion.3 = (f32[128,128]{1,0:T(8,128)S(1)}, f32[128,2,128]{2,1,0:T(2,128)S(1)}, f32[16384,128]{1,0:T(8,128)}) fusion(bf16[16384,128]{1,0:T(8,128)(2,1)S(1)} %get-tuple-element.1179, bf16[128,128]{1,0:T(8,128)(2,1)S(1)} %copy-done.5), kind=kOutput, calls=%fused_computation.116.clone.1 | convolution fusion | flops 541016064 | bytes 12812288 | tf_op jit(solution)/shard_map/while/body/eval_jaxpr/ne,de->nd/dot_general | solution.py:60
  244.8 3.9 %reduce_sum.168 = f32[64,128]{1,0:T(8,128)S(1)} reduce(f32[128,2,64,128]{3,2,1,0:T(8,128)} %bitcast.310, f32[]{:T(128)} %constant.237.clone.1..sunk.1), dimensions={0,1}, to_apply=%region_18.19 | reduce | flops 2088960 | bytes 8421380 | tf_op jit(solution)/shard_map/while/body/eval_jaxpr/reduce_sum | solution.py:206
  264.8 4.4 %fusion.138 = f32[4,128]{1,0:T(4,128)S(1)} fusion(f32[16384,128]{1,0:T(8,128)} %copy-done, f32[4,128]{1,0:T(4,128)S(1)} %get-tuple-element.1315, pred[]{:T(512)S(6)} %compare.19, f32[3,16384]{1,0:T(4,128)S(1)} %get-tuple-element.1174, f32[1,16384]{1,0:T(1,128)S(1)} %divide_multiply_fusion.2), kind=kOutput, calls=%fused_computation.59.clone.1 | convolution fusion | flops 21234688 | bytes 8654849 | tf_op jit(solution)/shard_map/while/body/eval_jaxpr/cn,nd->cd/dot_general | solution.py:56
  273.4 4.6 %bitcast_reduce_fusion.3 = (f32[128,128]{1,0:T(8,128)S(1)}, f32[128,2,128]{2,1,0:T(2,128)S(1)}, f32[16384,128]{1,0:T(8,128)}) fusion(bf16[16384,128]{1,0:T(8,128)(2,1)S(1)} %get-tuple-element.1179, bf16[128,128]{1,0:T(8,128)(2,1)S(1)} %copy-done.5), kind=kOutput, calls=%fused_computation.116.clone.1 | convolution fusion | flops 541016064 | bytes 12812288 | tf_op jit(solution)/shard_map/while/body/eval_jaxpr/ne,de->nd/dot_general | solution.py:60
  278.0 3.9 %reduce_sum.168 = f32[64,128]{1,0:T(8,128)S(1)} reduce(f32[128,2,64,128]{3,2,1,0:T(8,128)} %bitcast.310, f32[]{:T(128)} %constant.237.clone.1..sunk.1), dimensions={0,1}, to_apply=%region_18.19 | reduce | flops 2088960 | bytes 8421380 | tf_op jit(solution)/shard_map/while/body/eval_jaxpr/reduce_sum | solution.py:206
  285.6 11.1 %all-reduce = (f32[1,64,128]{2,1,0:T(8,128)}, f32[1,128]{1,0:T(1,128)}, f32[1,4,128]{2,1,0:T(4,128)}, f32[1,4]{1,0:T(1,128)}) all-reduce(f32[1,64,128]{2,1,0:T(8,128)S(1)} %bitcast.332, f32[1,128]{1,0:T(1,128)S(1)} %bitcast.346, f32[1,4,128]{2,1,0:T(4,128)S(1)} %bitcast.342, ...), channel_id=1, replica_groups=mesh['slab'=8,'ray'=4] {'ray'}, use_global_device_ids=true, to_apply=%region_24.26 | all-reduce | flops 8836 | bytes 70688 | tf_op jit(solution)/shard_map/psum | solution.py:226
  297.3 17.9 %all-reduce.3.cloned.1.call-done = f32[1,128,128]{2,1,0:T(8,128)} async-done(((f32[1,128,128]{2,1,0:T(8,128)}), f32[1,128,128]{2,1,0:T(8,128)}) %all-reduce.3.cloned.1.call-update) | async-done | bytes 65552 | tf_op jit(solution)/shard_map/psum | solution.py:226
  315.2 34.4 %reduce-scatter.3.cloned.1.call-done = f32[64,128]{1,0:T(8,128)} async-done(((f32[512,128]{1,0:T(8,128)}), f32[64,128]{1,0:T(8,128)}) %reduce-scatter.3.cloned.1.call-update) | async-done | bytes 32784 | tf_op jit(solution)/shard_map/reduce_scatter | solution.py:222
  349.6 23.6 %reduce-scatter.5.cloned.1.call-done = f32[256,128]{1,0:T(8,128)} async-done(((f32[1024,128]{1,0:T(8,128)}), f32[256,128]{1,0:T(8,128)}) %reduce-scatter.5.cloned.1.call-update) | async-done | bytes 131088 | tf_op jit(solution)/shard_map/reduce_scatter | solution.py:225
  (426 shorter events, 124.5 us)
Async XLA Ops:
  8.0 307.2 %all-reduce.3.cloned.1.call-start = ((), (), s32[]{:S(2)}) async-start(), calls=%async_computation.4 | async-start | bytes 131072 | tf_op jit(solution)/shard_map/psum | solution.py:226
  42.2 108.5 %copy-start.8 = (f32[3,512]{1,0:T(4,128)S(1)}, f32[3,512]{1,0:T(4,128)}, u32[]{:S(2)}) copy-start(f32[3,512]{1,0:T(4,128)} %param.23) | copy-start | bytes 18436
  154.8 6.5 %copy-start.7 = (bf16[4,128]{1,0:T(4,128)(2,1)S(1)}, bf16[4,128]{1,0:T(4,128)(2,1)}, u32[]{:S(2)}) copy-start(bf16[4,128]{1,0:T(4,128)(2,1)} %get-tuple-element.1351) | copy-start | bytes 3076 | tf_op jit(solution)/shard_map/while
  154.8 6.5 %copy-start.9 = (f32[1,4]{1,0:T(1,128)S(1)}, f32[1,4]{1,0:T(1,128)}, u32[]{:S(2)}) copy-start(f32[1,4]{1,0:T(1,128)} %get-tuple-element.1352) | copy-start | bytes 52 | tf_op jit(solution)/shard_map/while
  156.1 6.5 %copy-start.2 = (bf16[128,2,64,128]{3,2,1,0:T(8,128)(2,1)}, bf16[128,2,64,128]{3,2,1,0:T(8,128)(2,1)S(1)}, u32[]{:S(2)}) copy-start(bf16[128,2,64,128]{3,2,1,0:T(8,128)(2,1)S(1)} %add_convert_fusion.5) | copy-start | bytes 12582916 | tf_op jit(solution)/shard_map/while
  158.1 3.2 copy-start
  164.2 5.8 %copy-start.1 = (f32[16384,128]{1,0:T(8,128)S(1)}, f32[16384,128]{1,0:T(8,128)}, u32[]{:S(2)}) copy-start(f32[16384,128]{1,0:T(8,128)} %copy-done) | copy-start | bytes 25165828 | tf_op jit(solution)/shard_map/while
  188.1 6.5 %copy-start.7 = (bf16[4,128]{1,0:T(4,128)(2,1)S(1)}, bf16[4,128]{1,0:T(4,128)(2,1)}, u32[]{:S(2)}) copy-start(bf16[4,128]{1,0:T(4,128)(2,1)} %get-tuple-element.1351) | copy-start | bytes 3076 | tf_op jit(solution)/shard_map/while
  188.1 6.5 %copy-start.9 = (f32[1,4]{1,0:T(1,128)S(1)}, f32[1,4]{1,0:T(1,128)}, u32[]{:S(2)}) copy-start(f32[1,4]{1,0:T(1,128)} %get-tuple-element.1352) | copy-start | bytes 52 | tf_op jit(solution)/shard_map/while
  189.3 6.5 %copy-start.2 = (bf16[128,2,64,128]{3,2,1,0:T(8,128)(2,1)}, bf16[128,2,64,128]{3,2,1,0:T(8,128)(2,1)S(1)}, u32[]{:S(2)}) copy-start(bf16[128,2,64,128]{3,2,1,0:T(8,128)(2,1)S(1)} %add_convert_fusion.5) | copy-start | bytes 12582916 | tf_op jit(solution)/shard_map/while
  191.4 3.2 copy-start
  197.5 5.8 %copy-start.1 = (f32[16384,128]{1,0:T(8,128)S(1)}, f32[16384,128]{1,0:T(8,128)}, u32[]{:S(2)}) copy-start(f32[16384,128]{1,0:T(8,128)} %copy-done) | copy-start | bytes 25165828 | tf_op jit(solution)/shard_map/while
  221.3 6.5 %copy-start.7 = (bf16[4,128]{1,0:T(4,128)(2,1)S(1)}, bf16[4,128]{1,0:T(4,128)(2,1)}, u32[]{:S(2)}) copy-start(bf16[4,128]{1,0:T(4,128)(2,1)} %get-tuple-element.1351) | copy-start | bytes 3076 | tf_op jit(solution)/shard_map/while
  221.3 6.5 %copy-start.9 = (f32[1,4]{1,0:T(1,128)S(1)}, f32[1,4]{1,0:T(1,128)}, u32[]{:S(2)}) copy-start(f32[1,4]{1,0:T(1,128)} %get-tuple-element.1352) | copy-start | bytes 52 | tf_op jit(solution)/shard_map/while
  222.5 6.5 %copy-start.2 = (bf16[128,2,64,128]{3,2,1,0:T(8,128)(2,1)}, bf16[128,2,64,128]{3,2,1,0:T(8,128)(2,1)S(1)}, u32[]{:S(2)}) copy-start(bf16[128,2,64,128]{3,2,1,0:T(8,128)(2,1)S(1)} %add_convert_fusion.5) | copy-start | bytes 12582916 | tf_op jit(solution)/shard_map/while
  224.6 3.2 copy-start
  230.7 5.8 %copy-start.1 = (f32[16384,128]{1,0:T(8,128)S(1)}, f32[16384,128]{1,0:T(8,128)}, u32[]{:S(2)}) copy-start(f32[16384,128]{1,0:T(8,128)} %copy-done) | copy-start | bytes 25165828 | tf_op jit(solution)/shard_map/while
  254.5 6.5 %copy-start.7 = (bf16[4,128]{1,0:T(4,128)(2,1)S(1)}, bf16[4,128]{1,0:T(4,128)(2,1)}, u32[]{:S(2)}) copy-start(bf16[4,128]{1,0:T(4,128)(2,1)} %get-tuple-element.1351) | copy-start | bytes 3076 | tf_op jit(solution)/shard_map/while
  254.5 6.5 %copy-start.9 = (f32[1,4]{1,0:T(1,128)S(1)}, f32[1,4]{1,0:T(1,128)}, u32[]{:S(2)}) copy-start(f32[1,4]{1,0:T(1,128)} %get-tuple-element.1352) | copy-start | bytes 52 | tf_op jit(solution)/shard_map/while
  255.8 6.4 %copy-start.2 = (bf16[128,2,64,128]{3,2,1,0:T(8,128)(2,1)}, bf16[128,2,64,128]{3,2,1,0:T(8,128)(2,1)S(1)}, u32[]{:S(2)}) copy-start(bf16[128,2,64,128]{3,2,1,0:T(8,128)(2,1)S(1)} %add_convert_fusion.5) | copy-start | bytes 12582916 | tf_op jit(solution)/shard_map/while
  257.8 3.2 copy-start
  263.9 5.8 %copy-start.1 = (f32[16384,128]{1,0:T(8,128)S(1)}, f32[16384,128]{1,0:T(8,128)}, u32[]{:S(2)}) copy-start(f32[16384,128]{1,0:T(8,128)} %copy-done) | copy-start | bytes 25165828 | tf_op jit(solution)/shard_map/while
  284.4 65.1 %reduce-scatter.3.cloned.1.call-start = ((), (), s32[]{:S(2)}) async-start(), calls=%async_computation.2 | async-start | bytes 294912 | tf_op jit(solution)/shard_map/reduce_scatter | solution.py:222
  285.0 88.2 %reduce-scatter.5.cloned.1.call-start = ((), (), s32[]{:S(2)}) async-start(), calls=%async_computation.3 | async-start | bytes 655360 | tf_op jit(solution)/shard_map/reduce_scatter | solution.py:225
  (10 other events, 17.0 us)
Sparse Core Ops, SparseCore 0:
  284.6 30.5 all-reduce.2
Sparse Core Ops, SparseCore 1:
  288.8 60.7 reduce-scatter.2
  352.5 20.6 reduce-scatter.4
where the time goes:
time: 384 us; the launch traced here: 382 us
  blocking collectives  100 us (26%)
  matrix products  87.2 us (23%)
  waiting for transfers between devices  76.9 us (20%)
  other arithmetic  52.8 us (14%)
  local copies, waits for them, and re-layouts  47.1 us (12%)
  between operations  15.7 us (4%)
    reduce_scatter x1, waiting for transfers between devices, body(): lax.psum_scatter(ray_grads.reshape(total_rays, feature_width), 'slab', sc...  34.4 us
    all_gather x1, blocking collectives, body(): ray_rows_all = lax.all_gather(ray_code, 'slab', axis=0, tiled=True)  32.5 us
    all_gather x1, blocking collectives, body(): lax.all_gather(seg_color[None], 'slab', axis=0, tiled=True)  30.5 us
    all_gather x1, blocking collectives, body(): lax.all_gather(seg_trans[None], 'slab', axis=0, tiled=True)  26 us
    reduce_scatter x1, waiting for transfers between devices, body(): lax.psum_scatter(totals[5], 'ray', scatter_dimension=0, tiled=True)  23.6 us
    dot_general x8, matrix products, shade_forward(): jnp.einsum('cd,nd->cn', out_w, hidden, preferred_element_type=jnp.float32)  23.4 us
    dot_general x4, matrix products, shade_backward(): jnp.einsum('ne,de->nd', grad_pre, hidden_w, preferred_element_type=jnp.fl...  18.3 us
    psum x1, waiting for transfers between devices, body(): lax.psum((totals[4], totals[2], totals[3], totals[0], totals[1]), 'ray')  17.9 us
  transfers between devices with their start and end apart: 3, of which 3 were waited for; matrix products, arithmetic and copies ran while one was open for 0% of the time, Pallas kernels for 0%

commit v1 on v0

v1 whole, which is shorter than its diff:
```python
import functools

import jax
import jax.numpy as jnp
from jax import lax
from jax.experimental import pallas as pl
from jax.experimental.pallas import tpu as pltpu
from jax.sharding import PartitionSpec as P

step_length = 0.002
f32 = jnp.float32
bf16 = jnp.bfloat16
vmem_bytes = 48 * 1024 * 1024
exact = lax.Precision.HIGHEST


def bits_of(count):
    bits = count.bit_length() - 1
    assert count == 1 << bits
    return bits


def reversed_bits(value, bits):
    return sum(((value >> i) & 1) << (bits - 1 - i) for i in range(bits))


def nt_dot(a, b, precision=None):
    return lax.dot_general(
        a, b, (((1,), (1,)), ((), ())), precision=precision, preferred_element_type=f32
    )


def nn_dot(a, b, precision=None):
    return jnp.dot(a, b, precision=precision, preferred_element_type=f32)


def swap(array, axis, size, distance):
    return lax.ppermute(array, axis, [(i, i ^ distance) for i in range(size)])


def call(kernel, out_shape, name, scratch=(), smem=0, count=0):
    specs = [pl.BlockSpec(memory_space=pltpu.SMEM)] * smem
    specs += [pl.BlockSpec(memory_space=pltpu.VMEM)] * (count - smem)
    return pl.pallas_call(
        kernel,
        out_shape=out_shape,
        in_specs=specs,
        out_specs=jax.tree.map(lambda _: pl.BlockSpec(memory_space=pltpu.VMEM), out_shape),
        scratch_shapes=list(scratch),
        compiler_params=pltpu.CompilerParams(vmem_limit_bytes=vmem_bytes),
        name=name,
    )


def prepare_kernel(ids_ref, brick_ref, w_ref, chosen_ref, project_ref):
    slots, rays = ids_ref.shape
    bricks = brick_ref.shape[0]
    brick_t = brick_ref[...].astype(f32).T.astype(bf16)
    w_t = w_ref[...].astype(f32).T.astype(bf16)
    row = lax.broadcasted_iota(jnp.int32, (bricks, rays), 0)
    for k in range(slots):
        one_hot = jnp.where(row == ids_ref[k : k + 1, :], 1.0, 0.0).astype(bf16)
        chosen = nn_dot(brick_t, one_hot).astype(bf16)
        chosen_ref[:, k * rays : (k + 1) * rays] = chosen
        project_ref[:, k * rays : (k + 1) * rays] = nn_dot(w_t, chosen)


def forward_kernel(
    me_ref,
    project_ref,
    ray_ref,
    w_ref,
    b_ref,
    sample_ref,
    w_out_ref,
    b_out_ref,
    occ_ref,
    seg_ref,
    coef_ref,
    u_ref,
    s_ref,
    ray_sorted_ref,
    ut_ref,
    wide_ref,
    raw_ref,
    *,
    owners,
):
    width, total = project_ref.shape
    rays = ray_ref.shape[0]
    slots = total // rays
    samples = sample_ref.shape[0]
    own = rays // owners
    bits = bits_of(owners)
    me = me_ref[0, 0]
    for t in range(owners):
        place = pl.multiple_of((me ^ t) * own, own)
        at = reversed_bits(t, bits) * own
        ray_sorted_ref[pl.ds(place, own), :] = ray_ref[at : at + own, :]
    w_t = w_ref[...].astype(f32).T.astype(bf16)
    ray_t = nt_dot(w_t, ray_sorted_ref[...])
    for k in range(slots):
        part = (project_ref[:, k * rays : (k + 1) * rays] + ray_t).astype(bf16)
        ut_ref[:, k * rays : (k + 1) * rays] = part
        u_ref[k * rays : (k + 1) * rays, :] = part.astype(f32).T.astype(bf16)
    s = nn_dot(sample_ref[...], w_ref[...]) + b_ref[...]
    s_low = s.astype(bf16)
    s_ref[...] = s_low.astype(f32)
    s_t = jnp.concatenate([s, s], 0).T
    for j in range(samples):
        wide_ref[j] = jnp.broadcast_to(s_t[:, j : j + 1], (width, 128)).astype(bf16)
    outs = w_out_ref.shape[0]
    w_rows = jnp.concatenate(
        [jnp.broadcast_to(w_out_ref[c : c + 1, :].astype(f32), (8, width)) for c in range(outs)], 0
    )
    row8 = lax.broadcasted_iota(jnp.int32, (outs * 8, width), 0) % 8
    left = [jnp.where(row8 == i, w_rows, 0.0).astype(bf16) for i in range(8)]
    left = [jnp.concatenate([left[2 * i], left[2 * i + 1]], 1) for i in range(4)]

    def shade_block(block, carry):
        for n in range(total // 256):
            lanes = slice(n * 256, n * 256 + 256)
            ut = ut_ref[:, lanes]
            acc = None
            for i in range(4):
                parts = []
                for h in range(2):
                    column = wide_ref[block * 8 + 2 * i + h]
                    column = jnp.concatenate([column, column], 1)
                    parts.append(jnp.maximum(ut + column, 0))
                term = nn_dot(left[i], jnp.concatenate(parts, 0))
                acc = term if acc is None else acc + term
            for c in range(outs):
                raw_ref[c, pl.ds(pl.multiple_of(block * 8, 8), 8), lanes] = (
                    acc[c * 8 : c * 8 + 8, :] + b_out_ref[0, c]
                )
        return carry

    lax.fori_loop(0, samples // 8, shade_block, 0)
    r_i = lax.broadcasted_iota(jnp.int32, (samples, samples), 0)
    c_i = lax.broadcasted_iota(jnp.int32, (samples, samples), 1)
    earlier = jnp.where(c_i < r_i, 1.0, 0.0).astype(f32)
    later = jnp.where(c_i > r_i, 1.0, 0.0).astype(f32)
    chunk = 128
    for n in range(rays // chunk):
        occ = occ_ref[:, n * chunk : (n + 1) * chunk]
        before = jnp.zeros((1, chunk), f32)
        kept = []
        for k in range(slots):
            lanes = slice(k * rays + n * chunk, k * rays + (n + 1) * chunk)
            x = raw_ref[0, :, lanes]
            occupied = (k < occ).astype(f32)
            tail = jnp.exp(-jnp.abs(x))
            optical = step_length * (jnp.maximum(x, 0.0) + jnp.log1p(tail)) * occupied
            entered = nn_dot(earlier, optical, exact) + before
            before = before + jnp.sum(optical, 0, keepdims=True)
            half = jnp.tanh(0.5 * optical)
            weight = jnp.exp(-entered) * (2.0 * half / (1.0 + half))
            shading = [jax.nn.sigmoid(raw_ref[c, :, lanes]) for c in range(1, outs)]
            passed = jnp.exp(-(entered + optical))
            density = step_length * occupied * jax.nn.sigmoid(x)
            kept.append((lanes, weight, shading, passed, density))
        through = jnp.exp(-before)
        after = [jnp.zeros((1, chunk), f32)] * (outs - 1)
        for lanes, weight, shading, passed, density in reversed(kept):
            for c in range(outs - 1):
                light = weight * shading[c]
                behind = nn_dot(later, light, exact) + after[c]
                after[c] = after[c] + jnp.sum(light, 0, keepdims=True)
                coef_ref[c, :, lanes] = density * (shading[c] * passed - behind)
                coef_ref[outs + c, :, lanes] = light * (1.0 - shading[c])
            coef_ref[outs - 1, :, lanes] = density * through
        place = slice(n * chunk, (n + 1) * chunk)
        for c in range(outs - 1):
            seg_ref[c : c + 1, place] = after[c]
        seg_ref[outs - 1 : outs, place] = through


def merge(first, second, forward):
    fc, ft = first
    sc, st = second
    return jnp.where(forward, fc + ft * sc, sc + st * fc), ft * st


def backward_kernel(
    me_ref,
    seg_ref,
    got_ref,
    direction_ref,
    target_ref,
    coef_ref,
    u_ref,
    s_ref,
    ids_ref,
    chosen_ref,
    ray_ref,
    sample_ref,
    w_ref,
    w_out_ref,
    color_ref,
    ray_out_ref,
    brick_out_ref,
    small_ref,
    g_ref,
    gg_ref,
    slot_ref,
    by_sample_ref,
    *,
    owners,
    shares,
):
    me = me_ref[0, 0]
    share = me_ref[0, 1]
    channels = target_ref.shape[0]
    outs = channels + 1
    rays = target_ref.shape[1]
    total, width = u_ref.shape
    slots = total // rays
    samples = s_ref.shape[0]
    bricks = brick_out_ref.shape[0]
    bits = bits_of(owners)
    forward = direction_ref[...] == 0

    def pair(values):
        return values[:channels, :], values[channels : channels + 1, :]

    low = high = None
    for b in reversed(range(bits)):
        piece = pair(got_ref[b])
        is_low = ((me >> b) & 1) == 1
        piece = (jnp.where(is_low, piece[0], 0.0), jnp.where(is_low, piece[1], 1.0))
        low = piece if low is None else merge(low, piece, forward)
    for b in range(bits):
        piece = pair(got_ref[b])
        is_high = ((me >> b) & 1) == 0
        piece = (jnp.where(is_high, piece[0], 0.0), jnp.where(is_high, piece[1], 1.0))
        high = piece if high is None else merge(high, piece, forward)
    seg_color, seg_trans = pair(seg_ref[...])
    before_color = jnp.where(forward, low[0], high[0])
    before_trans = jnp.where(forward, low[1], high[1])
    after_color = jnp.where(forward, high[0], low[0])
    color = before_color + before_trans * (seg_color + seg_trans * after_color)
    residual = color - target_ref[...]
    color_cot = before_trans * residual
    trans_cot = before_trans * jnp.sum(after_color * residual, 0, keepdims=True)
    own = rays // owners
    r_i = lax.broadcasted_iota(jnp.int32, (rays, own), 0)
    c_i = lax.broadcasted_iota(jnp.int32, (rays, own), 1)
    pick = jnp.where(r_i == c_i + me * own, 1.0, 0.0).astype(f32)
    color_ref[...] = nn_dot(color, pick, exact)

    bias_sums = [jnp.zeros((1, 128), f32)] * outs
    for n in range(total // 128):
        lanes = slice(n * 128, n * 128 + 128)
        at = (n * 128) % rays
        cots = [color_cot[c : c + 1, at : at + 128] for c in range(channels)]
        grads = [
            sum(cots[c] * coef_ref[c, :, lanes] for c in range(channels))
            - trans_cot[:, at : at + 128] * coef_ref[channels, :, lanes]
        ]
        for c in range(channels):
            grads.append(cots[c] * coef_ref[outs + c, :, lanes])
        for c in range(outs):
            g = grads[c]
            bias_sums[c] = bias_sums[c] + jnp.sum(g, 0, keepdims=True)
            gg_ref[c, lanes, :] = jnp.concatenate([g] * (128 // samples), 0).T
        for j in range(0, samples, 8):
            g_ref[j // 8, :, lanes] = jnp.concatenate([g[j : j + 8] for g in grads], 0).astype(bf16)
    w_rows = [w_out_ref[c : c + 1, :].astype(f32) for c in range(outs)]
    negative = (-s_ref[...]).astype(bf16)
    one = jnp.ones((samples, width), bf16)
    zero = jnp.zeros((samples, width), bf16)
    lane = lax.broadcasted_iota(jnp.int32, (8, 8 * samples), 1) // samples
    row = lax.broadcasted_iota(jnp.int32, (8, 8 * samples), 0)
    block_mask = lane == row
    repeat = 8 * samples // 128

    def slot_block(block, sums):
        at = pl.multiple_of(block * 16, 16)
        u16 = u_ref[pl.ds(at, 16), :]
        sums = list(sums)
        for h in range(2):
            base = pl.multiple_of(block * 16 + h * 8, 8)
            left = [
                jnp.where(
                    block_mask, jnp.concatenate([gg_ref[c, pl.ds(base, 8), :]] * repeat, 1), 0.0
                )
                for c in range(outs)
            ]
            left = jnp.concatenate(left, 0).astype(bf16)
            tiles = [
                jnp.where(
                    jnp.broadcast_to(u16[h * 8 + i : h * 8 + i + 1, :], (samples, width))
                    > negative,
                    one,
                    zero,
                )
                for i in range(8)
            ]
            h1 = nn_dot(left, jnp.concatenate(tiles, 0))
            u8 = u16[h * 8 : h * 8 + 8, :].astype(f32)
            grad = None
            for c in range(outs):
                piece = h1[c * 8 : c * 8 + 8, :]
                sums[c] = sums[c] + u8 * piece
                term = w_rows[c] * piece
                grad = term if grad is None else grad + term
            slot_ref[pl.ds(base, 8), :] = grad
        return tuple(sums)

    sums = lax.fori_loop(0, total // 16, slot_block, tuple([jnp.zeros((8, width), f32)] * outs))
    row8 = lax.broadcasted_iota(jnp.int32, (8, width), 0)

    def sample_block(block, sums):
        at = pl.multiple_of(block * 8, 8)
        left = g_ref[block]
        s8 = s_ref[pl.ds(at, 8), :]
        acc = [jnp.zeros((8, width), f32)] * outs
        for i in range(8):
            edge = (-s8[i : i + 1, :]).astype(bf16)
            h2 = None
            for n in range(total // 256):
                u = u_ref[n * 256 : n * 256 + 256, :]
                live = jnp.where(
                    u > jnp.broadcast_to(edge, u.shape),
                    jnp.ones(u.shape, bf16),
                    jnp.zeros(u.shape, bf16),
                )
                term = nn_dot(left[:, n * 256 : n * 256 + 256], live)
                h2 = term if h2 is None else h2 + term
            for c in range(outs):
                acc[c] = acc[c] + jnp.where(row8 == i, h2[c * 8 : c * 8 + 8, :], 0.0)
        by_sample_ref[pl.ds(at, 8), :] = sum(w_rows[c] * acc[c] for c in range(outs))
        return tuple(sums[c] + s8 * acc[c] for c in range(outs))

    sums = lax.fori_loop(0, samples // 8, sample_block, sums)

    w = w_ref[...].astype(f32)
    slot = slot_ref[...]
    by_sample = by_sample_ref[...]
    moved = nt_dot(slot, w, exact)
    grad_ray = moved[:rays, :]
    for k in range(1, slots):
        grad_ray = grad_ray + moved[k * rays : (k + 1) * rays, :]
    slot_ref[:rays, :] = grad_ray
    for t in range(owners):
        place = pl.multiple_of((me ^ t) * own, own)
        at = reversed_bits(t, bits) * own
        ray_out_ref[at : at + own, :] = slot_ref[pl.ds(place, own), :].astype(ray_out_ref.dtype)
    share_bits = bits_of(shares)
    part = bricks // shares
    high_part = moved.astype(bf16)
    low_part = (moved - high_part.astype(f32)).astype(bf16)
    row = lax.broadcasted_iota(jnp.int32, (part, rays), 0)
    for t in range(shares):
        first = (share ^ t) * part
        at = reversed_bits(t, share_bits) * part
        acc = jnp.zeros((part, width), f32)
        for k in range(slots):
            one_hot = jnp.where(row + first == ids_ref[k : k + 1, :], 1.0, 0.0).astype(bf16)
            rows = slice(k * rays, (k + 1) * rays)
            acc = acc + nn_dot(one_hot, high_part[rows]) + nn_dot(one_hot, low_part[rows])
        brick_out_ref[at : at + part, :] = acc
    slot_ray = slot[:rays, :]
    for k in range(1, slots):
        slot_ray = slot_ray + slot[k * rays : (k + 1) * rays, :]
    small_ref[:samples, :] = nt_dot(by_sample, w, exact)
    ray_t = ray_ref[...].astype(f32).T
    sample_t = jnp.concatenate([sample_ref[...].astype(f32)] * (128 // samples), 0).T[:, :samples]
    small_ref[samples : samples + width, :] = (
        nn_dot(chosen_ref[...].astype(f32), slot, exact)
        + nn_dot(ray_t, slot_ray, exact)
        + nn_dot(sample_t, by_sample, exact)
    )
    at = samples + width
    small_ref[at : at + 1, :] = jnp.sum(by_sample, 0, keepdims=True)
    for c in range(outs):
        small_ref[at + 1 + c : at + 2 + c, :] = jnp.sum(sums[c], 0, keepdims=True)
    lane128 = lax.broadcasted_iota(jnp.int32, (1, 128), 1)
    bias = jnp.zeros((1, 128), f32)
    for c in range(outs):
        bias = bias + jnp.where(lane128 == c, jnp.sum(bias_sums[c], 1, keepdims=True), 0.0)
    small_ref[at + 1 + outs : at + 2 + outs, :] = bias
    rest = small_ref.shape[0] - (at + 2 + outs)
    small_ref[at + 2 + outs :, :] = jnp.zeros((rest, width), f32)


def gather_rays(rays, owners):
    for b in reversed(range(bits_of(owners))):
        rays = jnp.concatenate([rays, swap(rays, "slab", owners, 1 << b)], 0)
    return rays


def body(
    ray_code,
    direction,
    target,
    brick_code,
    sample_code,
    w_hidden,
    b_hidden,
    w_out,
    b_out,
    brick_ids,
    occupancy,
):
    owners = lax.axis_size("slab")
    shares = lax.axis_size("ray")
    me = lax.axis_index("slab")
    share = lax.axis_index("ray")
    ids = brick_ids[0]
    slots, rays = ids.shape
    total = slots * rays
    bricks, width = brick_code.shape[1:]
    samples = sample_code.shape[1]
    outs = w_out.shape[1]
    channels = outs - 1
    w = w_hidden[0]
    direction = direction[None]
    where_am_i = jnp.stack([me, share]).astype(jnp.int32)[None]

    chosen, project = call(
        prepare_kernel,
        (
            jax.ShapeDtypeStruct((width, total), bf16),
            jax.ShapeDtypeStruct((width, total), f32),
        ),
        "prepare",
        count=3,
    )(ids, brick_code[0], w)
    ray_all = gather_rays(ray_code, owners)
    seg, coef, u, s, ray_sorted = call(
        functools.partial(forward_kernel, owners=owners),
        (
            jax.ShapeDtypeStruct((outs, rays), f32),
            jax.ShapeDtypeStruct((outs + channels, samples, total), f32),
            jax.ShapeDtypeStruct((total, width), bf16),
            jax.ShapeDtypeStruct((samples, width), f32),
            jax.ShapeDtypeStruct((rays, width), bf16),
        ),
        "forward",
        scratch=(
            pltpu.VMEM((width, total), bf16),
            pltpu.VMEM((samples, width, 128), bf16),
            pltpu.VMEM((outs, samples, total), f32),
        ),
        smem=1,
        count=9,
    )(where_am_i, project, ray_all, w, b_hidden, sample_code[0], w_out[0], b_out, occupancy)

    forward = direction == 0
    group = (seg[:channels], seg[channels:])
    got = []
    for b in range(bits_of(owners)):
        packed = jnp.concatenate(group, 0)
        other = swap(packed, "slab", owners, 1 << b)
        got.append(other)
        theirs = (other[:channels], other[channels:])
        upper = ((me >> b) & 1) == 1
        first = jax.tree.map(lambda a, b: jnp.where(upper, b, a), group, theirs)
        second = jax.tree.map(lambda a, b: jnp.where(upper, a, b), group, theirs)
        group = merge(first, second, forward)

    small_rows = -(-(samples + width + 2 + outs) // 16) * 16
    color_own, ray_part, brick_part, small = call(
        functools.partial(backward_kernel, owners=owners, shares=shares),
        (
            jax.ShapeDtypeStruct((channels, rays // owners), f32),
            jax.ShapeDtypeStruct((rays, width), f32),
            jax.ShapeDtypeStruct((bricks, width), f32),
            jax.ShapeDtypeStruct((small_rows, width), f32),
        ),
        "backward",
        scratch=(
            pltpu.VMEM((samples // 8, outs * 8, total), bf16),
            pltpu.VMEM((outs, total, 128), f32),
            pltpu.VMEM((total, width), f32),
            pltpu.VMEM((samples, width), f32),
        ),
        smem=1,
        count=14,
    )(
        where_am_i,
        seg,
        jnp.stack(got),
        direction,
        target,
        coef,
        u,
        s,
        ids,
        chosen,
        ray_sorted,
        sample_code[0],
        w,
        w_out[0],
    )

    for b in range(bits_of(owners)):
        half = ray_part.shape[0] // 2
        ray_part = ray_part[:half] + swap(ray_part[half:].astype(bf16), "slab", owners, 1 << b)
    for b in range(bits_of(shares)):
        half = brick_part.shape[0] // 2
        brick_part = brick_part[:half] + swap(brick_part[half:].astype(bf16), "ray", shares, 1 << b)
        small = small + swap(small, "ray", shares, 1 << b)
    at = samples + width
    return (
        color_own,
        ray_part,
        brick_part[None],
        small[None, :samples],
        small[None, samples:at],
        small[at : at + 1],
        small[None, at + 1 : at + 1 + outs],
        small[at + 1 + outs : at + 2 + outs, :outs],
    )


def solution(mesh):
    in_specs = (
        P(("ray", "slab"), None),
        P("ray"),
        P(None, "ray"),
        P("slab", None, None),
        P("slab", None, None),
        P("slab", None, None),
        P("slab", None),
        P("slab", None, None),
        P("slab", None),
        P("slab", None, "ray"),
        P("slab", "ray"),
    )
    out_specs = (
        P(None, ("ray", "slab")),
        P(("ray", "slab"), None),
        P("slab", "ray", None),
        P("slab", None, None),
        P("slab", None, None),
        P("slab", None),
        P("slab", None, None),
        P("slab", None),
    )
    return jax.shard_map(body, mesh=mesh, in_specs=in_specs, out_specs=out_specs, check_vma=False)
```

time: 384 us -> 88.2 us (0.23)
  blocking collectives: 100 us -> 0 us
  matrix products: 87.2 us -> 0 us
  waiting for transfers between devices: 76.9 us -> 19.5 us
  other arithmetic: 52.8 us -> 4.38 us
  local copies, waits for them, and re-layouts: 47.1 us -> 12.9 us
  Pallas kernels: 0 us -> 29.4 us
  starting transfers between devices: 0.12 us -> 20.4 us
  between operations: 15.7 us -> 0.77 us
    all_gather x3 -> x0, blocking collectives: 89 us -> none  [the longest x1 32.5 us: body(): ray_rows_all = lax.all_gather(ray_code, 'slab', axis=0, tiled=True)]
    dot_general x32 -> x0, matrix products: 87.2 us -> none  [the longest x8 23.4 us: shade_forward(): jnp.einsum('cd,nd->cn', out_w, hidden, preferred_element_type=jnp.float32)]
    reduce_scatter x2 -> x0, waiting for transfers between devices: 58 us -> none  [the longest x1 34.4 us: body(): lax.psum_scatter(ray_grads.reshape(total_rays, feature_width), 'slab', sc...]
    pallas_call x0 -> x3, Pallas kernels: none -> 29.4 us  [the longest x1 21.2 us: body(): call(functools.partial(backward_kernel, owners=owners, shares=shares), (j...]
    convert_element_type x32 -> x0, other arithmetic: 25 us -> none  [the longest x8 17.6 us: shade_forward(): inputs = summed.astype(jnp.bfloat16).reshape(-1, summed.shape[-1])]
    ppermute x0 -> x13, starting transfers between devices: none -> 20.4 us  [swap(): return lax.ppermute(array, axis, [(i, i ^ distance) for i in range(size)])]
    reduce_sum x29 -> x0, other arithmetic: 20 us -> none  [the longest x4 15.6 us: backward_block(): jnp.sum(per_position, axis=(0, 1))]
    ppermute x0 -> x13, waiting for transfers between devices: none -> 19.5 us  [swap(): return lax.ppermute(array, axis, [(i, i ^ distance) for i in range(size)])]
  transfers between devices with their start and end apart: 3 -> 13, of which waited for: 3 -> 8; matrix products, arithmetic and copies ran while one was open for 0% -> 2% of each run, Pallas kernels for 0% -> 1%
where the time goes in v1:
time: 88.2 us; the launch traced here: 87.4 us
  Pallas kernels  29.4 us (33%)
  starting transfers between devices  20.4 us (23%)
  waiting for transfers between devices  19.5 us (22%)
  local copies, waits for them, and re-layouts  12.9 us (15%)
  other arithmetic  4.38 us (5%)
    pallas_call x1, Pallas kernels, body(): call(functools.partial(backward_kernel, owners=owners, shares=shares), (j...  21.2 us
    ppermute x13, starting transfers between devices, swap(): return lax.ppermute(array, axis, [(i, i ^ distance) for i in range(size)])  20.4 us
    ppermute x13, waiting for transfers between devices, swap(): return lax.ppermute(array, axis, [(i, i ^ distance) for i in range(size)])  19.5 us
    unnamed x28, local copies, waits for them, and re-layouts  9.99 us
    pallas_call x1, Pallas kernels, body(): call(functools.partial(forward_kernel, owners=owners), (jax.ShapeDtypeStr...  7.3 us
    concatenate x3, other arithmetic, gather_rays(): rays = jnp.concatenate([rays, swap(rays, 'slab', owners, 1 << b)], 0)  2.17 us
  transfers between devices with their start and end apart: 13, of which 8 were waited for; matrix products, arithmetic and copies ran while one was open for 2% of the time, Pallas kernels for 1%

profile of v1, /device:TPU:0, one launch (start us, length us, event | category | flops | bytes accessed | tf_op | source)
XLA Modules:
  0.0 87.4 jit_solution(4929600402942146851)
XLA Ops:
  0.6 4.1 %collective-permute-start = (bf16[64,128]{1,0:T(8,128)(2,1)}, bf16[64,128]{1,0:T(8,128)(2,1)S(1)}, u32[]{:S(2)}, u32[]{:S(2)}) collective-permute-start(bf16[64,128]{1,0:T(8,128)(2,1)} %param.11), channel_id=1, source_target_pairs={{0,16},{4,20},{8,24},{12,28},{16,0},{20,4},{24,8},{28,12},{1,17},{... | collective-permute-start | bytes 49160 | tf_op jit(solution)/shard_map/ppermute | solution.py:38
  4.7 1.9 %collective-permute-done = bf16[64,128]{1,0:T(8,128)(2,1)S(1)} collective-permute-done((bf16[64,128]{1,0:T(8,128)(2,1)}, bf16[64,128]{1,0:T(8,128)(2,1)S(1)}, u32[]{:S(2)}, u32[]{:S(2)}) %collective-permute-start) | collective-permute-done | bytes 16416 | tf_op jit(solution)/shard_map/ppermute | solution.py:38
  7.4 1.9 %collective-permute-start.1 = (bf16[128,128]{1,0:T(8,128)(2,1)S(1)}, bf16[128,128]{1,0:T(8,128)(2,1)S(1)}, u32[]{:S(2)}, u32[]{:S(2)}) collective-permute-start(bf16[128,128]{1,0:T(8,128)(2,1)S(1)} %pad_maximum_fusion.2), channel_id=1, source_target_pairs={{0,8},{4,12},{8,0},{12,4},{16,24},{20,28},{24,16},{28,20},{1,9},{5... | collective-permute-start | bytes 98312 | tf_op jit(solution)/shard_map/ppermute | solution.py:38
  9.3 0.8 copy-done
  10.1 0.9 %copy-done.2 = bf16[1,1024,128]{2,1,0:T(8,128)(2,1)S(1)} copy-done((bf16[1,1024,128]{2,1,0:T(8,128)(2,1)S(1)}, bf16[1,1024,128]{2,1,0:T(8,128)(2,1)}, u32[]{:S(2)}) %copy-start.2) | copy-done | bytes 262168
  11.7 0.9 %prepare.1 = (bf16[128,1024]{1,0:T(8,128)(2,1)S(1)}, f32[128,1024]{1,0:T(8,128)S(1)}) custom-call(s32[2,512]{1,0:T(2,128)S(1)} %bitcast.31, bf16[1024,128]{1,0:T(8,128)(2,1)S(1)} %bitcast.28, bf16[128,128]{1,0:T(8,128)(2,1)S(1)} %bitcast.25), custom_call_target="tpu_custom_call" | custom-call | tf_op jit(solution)/shard_map/prepare/pallas_call | solution.py:422
  12.6 0.7 pad_maximum_fusion.1
  13.4 1.5 %collective-permute-start.2 = (bf16[256,128]{1,0:T(8,128)(2,1)S(1)}, bf16[256,128]{1,0:T(8,128)(2,1)S(1)}, u32[]{:S(2)}, u32[]{:S(2)}) collective-permute-start(bf16[256,128]{1,0:T(8,128)(2,1)S(1)} %pad_maximum_fusion.1), channel_id=1, source_target_pairs={{0,4},{4,0},{8,12},{12,8},{16,20},{20,16},{24,28},{28,24},{1,5},{5... | collective-permute-start | bytes 196616 | tf_op jit(solution)/shard_map/ppermute | solution.py:38
  15.0 2.7 %collective-permute-done.2 = bf16[256,128]{1,0:T(8,128)(2,1)S(1)} collective-permute-done((bf16[256,128]{1,0:T(8,128)(2,1)S(1)}, bf16[256,128]{1,0:T(8,128)(2,1)S(1)}, u32[]{:S(2)}, u32[]{:S(2)}) %collective-permute-start.2) | collective-permute-done | bytes 65568 | tf_op jit(solution)/shard_map/ppermute | solution.py:38
  17.6 0.7 pad_maximum_fusion.ray_ref
  21.8 7.3 %forward.1 = (f32[4,512]{1,0:T(4,128)S(1)}, f32[7,64,1024]{2,1,0:T(8,128)S(1)}, bf16[1024,128]{1,0:T(8,128)(2,1)S(1)}, f32[64,128]{1,0:T(8,128)S(1)}, bf16[512,128]{1,0:T(8,128)(2,1)S(1)}) custom-call(s32[1,2]{1,0:T(1,128)S(1)} %add_bitcast_fusion.me_ref, f32[128,1024]{1,0:T(8,128)S(1)} %get-tuple-element.19.project_ref, ...), custom_call_target="tpu_custom_call" | custom-call | tf_op jit(solution)/shard_map/forward/pallas_call | solution.py:432
  29.1 1.6 %collective-permute-start.3 = (f32[4,512]{1,0:T(4,128)S(1)}, f32[4,512]{1,0:T(4,128)S(1)}, u32[]{:S(2)}, u32[]{:S(2)}) collective-permute-start(f32[4,512]{1,0:T(4,128)S(1)} %get-tuple-element.20.seg_ref), channel_id=1, source_target_pairs={{0,4},{4,0},{8,12},{12,8},{16,20},{20,16},{24,28},{28,24},{1,5},{5... | collective-permute-start | bytes 24584 | tf_op jit(solution)/shard_map/ppermute | solution.py:38
  31.3 1.4 %collective-permute-done.3 = f32[4,512]{1,0:T(4,128)S(1)} collective-permute-done((f32[4,512]{1,0:T(4,128)S(1)}, f32[4,512]{1,0:T(4,128)S(1)}, u32[]{:S(2)}, u32[]{:S(2)}) %collective-permute-start.3) | collective-permute-done | bytes 8224 | tf_op jit(solution)/shard_map/ppermute | solution.py:38
  33.5 3.1 %collective-permute-done.4 = f32[4,512]{1,0:T(4,128)S(1)} collective-permute-done((f32[4,512]{1,0:T(4,128)S(1)}, f32[4,512]{1,0:T(4,128)S(1)}, u32[]{:S(2)}, u32[]{:S(2)}) %collective-permute-start.4) | collective-permute-done | bytes 8224 | tf_op jit(solution)/shard_map/ppermute | solution.py:38
  36.6 2.7 %collective-permute-start.5 = (f32[4,512]{1,0:T(4,128)S(1)}, f32[4,512]{1,0:T(4,128)S(1)}, u32[]{:S(2)}, u32[]{:S(2)}) collective-permute-start(f32[4,512]{1,0:T(4,128)S(1)} %pad_maximum_fusion.5), channel_id=1, source_target_pairs={{0,16},{4,20},{8,24},{12,28},{16,0},{20,4},{24,8},{28,12},{1,17},{... | collective-permute-start | bytes 24584 | tf_op jit(solution)/shard_map/ppermute | solution.py:38
  39.3 1.9 %collective-permute-done.5 = f32[4,512]{1,0:T(4,128)S(1)} collective-permute-done((f32[4,512]{1,0:T(4,128)S(1)}, f32[4,512]{1,0:T(4,128)S(1)}, u32[]{:S(2)}, u32[]{:S(2)}) %collective-permute-start.5) | collective-permute-done | bytes 8224 | tf_op jit(solution)/shard_map/ppermute | solution.py:38
  41.2 0.8 copy-done.1
  45.4 21.2 %backward.1 = (f32[3,64]{1,0:T(4,128)}, f32[512,128]{1,0:T(8,128)S(1)}, f32[1024,128]{1,0:T(8,128)S(1)}, f32[208,128]{1,0:T(8,128)S(1)}) custom-call(s32[1,2]{1,0:T(1,128)S(1)} %add_bitcast_fusion.me_ref, f32[4,512]{1,0:T(4,128)S(1)} %get-tuple-element.20.seg_ref, f32[3,4,512]{2,1,0:T(4,128)S(1)} %pad_maximum_fusion.3.got_ref, s32[1,512]{1,0:T(1,128)S(1)} %bitcast.33, ...), custom_call_target="tpu_custom_call" | custom-call | tf_op jit(solution)/shard_map/backward/pallas_call | solution.py:465
  66.6 1.7 %collective-permute-start.6 = (bf16[256,128]{1,0:T(8,128)(2,1)S(1)}, bf16[256,128]{1,0:T(8,128)(2,1)S(1)}, u32[]{:S(2)}, u32[]{:S(2)}) collective-permute-start(bf16[256,128]{1,0:T(8,128)(2,1)S(1)} %slice.133), channel_id=1, source_target_pairs={{0,4},{4,0},{8,12},{12,8},{16,20},{20,16},{24,28},{28,24},{1,5},{5... | collective-permute-start | bytes 196616 | tf_op jit(solution)/shard_map/ppermute | solution.py:38
  68.3 2.7 %collective-permute-done.6 = bf16[256,128]{1,0:T(8,128)(2,1)S(1)} collective-permute-done((bf16[256,128]{1,0:T(8,128)(2,1)S(1)}, bf16[256,128]{1,0:T(8,128)(2,1)S(1)}, u32[]{:S(2)}, u32[]{:S(2)}) %collective-permute-start.6) | collective-permute-done | bytes 65568 | tf_op jit(solution)/shard_map/ppermute | solution.py:38
  72.3 2.7 %collective-permute-done.7 = bf16[128,128]{1,0:T(8,128)(2,1)S(1)} collective-permute-done((bf16[128,128]{1,0:T(8,128)(2,1)S(1)}, bf16[128,128]{1,0:T(8,128)(2,1)S(1)}, u32[]{:S(2)}, u32[]{:S(2)}) %collective-permute-start.7) | collective-permute-done | bytes 32800 | tf_op jit(solution)/shard_map/ppermute | solution.py:38
  75.0 2.9 %collective-permute-start.8 = (bf16[64,128]{1,0:T(8,128)(2,1)S(1)}, bf16[64,128]{1,0:T(8,128)(2,1)S(1)}, u32[]{:S(2)}, u32[]{:S(2)}) collective-permute-start(bf16[64,128]{1,0:T(8,128)(2,1)S(1)} %slice.135), channel_id=1, source_target_pairs={{0,16},{4,20},{8,24},{12,28},{16,0},{20,4},{24,8},{28,12},{1,17},{... | collective-permute-start | bytes 49160 | tf_op jit(solution)/shard_map/ppermute | solution.py:38
  77.9 1.6 %collective-permute-start.12 = (f32[208,128]{1,0:T(8,128)S(1)}, f32[208,128]{1,0:T(8,128)S(1)}, u32[]{:S(2)}, u32[]{:S(2)}) collective-permute-start(f32[208,128]{1,0:T(8,128)S(1)} %add.42), channel_id=1, source_target_pairs={{0,2},{1,3},{2,0},{3,1},{4,6},{5,7},{6,4},{7,5},{8,10},{9,11},{10,... | collective-permute-start | bytes 319496 | tf_op jit(solution)/shard_map/ppermute | solution.py:38
  80.7 3.1 %collective-permute-done.10 = bf16[256,128]{1,0:T(8,128)(2,1)S(1)} collective-permute-done((bf16[256,128]{1,0:T(8,128)(2,1)S(1)}, bf16[256,128]{1,0:T(8,128)(2,1)S(1)}, u32[]{:S(2)}, u32[]{:S(2)}) %collective-permute-start.10) | collective-permute-done | bytes 65568 | tf_op jit(solution)/shard_map/ppermute | solution.py:38
  (62 shorter events, 15.9 us)
Async XLA Ops:
  0.6 6.0 %collective-permute-start = (bf16[64,128]{1,0:T(8,128)(2,1)}, bf16[64,128]{1,0:T(8,128)(2,1)S(1)}, u32[]{:S(2)}, u32[]{:S(2)}) collective-permute-start(bf16[64,128]{1,0:T(8,128)(2,1)} %param.11), channel_id=1, source_target_pairs={{0,16},{4,20},{8,24},{12,28},{16,0},{20,4},{24,8},{28,12},{1,17},{... | collective-permute-start | bytes 49160 | tf_op jit(solution)/shard_map/ppermute | solution.py:38
  7.4 5.2 %collective-permute-start.1 = (bf16[128,128]{1,0:T(8,128)(2,1)S(1)}, bf16[128,128]{1,0:T(8,128)(2,1)S(1)}, u32[]{:S(2)}, u32[]{:S(2)}) collective-permute-start(bf16[128,128]{1,0:T(8,128)(2,1)S(1)} %pad_maximum_fusion.2), channel_id=1, source_target_pairs={{0,8},{4,12},{8,0},{12,4},{16,24},{20,28},{24,16},{28,20},{1,9},{5... | collective-permute-start | bytes 98312 | tf_op jit(solution)/shard_map/ppermute | solution.py:38
  9.3 0.8 copy-start
  10.0 0.9 %copy-start.2 = (bf16[1,1024,128]{2,1,0:T(8,128)(2,1)S(1)}, bf16[1,1024,128]{2,1,0:T(8,128)(2,1)}, u32[]{:S(2)}) copy-start(bf16[1,1024,128]{2,1,0:T(8,128)(2,1)} %param.14) | copy-start | bytes 786436
  11.0 0.7 copy-start.5
  13.4 4.3 %collective-permute-start.2 = (bf16[256,128]{1,0:T(8,128)(2,1)S(1)}, bf16[256,128]{1,0:T(8,128)(2,1)S(1)}, u32[]{:S(2)}, u32[]{:S(2)}) collective-permute-start(bf16[256,128]{1,0:T(8,128)(2,1)S(1)} %pad_maximum_fusion.1), channel_id=1, source_target_pairs={{0,4},{4,0},{8,12},{12,8},{16,20},{20,16},{24,28},{28,24},{1,5},{5... | collective-permute-start | bytes 196616 | tf_op jit(solution)/shard_map/ppermute | solution.py:38
  18.4 0.7 copy-start.3
  19.1 0.7 copy-start.9
  19.8 0.7 copy-start.11
  29.1 3.7 %collective-permute-start.3 = (f32[4,512]{1,0:T(4,128)S(1)}, f32[4,512]{1,0:T(4,128)S(1)}, u32[]{:S(2)}, u32[]{:S(2)}) collective-permute-start(f32[4,512]{1,0:T(4,128)S(1)} %get-tuple-element.20.seg_ref), channel_id=1, source_target_pairs={{0,4},{4,0},{8,12},{12,8},{16,20},{20,16},{24,28},{28,24},{1,5},{5... | collective-permute-start | bytes 24584 | tf_op jit(solution)/shard_map/ppermute | solution.py:38
  32.8 3.7 %collective-permute-start.4 = (f32[4,512]{1,0:T(4,128)S(1)}, f32[4,512]{1,0:T(4,128)S(1)}, u32[]{:S(2)}, u32[]{:S(2)}) collective-permute-start(f32[4,512]{1,0:T(4,128)S(1)} %pad_maximum_fusion.4), channel_id=1, source_target_pairs={{0,8},{4,12},{8,0},{12,4},{16,24},{20,28},{24,16},{28,20},{1,9},{5... | collective-permute-start | bytes 24584 | tf_op jit(solution)/shard_map/ppermute | solution.py:38
  36.6 4.6 %collective-permute-start.5 = (f32[4,512]{1,0:T(4,128)S(1)}, f32[4,512]{1,0:T(4,128)S(1)}, u32[]{:S(2)}, u32[]{:S(2)}) collective-permute-start(f32[4,512]{1,0:T(4,128)S(1)} %pad_maximum_fusion.5), channel_id=1, source_target_pairs={{0,16},{4,20},{8,24},{12,28},{16,0},{20,4},{24,8},{28,12},{1,17},{... | collective-permute-start | bytes 24584 | tf_op jit(solution)/shard_map/ppermute | solution.py:38
  41.2 0.8 copy-start.1
  42.0 0.7 copy-start.4
  42.7 0.7 copy-start.6
  43.4 0.7 copy-start.7
  44.1 0.7 copy-start.8
  66.6 4.3 %collective-permute-start.6 = (bf16[256,128]{1,0:T(8,128)(2,1)S(1)}, bf16[256,128]{1,0:T(8,128)(2,1)S(1)}, u32[]{:S(2)}, u32[]{:S(2)}) collective-permute-start(bf16[256,128]{1,0:T(8,128)(2,1)S(1)} %slice.133), channel_id=1, source_target_pairs={{0,4},{4,0},{8,12},{12,8},{16,20},{20,16},{24,28},{28,24},{1,5},{5... | collective-permute-start | bytes 196616 | tf_op jit(solution)/shard_map/ppermute | solution.py:38
  71.0 4.0 %collective-permute-start.7 = (bf16[128,128]{1,0:T(8,128)(2,1)S(1)}, bf16[128,128]{1,0:T(8,128)(2,1)S(1)}, u32[]{:S(2)}, u32[]{:S(2)}) collective-permute-start(bf16[128,128]{1,0:T(8,128)(2,1)S(1)} %slice.134), channel_id=1, source_target_pairs={{0,8},{4,12},{8,0},{12,4},{16,24},{20,28},{24,16},{28,20},{1,9},{5... | collective-permute-start | bytes 98312 | tf_op jit(solution)/shard_map/ppermute | solution.py:38
  71.7 6.2 %collective-permute-start.11 = (f32[208,128]{1,0:T(8,128)S(1)}, f32[208,128]{1,0:T(8,128)S(1)}, u32[]{:S(2)}, u32[]{:S(2)}) collective-permute-start(f32[208,128]{1,0:T(8,128)S(1)} %get-tuple-element.29), channel_id=1, source_target_pairs={{0,1},{1,0},{2,3},{3,2},{4,5},{5,4},{6,7},{7,6},{8,9},{9,8},{10,11... | collective-permute-start | bytes 319496 | tf_op jit(solution)/shard_map/ppermute | solution.py:38
  71.7 7.7 %collective-permute-start.9 = (bf16[512,128]{1,0:T(8,128)(2,1)S(1)}, bf16[512,128]{1,0:T(8,128)(2,1)S(1)}, u32[]{:S(2)}, u32[]{:S(2)}) collective-permute-start(bf16[512,128]{1,0:T(8,128)(2,1)S(1)} %slice.131), channel_id=1, source_target_pairs={{0,1},{1,0},{2,3},{3,2},{4,5},{5,4},{6,7},{7,6},{8,9},{9,8},{10,11... | collective-permute-start | bytes 393224 | tf_op jit(solution)/shard_map/ppermute | solution.py:38
  75.0 5.1 %collective-permute-start.8 = (bf16[64,128]{1,0:T(8,128)(2,1)S(1)}, bf16[64,128]{1,0:T(8,128)(2,1)S(1)}, u32[]{:S(2)}, u32[]{:S(2)}) collective-permute-start(bf16[64,128]{1,0:T(8,128)(2,1)S(1)} %slice.135), channel_id=1, source_target_pairs={{0,16},{4,20},{8,24},{12,28},{16,0},{20,4},{24,8},{28,12},{1,17},{... | collective-permute-start | bytes 49160 | tf_op jit(solution)/shard_map/ppermute | solution.py:38
  77.9 6.6 %collective-permute-start.12 = (f32[208,128]{1,0:T(8,128)S(1)}, f32[208,128]{1,0:T(8,128)S(1)}, u32[]{:S(2)}, u32[]{:S(2)}) collective-permute-start(f32[208,128]{1,0:T(8,128)S(1)} %add.42), channel_id=1, source_target_pairs={{0,2},{1,3},{2,0},{3,1},{4,6},{5,7},{6,4},{7,5},{8,10},{9,11},{10,... | collective-permute-start | bytes 319496 | tf_op jit(solution)/shard_map/ppermute | solution.py:38
  79.5 4.3 %collective-permute-start.10 = (bf16[256,128]{1,0:T(8,128)(2,1)S(1)}, bf16[256,128]{1,0:T(8,128)(2,1)S(1)}, u32[]{:S(2)}, u32[]{:S(2)}) collective-permute-start(bf16[256,128]{1,0:T(8,128)(2,1)S(1)} %slice.132), channel_id=1, source_target_pairs={{0,2},{1,3},{2,0},{3,1},{4,6},{5,7},{6,4},{7,5},{8,10},{9,11},{10,... | collective-permute-start | bytes 196616 | tf_op jit(solution)/shard_map/ppermute | solution.py:38
  (3 other events, 2.0 us)

commit v2 on v0

v2 whole, which is shorter than its diff:
```python
import functools

import jax
import jax.numpy as jnp
from jax import lax
from jax.experimental import pallas as pl
from jax.experimental.pallas import tpu as pltpu
from jax.sharding import PartitionSpec as P

step_length = 0.002
f32 = jnp.float32
bf16 = jnp.bfloat16
vmem_bytes = 24 * 1024 * 1024
exact = lax.Precision.HIGHEST


def bits_of(count):
    bits = count.bit_length() - 1
    assert count == 1 << bits
    return bits


def swap_order(count, descending):
    order = [0]
    for b in reversed(range(bits_of(count))) if descending else range(bits_of(count)):
        order = order + [t ^ (1 << b) for t in order]
    return order


def halving_order(count):
    order = [0]
    for b in reversed(range(bits_of(count))):
        order = order + [t ^ (1 << b) for t in order]
    return order


def split_dot(a, b, dot):
    high = a.astype(bf16)
    low = (a - high.astype(f32)).astype(bf16)
    return dot(high, b) + dot(low, b)


def nt_dot(a, b, precision=None):
    return lax.dot_general(
        a, b, (((1,), (1,)), ((), ())), precision=precision, preferred_element_type=f32
    )


def nn_dot(a, b, precision=None):
    return jnp.dot(a, b, precision=precision, preferred_element_type=f32)


def swap(array, axis, size, distance):
    return lax.ppermute(array, axis, [(i, i ^ distance) for i in range(size)])


def sum_dot(ones, b):
    high = b.astype(bf16)
    low = (b - high.astype(f32)).astype(bf16)
    return nn_dot(ones, high) + nn_dot(ones, low)


def call(kernel, out_shape, name, scratch=(), flops=0):
    def run(*operands):
        return pl.pallas_call(
            kernel,
            out_shape=out_shape,
            in_specs=[pl.BlockSpec(memory_space=pltpu.VMEM)] * len(operands),
            out_specs=jax.tree.map(lambda _: pl.BlockSpec(memory_space=pltpu.VMEM), out_shape),
            scratch_shapes=list(scratch),
            compiler_params=pltpu.CompilerParams(vmem_limit_bytes=vmem_bytes),
            cost_estimate=pl.CostEstimate(flops=flops, bytes_accessed=1 << 20, transcendentals=0),
            name=name,
        )(*operands)

    return run


def low_rows(width, samples):
    starts = {"w": 0, "sample": width, "w_out": width + samples}
    sizes = {"w": width, "sample": samples, "w_out": 16}
    return {name: slice(at, at + sizes[name]) for name, at in starts.items()}


def line_rows(slots, channels):
    return {
        "ids": 0,
        "occ": slots,
        "direction": slots + 1,
        "target": slots + 2,
        "b_out": slots + 2 + channels,
    }


def turn_kernel(brick_ref, ray_ref, brick_t_ref, own_ref):
    brick_t_ref[...] = brick_ref[...].astype(f32).T.astype(bf16)
    own_ref[...] = ray_ref[...]


def prepare_kernel(
    brick_t_ref,
    w_ref,
    sample_ref,
    w_out_ref,
    ids_ref,
    occ_ref,
    direction_ref,
    target_ref,
    b_ref,
    b_out_ref,
    low_ref,
    lines_ref,
    w_t_ref,
    s_ref,
    wide_ref,
    left_ref,
    chosen_ref,
    project_ref,
    *,
    rows,
    lines,
):
    slots, rays = ids_ref.shape
    width = w_t_ref.shape[0]
    samples = s_ref.shape[0]
    outs = w_out_ref.shape[0]
    bricks = brick_t_ref.shape[1]
    w = w_ref[...]
    w_out = w_out_ref[...].astype(f32)
    low_ref[rows["w"], :] = w
    low_ref[rows["sample"], :] = sample_ref[...]
    low_ref[rows["w_out"], :] = jnp.concatenate(
        [w_out, jnp.zeros((16 - outs, width), f32)], 0
    ).astype(bf16)
    lines_ref[:slots, :] = ids_ref[...].astype(f32)
    lines_ref[lines["occ"] : lines["occ"] + 1, :] = occ_ref[...].astype(f32)
    lines_ref[lines["direction"] : lines["direction"] + 1, :] = direction_ref[...].astype(f32)
    lines_ref[lines["target"] : lines["target"] + outs - 1, :] = target_ref[...]
    lines_ref[lines["b_out"] : lines["b_out"] + 1, :outs] = b_out_ref[...]
    w_t = w.astype(f32).T.astype(bf16)
    w_t_ref[...] = w_t
    s = nn_dot(sample_ref[...], w) + b_ref[...]
    s_ref[...] = s.astype(bf16).astype(f32)
    s_t = jnp.concatenate([s] * (128 // samples), 0).T
    for j in range(samples):
        wide_ref[j] = jnp.broadcast_to(s_t[:, j : j + 1], (width, 128)).astype(bf16)
    w_rows = jnp.concatenate(
        [jnp.broadcast_to(w_out[c : c + 1, :], (8, width)) for c in range(outs)], 0
    )
    row8 = lax.broadcasted_iota(jnp.int32, (outs * 8, width), 0) % 8
    for i in range(8):
        left_ref[:, i * width : (i + 1) * width] = jnp.where(row8 == i, w_rows, 0.0).astype(bf16)
    row = lax.broadcasted_iota(jnp.int32, (bricks, rays), 0)
    for k in range(slots):
        one_hot = jnp.where(row == ids_ref[k : k + 1, :], 1.0, 0.0).astype(bf16)
        chosen = nn_dot(brick_t_ref[...], one_hot).astype(bf16)
        chosen_ref[:, k * rays : (k + 1) * rays] = chosen
        project_ref[:, k * rays : (k + 1) * rays] = nn_dot(w_t, chosen)


def forward_kernel(*refs, owners, second, lines):
    ray_ref, project_ref, w_t_ref, wide_ref, left_ref, lines_ref, *refs = refs
    if second:
        before_refs, refs = refs[:4], refs[4:]
    seg_ref, kept_ref, u_ref, sorted_ref, order_ref, ut_ref, raw_ref = refs
    width, total = project_ref.shape
    samples = wide_ref.shape[0]
    outs = seg_ref.shape[0]
    half, rays = ray_ref.shape[0], lines_ref.shape[1]
    slots = total // rays
    blocks = owners // 2
    own = half // blocks
    me = lax.axis_index("slab")
    side = me // blocks
    if second:
        first_half = pl.multiple_of(side * half, half)
        for old, new in zip(before_refs[:2], (seg_ref, kept_ref)):
            for k in range(old.shape[-1] // half):
                lanes = pl.ds(pl.multiple_of(k * rays + first_half, half), half)
                new[..., lanes] = old[..., k * half : (k + 1) * half]
        for old, new in zip(before_refs[2:], (u_ref, sorted_ref)):
            for k in range(old.shape[0] // half):
                rows = pl.ds(pl.multiple_of(k * rays + first_half, half), half)
                new[rows, :] = old[k * half : (k + 1) * half, :]
        side = 1 - side
    here = pl.multiple_of(side * half, half)
    stride = rays if second else half
    base = here if second else 0

    def spot(offset, size):
        return pl.ds(pl.multiple_of(offset + base, 128), size) if second else pl.ds(offset, size)

    for i in range(blocks):
        place = pl.multiple_of(((me ^ i) & (blocks - 1)) * own, own)
        order_ref[pl.ds(place, own), :] = ray_ref[i * own : (i + 1) * own, :]
    sorted_ref[spot(0, half), :] = order_ref[...]
    ray_t = nt_dot(w_t_ref[...], order_ref[...])
    for k in range(slots):
        lanes = pl.ds(pl.multiple_of(k * rays + here, half), half)
        part = (project_ref[:, lanes] + ray_t).astype(bf16)
        ut_ref[:, k * half : (k + 1) * half] = part
        u_ref[spot(k * stride, half), :] = part.astype(f32).T.astype(bf16)
    b_out = [lines_ref[lines["b_out"], c] for c in range(outs)]

    def shade_block(block, carry):
        for n in range(slots * half // 256):
            lanes = slice(n * 256, n * 256 + 256)
            ut = ut_ref[:, lanes]
            acc = None
            for i in range(4):
                parts = []
                for h in range(2):
                    column = wide_ref[block * 8 + 2 * i + h]
                    column = jnp.concatenate([column, column], 1)
                    parts.append(jnp.maximum(ut + column, 0))
                left = left_ref[:, 2 * i * width : 2 * (i + 1) * width]
                term = nn_dot(left, jnp.concatenate(parts, 0))
                acc = term if acc is None else acc + term
            for c in range(outs):
                raw_ref[c, pl.ds(pl.multiple_of(block * 8, 8), 8), lanes] = (
                    acc[c * 8 : c * 8 + 8, :] + b_out[c]
                )
        return carry

    lax.fori_loop(0, samples // 8, shade_block, 0, unroll=4)
    r_i = lax.broadcasted_iota(jnp.int32, (samples, samples), 0)
    c_i = lax.broadcasted_iota(jnp.int32, (samples, samples), 1)
    earlier = jnp.where(c_i < r_i, 1.0, 0.0).astype(bf16)
    chunk = 128
    occ_row = lines["occ"]
    for n in range(half // chunk):
        occ = lines_ref[occ_row : occ_row + 1, pl.ds(pl.multiple_of(here + n * chunk, chunk), chunk)]
        raws = [
            raw_ref[0, :, k * half + n * chunk : k * half + (n + 1) * chunk] for k in range(slots)
        ]
        occupied = [(k < occ).astype(f32) for k in range(slots)]
        opticals = [
            step_length * (jnp.maximum(x, 0.0) + jnp.log1p(jnp.exp(-jnp.abs(x)))) * o
            for x, o in zip(raws, occupied)
        ]
        enters = sum_dot(earlier, jnp.concatenate(opticals, 1))
        before = jnp.zeros((1, chunk), f32)
        colors = [jnp.zeros((1, chunk), f32)] * (outs - 1)
        for k in range(slots):
            local = slice(k * half + n * chunk, k * half + (n + 1) * chunk)
            lanes = spot(k * stride + n * chunk, chunk)
            optical = opticals[k]
            entered = enters[:, k * chunk : (k + 1) * chunk] + before
            before = before + jnp.sum(optical, 0, keepdims=True)
            tanh = jnp.tanh(0.5 * optical)
            weight = jnp.exp(-entered) * (2.0 * tanh / (1.0 + tanh))
            for c in range(outs - 1):
                shading = jax.nn.sigmoid(raw_ref[c + 1, :, local])
                light = weight * shading
                colors[c] = colors[c] + jnp.sum(light, 0, keepdims=True)
                kept_ref[c, :, lanes] = shading
                kept_ref[outs + c, :, lanes] = light
            kept_ref[outs - 1, :, lanes] = jnp.exp(-(entered + optical))
            kept_ref[2 * outs - 1, :, lanes] = step_length * occupied[k] * jax.nn.sigmoid(raws[k])
        place = spot(n * chunk, chunk)
        for c in range(outs - 1):
            seg_ref[c : c + 1, place] = colors[c]
        seg_ref[outs - 1 : outs, place] = jnp.exp(-before)


def coefficient_kernel(seg_ref, kept_ref, coef_ref, turned_ref):
    outs, rays = seg_ref.shape
    samples, total = kept_ref.shape[1:]
    slots = total // rays
    r_i = lax.broadcasted_iota(jnp.int32, (samples, samples), 0)
    c_i = lax.broadcasted_iota(jnp.int32, (samples, samples), 1)
    later = jnp.where(c_i > r_i, 1.0, 0.0).astype(bf16)
    chunk = 128

    def keep(index, lanes, value):
        coef_ref[index, :, lanes] = value
        turned_ref[index, lanes, :] = jnp.concatenate([value] * (128 // samples), 0).T

    for n in range(rays // chunk):
        through = seg_ref[outs - 1 : outs, n * chunk : (n + 1) * chunk]
        after = [jnp.zeros((1, chunk), f32)] * (outs - 1)
        for k in reversed(range(slots)):
            lanes = slice(k * rays + n * chunk, k * rays + (n + 1) * chunk)
            passed = kept_ref[outs - 1, :, lanes]
            density = kept_ref[2 * outs - 1, :, lanes]
            lights = [kept_ref[outs + c, :, lanes] for c in range(outs - 1)]
            behinds = sum_dot(later, jnp.concatenate(lights, 1))
            for c in range(outs - 1):
                shading = kept_ref[c, :, lanes]
                light = lights[c]
                behind = behinds[:, c * chunk : (c + 1) * chunk] + after[c]
                after[c] = after[c] + jnp.sum(light, 0, keepdims=True)
                keep(c, lanes, density * (shading * passed - behind))
                keep(outs + c, lanes, light * (1.0 - shading))
            keep(outs - 1, lanes, density * through)


def basis_kernel(turned_ref, u_ref, s_ref, h1_ref, *, slot):
    count, rays, width = h1_ref.shape
    samples = s_ref.shape[0]
    negative = (-s_ref[...]).astype(bf16)
    one = jnp.ones((samples, width), bf16)
    zero = jnp.zeros((samples, width), bf16)
    lane = lax.broadcasted_iota(jnp.int32, (8, 8 * samples), 1) // samples
    row = lax.broadcasted_iota(jnp.int32, (8, 8 * samples), 0)
    block_mask = lane == row
    repeat = 8 * samples // 128
    step = 128

    def slot_block(block, carry):
        for h in range(step // 16):
            base = pl.multiple_of(block * step + h * 16, 16)
            u16 = u_ref[pl.ds(slot * rays + base, 16), :]
            for q in range(2):
                at = pl.multiple_of(block * step + h * 16 + q * 8, 8)
                left = [
                    jnp.where(
                        block_mask,
                        jnp.concatenate([turned_ref[c, pl.ds(slot * rays + at, 8), :]] * repeat, 1),
                        0.0,
                    )
                    for c in range(count)
                ]
                left = jnp.concatenate(left, 0).astype(bf16)
                tiles = [
                    jnp.where(
                        jnp.broadcast_to(u16[q * 8 + i : q * 8 + i + 1, :], (samples, width))
                        > negative,
                        one,
                        zero,
                    )
                    for i in range(8)
                ]
                h1 = nn_dot(left, jnp.concatenate(tiles, 0))
                for c in range(count):
                    h1_ref[c, pl.ds(at, 8), :] = h1[c * 8 : c * 8 + 8, :]
        return carry

    lax.fori_loop(0, rays // step, slot_block, 0)


def merge(first, second, forward):
    fc, ft = first
    sc, st = second
    return jnp.where(forward, fc + ft * sc, sc + st * fc), ft * st


def middle_kernel(*refs, owners, slots, rows, lines):
    bits = bits_of(owners)
    seg_ref, refs = refs[0], refs[1:]
    got_refs, refs = refs[:bits], refs[bits:]
    h1_refs, refs = refs[:slots], refs[slots:]
    lines_ref, low_ref, *refs = refs
    keep_ref, send_ref, moved_ref, slot_ref, cot_ref, ray_ref = refs
    me = lax.axis_index("slab")
    outs = seg_ref.shape[0]
    channels = outs - 1
    rays = lines_ref.shape[1]
    width = low_ref.shape[1]
    forward = lines_ref[lines["direction"] : lines["direction"] + 1, :] == 0.0
    target = lines_ref[lines["target"] : lines["target"] + channels, :]

    def pair(values):
        return values[:channels, :], values[channels : channels + 1, :]

    low = high = None
    for b in reversed(range(bits)):
        piece = pair(got_refs[b][...])
        is_low = ((me >> b) & 1) == 1
        piece = (jnp.where(is_low, piece[0], 0.0), jnp.where(is_low, piece[1], 1.0))
        low = piece if low is None else merge(low, piece, forward)
    for b in range(bits):
        piece = pair(got_refs[b][...])
        is_high = ((me >> b) & 1) == 0
        piece = (jnp.where(is_high, piece[0], 0.0), jnp.where(is_high, piece[1], 1.0))
        high = piece if high is None else merge(high, piece, forward)
    seg_color, seg_trans = pair(seg_ref[...])
    before_color = jnp.where(forward, low[0], high[0])
    before_trans = jnp.where(forward, low[1], high[1])
    after_color = jnp.where(forward, high[0], low[0])
    color = before_color + before_trans * (seg_color + seg_trans * after_color)
    residual = color - target
    color_cot = before_trans * residual
    trans_cot = -before_trans * jnp.sum(after_color * residual, 0, keepdims=True)
    cot_ref[:channels, :] = color_cot
    cot_ref[channels:outs, :] = trans_cot
    cot_ref[outs : outs + channels, :] = color
    cot_ref[outs + channels :, :] = jnp.zeros((8 - outs - channels, rays), f32)
    w_out = low_ref[rows["w_out"], :].astype(f32)
    w_rows = [w_out[c : c + 1, :] for c in range(outs)]
    w = low_ref[rows["w"], :]
    chunk = 128
    for n in range(rays // chunk):
        these = slice(n * chunk, (n + 1) * chunk)
        turned = cot_ref[:, these].T
        cots = [jnp.broadcast_to(turned[:, c : c + 1], (chunk, width)) for c in range(outs)]
        whole = None
        for k in range(slots):
            at = slice(k * rays + n * chunk, k * rays + (n + 1) * chunk)
            h1_ref = h1_refs[k]
            parts = [sum(cots[c] * h1_ref[c, these, :] for c in range(outs))]
            parts += [cots[c] * h1_ref[outs + c, these, :] for c in range(channels)]
            grad = sum(w_rows[c] * parts[c] for c in range(outs))
            slot_ref[at, :] = grad
            whole = grad if whole is None else whole + grad
            moved_ref[at, :] = split_dot(grad, w, nt_dot)
    own = rays // owners
    moved = moved_ref[:rays, :]
    for k in range(1, slots):
        moved = moved + moved_ref[k * rays : (k + 1) * rays, :]
    ray_ref[...] = moved
    for i, t in enumerate(halving_order(owners)):
        place = pl.multiple_of((me ^ t) * own, own)
        if i < owners // 2:
            keep_ref[i * own : (i + 1) * own, :] = ray_ref[pl.ds(place, own), :]
        else:
            at = i * own - rays // 2
            send_ref[at : at + own, :] = ray_ref[pl.ds(place, own), :].astype(bf16)


def brick_kernel(lines_ref, moved_ref, keep_ref, send_ref, *, shares):
    share = lax.axis_index("ray")
    rays = lines_ref.shape[1]
    total, width = moved_ref.shape
    slots = total // rays
    half = keep_ref.shape[0]
    part = 2 * half // shares
    moved = moved_ref[...]
    high = moved.astype(bf16)
    low = (moved - high.astype(f32)).astype(bf16)
    row = lax.broadcasted_iota(jnp.int32, (part, rays), 0).astype(f32)
    for i, t in enumerate(halving_order(shares)):
        first = ((share ^ t) * part).astype(f32)
        acc = jnp.zeros((part, width), f32)
        for k in range(slots):
            one_hot = jnp.where(row + first == lines_ref[k : k + 1, :], 1.0, 0.0).astype(bf16)
            rows = slice(k * rays, (k + 1) * rays)
            acc = acc + nn_dot(one_hot, high[rows]) + nn_dot(one_hot, low[rows])
        ref, at = (keep_ref, i * part) if i < shares // 2 else (send_ref, i * part - half)
        ref[at : at + part, :] = acc


def sample_kernel(
    cot_ref, coef_ref, u_ref, s_ref, low_ref, by_sample_ref, sums_ref, bias_ref, g_ref, *, first, rows
):
    outs = sums_ref.shape[0]
    channels = outs - 1
    rays = cot_ref.shape[1]
    total, width = u_ref.shape
    samples = by_sample_ref.shape[0]
    bias_sums = [jnp.zeros((1, 128), f32)] * outs
    for n in range(total // 128):
        lanes = slice(n * 128, n * 128 + 128)
        at = (n * 128) % rays
        cots = [cot_ref[c : c + 1, at : at + 128] for c in range(outs)]
        grads = [sum(cots[c] * coef_ref[c, first : first + samples, lanes] for c in range(outs))]
        for c in range(channels):
            grads.append(cots[c] * coef_ref[outs + c, first : first + samples, lanes])
        for c in range(outs):
            bias_sums[c] = bias_sums[c] + jnp.sum(grads[c], 0, keepdims=True)
        for j in range(0, samples, 8):
            g_ref[j // 8, :, lanes] = jnp.concatenate([g[j : j + 8] for g in grads], 0).astype(bf16)
    w_out = low_ref[rows["w_out"], :].astype(f32)
    w_rows = [w_out[c : c + 1, :] for c in range(outs)]
    row8 = lax.broadcasted_iota(jnp.int32, (8, width), 0)

    def sample_block(block, sums):
        left = g_ref[block]
        s8 = s_ref[pl.ds(pl.multiple_of(first + block * 8, 8), 8), :]
        acc = [jnp.zeros((8, width), f32)] * outs
        for i in range(0, 8, 2):
            edges = [(-s8[i + h : i + h + 1, :]).astype(bf16) for h in range(2)]
            h2 = None
            for n in range(total // 256):
                u = u_ref[n * 256 : n * 256 + 256, :]
                live = [
                    jnp.where(
                        u > jnp.broadcast_to(edge, u.shape),
                        jnp.ones(u.shape, bf16),
                        jnp.zeros(u.shape, bf16),
                    )
                    for edge in edges
                ]
                term = nn_dot(left[:, n * 256 : n * 256 + 256], jnp.concatenate(live, 1))
                h2 = term if h2 is None else h2 + term
            for c in range(outs):
                for h in range(2):
                    piece = h2[c * 8 : c * 8 + 8, h * width : (h + 1) * width]
                    acc[c] = acc[c] + jnp.where(row8 == i + h, piece, 0.0)
        by_sample_ref[pl.ds(pl.multiple_of(block * 8, 8), 8), :] = sum(
            w_rows[c] * acc[c] for c in range(outs)
        )
        return tuple(sums[c] + s8 * acc[c] for c in range(outs))

    sums = [jnp.zeros((8, width), f32)] * outs
    sums = lax.fori_loop(0, samples // 8, sample_block, tuple(sums), unroll=2)
    for c in range(outs):
        sums_ref[c] = sums[c]
        bias_ref[c : c + 1, :] = bias_sums[c]


def network_kernel(*refs, parts, slots, rows, owners):
    part_refs, refs = refs[: 3 * parts], refs[3 * parts :]
    h1_refs, refs = refs[:slots], refs[slots:]
    cot_ref, u_ref, slot_ref, chosen_ref, sorted_ref, low_ref, small_ref, color_ref = refs
    by_sample = jnp.concatenate([part_refs[3 * i][...] for i in range(parts)], 0)
    samples, width = by_sample.shape
    rays = sorted_ref.shape[0]
    outs = color_ref.shape[0] + 1
    channels = outs - 1
    own = rays // owners
    me = lax.axis_index("slab")
    r_i = lax.broadcasted_iota(jnp.int32, (rays, own), 0)
    c_i = lax.broadcasted_iota(jnp.int32, (rays, own), 1)
    pick = jnp.where(r_i == c_i + me * own, 1.0, 0.0).astype(f32)
    color_ref[...] = nn_dot(cot_ref[outs : outs + channels, :], pick, exact)
    sums = [jnp.zeros((8, width), f32)] * outs
    chunk = 128
    for n in range(rays // chunk):
        these = slice(n * chunk, (n + 1) * chunk)
        turned = cot_ref[:, these].T
        cots = [jnp.broadcast_to(turned[:, c : c + 1], (chunk, width)) for c in range(outs)]
        for k in range(slots):
            u = u_ref[k * rays + n * chunk : k * rays + (n + 1) * chunk, :].astype(f32)
            h1_ref = h1_refs[k]
            products = [sum(cots[c] * h1_ref[c, these, :] for c in range(outs))]
            products += [cots[c] * h1_ref[outs + c, these, :] for c in range(channels)]
            for c in range(outs):
                sums[c] = sums[c] + jnp.sum((u * products[c]).reshape(chunk // 8, 8, width), 0)
    w = low_ref[rows["w"], :]
    sample = low_ref[rows["sample"], :].astype(f32)
    slot = slot_ref[...]
    slot_ray = slot[:rays, :]
    for k in range(1, slots):
        slot_ray = slot_ray + slot[k * rays : (k + 1) * rays, :]
    ray_t = sorted_ref[...].astype(f32).T.astype(bf16)
    sample_t = jnp.concatenate([sample] * (128 // samples), 0).T[:, :samples]

    def flipped(a, b):
        return nn_dot(b, a)

    small_ref[:samples, :] = split_dot(by_sample, w, nt_dot)
    small_ref[samples : samples + width, :] = (
        split_dot(slot, chosen_ref[...], flipped)
        + split_dot(slot_ray, ray_t, flipped)
        + split_dot(by_sample, sample_t.astype(bf16), flipped)
    )
    at = samples + width
    small_ref[at : at + 1, :] = jnp.sum(by_sample, 0, keepdims=True)
    lane128 = lax.broadcasted_iota(jnp.int32, (1, 128), 1)
    bias = jnp.zeros((1, 128), f32)
    for c in range(outs):
        total = sums[c] + sum(part_refs[3 * i + 1][c] for i in range(parts))
        small_ref[at + 1 + c : at + 2 + c, :] = jnp.sum(total, 0, keepdims=True)
        row = sum(part_refs[3 * i + 2][c : c + 1, :] for i in range(parts))
        bias = bias + jnp.where(lane128 == c, jnp.sum(row, 1, keepdims=True), 0.0)
    small_ref[at + 1 + outs : at + 2 + outs, :] = bias
    rest = small_ref.shape[0] - (at + 2 + outs)
    small_ref[at + 2 + outs :, :] = jnp.zeros((rest, width), f32)


def finish_kernel(
    ray_ref,
    ray_got_ref,
    brick_ref,
    sent_ref,
    got_ref,
    ray_out_ref,
    brick_out_ref,
    sample_ref,
    w_ref,
    b_ref,
    w_out_ref,
    b_out_ref,
):
    ray_out_ref[...] = ray_ref[...] + ray_got_ref[...].astype(f32)
    part = brick_ref.shape[0]
    brick_out_ref[...] = brick_ref[...] + got_ref[:part, :].astype(f32)
    small = sent_ref[part:, :].astype(f32) + got_ref[part:, :].astype(f32)
    samples, width = sample_ref.shape
    outs = w_out_ref.shape[0]
    at = samples + width
    sample_ref[...] = small[:samples]
    w_ref[...] = small[samples:at]
    b_ref[...] = small[at : at + 1]
    w_out_ref[...] = small[at + 1 : at + 1 + outs]
    b_out_ref[...] = small[at + 1 + outs : at + 2 + outs, :outs]


def body(
    ray_code,
    direction,
    target,
    brick_code,
    sample_code,
    w_hidden,
    b_hidden,
    w_out,
    b_out,
    brick_ids,
    occupancy,
):
    owners = lax.axis_size("slab")
    shares = lax.axis_size("ray")
    me = lax.axis_index("slab")
    ids = brick_ids[0]
    slots, rays = ids.shape
    total = slots * rays
    bricks, width = brick_code.shape[1:]
    samples = sample_code.shape[1]
    outs = w_out.shape[1]
    channels = outs - 1
    count = outs + channels

    def shaped(*shape):
        return jax.ShapeDtypeStruct(shape, f32)

    def shaped16(*shape):
        return jax.ShapeDtypeStruct(shape, bf16)

    rows = low_rows(width, samples)
    lines = line_rows(slots, channels)
    brick_t, gathered = call(
        turn_kernel,
        (shaped16(width, bricks), shaped16(*ray_code.shape)),
        "turn",
        flops=1 << 34,
    )(brick_code[0], ray_code)
    low, packed, w_t, s, wide, left, chosen, project = call(
        functools.partial(prepare_kernel, rows=rows, lines=lines),
        (
            shaped16(rows["w_out"].stop, width),
            shaped(lines["b_out"] + 1, rays),
            shaped16(width, width),
            shaped(samples, width),
            shaped16(samples, width, 128),
            shaped16(outs * 8, 8 * width),
            shaped16(width, total),
            shaped(width, total),
        ),
        "prepare",
        flops=1 << 31,
    )(
        brick_t,
        w_hidden[0],
        sample_code[0],
        w_out[0],
        ids,
        occupancy,
        direction[None],
        target,
        b_hidden,
        b_out,
    )
    other = swap(ray_code, "slab", owners, 1)
    for b in range(1, bits_of(owners)):
        gathered = jnp.concatenate([gathered, other], 0)
        other = swap(gathered, "slab", owners, 1 << b)
    passes = ()
    for second, part in enumerate((gathered, other)):
        wide_rays = rays if second else rays // 2
        passes = call(
            functools.partial(forward_kernel, owners=owners, second=second, lines=lines),
            (
                shaped(outs, wide_rays),
                shaped(2 * outs, samples, slots * wide_rays),
                shaped16(slots * wide_rays, width),
                shaped16(wide_rays, width),
            ),
            "forward",
            scratch=(
                pltpu.VMEM((rays // 2, width), bf16),
                pltpu.VMEM((width, total // 2), bf16),
                pltpu.VMEM((outs, samples, total // 2), f32),
            ),
            flops=1 << 30,
        )(part, project, w_t, wide, left, packed, *passes)
    seg, kept, u, ray_sorted = passes

    coef, turned = call(
        coefficient_kernel,
        (shaped(count, samples, total), shaped(count, total, 128)),
        "coefficients",
        flops=1 << 31,
    )(seg, kept)
    basis = [
        call(
            functools.partial(basis_kernel, slot=k),
            shaped(count, rays, width),
            "basis",
            flops=1 << 31,
        )(turned, u, s)
        for k in range(slots)
    ]

    forward = packed[lines["direction"]][None] == 0.0
    group = (seg[:channels], seg[channels:])
    received = []
    for b in range(bits_of(owners)):
        sent = jnp.concatenate(group, 0) if b > 0 else seg
        other = swap(sent, "slab", owners, 1 << b)
        received.append(other)
        theirs = (other[:channels], other[channels:])
        upper = ((me >> b) & 1) == 1
        first = jax.tree.map(lambda a, b: jnp.where(upper, b, a), group, theirs)
        second = jax.tree.map(lambda a, b: jnp.where(upper, a, b), group, theirs)
        group = merge(first, second, forward)

    ray_keep, ray_send, moved, slot_grad, cots = call(
        functools.partial(middle_kernel, owners=owners, slots=slots, rows=rows, lines=lines),
        (
            shaped(rays // 2, width),
            shaped16(rays // 2, width),
            shaped(total, width),
            shaped(total, width),
            shaped(8, rays),
        ),
        "middle",
        scratch=(pltpu.VMEM((rays, width), f32),),
        flops=1 << 31,
    )(seg, *received, *basis, packed, low)
    def merged(keep, got):
        half = keep.shape[0] // 2
        return keep[:half] + got[:half].astype(f32), (keep[half:] + got[half:].astype(f32)).astype(bf16)

    def part_by_sample(i, cots):
        return call(
            functools.partial(sample_kernel, first=i * samples // parts, rows=rows),
            (
                shaped(samples // parts, width),
                shaped(outs, 8, width),
                shaped(outs, 128),
            ),
            "by_sample",
            scratch=(pltpu.VMEM((samples // parts // 8, outs * 8, total), bf16),),
            flops=1 << 28,
        )(cots, coef, u, s, low)

    parts = 2
    by_part = []
    later_cots = cots
    for b in range(bits_of(owners)):
        ray_got = swap(ray_send, "slab", owners, 1 << b)
        if b < parts:
            by_part += part_by_sample(b, later_cots)
        if b + 1 < bits_of(owners):
            ray_got, later_cots, moved = lax.optimization_barrier((ray_got, later_cots, moved))
            ray_keep, ray_send = merged(ray_keep, ray_got)
    brick_keep, brick_send = call(
        functools.partial(brick_kernel, shares=shares),
        (shaped(bricks // 2, width), shaped(bricks // 2, width)),
        "bricks",
        flops=1 << 28,
    )(packed, moved)
    small_rows = -(-(samples + width + 2 + outs) // 16) * 16
    small, color_own = call(
        functools.partial(network_kernel, parts=parts, slots=slots, rows=rows, owners=owners),
        (shaped(small_rows, width), shaped(channels, rays // owners)),
        "network",
        flops=1 << 28,
    )(*by_part, *basis, cots, u, slot_grad, chosen, ray_sorted, low)

    brick = brick_keep + swap(brick_send, "ray", shares, 1)
    small = small + swap(small, "ray", shares, 1)
    for b in range(1, bits_of(shares)):
        half = brick.shape[0] // 2
        sent = jnp.concatenate([brick[half:], small], 0).astype(bf16)
        other = swap(sent, "ray", shares, 1 << b)
        brick = brick[:half]
        if b + 1 < bits_of(shares):
            brick = brick + other[:half].astype(f32)
            small = sent[half:].astype(f32) + other[half:].astype(f32)
    ray_out, brick_out, sample_out, w_grad, b_grad, w_out_grad, b_out_grad = call(
        finish_kernel,
        (
            shaped(rays // owners, width),
            shaped(bricks // shares, width),
            shaped(samples, width),
            shaped(width, width),
            shaped(1, width),
            shaped(outs, width),
            shaped(1, outs),
        ),
        "finish",
    )(ray_keep, ray_got, brick, sent, other)
    return (
        color_own,
        ray_out,
        brick_out[None],
        sample_out[None],
        w_grad[None],
        b_grad,
        w_out_grad[None],
        b_out_grad,
    )


def solution(mesh):
    in_specs = (
        P(("ray", "slab"), None),
        P("ray"),
        P(None, "ray"),
        P("slab", None, None),
        P("slab", None, None),
        P("slab", None, None),
        P("slab", None),
        P("slab", None, None),
        P("slab", None),
        P("slab", None, "ray"),
        P("slab", "ray"),
    )
    out_specs = (
        P(None, ("ray", "slab")),
        P(("ray", "slab"), None),
        P("slab", "ray", None),
        P("slab", None, None),
        P("slab", None, None),
        P("slab", None),
        P("slab", None, None),
        P("slab", None),
    )
    return jax.shard_map(body, mesh=mesh, in_specs=in_specs, out_specs=out_specs, check_vma=False)
```

time: 384 us -> 54.8 us (0.14)
  blocking collectives: 100 us -> 0 us
  matrix products: 87.2 us -> 0 us
  waiting for transfers between devices: 76.9 us -> 12.2 us
  other arithmetic: 52.8 us -> 0.17 us
  local copies, waits for them, and re-layouts: 47.1 us -> 2.29 us
  Pallas kernels: 0 us -> 19.9 us
  starting transfers between devices: 0.12 us -> 19.1 us
  between operations: 15.7 us -> 0.92 us
    all_gather x3 -> x0, blocking collectives: 89 us -> none  [the longest x1 32.5 us: body(): ray_rows_all = lax.all_gather(ray_code, 'slab', axis=0, tiled=True)]
    dot_general x32 -> x0, matrix products: 87.2 us -> none  [the longest x8 23.4 us: shade_forward(): jnp.einsum('cd,nd->cn', out_w, hidden, preferred_element_type=jnp.float32)]
    reduce_scatter x2 -> x0, waiting for transfers between devices: 58 us -> none  [the longest x1 34.4 us: body(): lax.psum_scatter(ray_grads.reshape(total_rays, feature_width), 'slab', sc...]
    convert_element_type x32 -> x2, other arithmetic: 25 us -> 0.03 us  [merged(): (keep[half:] + got[half:].astype(f32)).astype(bf16)]
    reduce_sum x29 -> x0, other arithmetic: 20 us -> none  [the longest x4 15.6 us: backward_block(): jnp.sum(per_position, axis=(0, 1))]
    pallas_call x0 -> x13, Pallas kernels: none -> 19.9 us  [run(): pl.pallas_call(kernel, out_shape=out_shape, in_specs=[pl.BlockSpec(memory...]
    ppermute x0 -> x12, starting transfers between devices: none -> 19.1 us  [swap(): return lax.ppermute(array, axis, [(i, i ^ distance) for i in range(size)])]
    psum x1 -> x0, waiting for transfers between devices: 17.9 us -> none  [body(): lax.psum((totals[4], totals[2], totals[3], totals[0], totals[1]), 'ray')]
  transfers between devices with their start and end apart: 3 -> 12, of which waited for: 3 -> 8; matrix products, arithmetic and copies ran while one was open for 0% -> 0% of each run, Pallas kernels for 0% -> 22%
where the time goes in v2:
time: 54.8 us; the launch traced here: 54.6 us
  Pallas kernels  19.9 us (36%)
  starting transfers between devices  19.1 us (35%)
  waiting for transfers between devices  12.2 us (22%)
  local copies, waits for them, and re-layouts  2.29 us (4%)
  between operations  0.92 us (2%)
    pallas_call x13, Pallas kernels, run(): pl.pallas_call(kernel, out_shape=out_shape, in_specs=[pl.BlockSpec(memory...  19.9 us
    ppermute x12, starting transfers between devices, swap(): return lax.ppermute(array, axis, [(i, i ^ distance) for i in range(size)])  19.1 us
    ppermute x12, waiting for transfers between devices, swap(): return lax.ppermute(array, axis, [(i, i ^ distance) for i in range(size)])  12.2 us
    unnamed x24, local copies, waits for them, and re-layouts  2.26 us
  transfers between devices with their start and end apart: 12, of which 8 were waited for; matrix products, arithmetic and copies ran while one was open for 0% of the time, Pallas kernels for 22%

profile of v2, /device:TPU:0, one launch (start us, length us, event | category | flops | bytes accessed | tf_op | source)
XLA Modules:
  0.0 54.6 jit_solution(2550665857881637006)
XLA Ops:
  0.6 3.0 %collective-permute-start = (bf16[64,128]{1,0:T(8,128)(2,1)}, bf16[64,128]{1,0:T(8,128)(2,1)S(1)}, u32[]{:S(2)}, u32[]{:S(2)}) collective-permute-start(bf16[64,128]{1,0:T(8,128)(2,1)} %ray_ref.1), channel_id=1, source_target_pairs={{0,4},{4,0},{8,12},{12,8},{16,20},{20,16},{24,28},{28,24},{1,5},{5... | collective-permute-start | bytes 49160 | tf_op jit(solution)/shard_map/ppermute | solution.py:54
  6.1 1.3 %prepare.1 = (bf16[208,128]{1,0:T(8,128)(2,1)S(1)}, f32[8,512]{1,0:T(8,128)S(1)}, bf16[128,128]{1,0:T(8,128)(2,1)S(1)}, f32[64,128]{1,0:T(8,128)S(1)}, bf16[64,1...) custom-call(bf16[128,1024]{1,0:T(8,128)(2,1)S(1)} %get-tuple-element, ...), custom_call_target="tpu_custom_call" | custom-call | flops 2147483648 | bytes 1048576 | tf_op jit(solution)/shard_map/prepare/pallas_call | solution.py:65
  7.5 1.6 %collective-permute-start.1 = (bf16[128,128]{1,0:T(8,128)(2,1)S(1)}, bf16[128,128]{1,0:T(8,128)(2,1)S(1)}, u32[]{:S(2)}, u32[]{:S(2)}) collective-permute-start(bf16[128,128]{1,0:T(8,128)(2,1)S(1)} %pad_maximum_fusion.1), channel_id=1, source_target_pairs={{0,8},{4,12},{8,0},{12,4},{16,24},{20,28},{24,16},{28,20},{1,9},{5... | collective-permute-start | bytes 98312 | tf_op jit(solution)/shard_map/ppermute | solution.py:54
  9.2 2.3 %collective-permute-done.1 = bf16[128,128]{1,0:T(8,128)(2,1)S(1)} collective-permute-done((bf16[128,128]{1,0:T(8,128)(2,1)S(1)}, bf16[128,128]{1,0:T(8,128)(2,1)S(1)}, u32[]{:S(2)}, u32[]{:S(2)}) %collective-permute-start.1) | collective-permute-done | bytes 32800 | tf_op jit(solution)/shard_map/ppermute | solution.py:54
  11.5 2.6 %collective-permute-start.2 = (bf16[256,128]{1,0:T(8,128)(2,1)S(1)}, bf16[256,128]{1,0:T(8,128)(2,1)S(1)}, u32[]{:S(2)}, u32[]{:S(2)}) collective-permute-start(bf16[256,128]{1,0:T(8,128)(2,1)S(1)} %constant_dynamic-update-slice_fusion.refs_0_), channel_id=1, source_target_pairs={{0,16},{4,20},{8,24},{12,28},{16,0},{20,4},{24,8},{28,12},{1,17},{... | collective-permute-start | bytes 196616 | tf_op jit(solution)/shard_map/ppermute | solution.py:54
  14.1 2.3 %forward.2 = (f32[4,256]{1,0:T(4,128)S(1)}, f32[8,64,512]{2,1,0:T(8,128)S(1)}, bf16[512,128]{1,0:T(8,128)(2,1)S(1)}, bf16[256,128]{1,0:T(8,128)(2,1)S(1)}) custom-call(bf16[256,128]{1,0:T(8,128)(2,1)S(1)} %constant_dynamic-update-slice_fusion.refs_0_, f32[128,1024]{1,0:T(8,128)S(1)} %get-tuple-element.57.refs_1_, ...), custom_call_target="tpu_custom_call" | custom-call | flops 1073741824 | bytes 1048576 | tf_op jit(solution)/shard_map/forward/pallas_call | solution.py:65
  16.7 2.5 %forward.3 = (f32[4,512]{1,0:T(4,128)S(1)}, f32[8,64,1024]{2,1,0:T(8,128)S(1)}, bf16[1024,128]{1,0:T(8,128)(2,1)S(1)}, bf16[512,128]{1,0:T(8,128)(2,1)S(1)}) custom-call(bf16[256,128]{1,0:T(8,128)(2,1)S(1)} %collective-permute-done.2.refs_0_, f32[128,1024]{1,0:T(8,128)S(1)} %get-tuple-element.57.refs_1_, bf16[128,128]{1,0:T(8,128)(2,1)S(1)} %get-tuple-element.58.refs_2_, ...), custom_call_target="tpu_custom_call" | custom-call | flops 1073741824 | bytes 1048576 | tf_op jit(solution)/shard_map/forward/pallas_call | solution.py:65
  19.6 1.2 %coefficients.1 = (f32[7,64,1024]{2,1,0:T(8,128)S(1)}, f32[7,1024,128]{2,1,0:T(8,128)S(1)}) custom-call(f32[4,512]{1,0:T(4,128)S(1)} %get-tuple-element.66.seg_ref.refs_0_, f32[8,64,1024]{2,1,0:T(8,128)S(1)} %get-tuple-element.67.kept_ref), custom_call_target="tpu_custom_call" | custom-call | flops 2147483648 | bytes 1048576 | tf_op jit(solution)/shard_map/coefficients/pallas_call | solution.py:65
  20.7 2.2 %collective-permute-done.3.refs_1_ = f32[4,512]{1,0:T(4,128)S(1)} collective-permute-done((f32[4,512]{1,0:T(4,128)S(1)}, f32[4,512]{1,0:T(4,128)S(1)}, u32[]{:S(2)}, u32[]{:S(2)}) %collective-permute-start.3) | collective-permute-done | bytes 8224 | tf_op jit(solution)/shard_map/ppermute | solution.py:54
  23.0 1.6 %collective-permute-start.4 = (f32[4,512]{1,0:T(4,128)S(1)}, f32[4,512]{1,0:T(4,128)S(1)}, u32[]{:S(2)}, u32[]{:S(2)}) collective-permute-start(f32[4,512]{1,0:T(4,128)S(1)} %pad_maximum_fusion.2), channel_id=1, source_target_pairs={{0,8},{4,12},{8,0},{12,4},{16,24},{20,28},{24,16},{28,20},{1,9},{5... | collective-permute-start | bytes 24584 | tf_op jit(solution)/shard_map/ppermute | solution.py:54
  24.6 1.8 %basis.3.refs_5_.refs_7_ = f32[7,512,128]{2,1,0:T(8,128)S(1)} custom-call(f32[7,1024,128]{2,1,0:T(8,128)S(1)} %get-tuple-element.68.turned_ref, bf16[1024,128]{1,0:T(8,128)(2,1)S(1)} %get-tuple-element.69.u_ref.refs_9_, f32[64,128]{1,0:T(8,128)S(1)} %get-tuple-element.70.s_ref), custom_call_target="tpu_custom_call" | custom-call | flops 2147483648 | bytes 1048576 | tf_op jit(solution)/shard_map/basis/pallas_call | solution.py:65
  26.7 3.0 %collective-permute-start.5 = (f32[4,512]{1,0:T(4,128)S(1)}, f32[4,512]{1,0:T(4,128)S(1)}, u32[]{:S(2)}, u32[]{:S(2)}) collective-permute-start(f32[4,512]{1,0:T(4,128)S(1)} %pad_maximum_fusion.3), channel_id=1, source_target_pairs={{0,16},{4,20},{8,24},{12,28},{16,0},{20,4},{24,8},{28,12},{1,17},{... | collective-permute-start | bytes 24584 | tf_op jit(solution)/shard_map/ppermute | solution.py:54
  29.7 1.8 %basis.2.refs_4_.refs_6_ = f32[7,512,128]{2,1,0:T(8,128)S(1)} custom-call(f32[7,1024,128]{2,1,0:T(8,128)S(1)} %get-tuple-element.68.turned_ref, bf16[1024,128]{1,0:T(8,128)(2,1)S(1)} %get-tuple-element.69.u_ref.refs_9_, f32[64,128]{1,0:T(8,128)S(1)} %get-tuple-element.70.s_ref), custom_call_target="tpu_custom_call" | custom-call | flops 2147483648 | bytes 1048576 | tf_op jit(solution)/shard_map/basis/pallas_call | solution.py:65
  33.2 2.1 %by_sample.2 = (f32[32,128]{1,0:T(8,128)S(1)}, f32[4,8,128]{2,1,0:T(8,128)S(1)}, f32[4,128]{1,0:T(4,128)S(1)}) custom-call(f32[8,512]{1,0:T(8,128)S(1)} %get-tuple-element.79.cot_ref.refs_8_, f32[7,64,1024]{2,1,0:T(8,128)S(1)} %get-tuple-element.73.coef_ref, bf16[1024,128]{1,0:T(8,128)(2,1)S(1)} %get-tuple-element.69.u_ref.refs_9_, ...), custom_call_target="tpu_custom_call" | custom-call | flops 268435456 | bytes 1048576 | tf_op jit(solution)/shard_map/by_sample/pallas_call | solution.py:65
  35.3 1.7 %collective-permute-done.6 = bf16[256,128]{1,0:T(8,128)(2,1)S(1)} collective-permute-done((bf16[256,128]{1,0:T(8,128)(2,1)S(1)}, bf16[256,128]{1,0:T(8,128)(2,1)S(1)}, u32[]{:S(2)}, u32[]{:S(2)}) %collective-permute-start.6) | collective-permute-done | bytes 65568 | tf_op jit(solution)/shard_map/ppermute | solution.py:54
  37.0 2.1 %by_sample.3 = (f32[32,128]{1,0:T(8,128)S(1)}, f32[4,8,128]{2,1,0:T(8,128)S(1)}, f32[4,128]{1,0:T(4,128)S(1)}) custom-call(f32[8,512]{1,0:T(8,128)S(1)} %get-tuple-element.79.cot_ref.refs_8_, f32[7,64,1024]{2,1,0:T(8,128)S(1)} %get-tuple-element.73.coef_ref, bf16[1024,128]{1,0:T(8,128)(2,1)S(1)} %get-tuple-element.69.u_ref.refs_9_, ...), custom_call_target="tpu_custom_call" | custom-call | flops 268435456 | bytes 1048576 | tf_op jit(solution)/shard_map/by_sample/pallas_call | solution.py:65
  39.1 1.6 %network.1 = (f32[208,128]{1,0:T(8,128)S(1)}, f32[3,64]{1,0:T(4,128)}) custom-call(f32[32,128]{1,0:T(8,128)S(1)} %get-tuple-element.74.refs_0_, f32[4,8,128]{2,1,0:T(8,128)S(1)} %get-tuple-element.75.refs_1_, f32[4,128]{1,0:T(4,128)S(1)} %get-tuple-element.76.refs_2_, f32[32,128]{1,0:T(8,128)S(1)} %get-tuple-element.80.refs_3_, ...), custom_call_target="tpu_custom_call" | custom-call | flops 268435456 | bytes 1048576 | tf_op jit(solution)/shard_map/network/pallas_call | solution.py:65
  40.6 1.9 %collective-permute-start.7 = (bf16[128,128]{1,0:T(8,128)(2,1)S(1)}, bf16[128,128]{1,0:T(8,128)(2,1)S(1)}, u32[]{:S(2)}, u32[]{:S(2)}) collective-permute-start(bf16[128,128]{1,0:T(8,128)(2,1)S(1)} %get-tuple-element.108), channel_id=1, source_target_pairs={{0,8},{4,12},{8,0},{12,4},{16,24},{20,28},{24,16},{28,20},{1,9},{5... | collective-permute-start | bytes 98312 | tf_op jit(solution)/shard_map/ppermute | solution.py:54
  42.5 2.1 %collective-permute-done.7 = bf16[128,128]{1,0:T(8,128)(2,1)S(1)} collective-permute-done((bf16[128,128]{1,0:T(8,128)(2,1)S(1)}, bf16[128,128]{1,0:T(8,128)(2,1)S(1)}, u32[]{:S(2)}, u32[]{:S(2)}) %collective-permute-start.7) | collective-permute-done | bytes 32800 | tf_op jit(solution)/shard_map/ppermute | solution.py:54
  44.6 1.3 %bricks.1 = (f32[512,128]{1,0:T(8,128)S(1)}, f32[512,128]{1,0:T(8,128)S(1)}) custom-call(f32[8,512]{1,0:T(8,128)S(1)} %get-tuple-element.61.refs_5_.refs_6_.lines_ref, f32[1024,128]{1,0:T(8,128)S(1)} %get-tuple-element.91.moved_ref), custom_call_target="tpu_custom_call" | custom-call | flops 268435456 | bytes 1048576 | tf_op jit(solution)/shard_map/bricks/pallas_call | solution.py:65
  46.0 1.5 %collective-permute-done.9 = f32[512,128]{1,0:T(8,128)S(1)} collective-permute-done((f32[512,128]{1,0:T(8,128)S(1)}, f32[512,128]{1,0:T(8,128)S(1)}, u32[]{:S(2)}, u32[]{:S(2)}) %collective-permute-start.9) | collective-permute-done | bytes 262176 | tf_op jit(solution)/shard_map/ppermute | solution.py:54
  47.6 1.6 %collective-permute-start.11 = (bf16[464,128]{1,0:T(8,128)(2,1)S(1)}, bf16[464,128]{1,0:T(8,128)(2,1)S(1)}, u32[]{:S(2)}, u32[]{:S(2)}) collective-permute-start(bf16[464,128]{1,0:T(8,128)(2,1)S(1)} %pad_maximum_fusion.sent_ref), channel_id=1, source_target_pairs={{0,2},{1,3},{2,0},{3,1},{4,6},{5,7},{6,4},{7,5},{8,10},{9,11},{10,... | collective-permute-start | bytes 356360 | tf_op jit(solution)/shard_map/ppermute | solution.py:54
  49.1 2.8 %collective-permute-start.8 = (bf16[64,128]{1,0:T(8,128)(2,1)S(1)}, bf16[64,128]{1,0:T(8,128)(2,1)S(1)}, u32[]{:S(2)}, u32[]{:S(2)}) collective-permute-start(bf16[64,128]{1,0:T(8,128)(2,1)S(1)} %get-tuple-element.110), channel_id=1, source_target_pairs={{0,16},{4,20},{8,24},{12,28},{16,0},{20,4},{24,8},{28,12},{1,17},{... | collective-permute-start | bytes 49160 | tf_op jit(solution)/shard_map/ppermute | solution.py:54
  51.9 1.9 %collective-permute-done.8.ray_got_ref = bf16[64,128]{1,0:T(8,128)(2,1)S(1)} collective-permute-done((bf16[64,128]{1,0:T(8,128)(2,1)S(1)}, bf16[64,128]{1,0:T(8,128)(2,1)S(1)}, u32[]{:S(2)}, u32[]{:S(2)}) %collective-permute-start.8) | collective-permute-done | bytes 16416 | tf_op jit(solution)/shard_map/ppermute | solution.py:54
  (53 shorter events, 6.0 us)
Async XLA Ops:
  0.6 6.8 %collective-permute-start = (bf16[64,128]{1,0:T(8,128)(2,1)}, bf16[64,128]{1,0:T(8,128)(2,1)S(1)}, u32[]{:S(2)}, u32[]{:S(2)}) collective-permute-start(bf16[64,128]{1,0:T(8,128)(2,1)} %ray_ref.1), channel_id=1, source_target_pairs={{0,4},{4,0},{8,12},{12,8},{16,20},{20,16},{24,28},{28,24},{1,5},{5... | collective-permute-start | bytes 49160 | tf_op jit(solution)/shard_map/ppermute | solution.py:54
  3.7 0.9 %copy-start = (bf16[1,1024,128]{2,1,0:T(8,128)(2,1)S(1)}, bf16[1,1024,128]{2,1,0:T(8,128)(2,1)}, u32[]{:S(2)}) copy-start(bf16[1,1024,128]{2,1,0:T(8,128)(2,1)} %param.14) | copy-start | bytes 786436
  4.6 0.7 %copy-start.3 = (bf16[64,128]{1,0:T(8,128)(2,1)S(1)}, bf16[64,128]{1,0:T(8,128)(2,1)}, u32[]{:S(2)}) copy-start(bf16[64,128]{1,0:T(8,128)(2,1)} %ray_ref.1) | copy-start | bytes 49156
  5.3 0.8 %copy-start.1 = (bf16[1,128,128]{2,1,0:T(8,128)(2,1)S(1)}, bf16[1,128,128]{2,1,0:T(8,128)(2,1)}, u32[]{:S(2)}) copy-start(bf16[1,128,128]{2,1,0:T(8,128)(2,1)} %param.16) | copy-start | bytes 98308
  5.3 0.8 %copy-start.2 = (bf16[1,64,128]{2,1,0:T(8,128)(2,1)S(1)}, bf16[1,64,128]{2,1,0:T(8,128)(2,1)}, u32[]{:S(2)}) copy-start(bf16[1,64,128]{2,1,0:T(8,128)(2,1)} %param.15) | copy-start | bytes 49156
  5.3 0.8 %copy-start.4 = (f32[3,512]{1,0:T(4,128)S(1)}, f32[3,512]{1,0:T(4,128)}, u32[]{:S(2)}) copy-start(f32[3,512]{1,0:T(4,128)} %target_ref.1) | copy-start | bytes 18436
  5.3 0.8 %copy-start.5 = (s32[1,2,512]{2,1,0:T(2,128)S(1)}, s32[1,2,512]{2,1,0:T(2,128)}, u32[]{:S(2)}) copy-start(s32[1,2,512]{2,1,0:T(2,128)} %param.20) | copy-start | bytes 12292
  5.3 0.8 %copy-start.6 = (s32[1,512]{1,0:T(1,128)S(1)}, s32[1,512]{1,0:T(1,128)}, u32[]{:S(2)}) copy-start(s32[1,512]{1,0:T(1,128)} %occ_ref.1) | copy-start | bytes 6148
  5.4 0.8 %copy-start.7 = (s32[512]{0:T(512)S(1)}, s32[512]{0:T(512)}, u32[]{:S(2)}) copy-start(s32[512]{0:T(512)} %param.12) | copy-start | bytes 6148
  5.4 0.8 %copy-start.8 = (bf16[1,4,128]{2,1,0:T(4,128)(2,1)S(1)}, bf16[1,4,128]{2,1,0:T(4,128)(2,1)}, u32[]{:S(2)}) copy-start(bf16[1,4,128]{2,1,0:T(4,128)(2,1)} %param.18) | copy-start | bytes 3076
  5.4 0.8 %copy-start.9 = (f32[1,128]{1,0:T(1,128)S(1)}, f32[1,128]{1,0:T(1,128)}, u32[]{:S(2)}) copy-start(f32[1,128]{1,0:T(1,128)} %b_ref.1) | copy-start | bytes 1540
  5.4 0.8 %copy-start.10 = (f32[1,4]{1,0:T(1,128)S(1)}, f32[1,4]{1,0:T(1,128)}, u32[]{:S(2)}) copy-start(f32[1,4]{1,0:T(1,128)} %b_out_ref.1) | copy-start | bytes 52
  7.5 4.0 %collective-permute-start.1 = (bf16[128,128]{1,0:T(8,128)(2,1)S(1)}, bf16[128,128]{1,0:T(8,128)(2,1)S(1)}, u32[]{:S(2)}, u32[]{:S(2)}) collective-permute-start(bf16[128,128]{1,0:T(8,128)(2,1)S(1)} %pad_maximum_fusion.1), channel_id=1, source_target_pairs={{0,8},{4,12},{8,0},{12,4},{16,24},{20,28},{24,16},{28,20},{1,9},{5... | collective-permute-start | bytes 98312 | tf_op jit(solution)/shard_map/ppermute | solution.py:54
  11.5 5.2 %collective-permute-start.2 = (bf16[256,128]{1,0:T(8,128)(2,1)S(1)}, bf16[256,128]{1,0:T(8,128)(2,1)S(1)}, u32[]{:S(2)}, u32[]{:S(2)}) collective-permute-start(bf16[256,128]{1,0:T(8,128)(2,1)S(1)} %constant_dynamic-update-slice_fusion.refs_0_), channel_id=1, source_target_pairs={{0,16},{4,20},{8,24},{12,28},{16,0},{20,4},{24,8},{28,12},{1,17},{... | collective-permute-start | bytes 196616 | tf_op jit(solution)/shard_map/ppermute | solution.py:54
  19.2 3.7 %collective-permute-start.3 = (f32[4,512]{1,0:T(4,128)S(1)}, f32[4,512]{1,0:T(4,128)S(1)}, u32[]{:S(2)}, u32[]{:S(2)}) collective-permute-start(f32[4,512]{1,0:T(4,128)S(1)} %get-tuple-element.66.seg_ref.refs_0_), channel_id=1, source_target_pairs={{0,4},{4,0},{8,12},{12,8},{16,20},{20,16},{24,28},{28,24},{1,5},{5... | collective-permute-start | bytes 24584 | tf_op jit(solution)/shard_map/ppermute | solution.py:54
  23.0 3.7 %collective-permute-start.4 = (f32[4,512]{1,0:T(4,128)S(1)}, f32[4,512]{1,0:T(4,128)S(1)}, u32[]{:S(2)}, u32[]{:S(2)}) collective-permute-start(f32[4,512]{1,0:T(4,128)S(1)} %pad_maximum_fusion.2), channel_id=1, source_target_pairs={{0,8},{4,12},{8,0},{12,4},{16,24},{20,28},{24,16},{28,20},{1,9},{5... | collective-permute-start | bytes 24584 | tf_op jit(solution)/shard_map/ppermute | solution.py:54
  26.7 4.8 %collective-permute-start.5 = (f32[4,512]{1,0:T(4,128)S(1)}, f32[4,512]{1,0:T(4,128)S(1)}, u32[]{:S(2)}, u32[]{:S(2)}) collective-permute-start(f32[4,512]{1,0:T(4,128)S(1)} %pad_maximum_fusion.3), channel_id=1, source_target_pairs={{0,16},{4,20},{8,24},{12,28},{16,0},{20,4},{24,8},{28,12},{1,17},{... | collective-permute-start | bytes 24584 | tf_op jit(solution)/shard_map/ppermute | solution.py:54
  32.7 4.3 %collective-permute-start.6 = (bf16[256,128]{1,0:T(8,128)(2,1)S(1)}, bf16[256,128]{1,0:T(8,128)(2,1)S(1)}, u32[]{:S(2)}, u32[]{:S(2)}) collective-permute-start(bf16[256,128]{1,0:T(8,128)(2,1)S(1)} %get-tuple-element.77), channel_id=1, source_target_pairs={{0,4},{4,0},{8,12},{12,8},{16,20},{20,16},{24,28},{28,24},{1,5},{5... | collective-permute-start | bytes 196616 | tf_op jit(solution)/shard_map/ppermute | solution.py:54
  40.6 5.4 %collective-permute-start.10 = (f32[208,128]{1,0:T(8,128)S(1)}, f32[208,128]{1,0:T(8,128)S(1)}, u32[]{:S(2)}, u32[]{:S(2)}) collective-permute-start(f32[208,128]{1,0:T(8,128)S(1)} %get-tuple-element.94), channel_id=1, source_target_pairs={{0,1},{1,0},{2,3},{3,2},{4,5},{5,4},{6,7},{7,6},{8,9},{9,8},{10,11... | collective-permute-start | bytes 319496 | tf_op jit(solution)/shard_map/ppermute | solution.py:54
  40.6 4.0 %collective-permute-start.7 = (bf16[128,128]{1,0:T(8,128)(2,1)S(1)}, bf16[128,128]{1,0:T(8,128)(2,1)S(1)}, u32[]{:S(2)}, u32[]{:S(2)}) collective-permute-start(bf16[128,128]{1,0:T(8,128)(2,1)S(1)} %get-tuple-element.108), channel_id=1, source_target_pairs={{0,8},{4,12},{8,0},{12,4},{16,24},{20,28},{24,16},{28,20},{1,9},{5... | collective-permute-start | bytes 98312 | tf_op jit(solution)/shard_map/ppermute | solution.py:54
  45.9 1.6 %collective-permute-start.9 = (f32[512,128]{1,0:T(8,128)S(1)}, f32[512,128]{1,0:T(8,128)S(1)}, u32[]{:S(2)}, u32[]{:S(2)}) collective-permute-start(f32[512,128]{1,0:T(8,128)S(1)} %get-tuple-element.93), channel_id=1, source_target_pairs={{0,1},{1,0},{2,3},{3,2},{4,5},{5,4},{6,7},{7,6},{8,9},{9,8},{10,11... | collective-permute-start | bytes 786440 | tf_op jit(solution)/shard_map/ppermute | solution.py:54
  47.6 6.3 %collective-permute-start.11 = (bf16[464,128]{1,0:T(8,128)(2,1)S(1)}, bf16[464,128]{1,0:T(8,128)(2,1)S(1)}, u32[]{:S(2)}, u32[]{:S(2)}) collective-permute-start(bf16[464,128]{1,0:T(8,128)(2,1)S(1)} %pad_maximum_fusion.sent_ref), channel_id=1, source_target_pairs={{0,2},{1,3},{2,0},{3,1},{4,6},{5,7},{6,4},{7,5},{8,10},{9,11},{10,... | collective-permute-start | bytes 356360 | tf_op jit(solution)/shard_map/ppermute | solution.py:54
  49.1 4.7 %collective-permute-start.8 = (bf16[64,128]{1,0:T(8,128)(2,1)S(1)}, bf16[64,128]{1,0:T(8,128)(2,1)S(1)}, u32[]{:S(2)}, u32[]{:S(2)}) collective-permute-start(bf16[64,128]{1,0:T(8,128)(2,1)S(1)} %get-tuple-element.110), channel_id=1, source_target_pairs={{0,16},{4,20},{8,24},{12,28},{16,0},{20,4},{24,8},{28,12},{1,17},{... | collective-permute-start | bytes 49160 | tf_op jit(solution)/shard_map/ppermute | solution.py:54

commit v3 on v2

--- a/solution.py
+++ b/solution.py
@@ -20,16 +20,14 @@
     return bits
 
 
-def swap_order(count, descending):
+def gather_bits(owners, own):
+    last = max(bits_of(128 // own), 0) if own < 128 else 0
+    return [b for b in reversed(range(bits_of(owners))) if b != last] + [last]
+
+
+def gather_order(owners, own):
     order = [0]
-    for b in reversed(range(bits_of(count))) if descending else range(bits_of(count)):
-        order = order + [t ^ (1 << b) for t in order]
-    return order
-
-
-def halving_order(count):
-    order = [0]
-    for b in reversed(range(bits_of(count))):
+    for b in gather_bits(owners, own)[:-1]:
         order = order + [t ^ (1 << b) for t in order]
     return order
 
@@ -92,13 +90,30 @@
     }
 
 
-def turn_kernel(brick_ref, ray_ref, brick_t_ref, own_ref):
-    brick_t_ref[...] = brick_ref[...].astype(f32).T.astype(bf16)
-    own_ref[...] = ray_ref[...]
+def order_kernel(earlier_ref, later_ref):
+    shape = earlier_ref.shape
+    r_i = lax.broadcasted_iota(jnp.int32, shape, 0)
+    c_i = lax.broadcasted_iota(jnp.int32, shape, 1)
+    earlier_ref[...] = jnp.where(c_i < r_i, 1.0, 0.0).astype(bf16)
+    later_ref[...] = jnp.where(c_i > r_i, 1.0, 0.0).astype(bf16)
+
+
+def chosen_kernel(lines_ref, brick_ref, w_t_ref, chosen_ref, project_ref):
+    total = chosen_ref.shape[1]
+    rays = lines_ref.shape[1]
+    bricks = brick_ref.shape[0]
+    brick_t = brick_ref[...].astype(f32).T.astype(bf16)
+    w_t = w_t_ref[...]
+    row = lax.broadcasted_iota(jnp.int32, (bricks, rays), 0).astype(f32)
+    for k in range(total // rays):
+        one_hot = jnp.where(row == lines_ref[k : k + 1, :], 1.0, 0.0).astype(bf16)
+        chosen = nn_dot(brick_t, one_hot).astype(bf16)
+        chosen_ref[:, k * rays : (k + 1) * rays] = chosen
+        project_ref[:, k * rays : (k + 1) * rays] = nn_dot(w_t, chosen)
 
 
 def prepare_kernel(
-    brick_t_ref,
+    ray_ref,
     w_ref,
     sample_ref,
     w_out_ref,
@@ -108,14 +123,13 @@
     target_ref,
     b_ref,
     b_out_ref,
+    own_ref,
     low_ref,
     lines_ref,
     w_t_ref,
     s_ref,
     wide_ref,
     left_ref,
-    chosen_ref,
-    project_ref,
     *,
     rows,
     lines,
@@ -124,7 +138,7 @@
     width = w_t_ref.shape[0]
     samples = s_ref.shape[0]
     outs = w_out_ref.shape[0]
-    bricks = brick_t_ref.shape[1]
+    own_ref[...] = ray_ref[...]
     w = w_ref[...]
     w_out = w_out_ref[...].astype(f32)
     low_ref[rows["w"], :] = w
@@ -150,56 +164,55 @@
     row8 = lax.broadcasted_iota(jnp.int32, (outs * 8, width), 0) % 8
     for i in range(8):
         left_ref[:, i * width : (i + 1) * width] = jnp.where(row8 == i, w_rows, 0.0).astype(bf16)
-    row = lax.broadcasted_iota(jnp.int32, (bricks, rays), 0)
-    for k in range(slots):
-        one_hot = jnp.where(row == ids_ref[k : k + 1, :], 1.0, 0.0).astype(bf16)
-        chosen = nn_dot(brick_t_ref[...], one_hot).astype(bf16)
-        chosen_ref[:, k * rays : (k + 1) * rays] = chosen
-        project_ref[:, k * rays : (k + 1) * rays] = nn_dot(w_t, chosen)
 
 
 def forward_kernel(*refs, owners, second, lines):
-    ray_ref, project_ref, w_t_ref, wide_ref, left_ref, lines_ref, *refs = refs
+    ray_ref, project_ref, w_t_ref, wide_ref, left_ref, lines_ref, earlier_ref, *refs = refs
     if second:
-        before_refs, refs = refs[:4], refs[4:]
+        before_refs, refs = refs[:3], refs[3:]
     seg_ref, kept_ref, u_ref, sorted_ref, order_ref, ut_ref, raw_ref = refs
     width, total = project_ref.shape
     samples = wide_ref.shape[0]
     outs = seg_ref.shape[0]
     half, rays = ray_ref.shape[0], lines_ref.shape[1]
     slots = total // rays
-    blocks = owners // 2
-    own = half // blocks
+    chunk = 128
+    own = 2 * half // owners
+    last = gather_bits(owners, own)[-1]
     me = lax.axis_index("slab")
-    side = me // blocks
+    side = (me >> last) & 1
+
+    def whole(n, k=0, side=side):
+        return pl.ds(pl.multiple_of(k * rays + (2 * n + side) * chunk, chunk), chunk)
+
     if second:
-        first_half = pl.multiple_of(side * half, half)
-        for old, new in zip(before_refs[:2], (seg_ref, kept_ref)):
-            for k in range(old.shape[-1] // half):
-                lanes = pl.ds(pl.multiple_of(k * rays + first_half, half), half)
-                new[..., lanes] = old[..., k * half : (k + 1) * half]
-        for old, new in zip(before_refs[2:], (u_ref, sorted_ref)):
-            for k in range(old.shape[0] // half):
-                rows = pl.ds(pl.multiple_of(k * rays + first_half, half), half)
-                new[rows, :] = old[k * half : (k + 1) * half, :]
+        for n in range(half // chunk):
+            part = slice(n * chunk, (n + 1) * chunk)
+            seg_ref[:, whole(n)] = before_refs[0][:, part]
+            sorted_ref[whole(n), :] = before_refs[2][part, :]
+            for k in range(slots):
+                u_ref[whole(n, k), :] = before_refs[1][k * half + n * chunk : k * half + (n + 1) * chunk, :]
         side = 1 - side
-    here = pl.multiple_of(side * half, half)
-    stride = rays if second else half
-    base = here if second else 0
-
-    def spot(offset, size):
-        return pl.ds(pl.multiple_of(offset + base, 128), size) if second else pl.ds(offset, size)
-
-    for i in range(blocks):
-        place = pl.multiple_of(((me ^ i) & (blocks - 1)) * own, own)
-        order_ref[pl.ds(place, own), :] = ray_ref[i * own : (i + 1) * own, :]
-    sorted_ref[spot(0, half), :] = order_ref[...]
+
+    def spot(n, k=0):
+        at = k * half + n * chunk
+        return whole(n, k, side) if second else slice(at, at + chunk)
+
+    flip = (1 << last) if second else 0
+    for i, t in enumerate(gather_order(owners, own)):
+        owner = me ^ (t ^ flip)
+        place = ((owner >> (last + 1)) << last) | (owner & ((1 << last) - 1))
+        order_ref[pl.ds(pl.multiple_of(place * own, own), own), :] = ray_ref[
+            i * own : (i + 1) * own, :
+        ]
     ray_t = nt_dot(w_t_ref[...], order_ref[...])
-    for k in range(slots):
-        lanes = pl.ds(pl.multiple_of(k * rays + here, half), half)
-        part = (project_ref[:, lanes] + ray_t).astype(bf16)
-        ut_ref[:, k * half : (k + 1) * half] = part
-        u_ref[spot(k * stride, half), :] = part.astype(f32).T.astype(bf16)
+    for n in range(half // chunk):
+        sorted_ref[spot(n), :] = order_ref[n * chunk : (n + 1) * chunk, :]
+        for k in range(slots):
+            part = project_ref[:, whole(n, k, side)] + ray_t[:, n * chunk : (n + 1) * chunk]
+            part = part.astype(bf16)
+            ut_ref[:, k * half + n * chunk : k * half + (n + 1) * chunk] = part
+            u_ref[spot(n, k), :] = part.astype(f32).T.astype(bf16)
     b_out = [lines_ref[lines["b_out"], c] for c in range(outs)]
 
     def shade_block(block, carry):
@@ -222,14 +235,11 @@
                 )
         return carry
 
-    lax.fori_loop(0, samples // 8, shade_block, 0, unroll=4)
-    r_i = lax.broadcasted_iota(jnp.int32, (samples, samples), 0)
-    c_i = lax.broadcasted_iota(jnp.int32, (samples, samples), 1)
-    earlier = jnp.where(c_i < r_i, 1.0, 0.0).astype(bf16)
-    chunk = 128
+    lax.fori_loop(0, samples // 8, shade_block, 0, unroll=8)
+    earlier = earlier_ref[...]
     occ_row = lines["occ"]
     for n in range(half // chunk):
-        occ = lines_ref[occ_row : occ_row + 1, pl.ds(pl.multiple_of(here + n * chunk, chunk), chunk)]
+        occ = lines_ref[occ_row : occ_row + 1, whole(n, 0, side)]
         raws = [
             raw_ref[0, :, k * half + n * chunk : k * half + (n + 1) * chunk] for k in range(slots)
         ]
@@ -243,7 +253,6 @@
         colors = [jnp.zeros((1, chunk), f32)] * (outs - 1)
         for k in range(slots):
             local = slice(k * half + n * chunk, k * half + (n + 1) * chunk)
-            lanes = spot(k * stride + n * chunk, chunk)
             optical = opticals[k]
             entered = enters[:, k * chunk : (k + 1) * chunk] + before
             before = before + jnp.sum(optical, 0, keepdims=True)
@@ -253,49 +262,53 @@
                 shading = jax.nn.sigmoid(raw_ref[c + 1, :, local])
                 light = weight * shading
                 colors[c] = colors[c] + jnp.sum(light, 0, keepdims=True)
-                kept_ref[c, :, lanes] = shading
-                kept_ref[outs + c, :, lanes] = light
-            kept_ref[outs - 1, :, lanes] = jnp.exp(-(entered + optical))
-            kept_ref[2 * outs - 1, :, lanes] = step_length * occupied[k] * jax.nn.sigmoid(raws[k])
-        place = spot(n * chunk, chunk)
+                kept_ref[c, :, local] = shading
+                kept_ref[outs + c, :, local] = light
+            kept_ref[outs - 1, :, local] = jnp.exp(-(entered + optical))
+            kept_ref[2 * outs - 1, :, local] = step_length * occupied[k] * jax.nn.sigmoid(raws[k])
+        place = spot(n)
         for c in range(outs - 1):
             seg_ref[c : c + 1, place] = colors[c]
         seg_ref[outs - 1 : outs, place] = jnp.exp(-before)
 
 
-def coefficient_kernel(seg_ref, kept_ref, coef_ref, turned_ref):
+def coefficient_kernel(seg_ref, first_ref, second_ref, later_ref, coef_ref, turned_ref, *, owners):
     outs, rays = seg_ref.shape
-    samples, total = kept_ref.shape[1:]
-    slots = total // rays
-    r_i = lax.broadcasted_iota(jnp.int32, (samples, samples), 0)
-    c_i = lax.broadcasted_iota(jnp.int32, (samples, samples), 1)
-    later = jnp.where(c_i > r_i, 1.0, 0.0).astype(bf16)
+    samples, local = first_ref.shape[1:]
+    half = rays // 2
+    slots = local // half
+    last = gather_bits(owners, rays // owners)[-1]
+    side = (lax.axis_index("slab") >> last) & 1
+    later = later_ref[...]
     chunk = 128
 
     def keep(index, lanes, value):
         coef_ref[index, :, lanes] = value
         turned_ref[index, lanes, :] = jnp.concatenate([value] * (128 // samples), 0).T
 
-    for n in range(rays // chunk):
-        through = seg_ref[outs - 1 : outs, n * chunk : (n + 1) * chunk]
-        after = [jnp.zeros((1, chunk), f32)] * (outs - 1)
-        for k in reversed(range(slots)):
-            lanes = slice(k * rays + n * chunk, k * rays + (n + 1) * chunk)
-            passed = kept_ref[outs - 1, :, lanes]
-            density = kept_ref[2 * outs - 1, :, lanes]
-            lights = [kept_ref[outs + c, :, lanes] for c in range(outs - 1)]
-            behinds = sum_dot(later, jnp.concatenate(lights, 1))
-            for c in range(outs - 1):
-                shading = kept_ref[c, :, lanes]
-                light = lights[c]
-                behind = behinds[:, c * chunk : (c + 1) * chunk] + after[c]
-                after[c] = after[c] + jnp.sum(light, 0, keepdims=True)
-                keep(c, lanes, density * (shading * passed - behind))
-                keep(outs + c, lanes, light * (1.0 - shading))
-            keep(outs - 1, lanes, density * through)
-
-
-def basis_kernel(turned_ref, u_ref, s_ref, h1_ref, *, slot):
+    for kept_ref, where in ((first_ref, side), (second_ref, 1 - side)):
+        for n in range(half // chunk):
+            base = (2 * n + where) * chunk
+            through = seg_ref[outs - 1 : outs, pl.ds(pl.multiple_of(base, chunk), chunk)]
+            after = [jnp.zeros((1, chunk), f32)] * (outs - 1)
+            for k in reversed(range(slots)):
+                lanes = pl.ds(pl.multiple_of(k * rays + base, chunk), chunk)
+                at = slice(k * half + n * chunk, k * half + (n + 1) * chunk)
+                passed = kept_ref[outs - 1, :, at]
+                density = kept_ref[2 * outs - 1, :, at]
+                lights = [kept_ref[outs + c, :, at] for c in range(outs - 1)]
+                behinds = sum_dot(later, jnp.concatenate(lights, 1))
+                for c in range(outs - 1):
+                    shading = kept_ref[c, :, at]
+                    light = lights[c]
+                    behind = behinds[:, c * chunk : (c + 1) * chunk] + after[c]
+                    after[c] = after[c] + jnp.sum(light, 0, keepdims=True)
+                    keep(c, lanes, density * (shading * passed - behind))
+                    keep(outs + c, lanes, light * (1.0 - shading))
+                keep(outs - 1, lanes, density * through)
+
+
+def basis_kernel(turned_ref, u_ref, s_ref, low_ref, h1_ref, moved_ref, *, first, row_of):
     count, rays, width = h1_ref.shape
     samples = s_ref.shape[0]
     negative = (-s_ref[...]).astype(bf16)
@@ -306,17 +319,21 @@
     block_mask = lane == row
     repeat = 8 * samples // 128
     step = 128
+    outs = moved_ref.shape[0]
+    w = low_ref[row_of["w"], :]
+    w_out = low_ref[row_of["w_out"], :].astype(f32)
+    w_rows = [w_out[c : c + 1, :] for c in range(outs)]
 
     def slot_block(block, carry):
         for h in range(step // 16):
             base = pl.multiple_of(block * step + h * 16, 16)
-            u16 = u_ref[pl.ds(slot * rays + base, 16), :]
+            u16 = u_ref[pl.ds(first + base, 16), :]
             for q in range(2):
                 at = pl.multiple_of(block * step + h * 16 + q * 8, 8)
                 left = [
                     jnp.where(
                         block_mask,
-                        jnp.concatenate([turned_ref[c, pl.ds(slot * rays + at, 8), :]] * repeat, 1),
+                        jnp.concatenate([turned_ref[c, pl.ds(first + at, 8), :]] * repeat, 1),
                         0.0,
                     )
                     for c in range(count)
@@ -337,6 +354,11 @@
         return carry
 
     lax.fori_loop(0, rays // step, slot_block, 0)
+    for c in range(outs):
+        grad = w_rows[0] * h1_ref[c]
+        if c + 1 < outs:
+            grad = grad + w_rows[c + 1] * h1_ref[outs + c]
+        moved_ref[c] = nt_dot(grad.astype(bf16), w)
 
 
 def merge(first, second, forward):
@@ -345,18 +367,18 @@
     return jnp.where(forward, fc + ft * sc, sc + st * fc), ft * st
 
 
-def middle_kernel(*refs, owners, slots, rows, lines):
+def middle_kernel(*refs, owners, pieces, lines):
     bits = bits_of(owners)
     seg_ref, refs = refs[0], refs[1:]
     got_refs, refs = refs[:bits], refs[bits:]
-    h1_refs, refs = refs[:slots], refs[slots:]
-    lines_ref, low_ref, *refs = refs
-    keep_ref, send_ref, moved_ref, slot_ref, cot_ref, ray_ref = refs
+    moved_refs, refs = refs[:pieces], refs[pieces:]
+    lines_ref, keep_ref, send_ref, cot_ref, ray_ref = refs
     me = lax.axis_index("slab")
     outs = seg_ref.shape[0]
     channels = outs - 1
     rays = lines_ref.shape[1]
-    width = low_ref.shape[1]
+    span, width = moved_refs[0].shape[1:]
+    slots = pieces * span // rays
     forward = lines_ref[lines["direction"] : lines["direction"] + 1, :] == 0.0
     target = lines_ref[lines["target"] : lines["target"] + channels, :]
 
@@ -386,31 +408,23 @@
     cot_ref[channels:outs, :] = trans_cot
     cot_ref[outs : outs + channels, :] = color
     cot_ref[outs + channels :, :] = jnp.zeros((8 - outs - channels, rays), f32)
-    w_out = low_ref[rows["w_out"], :].astype(f32)
-    w_rows = [w_out[c : c + 1, :] for c in range(outs)]
-    w = low_ref[rows["w"], :]
     chunk = 128
     for n in range(rays // chunk):
         these = slice(n * chunk, (n + 1) * chunk)
         turned = cot_ref[:, these].T
-        cots = [jnp.broadcast_to(turned[:, c : c + 1], (chunk, width)) for c in range(outs)]
-        whole = None
-        for k in range(slots):
-            at = slice(k * rays + n * chunk, k * rays + (n + 1) * chunk)
-            h1_ref = h1_refs[k]
-            parts = [sum(cots[c] * h1_ref[c, these, :] for c in range(outs))]
-            parts += [cots[c] * h1_ref[outs + c, these, :] for c in range(channels)]
-            grad = sum(w_rows[c] * parts[c] for c in range(outs))
-            slot_ref[at, :] = grad
-            whole = grad if whole is None else whole + grad
-            moved_ref[at, :] = split_dot(grad, w, nt_dot)
+        grad = None
+        for c in range(outs):
+            whole = None
+            for k in range(slots):
+                at = k * rays + n * chunk
+                part = moved_refs[at // span][c, at % span : at % span + chunk, :]
+                whole = part if whole is None else whole + part
+            term = jnp.broadcast_to(turned[:, c : c + 1], (chunk, width)) * whole
+            grad = term if grad is None else grad + term
+        ray_ref[these, :] = grad
     own = rays // owners
-    moved = moved_ref[:rays, :]
-    for k in range(1, slots):
-        moved = moved + moved_ref[k * rays : (k + 1) * rays, :]
-    ray_ref[...] = moved
-    for i, t in enumerate(halving_order(owners)):
-        place = pl.multiple_of((me ^ t) * own, own)
+    for i in range(owners):
+        place = pl.multiple_of((me ^ i) * own, own)
         if i < owners // 2:
             keep_ref[i * own : (i + 1) * own, :] = ray_ref[pl.ds(place, own), :]
         else:
@@ -425,17 +439,15 @@
     slots = total // rays
     half = keep_ref.shape[0]
     part = 2 * half // shares
-    moved = moved_ref[...]
-    high = moved.astype(bf16)
-    low = (moved - high.astype(f32)).astype(bf16)
+    moved = moved_ref[...].astype(bf16)
     row = lax.broadcasted_iota(jnp.int32, (part, rays), 0).astype(f32)
-    for i, t in enumerate(halving_order(shares)):
-        first = ((share ^ t) * part).astype(f32)
+    for i in range(shares):
+        first = ((share ^ i) * part).astype(f32)
         acc = jnp.zeros((part, width), f32)
         for k in range(slots):
             one_hot = jnp.where(row + first == lines_ref[k : k + 1, :], 1.0, 0.0).astype(bf16)
             rows = slice(k * rays, (k + 1) * rays)
-            acc = acc + nn_dot(one_hot, high[rows]) + nn_dot(one_hot, low[rows])
+            acc = acc + nn_dot(one_hot, moved[rows])
         ref, at = (keep_ref, i * part) if i < shares // 2 else (send_ref, i * part - half)
         ref[at : at + part, :] = acc
 
@@ -493,64 +505,89 @@
         return tuple(sums[c] + s8 * acc[c] for c in range(outs))
 
     sums = [jnp.zeros((8, width), f32)] * outs
-    sums = lax.fori_loop(0, samples // 8, sample_block, tuple(sums), unroll=2)
+    sums = lax.fori_loop(0, samples // 8, sample_block, tuple(sums), unroll=4)
     for c in range(outs):
         sums_ref[c] = sums[c]
         bias_ref[c : c + 1, :] = bias_sums[c]
 
 
-def network_kernel(*refs, parts, slots, rows, owners):
-    part_refs, refs = refs[: 3 * parts], refs[3 * parts :]
-    h1_refs, refs = refs[:slots], refs[slots:]
-    cot_ref, u_ref, slot_ref, chosen_ref, sorted_ref, low_ref, small_ref, color_ref = refs
-    by_sample = jnp.concatenate([part_refs[3 * i][...] for i in range(parts)], 0)
-    samples, width = by_sample.shape
-    rays = sorted_ref.shape[0]
+def slots_kernel(*refs, pieces, rows, owners):
+    h1_refs, refs = refs[:pieces], refs[pieces:]
+    basis_refs, refs = refs[:pieces], refs[pieces:]
+    cot_ref, u_ref, chosen_ref, sorted_ref, low_ref, *refs = refs
+    moved_ref, w_grad_ref, sums_ref, color_ref, slot_ref = refs
+    rays, width = sorted_ref.shape
+    span = h1_refs[0].shape[1]
+    slots = pieces * span // rays
     outs = color_ref.shape[0] + 1
     channels = outs - 1
     own = rays // owners
     me = lax.axis_index("slab")
     r_i = lax.broadcasted_iota(jnp.int32, (rays, own), 0)
     c_i = lax.broadcasted_iota(jnp.int32, (rays, own), 1)
-    pick = jnp.where(r_i == c_i + me * own, 1.0, 0.0).astype(f32)
-    color_ref[...] = nn_dot(cot_ref[outs : outs + channels, :], pick, exact)
+    pick = jnp.where(r_i == c_i + me * own, 1.0, 0.0).astype(bf16)
+    color = cot_ref[outs : outs + channels, :]
+    high = color.astype(bf16)
+    middle = (color - high.astype(f32)).astype(bf16)
+    low = (color - high.astype(f32) - middle.astype(f32)).astype(bf16)
+    picked = nn_dot(jnp.concatenate([high, middle, low], 0), pick)
+    color_ref[...] = picked[:channels] + picked[channels : 2 * channels] + picked[2 * channels :]
+    w_out = low_ref[rows["w_out"], :].astype(f32)
+    w_rows = [w_out[c : c + 1, :] for c in range(outs)]
     sums = [jnp.zeros((8, width), f32)] * outs
-    chunk = 128
+    chunk = 32
     for n in range(rays // chunk):
-        these = slice(n * chunk, (n + 1) * chunk)
-        turned = cot_ref[:, these].T
-        cots = [jnp.broadcast_to(turned[:, c : c + 1], (chunk, width)) for c in range(outs)]
+        if n % (128 // chunk) == 0:
+            turned = cot_ref[:, n * chunk : n * chunk + 128].T
+        at = (n * chunk) % 128
+        cots = [
+            jnp.broadcast_to(turned[at : at + chunk, c : c + 1], (chunk, width))
+            for c in range(outs)
+        ]
         for k in range(slots):
-            u = u_ref[k * rays + n * chunk : k * rays + (n + 1) * chunk, :].astype(f32)
-            h1_ref = h1_refs[k]
-            products = [sum(cots[c] * h1_ref[c, these, :] for c in range(outs))]
-            products += [cots[c] * h1_ref[outs + c, these, :] for c in range(channels)]
+            at = k * rays + n * chunk
+            u = u_ref[at : at + chunk, :].astype(f32)
+            h1_ref, spot = h1_refs[at // span], slice(at % span, at % span + chunk)
+            products = [sum(cots[c] * h1_ref[c, spot, :] for c in range(outs))]
+            products += [cots[c] * h1_ref[outs + c, spot, :] for c in range(channels)]
             for c in range(outs):
                 sums[c] = sums[c] + jnp.sum((u * products[c]).reshape(chunk // 8, 8, width), 0)
-    w = low_ref[rows["w"], :]
-    sample = low_ref[rows["sample"], :].astype(f32)
+            slot_ref[at : at + chunk, :] = sum(w_rows[c] * products[c] for c in range(outs))
+            basis_ref = basis_refs[at // span]
+            moved_ref[at : at + chunk, :] = sum(cots[c] * basis_ref[c, spot, :] for c in range(outs))
+    for c in range(outs):
+        sums_ref[c] = sums[c]
     slot = slot_ref[...]
     slot_ray = slot[:rays, :]
     for k in range(1, slots):
         slot_ray = slot_ray + slot[k * rays : (k + 1) * rays, :]
     ray_t = sorted_ref[...].astype(f32).T.astype(bf16)
+    w_grad_ref[...] = nn_dot(chosen_ref[...], slot.astype(bf16)) + nn_dot(ray_t, slot_ray.astype(bf16))
+
+
+def flipped(a, b):
+    return nn_dot(b, a)
+
+
+def network_kernel(*refs, parts, rows):
+    part_refs, refs = refs[: 3 * parts], refs[3 * parts :]
+    w_grad_ref, sums_ref, low_ref, small_ref = refs
+    by_sample = jnp.concatenate([part_refs[3 * i][...] for i in range(parts)], 0)
+    samples, width = by_sample.shape
+    outs = sums_ref.shape[0]
+    w = low_ref[rows["w"], :]
+    sample = low_ref[rows["sample"], :].astype(f32)
     sample_t = jnp.concatenate([sample] * (128 // samples), 0).T[:, :samples]
-
-    def flipped(a, b):
-        return nn_dot(b, a)
-
     small_ref[:samples, :] = split_dot(by_sample, w, nt_dot)
-    small_ref[samples : samples + width, :] = (
-        split_dot(slot, chosen_ref[...], flipped)
-        + split_dot(slot_ray, ray_t, flipped)
-        + split_dot(by_sample, sample_t.astype(bf16), flipped)
+    small_ref[samples : samples + width, :] = w_grad_ref[...] + split_dot(
+        by_sample, sample_t.astype(bf16), flipped
     )
     at = samples + width
     small_ref[at : at + 1, :] = jnp.sum(by_sample, 0, keepdims=True)
     lane128 = lax.broadcasted_iota(jnp.int32, (1, 128), 1)
     bias = jnp.zeros((1, 128), f32)
     for c in range(outs):
-        total = sums[c] + sum(part_refs[3 * i + 1][c] for i in range(parts))
+        total = sums_ref[c] + sum(part_refs[3 * i + 1][c] for i in range(parts))
         small_ref[at + 1 + c : at + 2 + c, :] = jnp.sum(total, 0, keepdims=True)
         row = sum(part_refs[3 * i + 2][c : c + 1, :] for i in range(parts))
         bias = bias + jnp.where(lane128 == c, jnp.sum(row, 1, keepdims=True), 0.0)
@@ -559,13 +596,14 @@
     small_ref[at + 2 + outs :, :] = jnp.zeros((rest, width), f32)
 
 
+def finish_ray_kernel(keep_ref, got_ref, out_ref):
+    out_ref[...] = keep_ref[...] + got_ref[...].astype(f32)
+
+
 def finish_kernel(
-    ray_ref,
-    ray_got_ref,
     brick_ref,
     sent_ref,
     got_ref,
-    ray_out_ref,
     brick_out_ref,
     sample_ref,
     w_ref,
@@ -573,7 +611,6 @@
     w_out_ref,
     b_out_ref,
 ):
-    ray_out_ref[...] = ray_ref[...] + ray_got_ref[...].astype(f32)
     part = brick_ref.shape[0]
     brick_out_ref[...] = brick_ref[...] + got_ref[:part, :].astype(f32)
     small = sent_ref[part:, :].astype(f32) + got_ref[part:, :].astype(f32)
@@ -620,28 +657,27 @@
 
     rows = low_rows(width, samples)
     lines = line_rows(slots, channels)
-    brick_t, gathered = call(
-        turn_kernel,
-        (shaped16(width, bricks), shaped16(*ray_code.shape)),
-        "turn",
+    earlier, later = call(
+        order_kernel,
+        (shaped16(samples, samples), shaped16(samples, samples)),
+        "order",
         flops=1 << 34,
-    )(brick_code[0], ray_code)
-    low, packed, w_t, s, wide, left, chosen, project = call(
+    )()
+    gathered, low, packed, w_t, s, wide, left = call(
         functools.partial(prepare_kernel, rows=rows, lines=lines),
         (
+            shaped16(*ray_code.shape),
             shaped16(rows["w_out"].stop, width),
             shaped(lines["b_out"] + 1, rays),
             shaped16(width, width),
             shaped(samples, width),
             shaped16(samples, width, 128),
             shaped16(outs * 8, 8 * width),
-            shaped16(width, total),
-            shaped(width, total),
         ),
         "prepare",
         flops=1 << 31,
     )(
-        brick_t,
+        ray_code,
         w_hidden[0],
         sample_code[0],
         w_out[0],
@@ -652,18 +688,27 @@
         b_hidden,
         b_out,
     )
-    other = swap(ray_code, "slab", owners, 1)
-    for b in range(1, bits_of(owners)):
+    turns = gather_bits(owners, ray_code.shape[0])
+    other = swap(ray_code, "slab", owners, 1 << turns[0])
+    other, lines_later = lax.optimization_barrier((other, packed))
+    for b in turns[1:]:
         gathered = jnp.concatenate([gathered, other], 0)
         other = swap(gathered, "slab", owners, 1 << b)
+    chosen, project = call(
+        chosen_kernel,
+        (shaped16(width, total), shaped(width, total)),
+        "chosen",
+        flops=1 << 29,
+    )(lines_later, brick_code[0], w_t)
     passes = ()
+    kept = []
     for second, part in enumerate((gathered, other)):
         wide_rays = rays if second else rays // 2
-        passes = call(
+        seg, kept_half, *passes = call(
             functools.partial(forward_kernel, owners=owners, second=second, lines=lines),
             (
                 shaped(outs, wide_rays),
-                shaped(2 * outs, samples, slots * wide_rays),
+                shaped(2 * outs, samples, total // 2),
                 shaped16(slots * wide_rays, width),
                 shaped16(wide_rays, width),
             ),
@@ -674,31 +719,38 @@
                 pltpu.VMEM((outs, samples, total // 2), f32),
             ),
             flops=1 << 30,
-        )(part, project, w_t, wide, left, packed, *passes)
-    seg, kept, u, ray_sorted = passes
+        )(part, project, w_t, wide, left, packed, earlier, *passes)
+        passes = (seg, *passes)
+        kept.append(kept_half)
+    seg, u, ray_sorted = passes
 
     coef, turned = call(
-        coefficient_kernel,
+        functools.partial(coefficient_kernel, owners=owners),
         (shaped(count, samples, total), shaped(count, total, 128)),
         "coefficients",
-        flops=1 << 31,
-    )(seg, kept)
-    basis = [
-        call(
-            functools.partial(basis_kernel, slot=k),
-            shaped(count, rays, width),
-            "basis",
-            flops=1 << 31,
-        )(turned, u, s)
-        for k in range(slots)
-    ]
-
+        flops=1 << 30,
+    )(seg, *kept, later)
     forward = packed[lines["direction"]][None] == 0.0
     group = (seg[:channels], seg[channels:])
     received = []
-    for b in range(bits_of(owners)):
+    basis = []
+    pieces = 4
+    piece = total // pieces
+    bits = bits_of(owners)
+    turned_later = turned
+    for b in range(bits):
         sent = jnp.concatenate(group, 0) if b > 0 else seg
         other = swap(sent, "slab", owners, 1 << b)
+        while len(basis) < min(pieces, pieces * (b + 1) // bits):
+            basis.append(
+                call(
+                    functools.partial(basis_kernel, first=len(basis) * piece, row_of=rows),
+                    (shaped(count, piece, width), shaped(outs, piece, width)),
+                    "basis",
+                    flops=1 << 29,
+                )(turned_later, u, s, low)
+            )
+        other, turned_later = lax.optimization_barrier((other, turned_later))
         received.append(other)
         theirs = (other[:channels], other[channels:])
         upper = ((me >> b) & 1) == 1
@@ -706,19 +758,31 @@
         second = jax.tree.map(lambda a, b: jnp.where(upper, a, b), group, theirs)
         group = merge(first, second, forward)
 
-    ray_keep, ray_send, moved, slot_grad, cots = call(
-        functools.partial(middle_kernel, owners=owners, slots=slots, rows=rows, lines=lines),
+    h1, moved_basis = zip(*basis)
+    ray_keep, ray_send, cots = call(
+        functools.partial(middle_kernel, owners=owners, pieces=pieces, lines=lines),
         (
             shaped(rays // 2, width),
             shaped16(rays // 2, width),
-            shaped(total, width),
-            shaped(total, width),
             shaped(8, rays),
         ),
         "middle",
         scratch=(pltpu.VMEM((rays, width), f32),),
-        flops=1 << 31,
-    )(seg, *received, *basis, packed, low)
+        flops=1 << 29,
+    )(seg, *received, *moved_basis, packed)
+    moved, w_grad, sums, color_own = call(
+        functools.partial(slots_kernel, pieces=pieces, rows=rows, owners=owners),
+        (
+            shaped(total, width),
+            shaped(width, width),
+            shaped(outs, 8, width),
+            shaped(channels, rays // owners),
+        ),
+        "slots",
+        scratch=(pltpu.VMEM((total, width), f32),),
+        flops=1 << 28,
+    )(*h1, *moved_basis, cots, u, chosen, ray_sorted, low)
+
     def merged(keep, got):
         half = keep.shape[0] // 2
         return keep[:half] + got[:half].astype(f32), (keep[half:] + got[half:].astype(f32)).astype(bf16)
@@ -739,41 +803,47 @@
     parts = 2
     by_part = []
     later_cots = cots
-    for b in range(bits_of(owners)):
-        ray_got = swap(ray_send, "slab", owners, 1 << b)
+    for b in range(bits):
+        if b + 1 == bits:
+            brick_keep, brick_send = call(
+                functools.partial(brick_kernel, shares=shares),
+                (shaped(bricks // 2, width), shaped(bricks // 2, width)),
+                "bricks",
+                flops=1 << 28,
+            )(packed, moved)
+            small_rows = -(-(samples + width + 2 + outs) // 16) * 16
+            small = call(
+                functools.partial(network_kernel, parts=parts, rows=rows),
+                shaped(small_rows, width),
+                "network",
+                flops=1 << 28,
+            )(*by_part, w_grad, sums, low)
+            held = (ray_send, brick_send, small)
+            ray_send, brick_send, small = lax.optimization_barrier(held)
+        ray_got = swap(ray_send, "slab", owners, owners >> (b + 1))
         if b < parts:
             by_part += part_by_sample(b, later_cots)
-        if b + 1 < bits_of(owners):
-            ray_got, later_cots, moved = lax.optimization_barrier((ray_got, later_cots, moved))
+        if b + 1 < bits:
+            held = (ray_got, later_cots, moved)
+            ray_got, later_cots, moved = lax.optimization_barrier(held)
             ray_keep, ray_send = merged(ray_keep, ray_got)
-    brick_keep, brick_send = call(
-        functools.partial(brick_kernel, shares=shares),
-        (shaped(bricks // 2, width), shaped(bricks // 2, width)),
-        "bricks",
-        flops=1 << 28,
-    )(packed, moved)
-    small_rows = -(-(samples + width + 2 + outs) // 16) * 16
-    small, color_own = call(
-        functools.partial(network_kernel, parts=parts, slots=slots, rows=rows, owners=owners),
-        (shaped(small_rows, width), shaped(channels, rays // owners)),
-        "network",
-        flops=1 << 28,
-    )(*by_part, *basis, cots, u, slot_grad, chosen, ray_sorted, low)
-
-    brick = brick_keep + swap(brick_send, "ray", shares, 1)
-    small = small + swap(small, "ray", shares, 1)
-    for b in range(1, bits_of(shares)):
-        half = brick.shape[0] // 2
-        sent = jnp.concatenate([brick[half:], small], 0).astype(bf16)
+
+    brick = brick_keep
+    brick_sent = brick_send.astype(bf16)
+    for b in reversed(range(bits_of(shares))):
+        sent = jnp.concatenate([brick_sent, small.astype(bf16)], 0)
         other = swap(sent, "ray", shares, 1 << b)
-        brick = brick[:half]
-        if b + 1 < bits_of(shares):
-            brick = brick + other[:half].astype(f32)
+        if b > 0:
+            half = brick.shape[0]
             small = sent[half:].astype(f32) + other[half:].astype(f32)
-    ray_out, brick_out, sample_out, w_grad, b_grad, w_out_grad, b_out_grad = call(
+            brick_sent = (brick[half // 2 :] + other[half // 2 : half].astype(f32)).astype(bf16)
+            brick = brick[: half // 2] + other[: half // 2].astype(f32)
+    ray_out = call(finish_ray_kernel, shaped(rays // owners, width), "finish_ray", flops=1 << 31)(
+        ray_keep, ray_got
+    )
+    brick_out, sample_out, w_grad, b_grad, w_out_grad, b_out_grad = call(
         finish_kernel,
         (
-            shaped(rays // owners, width),
             shaped(bricks // shares, width),
             shaped(samples, width),
             shaped(width, width),
@@ -782,7 +852,7 @@
             shaped(1, outs),
         ),
         "finish",
-    )(ray_keep, ray_got, brick, sent, other)
+    )(brick, sent, other)
     return (
         color_own,
         ray_out,

time: 54.8 us -> 49.9 us (0.911)
  waiting for transfers between devices: 12.2 us -> 7.1 us
  local copies, waits for them, and re-layouts: 2.29 us -> 0.07 us
  starting transfers between devices: 19.1 us -> 20.8 us
  Pallas kernels: 19.9 us -> 20.5 us
    ppermute x12 -> x11, waiting for transfers between devices: 12.2 us -> 7.1 us  [swap(): return lax.ppermute(array, axis, [(i, i ^ distance) for i in range(size)])]
    unnamed x24, local copies, waits for them, and re-layouts: 2.26 us -> 0.06 us
    ppermute x12 -> x11, starting transfers between devices: 19.1 us -> 20.8 us  [swap(): return lax.ppermute(array, axis, [(i, i ^ distance) for i in range(size)])]
    pallas_call x13 -> x18, Pallas kernels: 19.9 us -> 20.5 us  [run(): pl.pallas_call(kernel, out_shape=out_shape, in_specs=[pl.BlockSpec(memory...]
  transfers between devices with their start and end apart: 12 -> 11, of which waited for: 8 -> 7; matrix products, arithmetic and copies ran while one was open for 0% -> 0% of each run, Pallas kernels for 22% -> 33%
where the time goes in v3:
time: 49.9 us; the launch traced here: 49.7 us
  starting transfers between devices  20.8 us (42%)
  Pallas kernels  20.5 us (41%)
  waiting for transfers between devices  7.1 us (14%)
  between operations  1.04 us (2%)
    ppermute x11, starting transfers between devices, swap(): return lax.ppermute(array, axis, [(i, i ^ distance) for i in range(size)])  20.8 us
    pallas_call x18, Pallas kernels, run(): pl.pallas_call(kernel, out_shape=out_shape, in_specs=[pl.BlockSpec(memory...  20.5 us
    ppermute x11, waiting for transfers between devices, swap(): return lax.ppermute(array, axis, [(i, i ^ distance) for i in range(size)])  7.1 us
  transfers between devices with their start and end apart: 11, of which 7 were waited for; matrix products, arithmetic and copies ran while one was open for 0% of the time, Pallas kernels for 33%

profile of v3, /device:TPU:0, one launch (start us, length us, event | category | flops | bytes accessed | tf_op | source)
XLA Modules:
  0.0 49.7 jit_solution(17016608078466579499)
XLA Ops:
  0.7 4.1 %collective-permute-start = (bf16[64,128]{1,0:T(8,128)(2,1)}, bf16[64,128]{1,0:T(8,128)(2,1)S(1)}, u32[]{:S(2)}, u32[]{:S(2)}) collective-permute-start(bf16[64,128]{1,0:T(8,128)(2,1)} %ray_ref.1), channel_id=1, source_target_pairs={{0,16},{4,20},{8,24},{12,28},{16,0},{20,4},{24,8},{28,12},{1,17},{... | collective-permute-start | bytes 49160 | tf_op jit(solution)/shard_map/ppermute | solution.py:52
  5.0 1.0 %prepare.1 = (bf16[64,128]{1,0:T(8,128)(2,1)S(1)}, bf16[208,128]{1,0:T(8,128)(2,1)S(1)}, f32[8,512]{1,0:T(8,128)S(1)}, bf16[128,128]{1,0:T(8,128)(2,1)S(1)}, f32...) custom-call(bf16[64,128]{1,0:T(8,128)(2,1)S(1)} %copy-done.3, ...), custom_call_target="tpu_custom_call" | custom-call | flops 2147483648 | bytes 1048576 | tf_op jit(solution)/shard_map/prepare/pallas_call | solution.py:63
  6.8 1.9 %collective-permute-start.1 = (bf16[128,128]{1,0:T(8,128)(2,1)S(1)}, bf16[128,128]{1,0:T(8,128)(2,1)S(1)}, u32[]{:S(2)}, u32[]{:S(2)}) collective-permute-start(bf16[128,128]{1,0:T(8,128)(2,1)S(1)} %pad_maximum_fusion.2), channel_id=1, source_target_pairs={{0,4},{4,0},{8,12},{12,8},{16,20},{20,16},{24,28},{28,24},{1,5},{5... | collective-permute-start | bytes 98312 | tf_op jit(solution)/shard_map/ppermute | solution.py:52
  9.5 1.2 %collective-permute-done.1 = bf16[128,128]{1,0:T(8,128)(2,1)S(1)} collective-permute-done((bf16[128,128]{1,0:T(8,128)(2,1)S(1)}, bf16[128,128]{1,0:T(8,128)(2,1)S(1)}, u32[]{:S(2)}, u32[]{:S(2)}) %collective-permute-start.1) | collective-permute-done | bytes 32800 | tf_op jit(solution)/shard_map/ppermute | solution.py:52
  10.7 1.9 %collective-permute-start.2 = (bf16[256,128]{1,0:T(8,128)(2,1)S(1)}, bf16[256,128]{1,0:T(8,128)(2,1)S(1)}, u32[]{:S(2)}, u32[]{:S(2)}) collective-permute-start(bf16[256,128]{1,0:T(8,128)(2,1)S(1)} %constant_dynamic-update-slice_fusion.refs_0_), channel_id=1, source_target_pairs={{0,8},{4,12},{8,0},{12,4},{16,24},{20,28},{24,16},{28,20},{1,9},{5... | collective-permute-start | bytes 196616 | tf_op jit(solution)/shard_map/ppermute | solution.py:52
  12.6 2.0 %forward.2 = (f32[4,256]{1,0:T(4,128)S(1)}, f32[8,64,512]{2,1,0:T(8,128)S(1)}, bf16[512,128]{1,0:T(8,128)(2,1)S(1)}, bf16[256,128]{1,0:T(8,128)(2,1)S(1)}) custom-call(bf16[256,128]{1,0:T(8,128)(2,1)S(1)} %constant_dynamic-update-slice_fusion.refs_0_, f32[128,1024]{1,0:T(8,128)S(1)} %get-tuple-element.78.refs_1_, ...), custom_call_target="tpu_custom_call" | custom-call | flops 1073741824 | bytes 1048576 | tf_op jit(solution)/shard_map/forward/pallas_call | solution.py:63
  15.0 2.0 %forward.3 = (f32[4,512]{1,0:T(4,128)S(1)}, f32[8,64,512]{2,1,0:T(8,128)S(1)}, bf16[1024,128]{1,0:T(8,128)(2,1)S(1)}, bf16[512,128]{1,0:T(8,128)(2,1)S(1)}) custom-call(bf16[256,128]{1,0:T(8,128)(2,1)S(1)} %collective-permute-done.2.refs_0_, f32[128,1024]{1,0:T(8,128)S(1)} %get-tuple-element.78.refs_1_, ...), custom_call_target="tpu_custom_call" | custom-call | flops 1073741824 | bytes 1048576 | tf_op jit(solution)/shard_map/forward/pallas_call | solution.py:63
  17.0 2.0 %collective-permute-start.3 = (f32[4,512]{1,0:T(4,128)S(1)}, f32[4,512]{1,0:T(4,128)S(1)}, u32[]{:S(2)}, u32[]{:S(2)}) collective-permute-start(f32[4,512]{1,0:T(4,128)S(1)} %get-tuple-element.85.seg_ref.refs_0_), channel_id=1, source_target_pairs={{0,4},{4,0},{8,12},{12,8},{16,20},{20,16},{24,28},{28,24},{1,5},{5... | collective-permute-start | bytes 24584 | tf_op jit(solution)/shard_map/ppermute | solution.py:52
  19.0 1.3 %coefficients.1 = (f32[7,64,1024]{2,1,0:T(8,128)S(1)}, f32[7,1024,128]{2,1,0:T(8,128)S(1)}) custom-call(f32[4,512]{1,0:T(4,128)S(1)} %get-tuple-element.85.seg_ref.refs_0_, f32[8,64,512]{2,1,0:T(8,128)S(1)} %get-tuple-element.86.first_ref, f32[8,64,512]{2,1,0:T(8,128)S(1)} %get-tuple-element.87.second_ref, bf16[64,64]{1,0:T(8,128)(2,1)S(1)} %get-tuple-element.88.later_ref), custom_call_target="tpu_custom_call" | custom-call | flops 1073741824 | bytes 1048576 | tf_op jit(solution)/shard_map/coefficients/pallas_call | solution.py:63
  20.3 1.3 %basis.4 = (f32[7,256,128]{2,1,0:T(8,128)S(1)}, f32[4,256,128]{2,1,0:T(8,128)S(1)}) custom-call(f32[7,1024,128]{2,1,0:T(8,128)S(1)} %get-tuple-element.97.turned_ref, bf16[1024,128]{1,0:T(8,128)(2,1)S(1)} %get-tuple-element.90.u_ref.refs_9_, f32[64,128]{1,0:T(8,128)S(1)} %get-tuple-element.91.s_ref, ...), custom_call_target="tpu_custom_call" | custom-call | flops 536870912 | bytes 1048576 | tf_op jit(solution)/shard_map/basis/pallas_call | solution.py:63
  21.7 1.6 %collective-permute-start.4 = (f32[4,512]{1,0:T(4,128)S(1)}, f32[4,512]{1,0:T(4,128)S(1)}, u32[]{:S(2)}, u32[]{:S(2)}) collective-permute-start(f32[4,512]{1,0:T(4,128)S(1)} %pad_maximum_fusion.3), channel_id=1, source_target_pairs={{0,8},{4,12},{8,0},{12,4},{16,24},{20,28},{24,16},{28,20},{1,9},{5... | collective-permute-start | bytes 24584 | tf_op jit(solution)/shard_map/ppermute | solution.py:52
  23.2 1.1 %basis.5 = (f32[7,256,128]{2,1,0:T(8,128)S(1)}, f32[4,256,128]{2,1,0:T(8,128)S(1)}) custom-call(f32[7,1024,128]{2,1,0:T(8,128)S(1)} %get-tuple-element.97.turned_ref, bf16[1024,128]{1,0:T(8,128)(2,1)S(1)} %get-tuple-element.90.u_ref.refs_9_, f32[64,128]{1,0:T(8,128)S(1)} %get-tuple-element.91.s_ref, ...), custom_call_target="tpu_custom_call" | custom-call | flops 536870912 | bytes 1048576 | tf_op jit(solution)/shard_map/basis/pallas_call | solution.py:63
  24.3 1.0 %collective-permute-done.4.refs_2_ = f32[4,512]{1,0:T(4,128)S(1)} collective-permute-done((f32[4,512]{1,0:T(4,128)S(1)}, f32[4,512]{1,0:T(4,128)S(1)}, u32[]{:S(2)}, u32[]{:S(2)}) %collective-permute-start.4) | collective-permute-done | bytes 8224 | tf_op jit(solution)/shard_map/ppermute | solution.py:52
  25.4 2.6 %collective-permute-start.5 = (f32[4,512]{1,0:T(4,128)S(1)}, f32[4,512]{1,0:T(4,128)S(1)}, u32[]{:S(2)}, u32[]{:S(2)}) collective-permute-start(f32[4,512]{1,0:T(4,128)S(1)} %pad_maximum_fusion.4), channel_id=1, source_target_pairs={{0,16},{4,20},{8,24},{12,28},{16,0},{20,4},{24,8},{28,12},{1,17},{... | collective-permute-start | bytes 24584 | tf_op jit(solution)/shard_map/ppermute | solution.py:52
  28.0 1.1 %basis.7 = (f32[7,256,128]{2,1,0:T(8,128)S(1)}, f32[4,256,128]{2,1,0:T(8,128)S(1)}) custom-call(f32[7,1024,128]{2,1,0:T(8,128)S(1)} %get-tuple-element.97.turned_ref, bf16[1024,128]{1,0:T(8,128)(2,1)S(1)} %get-tuple-element.90.u_ref.refs_9_, f32[64,128]{1,0:T(8,128)S(1)} %get-tuple-element.91.s_ref, ...), custom_call_target="tpu_custom_call" | custom-call | flops 536870912 | bytes 1048576 | tf_op jit(solution)/shard_map/basis/pallas_call | solution.py:63
  29.1 1.1 %basis.6 = (f32[7,256,128]{2,1,0:T(8,128)S(1)}, f32[4,256,128]{2,1,0:T(8,128)S(1)}) custom-call(f32[7,1024,128]{2,1,0:T(8,128)S(1)} %get-tuple-element.97.turned_ref, bf16[1024,128]{1,0:T(8,128)(2,1)S(1)} %get-tuple-element.90.u_ref.refs_9_, f32[64,128]{1,0:T(8,128)S(1)} %get-tuple-element.91.s_ref, ...), custom_call_target="tpu_custom_call" | custom-call | flops 536870912 | bytes 1048576 | tf_op jit(solution)/shard_map/basis/pallas_call | solution.py:63
  30.9 2.4 %collective-permute-start.6 = (bf16[256,128]{1,0:T(8,128)(2,1)S(1)}, bf16[256,128]{1,0:T(8,128)(2,1)S(1)}, u32[]{:S(2)}, u32[]{:S(2)}) collective-permute-start(bf16[256,128]{1,0:T(8,128)(2,1)S(1)} %get-tuple-element.111), channel_id=1, source_target_pairs={{0,16},{4,20},{8,24},{12,28},{16,0},{20,4},{24,8},{28,12},{1,17},{... | collective-permute-start | bytes 196616 | tf_op jit(solution)/shard_map/ppermute | solution.py:52
  33.3 1.9 %by_sample.2 = (f32[32,128]{1,0:T(8,128)S(1)}, f32[4,8,128]{2,1,0:T(8,128)S(1)}, f32[4,128]{1,0:T(4,128)S(1)}) custom-call(f32[8,512]{1,0:T(8,128)S(1)} %get-tuple-element.114.refs_8_.cot_ref, f32[7,64,1024]{2,1,0:T(8,128)S(1)} %get-tuple-element.119.coef_ref, bf16[1024,128]{1,0:T(8,128)(2,1)S(1)} %get-tuple-element.90.u_ref.refs_9_, ...), custom_call_target="tpu_custom_call" | custom-call | flops 268435456 | bytes 1048576 | tf_op jit(solution)/shard_map/by_sample/pallas_call | solution.py:63
  35.2 1.9 %slots.1 = (f32[1024,128]{1,0:T(8,128)S(1)}, f32[128,128]{1,0:T(8,128)S(1)}, f32[4,8,128]{2,1,0:T(8,128)S(1)}, f32[3,64]{1,0:T(4,128)}) custom-call(f32[7,256,128]{2,1,0:T(8,128)S(1)} %get-tuple-element.93.refs_0_, f32[7,256,128]{2,1,0:T(8,128)S(1)} %get-tuple-element.95.refs_1_, f32[7,256,128]{2,1,0:T(8,128)S(1)} %get-tuple-element.98.refs_2_, ...), custom_call_target="tpu_custom_call" | custom-call | flops 268435456 | bytes 1048576 | tf_op jit(solution)/shard_map/slots/pallas_call | solution.py:63
  37.1 1.7 %collective-permute-start.7 = (bf16[128,128]{1,0:T(8,128)(2,1)S(1)}, bf16[128,128]{1,0:T(8,128)(2,1)S(1)}, u32[]{:S(2)}, u32[]{:S(2)}) collective-permute-start(bf16[128,128]{1,0:T(8,128)(2,1)S(1)} %get-tuple-element.146), channel_id=1, source_target_pairs={{0,8},{4,12},{8,0},{12,4},{16,24},{20,28},{24,16},{28,20},{1,9},{5... | collective-permute-start | bytes 98312 | tf_op jit(solution)/shard_map/ppermute | solution.py:52
  38.8 1.9 %by_sample.3 = (f32[32,128]{1,0:T(8,128)S(1)}, f32[4,8,128]{2,1,0:T(8,128)S(1)}, f32[4,128]{1,0:T(4,128)S(1)}) custom-call(f32[8,512]{1,0:T(8,128)S(1)} %get-tuple-element.114.refs_8_.cot_ref, f32[7,64,1024]{2,1,0:T(8,128)S(1)} %get-tuple-element.119.coef_ref, bf16[1024,128]{1,0:T(8,128)(2,1)S(1)} %get-tuple-element.90.u_ref.refs_9_, ...), custom_call_target="tpu_custom_call" | custom-call | flops 268435456 | bytes 1048576 | tf_op jit(solution)/shard_map/by_sample/pallas_call | solution.py:63
  41.9 1.6 %collective-permute-start.9 = (bf16[720,128]{1,0:T(8,128)(2,1)S(1)}, bf16[720,128]{1,0:T(8,128)(2,1)S(1)}, u32[]{:S(2)}, u32[]{:S(2)}) collective-permute-start(bf16[720,128]{1,0:T(8,128)(2,1)S(1)} %pad_maximum_fusion), channel_id=1, source_target_pairs={{0,2},{1,3},{2,0},{3,1},{4,6},{5,7},{6,4},{7,5},{8,10},{9,11},{10,... | collective-permute-start | bytes 552968 | tf_op jit(solution)/shard_map/ppermute | solution.py:52
  43.5 1.0 %collective-permute-start.8 = (bf16[64,128]{1,0:T(8,128)(2,1)S(1)}, bf16[64,128]{1,0:T(8,128)(2,1)S(1)}, u32[]{:S(2)}, u32[]{:S(2)}) collective-permute-start(bf16[64,128]{1,0:T(8,128)(2,1)S(1)} %get-tuple-element.128), channel_id=1, source_target_pairs={{0,4},{4,0},{8,12},{12,8},{16,20},{20,16},{24,28},{28,24},{1,5},{5... | collective-permute-start | bytes 49160 | tf_op jit(solution)/shard_map/ppermute | solution.py:52
  44.5 3.0 %collective-permute-done.9 = bf16[720,128]{1,0:T(8,128)(2,1)S(1)} collective-permute-done((bf16[720,128]{1,0:T(8,128)(2,1)S(1)}, bf16[720,128]{1,0:T(8,128)(2,1)S(1)}, u32[]{:S(2)}, u32[]{:S(2)}) %collective-permute-start.9) | collective-permute-done | bytes 184352 | tf_op jit(solution)/shard_map/ppermute | solution.py:52
  (57 shorter events, 6.0 us)
Async XLA Ops:
  0.6 4.2 %copy-start.3 = (bf16[64,128]{1,0:T(8,128)(2,1)S(1)}, bf16[64,128]{1,0:T(8,128)(2,1)}, u32[]{:S(2)}) copy-start(bf16[64,128]{1,0:T(8,128)(2,1)} %ray_ref.1) | copy-start | bytes 49156
  0.6 4.2 %copy-start.6 = (s32[1,512]{1,0:T(1,128)S(1)}, s32[1,512]{1,0:T(1,128)}, u32[]{:S(2)}) copy-start(s32[1,512]{1,0:T(1,128)} %occ_ref.1) | copy-start | bytes 6148
  0.7 4.2 %copy-start.5 = (s32[1,2,512]{2,1,0:T(2,128)S(1)}, s32[1,2,512]{2,1,0:T(2,128)}, u32[]{:S(2)}) copy-start(s32[1,2,512]{2,1,0:T(2,128)} %param.20) | copy-start | bytes 12292
  0.7 4.2 %copy-start.10 = (f32[1,4]{1,0:T(1,128)S(1)}, f32[1,4]{1,0:T(1,128)}, u32[]{:S(2)}) copy-start(f32[1,4]{1,0:T(1,128)} %b_out_ref.1) | copy-start | bytes 52
  0.7 4.2 %copy-start.8 = (bf16[1,4,128]{2,1,0:T(4,128)(2,1)S(1)}, bf16[1,4,128]{2,1,0:T(4,128)(2,1)}, u32[]{:S(2)}) copy-start(bf16[1,4,128]{2,1,0:T(4,128)(2,1)} %param.18) | copy-start | bytes 3076
  0.7 4.2 %copy-start.9 = (f32[1,128]{1,0:T(1,128)S(1)}, f32[1,128]{1,0:T(1,128)}, u32[]{:S(2)}) copy-start(f32[1,128]{1,0:T(1,128)} %b_ref.1) | copy-start | bytes 1540
  0.7 4.2 %copy-start.1 = (bf16[1,128,128]{2,1,0:T(8,128)(2,1)S(1)}, bf16[1,128,128]{2,1,0:T(8,128)(2,1)}, u32[]{:S(2)}) copy-start(bf16[1,128,128]{2,1,0:T(8,128)(2,1)} %param.16) | copy-start | bytes 98308
  0.7 4.2 %copy-start.2 = (bf16[1,64,128]{2,1,0:T(8,128)(2,1)S(1)}, bf16[1,64,128]{2,1,0:T(8,128)(2,1)}, u32[]{:S(2)}) copy-start(bf16[1,64,128]{2,1,0:T(8,128)(2,1)} %param.15) | copy-start | bytes 49156
  0.7 4.2 %copy-start.4 = (f32[3,512]{1,0:T(4,128)S(1)}, f32[3,512]{1,0:T(4,128)}, u32[]{:S(2)}) copy-start(f32[3,512]{1,0:T(4,128)} %target_ref.1) | copy-start | bytes 18436
  0.7 4.2 %copy-start.7 = (s32[512]{0:T(512)S(1)}, s32[512]{0:T(512)}, u32[]{:S(2)}) copy-start(s32[512]{0:T(512)} %param.12) | copy-start | bytes 6148
  0.7 6.0 %collective-permute-start = (bf16[64,128]{1,0:T(8,128)(2,1)}, bf16[64,128]{1,0:T(8,128)(2,1)S(1)}, u32[]{:S(2)}, u32[]{:S(2)}) collective-permute-start(bf16[64,128]{1,0:T(8,128)(2,1)} %ray_ref.1), channel_id=1, source_target_pairs={{0,16},{4,20},{8,24},{12,28},{16,0},{20,4},{24,8},{28,12},{1,17},{... | collective-permute-start | bytes 49160 | tf_op jit(solution)/shard_map/ppermute | solution.py:52
  5.0 3.7 %copy-start = (bf16[1,1024,128]{2,1,0:T(8,128)(2,1)S(1)}, bf16[1,1024,128]{2,1,0:T(8,128)(2,1)}, u32[]{:S(2)}) copy-start(bf16[1,1024,128]{2,1,0:T(8,128)(2,1)} %param.14) | copy-start | bytes 786436
  6.8 3.9 %collective-permute-start.1 = (bf16[128,128]{1,0:T(8,128)(2,1)S(1)}, bf16[128,128]{1,0:T(8,128)(2,1)S(1)}, u32[]{:S(2)}, u32[]{:S(2)}) collective-permute-start(bf16[128,128]{1,0:T(8,128)(2,1)S(1)} %pad_maximum_fusion.2), channel_id=1, source_target_pairs={{0,4},{4,0},{8,12},{12,8},{16,20},{20,16},{24,28},{28,24},{1,5},{5... | collective-permute-start | bytes 98312 | tf_op jit(solution)/shard_map/ppermute | solution.py:52
  10.7 4.3 %collective-permute-start.2 = (bf16[256,128]{1,0:T(8,128)(2,1)S(1)}, bf16[256,128]{1,0:T(8,128)(2,1)S(1)}, u32[]{:S(2)}, u32[]{:S(2)}) collective-permute-start(bf16[256,128]{1,0:T(8,128)(2,1)S(1)} %constant_dynamic-update-slice_fusion.refs_0_), channel_id=1, source_target_pairs={{0,8},{4,12},{8,0},{12,4},{16,24},{20,28},{24,16},{28,20},{1,9},{5... | collective-permute-start | bytes 196616 | tf_op jit(solution)/shard_map/ppermute | solution.py:52
  17.0 4.6 %collective-permute-start.3 = (f32[4,512]{1,0:T(4,128)S(1)}, f32[4,512]{1,0:T(4,128)S(1)}, u32[]{:S(2)}, u32[]{:S(2)}) collective-permute-start(f32[4,512]{1,0:T(4,128)S(1)} %get-tuple-element.85.seg_ref.refs_0_), channel_id=1, source_target_pairs={{0,4},{4,0},{8,12},{12,8},{16,20},{20,16},{24,28},{28,24},{1,5},{5... | collective-permute-start | bytes 24584 | tf_op jit(solution)/shard_map/ppermute | solution.py:52
  21.7 3.7 %collective-permute-start.4 = (f32[4,512]{1,0:T(4,128)S(1)}, f32[4,512]{1,0:T(4,128)S(1)}, u32[]{:S(2)}, u32[]{:S(2)}) collective-permute-start(f32[4,512]{1,0:T(4,128)S(1)} %pad_maximum_fusion.3), channel_id=1, source_target_pairs={{0,8},{4,12},{8,0},{12,4},{16,24},{20,28},{24,16},{28,20},{1,9},{5... | collective-permute-start | bytes 24584 | tf_op jit(solution)/shard_map/ppermute | solution.py:52
  25.4 4.8 %collective-permute-start.5 = (f32[4,512]{1,0:T(4,128)S(1)}, f32[4,512]{1,0:T(4,128)S(1)}, u32[]{:S(2)}, u32[]{:S(2)}) collective-permute-start(f32[4,512]{1,0:T(4,128)S(1)} %pad_maximum_fusion.4), channel_id=1, source_target_pairs={{0,16},{4,20},{8,24},{12,28},{16,0},{20,4},{24,8},{28,12},{1,17},{... | collective-permute-start | bytes 24584 | tf_op jit(solution)/shard_map/ppermute | solution.py:52
  30.9 6.2 %collective-permute-start.6 = (bf16[256,128]{1,0:T(8,128)(2,1)S(1)}, bf16[256,128]{1,0:T(8,128)(2,1)S(1)}, u32[]{:S(2)}, u32[]{:S(2)}) collective-permute-start(bf16[256,128]{1,0:T(8,128)(2,1)S(1)} %get-tuple-element.111), channel_id=1, source_target_pairs={{0,16},{4,20},{8,24},{12,28},{16,0},{20,4},{24,8},{28,12},{1,17},{... | collective-permute-start | bytes 196616 | tf_op jit(solution)/shard_map/ppermute | solution.py:52
  37.1 4.0 %collective-permute-start.7 = (bf16[128,128]{1,0:T(8,128)(2,1)S(1)}, bf16[128,128]{1,0:T(8,128)(2,1)S(1)}, u32[]{:S(2)}, u32[]{:S(2)}) collective-permute-start(bf16[128,128]{1,0:T(8,128)(2,1)S(1)} %get-tuple-element.146), channel_id=1, source_target_pairs={{0,8},{4,12},{8,0},{12,4},{16,24},{20,28},{24,16},{28,20},{1,9},{5... | collective-permute-start | bytes 98312 | tf_op jit(solution)/shard_map/ppermute | solution.py:52
  41.9 5.6 %collective-permute-start.9 = (bf16[720,128]{1,0:T(8,128)(2,1)S(1)}, bf16[720,128]{1,0:T(8,128)(2,1)S(1)}, u32[]{:S(2)}, u32[]{:S(2)}) collective-permute-start(bf16[720,128]{1,0:T(8,128)(2,1)S(1)} %pad_maximum_fusion), channel_id=1, source_target_pairs={{0,2},{1,3},{2,0},{3,1},{4,6},{5,7},{6,4},{7,5},{8,10},{9,11},{10,... | collective-permute-start | bytes 552968 | tf_op jit(solution)/shard_map/ppermute | solution.py:52
  43.5 4.2 %collective-permute-start.8 = (bf16[64,128]{1,0:T(8,128)(2,1)S(1)}, bf16[64,128]{1,0:T(8,128)(2,1)S(1)}, u32[]{:S(2)}, u32[]{:S(2)}) collective-permute-start(bf16[64,128]{1,0:T(8,128)(2,1)S(1)} %get-tuple-element.128), channel_id=1, source_target_pairs={{0,4},{4,0},{8,12},{12,8},{16,20},{20,16},{24,28},{28,24},{1,5},{5... | collective-permute-start | bytes 49160 | tf_op jit(solution)/shard_map/ppermute | solution.py:52
  47.6 1.4 %collective-permute-start.10 = (bf16[464,128]{1,0:T(8,128)(2,1)S(1)}, bf16[464,128]{1,0:T(8,128)(2,1)S(1)}, u32[]{:S(2)}, u32[]{:S(2)}) collective-permute-start(bf16[464,128]{1,0:T(8,128)(2,1)S(1)} %pad_maximum_fusion.1.sent_ref), channel_id=1, source_target_pairs={{0,1},{1,0},{2,3},{3,2},{4,5},{5,4},{6,7},{7,6},{8,9},{9,8},{10,11... | collective-permute-start | bytes 356360 | tf_op jit(solution)/shard_map/ppermute | solution.py:52

commit v4 on v3

--- a/solution.py
+++ b/solution.py
@@ -28,6 +28,18 @@
 def gather_order(owners, own):
     order = [0]
     for b in gather_bits(owners, own)[:-1]:
+        order = order + [t ^ (1 << b) for t in order]
+    return order
+
+
+def halving_bits(owners):
+    bits = list(range(bits_of(owners)))
+    return bits[1:-1] + bits[:1] + bits[1:][-1:]
+
+
+def halving_order(owners):
+    order = [0]
+    for b in reversed(halving_bits(owners)):
         order = order + [t ^ (1 << b) for t in order]
     return order
 
@@ -361,6 +373,18 @@
         moved_ref[c] = nt_dot(grad.astype(bf16), w)
 
 
+def basis_cuts(total, bits):
+    eighth = total // 8
+    return [0, eighth, 5 * eighth, total] if bits > 2 else [0, total]
+
+
+def basis_part(refs, row):
+    for ref in refs:
+        if row < ref.shape[1]:
+            return ref, row
+        row -= ref.shape[1]
+
+
 def merge(first, second, forward):
     fc, ft = first
     sc, st = second
@@ -372,13 +396,13 @@
     seg_ref, refs = refs[0], refs[1:]
     got_refs, refs = refs[:bits], refs[bits:]
     moved_refs, refs = refs[:pieces], refs[pieces:]
-    lines_ref, keep_ref, send_ref, cot_ref, ray_ref = refs
+    lines_ref, keep_ref, send_ref, cot_ref, cot_t_ref, ray_ref = refs
     me = lax.axis_index("slab")
     outs = seg_ref.shape[0]
     channels = outs - 1
     rays = lines_ref.shape[1]
-    span, width = moved_refs[0].shape[1:]
-    slots = pieces * span // rays
+    width = moved_refs[0].shape[2]
+    slots = sum(ref.shape[1] for ref in moved_refs) // rays
     forward = lines_ref[lines["direction"] : lines["direction"] + 1, :] == 0.0
     target = lines_ref[lines["target"] : lines["target"] + channels, :]
 
@@ -412,19 +436,20 @@
     for n in range(rays // chunk):
         these = slice(n * chunk, (n + 1) * chunk)
         turned = cot_ref[:, these].T
+        cot_t_ref[these, :] = turned
         grad = None
         for c in range(outs):
             whole = None
             for k in range(slots):
-                at = k * rays + n * chunk
-                part = moved_refs[at // span][c, at % span : at % span + chunk, :]
+                ref, at = basis_part(moved_refs, k * rays + n * chunk)
+                part = ref[c, at : at + chunk, :]
                 whole = part if whole is None else whole + part
             term = jnp.broadcast_to(turned[:, c : c + 1], (chunk, width)) * whole
             grad = term if grad is None else grad + term
         ray_ref[these, :] = grad
     own = rays // owners
-    for i in range(owners):
-        place = pl.multiple_of((me ^ i) * own, own)
+    for i, t in enumerate(halving_order(owners)):
+        place = pl.multiple_of((me ^ t) * own, own)
         if i < owners // 2:
             keep_ref[i * own : (i + 1) * own, :] = ray_ref[pl.ds(place, own), :]
         else:
@@ -439,7 +464,7 @@
     slots = total // rays
     half = keep_ref.shape[0]
     part = 2 * half // shares
-    moved = moved_ref[...].astype(bf16)
+    moved = moved_ref[...]
     row = lax.broadcasted_iota(jnp.int32, (part, rays), 0).astype(f32)
     for i in range(shares):
         first = ((share ^ i) * part).astype(f32)
@@ -511,58 +536,44 @@
         bias_ref[c : c + 1, :] = bias_sums[c]
 
 
-def slots_kernel(*refs, pieces, rows, owners):
+def inputs_kernel(chosen_ref, sorted_ref, inputs_ref):
+    total = chosen_ref.shape[1]
+    ray_t = sorted_ref[...].astype(f32).T
+    inputs = chosen_ref[...].astype(f32) + jnp.concatenate([ray_t] * (total // ray_t.shape[1]), 1)
+    inputs_ref[...] = inputs.astype(bf16)
+
+
+def slots_kernel(*refs, pieces, rows):
     h1_refs, refs = refs[:pieces], refs[pieces:]
     basis_refs, refs = refs[:pieces], refs[pieces:]
-    cot_ref, u_ref, chosen_ref, sorted_ref, low_ref, *refs = refs
-    moved_ref, w_grad_ref, sums_ref, color_ref, slot_ref = refs
-    rays, width = sorted_ref.shape
-    span = h1_refs[0].shape[1]
-    slots = pieces * span // rays
-    outs = color_ref.shape[0] + 1
-    channels = outs - 1
-    own = rays // owners
-    me = lax.axis_index("slab")
-    r_i = lax.broadcasted_iota(jnp.int32, (rays, own), 0)
-    c_i = lax.broadcasted_iota(jnp.int32, (rays, own), 1)
-    pick = jnp.where(r_i == c_i + me * own, 1.0, 0.0).astype(bf16)
-    color = cot_ref[outs : outs + channels, :]
-    high = color.astype(bf16)
-    middle = (color - high.astype(f32)).astype(bf16)
-    low = (color - high.astype(f32) - middle.astype(f32)).astype(bf16)
-    picked = nn_dot(jnp.concatenate([high, middle, low], 0), pick)
-    color_ref[...] = picked[:channels] + picked[channels : 2 * channels] + picked[2 * channels :]
+    cot_t_ref, u_ref, inputs_ref, low_ref, *refs = refs
+    moved_ref, w_grad_ref, sums_ref, slot_ref = refs
+    rays = cot_t_ref.shape[0]
+    total, width = u_ref.shape
+    outs = sums_ref.shape[0]
     w_out = low_ref[rows["w_out"], :].astype(f32)
     w_rows = [w_out[c : c + 1, :] for c in range(outs)]
+    chunk = 32
     sums = [jnp.zeros((8, width), f32)] * outs
-    chunk = 32
     for n in range(rays // chunk):
-        if n % (128 // chunk) == 0:
-            turned = cot_ref[:, n * chunk : n * chunk + 128].T
-        at = (n * chunk) % 128
-        cots = [
-            jnp.broadcast_to(turned[at : at + chunk, c : c + 1], (chunk, width))
-            for c in range(outs)
-        ]
-        for k in range(slots):
-            at = k * rays + n * chunk
-            u = u_ref[at : at + chunk, :].astype(f32)
-            h1_ref, spot = h1_refs[at // span], slice(at % span, at % span + chunk)
-            products = [sum(cots[c] * h1_ref[c, spot, :] for c in range(outs))]
-            products += [cots[c] * h1_ref[outs + c, spot, :] for c in range(channels)]
+        turned = cot_t_ref[n * chunk : (n + 1) * chunk, :]
+        cots = [jnp.broadcast_to(turned[:, c : c + 1], (chunk, width)) for c in range(outs)]
+        for k in range(total // rays):
+            whole = slice(k * rays + n * chunk, k * rays + (n + 1) * chunk)
+            u = u_ref[whole, :].astype(f32)
+            h1_ref, at = basis_part(h1_refs, whole.start)
+            basis_ref, at = basis_part(basis_refs, whole.start)
+            here = slice(at, at + chunk)
+            products = [sum(cots[c] * h1_ref[c, here, :] for c in range(outs))]
+            products += [cots[c] * h1_ref[outs + c, here, :] for c in range(outs - 1)]
             for c in range(outs):
                 sums[c] = sums[c] + jnp.sum((u * products[c]).reshape(chunk // 8, 8, width), 0)
-            slot_ref[at : at + chunk, :] = sum(w_rows[c] * products[c] for c in range(outs))
-            basis_ref = basis_refs[at // span]
-            moved_ref[at : at + chunk, :] = sum(cots[c] * basis_ref[c, spot, :] for c in range(outs))
+            slot_ref[whole, :] = sum(w_rows[c] * products[c] for c in range(outs)).astype(bf16)
+            moved = sum(cots[c] * basis_ref[c, here, :] for c in range(outs))
+            moved_ref[whole, :] = moved.astype(bf16)
     for c in range(outs):
         sums_ref[c] = sums[c]
-    slot = slot_ref[...]
-    slot_ray = slot[:rays, :]
-    for k in range(1, slots):
-        slot_ray = slot_ray + slot[k * rays : (k + 1) * rays, :]
-    ray_t = sorted_ref[...].astype(f32).T.astype(bf16)
-    w_grad_ref[...] = nn_dot(chosen_ref[...], slot.astype(bf16)) + nn_dot(ray_t, slot_ray.astype(bf16))
+    w_grad_ref[...] = nn_dot(inputs_ref[...], slot_ref[...])
 
 
 def flipped(a, b):
@@ -596,14 +607,30 @@
     small_ref[at + 2 + outs :, :] = jnp.zeros((rest, width), f32)
 
 
-def finish_ray_kernel(keep_ref, got_ref, out_ref):
+def ray_sum_kernel(keep_ref, got_ref, cot_ref, out_ref, color_ref):
     out_ref[...] = keep_ref[...] + got_ref[...].astype(f32)
+    channels, own = color_ref.shape
+    rays = cot_ref.shape[1]
+    me = lax.axis_index("slab")
+    r_i = lax.broadcasted_iota(jnp.int32, (rays, own), 0)
+    c_i = lax.broadcasted_iota(jnp.int32, (rays, own), 1)
+    pick = jnp.where(r_i == c_i + me * own, 1.0, 0.0).astype(bf16)
+    color = cot_ref[channels + 1 : 2 * channels + 1, :]
+    high = color.astype(bf16)
+    middle = (color - high.astype(f32)).astype(bf16)
+    low = (color - high.astype(f32) - middle.astype(f32)).astype(bf16)
+    picked = nn_dot(jnp.concatenate([high, middle, low], 0), pick)
+    color_ref[...] = picked[:channels] + picked[channels : 2 * channels] + picked[2 * channels :]
 
 
 def finish_kernel(
+    ray_ref,
+    color_ref,
     brick_ref,
     sent_ref,
     got_ref,
+    color_out_ref,
+    ray_out_ref,
     brick_out_ref,
     sample_ref,
     w_ref,
@@ -611,6 +638,8 @@
     w_out_ref,
     b_out_ref,
 ):
+    ray_out_ref[...] = ray_ref[...]
+    color_out_ref[...] = color_ref[...]
     part = brick_ref.shape[0]
     brick_out_ref[...] = brick_ref[...] + got_ref[:part, :].astype(f32)
     small = sent_ref[part:, :].astype(f32) + got_ref[part:, :].astype(f32)
@@ -734,23 +763,31 @@
     group = (seg[:channels], seg[channels:])
     received = []
     basis = []
-    pieces = 4
-    piece = total // pieces
     bits = bits_of(owners)
-    turned_later = turned
+    cuts = basis_cuts(total, bits)
+    pieces = len(cuts) - 1
+    turned_later, chosen_later = turned, chosen
     for b in range(bits):
         sent = jnp.concatenate(group, 0) if b > 0 else seg
         other = swap(sent, "slab", owners, 1 << b)
-        while len(basis) < min(pieces, pieces * (b + 1) // bits):
+        if b < pieces:
+            piece = cuts[b + 1] - cuts[b]
             basis.append(
                 call(
-                    functools.partial(basis_kernel, first=len(basis) * piece, row_of=rows),
+                    functools.partial(basis_kernel, first=cuts[b], row_of=rows),
                     (shaped(count, piece, width), shaped(outs, piece, width)),
                     "basis",
                     flops=1 << 29,
                 )(turned_later, u, s, low)
             )
-        other, turned_later = lax.optimization_barrier((other, turned_later))
+        if b + 1 == bits:
+            inputs = call(inputs_kernel, shaped16(width, total), "inputs", flops=1 << 28)(
+                chosen_later, ray_sorted
+            )
+            other, inputs = lax.optimization_barrier((other, inputs))
+        other, turned_later, chosen_later = lax.optimization_barrier(
+            (other, turned_later, chosen_later)
+        )
         received.append(other)
         theirs = (other[:channels], other[channels:])
         upper = ((me >> b) & 1) == 1
@@ -759,29 +796,29 @@
         group = merge(first, second, forward)
 
     h1, moved_basis = zip(*basis)
-    ray_keep, ray_send, cots = call(
+    ray_keep, ray_send, cots, cots_t = call(
         functools.partial(middle_kernel, owners=owners, pieces=pieces, lines=lines),
         (
             shaped(rays // 2, width),
             shaped16(rays // 2, width),
             shaped(8, rays),
+            shaped(rays, 8),
         ),
         "middle",
         scratch=(pltpu.VMEM((rays, width), f32),),
         flops=1 << 29,
     )(seg, *received, *moved_basis, packed)
-    moved, w_grad, sums, color_own = call(
-        functools.partial(slots_kernel, pieces=pieces, rows=rows, owners=owners),
+    moved, w_grad, sums = call(
+        functools.partial(slots_kernel, pieces=pieces, rows=rows),
         (
-            shaped(total, width),
+            shaped16(total, width),
             shaped(width, width),
             shaped(outs, 8, width),
-            shaped(channels, rays // owners),
         ),
         "slots",
-        scratch=(pltpu.VMEM((total, width), f32),),
+        scratch=(pltpu.VMEM((total, width), bf16),),
         flops=1 << 28,
-    )(*h1, *moved_basis, cots, u, chosen, ray_sorted, low)
+    )(*h1, *moved_basis, cots_t, u, inputs, low)
 
     def merged(keep, got):
         half = keep.shape[0] // 2
@@ -820,7 +857,7 @@
             )(*by_part, w_grad, sums, low)
             held = (ray_send, brick_send, small)
             ray_send, brick_send, small = lax.optimization_barrier(held)
-        ray_got = swap(ray_send, "slab", owners, owners >> (b + 1))
+        ray_got = swap(ray_send, "slab", owners, 1 << halving_bits(owners)[b])
         if b < parts:
             by_part += part_by_sample(b, later_cots)
         if b + 1 < bits:
@@ -838,12 +875,17 @@
             small = sent[half:].astype(f32) + other[half:].astype(f32)
             brick_sent = (brick[half // 2 :] + other[half // 2 : half].astype(f32)).astype(bf16)
             brick = brick[: half // 2] + other[: half // 2].astype(f32)
-    ray_out = call(finish_ray_kernel, shaped(rays // owners, width), "finish_ray", flops=1 << 31)(
-        ray_keep, ray_got
-    )
-    brick_out, sample_out, w_grad, b_grad, w_out_grad, b_out_grad = call(
+    ray_sum, color_own = call(
+        ray_sum_kernel,
+        (shaped(rays // owners, width), shaped(channels, rays // owners)),
+        "ray_sum",
+        flops=1 << 31,
+    )(ray_keep, ray_got, cots)
+    color_out, ray_out, brick_out, sample_out, w_grad, b_grad, w_out_grad, b_out_grad = call(
         finish_kernel,
         (
+            shaped(channels, rays // owners),
+            shaped(rays // owners, width),
             shaped(bricks // shares, width),
             shaped(samples, width),
             shaped(width, width),
@@ -852,9 +894,9 @@
             shaped(1, outs),
         ),
         "finish",
-    )(brick, sent, other)
+    )(ray_sum, color_own, brick, sent, other)
     return (
-        color_own,
+        color_out,
         ray_out,
         brick_out[None],
         sample_out[None],

time: 49.9 us -> 47.6 us (0.954)
  waiting for transfers between devices: 7.1 us -> 5.18 us
  Pallas kernels: 20.5 us -> 19.1 us
  starting transfers between devices: 20.8 us -> 21.9 us
    ppermute x11, waiting for transfers between devices: 7.1 us -> 5.18 us  [swap(): return lax.ppermute(array, axis, [(i, i ^ distance) for i in range(size)])]
    pallas_call x18, Pallas kernels: 20.5 us -> 19.1 us  [run(): pl.pallas_call(kernel, out_shape=out_shape, in_specs=[pl.BlockSpec(memory...]
    ppermute x11, starting transfers between devices: 20.8 us -> 21.9 us  [swap(): return lax.ppermute(array, axis, [(i, i ^ distance) for i in range(size)])]
  transfers between devices with their start and end apart: 11 -> 11, of which waited for: 7 -> 8; matrix products, arithmetic and copies ran while one was open for 0% -> 0% of each run, Pallas kernels for 33% -> 31%
where the time goes in v4:
time: 47.6 us; the launch traced here: 47.5 us
  starting transfers between devices  21.9 us (46%)
  Pallas kernels  19.1 us (40%)
  waiting for transfers between devices  5.18 us (11%)
  between operations  1.05 us (2%)
    ppermute x11, starting transfers between devices, swap(): return lax.ppermute(array, axis, [(i, i ^ distance) for i in range(size)])  21.9 us
    pallas_call x18, Pallas kernels, run(): pl.pallas_call(kernel, out_shape=out_shape, in_specs=[pl.BlockSpec(memory...  19.1 us
    ppermute x11, waiting for transfers between devices, swap(): return lax.ppermute(array, axis, [(i, i ^ distance) for i in range(size)])  5.18 us
  transfers between devices with their start and end apart: 11, of which 8 were waited for; matrix products, arithmetic and copies ran while one was open for 0% of the time, Pallas kernels for 31%

profile of v4, /device:TPU:0, one launch (start us, length us, event | category | flops | bytes accessed | tf_op | source)
XLA Modules:
  0.0 47.5 jit_solution(10894080741016741517)
XLA Ops:
  0.7 4.1 %collective-permute-start = (bf16[64,128]{1,0:T(8,128)(2,1)}, bf16[64,128]{1,0:T(8,128)(2,1)S(1)}, u32[]{:S(2)}, u32[]{:S(2)}) collective-permute-start(bf16[64,128]{1,0:T(8,128)(2,1)} %ray_ref.1), channel_id=1, source_target_pairs={{0,16},{4,20},{8,24},{12,28},{16,0},{20,4},{24,8},{28,12},{1,17},{... | collective-permute-start | bytes 49160 | tf_op jit(solution)/shard_map/ppermute | solution.py:64
  5.0 1.0 %prepare.1 = (bf16[64,128]{1,0:T(8,128)(2,1)S(1)}, bf16[208,128]{1,0:T(8,128)(2,1)S(1)}, f32[8,512]{1,0:T(8,128)S(1)}, bf16[128,128]{1,0:T(8,128)(2,1)S(1)}, f32...) custom-call(bf16[64,128]{1,0:T(8,128)(2,1)S(1)} %copy-done.3, ...), custom_call_target="tpu_custom_call" | custom-call | flops 2147483648 | bytes 1048576 | tf_op jit(solution)/shard_map/prepare/pallas_call | solution.py:75
  6.0 0.8 %collective-permute-done = bf16[64,128]{1,0:T(8,128)(2,1)S(1)} collective-permute-done((bf16[64,128]{1,0:T(8,128)(2,1)}, bf16[64,128]{1,0:T(8,128)(2,1)S(1)}, u32[]{:S(2)}, u32[]{:S(2)}) %collective-permute-start) | collective-permute-done | bytes 16416 | tf_op jit(solution)/shard_map/ppermute | solution.py:64
  6.8 1.9 %collective-permute-start.1 = (bf16[128,128]{1,0:T(8,128)(2,1)S(1)}, bf16[128,128]{1,0:T(8,128)(2,1)S(1)}, u32[]{:S(2)}, u32[]{:S(2)}) collective-permute-start(bf16[128,128]{1,0:T(8,128)(2,1)S(1)} %pad_maximum_fusion.2), channel_id=1, source_target_pairs={{0,4},{4,0},{8,12},{12,8},{16,20},{20,16},{24,28},{28,24},{1,5},{5... | collective-permute-start | bytes 98312 | tf_op jit(solution)/shard_map/ppermute | solution.py:64
  8.7 0.8 %chosen.1 = (bf16[128,1024]{1,0:T(8,128)(2,1)S(1)}, f32[128,1024]{1,0:T(8,128)S(1)}) custom-call(f32[8,512]{1,0:T(8,128)S(1)} %get-tuple-element.82.lines_ref.refs_5_.refs_7_, bf16[1024,128]{1,0:T(8,128)(2,1)S(1)} %bitcast.14, bf16[128,128]{1,0:T(8,128)(2,1)S(1)} %get-tuple-element.83.w_t_ref.refs_2_), custom_call_target="tpu_custom_call" | custom-call | flops 536870912 | bytes 1048576 | tf_op jit(solution)/shard_map/chosen/pallas_call | solution.py:75
  9.5 1.2 %collective-permute-done.1 = bf16[128,128]{1,0:T(8,128)(2,1)S(1)} collective-permute-done((bf16[128,128]{1,0:T(8,128)(2,1)S(1)}, bf16[128,128]{1,0:T(8,128)(2,1)S(1)}, u32[]{:S(2)}, u32[]{:S(2)}) %collective-permute-start.1) | collective-permute-done | bytes 32800 | tf_op jit(solution)/shard_map/ppermute | solution.py:64
  10.7 1.9 %collective-permute-start.2 = (bf16[256,128]{1,0:T(8,128)(2,1)S(1)}, bf16[256,128]{1,0:T(8,128)(2,1)S(1)}, u32[]{:S(2)}, u32[]{:S(2)}) collective-permute-start(bf16[256,128]{1,0:T(8,128)(2,1)S(1)} %constant_dynamic-update-slice_fusion.refs_0_), channel_id=1, source_target_pairs={{0,8},{4,12},{8,0},{12,4},{16,24},{20,28},{24,16},{28,20},{1,9},{5... | collective-permute-start | bytes 196616 | tf_op jit(solution)/shard_map/ppermute | solution.py:64
  12.6 2.1 %forward.2 = (f32[4,256]{1,0:T(4,128)S(1)}, f32[8,64,512]{2,1,0:T(8,128)S(1)}, bf16[512,128]{1,0:T(8,128)(2,1)S(1)}, bf16[256,128]{1,0:T(8,128)(2,1)S(1)}) custom-call(bf16[256,128]{1,0:T(8,128)(2,1)S(1)} %constant_dynamic-update-slice_fusion.refs_0_, f32[128,1024]{1,0:T(8,128)S(1)} %get-tuple-element.84.refs_1_, ...), custom_call_target="tpu_custom_call" | custom-call | flops 1073741824 | bytes 1048576 | tf_op jit(solution)/shard_map/forward/pallas_call | solution.py:75
  15.0 2.0 %forward.3 = (f32[4,512]{1,0:T(4,128)S(1)}, f32[8,64,512]{2,1,0:T(8,128)S(1)}, bf16[1024,128]{1,0:T(8,128)(2,1)S(1)}, bf16[512,128]{1,0:T(8,128)(2,1)S(1)}) custom-call(bf16[256,128]{1,0:T(8,128)(2,1)S(1)} %collective-permute-done.2.refs_0_, f32[128,1024]{1,0:T(8,128)S(1)} %get-tuple-element.84.refs_1_, ...), custom_call_target="tpu_custom_call" | custom-call | flops 1073741824 | bytes 1048576 | tf_op jit(solution)/shard_map/forward/pallas_call | solution.py:75
  17.0 2.0 %collective-permute-start.3 = (f32[4,512]{1,0:T(4,128)S(1)}, f32[4,512]{1,0:T(4,128)S(1)}, u32[]{:S(2)}, u32[]{:S(2)}) collective-permute-start(f32[4,512]{1,0:T(4,128)S(1)} %get-tuple-element.91.seg_ref.refs_0_), channel_id=1, source_target_pairs={{0,4},{4,0},{8,12},{12,8},{16,20},{20,16},{24,28},{28,24},{1,5},{5... | collective-permute-start | bytes 24584 | tf_op jit(solution)/shard_map/ppermute | solution.py:64
  19.0 1.3 %coefficients.1 = (f32[7,64,1024]{2,1,0:T(8,128)S(1)}, f32[7,1024,128]{2,1,0:T(8,128)S(1)}) custom-call(f32[4,512]{1,0:T(4,128)S(1)} %get-tuple-element.91.seg_ref.refs_0_, f32[8,64,512]{2,1,0:T(8,128)S(1)} %get-tuple-element.92.first_ref, f32[8,64,512]{2,1,0:T(8,128)S(1)} %get-tuple-element.93.second_ref, bf16[64,64]{1,0:T(8,128)(2,1)S(1)} %get-tuple-element.94.later_ref), custom_call_target="tpu_custom_call" | custom-call | flops 1073741824 | bytes 1048576 | tf_op jit(solution)/shard_map/coefficients/pallas_call | solution.py:75
  20.9 1.8 %collective-permute-start.4 = (f32[4,512]{1,0:T(4,128)S(1)}, f32[4,512]{1,0:T(4,128)S(1)}, u32[]{:S(2)}, u32[]{:S(2)}) collective-permute-start(f32[4,512]{1,0:T(4,128)S(1)} %pad_maximum_fusion.3), channel_id=1, source_target_pairs={{0,8},{4,12},{8,0},{12,4},{16,24},{20,28},{24,16},{28,20},{1,9},{5... | collective-permute-start | bytes 24584 | tf_op jit(solution)/shard_map/ppermute | solution.py:64
  22.7 2.1 %basis.4 = (f32[7,512,128]{2,1,0:T(8,128)S(1)}, f32[4,512,128]{2,1,0:T(8,128)S(1)}) custom-call(f32[7,1024,128]{2,1,0:T(8,128)S(1)} %get-tuple-element.104.turned_ref, bf16[1024,128]{1,0:T(8,128)(2,1)S(1)} %get-tuple-element.106.u_ref.refs_7_, f32[64,128]{1,0:T(8,128)S(1)} %get-tuple-element.107.s_ref, ...), custom_call_target="tpu_custom_call" | custom-call | flops 536870912 | bytes 1048576 | tf_op jit(solution)/shard_map/basis/pallas_call | solution.py:75
  24.9 2.7 %collective-permute-start.5 = (f32[4,512]{1,0:T(4,128)S(1)}, f32[4,512]{1,0:T(4,128)S(1)}, u32[]{:S(2)}, u32[]{:S(2)}) collective-permute-start(f32[4,512]{1,0:T(4,128)S(1)} %pad_maximum_fusion.4), channel_id=1, source_target_pairs={{0,16},{4,20},{8,24},{12,28},{16,0},{20,4},{24,8},{28,12},{1,17},{... | collective-permute-start | bytes 24584 | tf_op jit(solution)/shard_map/ppermute | solution.py:64
  27.6 1.6 %basis.5 = (f32[7,384,128]{2,1,0:T(8,128)S(1)}, f32[4,384,128]{2,1,0:T(8,128)S(1)}) custom-call(f32[7,1024,128]{2,1,0:T(8,128)S(1)} %get-tuple-element.104.turned_ref, bf16[1024,128]{1,0:T(8,128)(2,1)S(1)} %get-tuple-element.106.u_ref.refs_7_, f32[64,128]{1,0:T(8,128)S(1)} %get-tuple-element.107.s_ref, ...), custom_call_target="tpu_custom_call" | custom-call | flops 536870912 | bytes 1048576 | tf_op jit(solution)/shard_map/basis/pallas_call | solution.py:75
  30.2 1.6 %collective-permute-start.6 = (bf16[256,128]{1,0:T(8,128)(2,1)S(1)}, bf16[256,128]{1,0:T(8,128)(2,1)S(1)}, u32[]{:S(2)}, u32[]{:S(2)}) collective-permute-start(bf16[256,128]{1,0:T(8,128)(2,1)S(1)} %get-tuple-element.113), channel_id=1, source_target_pairs={{0,8},{4,12},{8,0},{12,4},{16,24},{20,28},{24,16},{28,20},{1,9},{5... | collective-permute-start | bytes 196616 | tf_op jit(solution)/shard_map/ppermute | solution.py:64
  31.8 1.9 %by_sample.2 = (f32[32,128]{1,0:T(8,128)S(1)}, f32[4,8,128]{2,1,0:T(8,128)S(1)}, f32[4,128]{1,0:T(4,128)S(1)}) custom-call(f32[8,512]{1,0:T(8,128)S(1)} %get-tuple-element.122.cot_ref, f32[7,64,1024]{2,1,0:T(8,128)S(1)} %get-tuple-element.127.coef_ref, bf16[1024,128]{1,0:T(8,128)(2,1)S(1)} %get-tuple-element.106.u_ref.refs_7_, ...), custom_call_target="tpu_custom_call" | custom-call | flops 268435456 | bytes 1048576 | tf_op jit(solution)/shard_map/by_sample/pallas_call | solution.py:75
  33.7 1.1 %slots.1 = (bf16[1024,128]{1,0:T(8,128)(2,1)S(1)}, f32[128,128]{1,0:T(8,128)S(1)}, f32[4,8,128]{2,1,0:T(8,128)S(1)}) custom-call(f32[7,128,128]{2,1,0:T(8,128)S(1)} %get-tuple-element.115.refs_0_, f32[7,512,128]{2,1,0:T(8,128)S(1)} %get-tuple-element.116.refs_1_, f32[7,384,128]{2,1,0:T(8,128)S(1)} %get-tuple-element.117.refs_2_, ...), custom_call_target="tpu_custom_call" | custom-call | flops 268435456 | bytes 1048576 | tf_op jit(solution)/shard_map/slots/pallas_call | solution.py:75
  34.9 1.6 %collective-permute-start.7 = (bf16[128,128]{1,0:T(8,128)(2,1)S(1)}, bf16[128,128]{1,0:T(8,128)(2,1)S(1)}, u32[]{:S(2)}, u32[]{:S(2)}) collective-permute-start(bf16[128,128]{1,0:T(8,128)(2,1)S(1)} %get-tuple-element.158), channel_id=1, source_target_pairs={{0,4},{4,0},{8,12},{12,8},{16,20},{20,16},{24,28},{28,24},{1,5},{5... | collective-permute-start | bytes 98312 | tf_op jit(solution)/shard_map/ppermute | solution.py:64
  36.5 1.9 %by_sample.3 = (f32[32,128]{1,0:T(8,128)S(1)}, f32[4,8,128]{2,1,0:T(8,128)S(1)}, f32[4,128]{1,0:T(4,128)S(1)}) custom-call(f32[8,512]{1,0:T(8,128)S(1)} %get-tuple-element.122.cot_ref, f32[7,64,1024]{2,1,0:T(8,128)S(1)} %get-tuple-element.127.coef_ref, bf16[1024,128]{1,0:T(8,128)(2,1)S(1)} %get-tuple-element.106.u_ref.refs_7_, ...), custom_call_target="tpu_custom_call" | custom-call | flops 268435456 | bytes 1048576 | tf_op jit(solution)/shard_map/by_sample/pallas_call | solution.py:75
  39.7 1.6 %collective-permute-start.9 = (bf16[720,128]{1,0:T(8,128)(2,1)S(1)}, bf16[720,128]{1,0:T(8,128)(2,1)S(1)}, u32[]{:S(2)}, u32[]{:S(2)}) collective-permute-start(bf16[720,128]{1,0:T(8,128)(2,1)S(1)} %pad_maximum_fusion), channel_id=1, source_target_pairs={{0,2},{1,3},{2,0},{3,1},{4,6},{5,7},{6,4},{7,5},{8,10},{9,11},{10,... | collective-permute-start | bytes 552968 | tf_op jit(solution)/shard_map/ppermute | solution.py:64
  41.2 2.7 %collective-permute-start.8 = (bf16[64,128]{1,0:T(8,128)(2,1)S(1)}, bf16[64,128]{1,0:T(8,128)(2,1)S(1)}, u32[]{:S(2)}, u32[]{:S(2)}) collective-permute-start(bf16[64,128]{1,0:T(8,128)(2,1)S(1)} %get-tuple-element.136), channel_id=1, source_target_pairs={{0,16},{4,20},{8,24},{12,28},{16,0},{20,4},{24,8},{28,12},{1,17},{... | collective-permute-start | bytes 49160 | tf_op jit(solution)/shard_map/ppermute | solution.py:64
  43.9 1.4 %collective-permute-done.9 = bf16[720,128]{1,0:T(8,128)(2,1)S(1)} collective-permute-done((bf16[720,128]{1,0:T(8,128)(2,1)S(1)}, bf16[720,128]{1,0:T(8,128)(2,1)S(1)}, u32[]{:S(2)}, u32[]{:S(2)}) %collective-permute-start.9) | collective-permute-done | bytes 184352 | tf_op jit(solution)/shard_map/ppermute | solution.py:64
  46.7 0.7 %finish.1 = (f32[3,64]{1,0:T(4,128)}, f32[64,128]{1,0:T(8,128)}, f32[256,128]{1,0:T(8,128)}, f32[64,128]{1,0:T(8,128)}, f32[128,128]{1,0:T(8,128)}, /*index=5*/f...) custom-call(f32[64,128]{1,0:T(8,128)S(1)} %get-tuple-element.137.ray_ref, f32[3,64]{1,0:T(4,128)S(1)} %get-tuple-element.138.color_ref, ...), custom_call_target="tpu_custom_call" | custom-call | bytes 1048576 | tf_op jit(solution)/shard_map/finish/pallas_call | solution.py:75
  (57 shorter events, 4.7 us)
Async XLA Ops:
  0.6 4.2 %copy-start.3 = (bf16[64,128]{1,0:T(8,128)(2,1)S(1)}, bf16[64,128]{1,0:T(8,128)(2,1)}, u32[]{:S(2)}) copy-start(bf16[64,128]{1,0:T(8,128)(2,1)} %ray_ref.1) | copy-start | bytes 49156
  0.6 4.2 %copy-start.6 = (s32[1,512]{1,0:T(1,128)S(1)}, s32[1,512]{1,0:T(1,128)}, u32[]{:S(2)}) copy-start(s32[1,512]{1,0:T(1,128)} %occ_ref.1) | copy-start | bytes 6148
  0.7 4.2 %copy-start.5 = (s32[1,2,512]{2,1,0:T(2,128)S(1)}, s32[1,2,512]{2,1,0:T(2,128)}, u32[]{:S(2)}) copy-start(s32[1,2,512]{2,1,0:T(2,128)} %param.20) | copy-start | bytes 12292
  0.7 4.2 %copy-start.10 = (f32[1,4]{1,0:T(1,128)S(1)}, f32[1,4]{1,0:T(1,128)}, u32[]{:S(2)}) copy-start(f32[1,4]{1,0:T(1,128)} %b_out_ref.1) | copy-start | bytes 52
  0.7 4.2 %copy-start.8 = (bf16[1,4,128]{2,1,0:T(4,128)(2,1)S(1)}, bf16[1,4,128]{2,1,0:T(4,128)(2,1)}, u32[]{:S(2)}) copy-start(bf16[1,4,128]{2,1,0:T(4,128)(2,1)} %param.18) | copy-start | bytes 3076
  0.7 4.2 %copy-start.9 = (f32[1,128]{1,0:T(1,128)S(1)}, f32[1,128]{1,0:T(1,128)}, u32[]{:S(2)}) copy-start(f32[1,128]{1,0:T(1,128)} %b_ref.1) | copy-start | bytes 1540
  0.7 4.2 %copy-start.1 = (bf16[1,128,128]{2,1,0:T(8,128)(2,1)S(1)}, bf16[1,128,128]{2,1,0:T(8,128)(2,1)}, u32[]{:S(2)}) copy-start(bf16[1,128,128]{2,1,0:T(8,128)(2,1)} %param.16) | copy-start | bytes 98308
  0.7 4.2 %copy-start.2 = (bf16[1,64,128]{2,1,0:T(8,128)(2,1)S(1)}, bf16[1,64,128]{2,1,0:T(8,128)(2,1)}, u32[]{:S(2)}) copy-start(bf16[1,64,128]{2,1,0:T(8,128)(2,1)} %param.15) | copy-start | bytes 49156
  0.7 4.2 %copy-start.4 = (f32[3,512]{1,0:T(4,128)S(1)}, f32[3,512]{1,0:T(4,128)}, u32[]{:S(2)}) copy-start(f32[3,512]{1,0:T(4,128)} %target_ref.1) | copy-start | bytes 18436
  0.7 4.2 %copy-start.7 = (s32[512]{0:T(512)S(1)}, s32[512]{0:T(512)}, u32[]{:S(2)}) copy-start(s32[512]{0:T(512)} %param.12) | copy-start | bytes 6148
  0.7 6.0 %collective-permute-start = (bf16[64,128]{1,0:T(8,128)(2,1)}, bf16[64,128]{1,0:T(8,128)(2,1)S(1)}, u32[]{:S(2)}, u32[]{:S(2)}) collective-permute-start(bf16[64,128]{1,0:T(8,128)(2,1)} %ray_ref.1), channel_id=1, source_target_pairs={{0,16},{4,20},{8,24},{12,28},{16,0},{20,4},{24,8},{28,12},{1,17},{... | collective-permute-start | bytes 49160 | tf_op jit(solution)/shard_map/ppermute | solution.py:64
  5.0 3.7 %copy-start = (bf16[1,1024,128]{2,1,0:T(8,128)(2,1)S(1)}, bf16[1,1024,128]{2,1,0:T(8,128)(2,1)}, u32[]{:S(2)}) copy-start(bf16[1,1024,128]{2,1,0:T(8,128)(2,1)} %param.14) | copy-start | bytes 786436
  6.8 3.9 %collective-permute-start.1 = (bf16[128,128]{1,0:T(8,128)(2,1)S(1)}, bf16[128,128]{1,0:T(8,128)(2,1)S(1)}, u32[]{:S(2)}, u32[]{:S(2)}) collective-permute-start(bf16[128,128]{1,0:T(8,128)(2,1)S(1)} %pad_maximum_fusion.2), channel_id=1, source_target_pairs={{0,4},{4,0},{8,12},{12,8},{16,20},{20,16},{24,28},{28,24},{1,5},{5... | collective-permute-start | bytes 98312 | tf_op jit(solution)/shard_map/ppermute | solution.py:64
  10.7 4.3 %collective-permute-start.2 = (bf16[256,128]{1,0:T(8,128)(2,1)S(1)}, bf16[256,128]{1,0:T(8,128)(2,1)S(1)}, u32[]{:S(2)}, u32[]{:S(2)}) collective-permute-start(bf16[256,128]{1,0:T(8,128)(2,1)S(1)} %constant_dynamic-update-slice_fusion.refs_0_), channel_id=1, source_target_pairs={{0,8},{4,12},{8,0},{12,4},{16,24},{20,28},{24,16},{28,20},{1,9},{5... | collective-permute-start | bytes 196616 | tf_op jit(solution)/shard_map/ppermute | solution.py:64
  17.0 3.9 %collective-permute-start.3 = (f32[4,512]{1,0:T(4,128)S(1)}, f32[4,512]{1,0:T(4,128)S(1)}, u32[]{:S(2)}, u32[]{:S(2)}) collective-permute-start(f32[4,512]{1,0:T(4,128)S(1)} %get-tuple-element.91.seg_ref.refs_0_), channel_id=1, source_target_pairs={{0,4},{4,0},{8,12},{12,8},{16,20},{20,16},{24,28},{28,24},{1,5},{5... | collective-permute-start | bytes 24584 | tf_op jit(solution)/shard_map/ppermute | solution.py:64
  20.9 3.9 %collective-permute-start.4 = (f32[4,512]{1,0:T(4,128)S(1)}, f32[4,512]{1,0:T(4,128)S(1)}, u32[]{:S(2)}, u32[]{:S(2)}) collective-permute-start(f32[4,512]{1,0:T(4,128)S(1)} %pad_maximum_fusion.3), channel_id=1, source_target_pairs={{0,8},{4,12},{8,0},{12,4},{16,24},{20,28},{24,16},{28,20},{1,9},{5... | collective-permute-start | bytes 24584 | tf_op jit(solution)/shard_map/ppermute | solution.py:64
  24.9 4.6 %collective-permute-start.5 = (f32[4,512]{1,0:T(4,128)S(1)}, f32[4,512]{1,0:T(4,128)S(1)}, u32[]{:S(2)}, u32[]{:S(2)}) collective-permute-start(f32[4,512]{1,0:T(4,128)S(1)} %pad_maximum_fusion.4), channel_id=1, source_target_pairs={{0,16},{4,20},{8,24},{12,28},{16,0},{20,4},{24,8},{28,12},{1,17},{... | collective-permute-start | bytes 24584 | tf_op jit(solution)/shard_map/ppermute | solution.py:64
  30.2 4.7 %collective-permute-start.6 = (bf16[256,128]{1,0:T(8,128)(2,1)S(1)}, bf16[256,128]{1,0:T(8,128)(2,1)S(1)}, u32[]{:S(2)}, u32[]{:S(2)}) collective-permute-start(bf16[256,128]{1,0:T(8,128)(2,1)S(1)} %get-tuple-element.113), channel_id=1, source_target_pairs={{0,8},{4,12},{8,0},{12,4},{16,24},{20,28},{24,16},{28,20},{1,9},{5... | collective-permute-start | bytes 196616 | tf_op jit(solution)/shard_map/ppermute | solution.py:64
  34.9 4.0 %collective-permute-start.7 = (bf16[128,128]{1,0:T(8,128)(2,1)S(1)}, bf16[128,128]{1,0:T(8,128)(2,1)S(1)}, u32[]{:S(2)}, u32[]{:S(2)}) collective-permute-start(bf16[128,128]{1,0:T(8,128)(2,1)S(1)} %get-tuple-element.158), channel_id=1, source_target_pairs={{0,4},{4,0},{8,12},{12,8},{16,20},{20,16},{24,28},{28,24},{1,5},{5... | collective-permute-start | bytes 98312 | tf_op jit(solution)/shard_map/ppermute | solution.py:64
  39.7 5.6 %collective-permute-start.9 = (bf16[720,128]{1,0:T(8,128)(2,1)S(1)}, bf16[720,128]{1,0:T(8,128)(2,1)S(1)}, u32[]{:S(2)}, u32[]{:S(2)}) collective-permute-start(bf16[720,128]{1,0:T(8,128)(2,1)S(1)} %pad_maximum_fusion), channel_id=1, source_target_pairs={{0,2},{1,3},{2,0},{3,1},{4,6},{5,7},{6,4},{7,5},{8,10},{9,11},{10,... | collective-permute-start | bytes 552968 | tf_op jit(solution)/shard_map/ppermute | solution.py:64
  41.2 4.6 %collective-permute-start.8 = (bf16[64,128]{1,0:T(8,128)(2,1)S(1)}, bf16[64,128]{1,0:T(8,128)(2,1)S(1)}, u32[]{:S(2)}, u32[]{:S(2)}) collective-permute-start(bf16[64,128]{1,0:T(8,128)(2,1)S(1)} %get-tuple-element.136), channel_id=1, source_target_pairs={{0,16},{4,20},{8,24},{12,28},{16,0},{20,4},{24,8},{28,12},{1,17},{... | collective-permute-start | bytes 49160 | tf_op jit(solution)/shard_map/ppermute | solution.py:64
  45.3 1.4 %collective-permute-start.10 = (bf16[464,128]{1,0:T(8,128)(2,1)S(1)}, bf16[464,128]{1,0:T(8,128)(2,1)S(1)}, u32[]{:S(2)}, u32[]{:S(2)}) collective-permute-start(bf16[464,128]{1,0:T(8,128)(2,1)S(1)} %pad_maximum_fusion.1.sent_ref), channel_id=1, source_target_pairs={{0,1},{1,0},{2,3},{3,2},{4,5},{5,4},{6,7},{7,6},{8,9},{9,8},{10,11... | collective-permute-start | bytes 356360 | tf_op jit(solution)/shard_map/ppermute | solution.py:64

commit v5 on v4

--- a/solution.py
+++ b/solution.py
@@ -79,7 +79,7 @@
             out_specs=jax.tree.map(lambda _: pl.BlockSpec(memory_space=pltpu.VMEM), out_shape),
             scratch_shapes=list(scratch),
             compiler_params=pltpu.CompilerParams(vmem_limit_bytes=vmem_bytes),
-            cost_estimate=pl.CostEstimate(flops=flops, bytes_accessed=1 << 20, transcendentals=0),
+            cost_estimate=pl.CostEstimate(flops=flops, bytes_accessed=1 << 10, transcendentals=0),
             name=name,
         )(*operands)
 
@@ -396,7 +396,7 @@
     seg_ref, refs = refs[0], refs[1:]
     got_refs, refs = refs[:bits], refs[bits:]
     moved_refs, refs = refs[:pieces], refs[pieces:]
-    lines_ref, keep_ref, send_ref, cot_ref, cot_t_ref, ray_ref = refs
+    lines_ref, keep_ref, send_ref, cot_ref, spread_ref, ray_ref = refs
     me = lax.axis_index("slab")
     outs = seg_ref.shape[0]
     channels = outs - 1
@@ -433,10 +433,15 @@
     cot_ref[outs : outs + channels, :] = color
     cot_ref[outs + channels :, :] = jnp.zeros((8 - outs - channels, rays), f32)
     chunk = 128
+    values = jnp.concatenate([color_cot, trans_cot], 0)
+    rounded = values.astype(bf16).astype(f32)
+    values = jnp.concatenate([rounded, values - rounded], 0)
+    row = lax.broadcasted_iota(jnp.int32, (2 * outs, outs * width), 0) % outs
+    lane = lax.broadcasted_iota(jnp.int32, (2 * outs, outs * width), 1) // width
+    spread = jnp.where(row == lane, 1.0, 0.0).astype(bf16)
     for n in range(rays // chunk):
         these = slice(n * chunk, (n + 1) * chunk)
-        turned = cot_ref[:, these].T
-        cot_t_ref[these, :] = turned
+        spread_ref[these, :] = nn_dot(values[:, these].T.astype(bf16), spread)
         grad = None
         for c in range(outs):
             whole = None
@@ -444,7 +449,7 @@
                 ref, at = basis_part(moved_refs, k * rays + n * chunk)
                 part = ref[c, at : at + chunk, :]
                 whole = part if whole is None else whole + part
-            term = jnp.broadcast_to(turned[:, c : c + 1], (chunk, width)) * whole
+            term = spread_ref[these, c * width : (c + 1) * width] * whole
             grad = term if grad is None else grad + term
         ray_ref[these, :] = grad
     own = rays // owners
@@ -546,9 +551,9 @@
 def slots_kernel(*refs, pieces, rows):
     h1_refs, refs = refs[:pieces], refs[pieces:]
     basis_refs, refs = refs[:pieces], refs[pieces:]
-    cot_t_ref, u_ref, inputs_ref, low_ref, *refs = refs
+    spread_ref, u_ref, inputs_ref, low_ref, *refs = refs
     moved_ref, w_grad_ref, sums_ref, slot_ref = refs
-    rays = cot_t_ref.shape[0]
+    rays = spread_ref.shape[0]
     total, width = u_ref.shape
     outs = sums_ref.shape[0]
     w_out = low_ref[rows["w_out"], :].astype(f32)
@@ -556,8 +561,8 @@
     chunk = 32
     sums = [jnp.zeros((8, width), f32)] * outs
     for n in range(rays // chunk):
-        turned = cot_t_ref[n * chunk : (n + 1) * chunk, :]
-        cots = [jnp.broadcast_to(turned[:, c : c + 1], (chunk, width)) for c in range(outs)]
+        these = slice(n * chunk, (n + 1) * chunk)
+        cots = [spread_ref[these, c * width : (c + 1) * width] for c in range(outs)]
         for k in range(total // rays):
             whole = slice(k * rays + n * chunk, k * rays + (n + 1) * chunk)
             u = u_ref[whole, :].astype(f32)
@@ -781,7 +786,7 @@
                 )(turned_later, u, s, low)
             )
         if b + 1 == bits:
-            inputs = call(inputs_kernel, shaped16(width, total), "inputs", flops=1 << 28)(
+            inputs = call(inputs_kernel, shaped16(width, total), "inputs", flops=1 << 20)(
                 chosen_later, ray_sorted
             )
             other, inputs = lax.optimization_barrier((other, inputs))
@@ -796,13 +801,13 @@
         group = merge(first, second, forward)
 
     h1, moved_basis = zip(*basis)
-    ray_keep, ray_send, cots, cots_t = call(
+    ray_keep, ray_send, cots, spread = call(
         functools.partial(middle_kernel, owners=owners, pieces=pieces, lines=lines),
         (
             shaped(rays // 2, width),
             shaped16(rays // 2, width),
             shaped(8, rays),
-            shaped(rays, 8),
+            shaped(rays, outs * width),
         ),
         "middle",
         scratch=(pltpu.VMEM((rays, width), f32),),
@@ -817,8 +822,8 @@
         ),
         "slots",
         scratch=(pltpu.VMEM((total, width), bf16),),
-        flops=1 << 28,
-    )(*h1, *moved_basis, cots_t, u, inputs, low)
+        flops=1 << 20,
+    )(*h1, *moved_basis, spread, u, inputs, low)
 
     def merged(keep, got):
         half = keep.shape[0] // 2
@@ -834,7 +839,7 @@
             ),
             "by_sample",
             scratch=(pltpu.VMEM((samples // parts // 8, outs * 8, total), bf16),),
-            flops=1 << 28,
+            flops=1 << 20,
         )(cots, coef, u, s, low)
 
     parts = 2
@@ -842,27 +847,28 @@
     later_cots = cots
     for b in range(bits):
         if b + 1 == bits:
-            brick_keep, brick_send = call(
-                functools.partial(brick_kernel, shares=shares),
-                (shaped(bricks // 2, width), shaped(bricks // 2, width)),
-                "bricks",
-                flops=1 << 28,
-            )(packed, moved)
             small_rows = -(-(samples + width + 2 + outs) // 16) * 16
             small = call(
                 functools.partial(network_kernel, parts=parts, rows=rows),
                 shaped(small_rows, width),
                 "network",
-                flops=1 << 28,
+                flops=1 << 20,
             )(*by_part, w_grad, sums, low)
-            held = (ray_send, brick_send, small)
-            ray_send, brick_send, small = lax.optimization_barrier(held)
+            ray_send, small = lax.optimization_barrier((ray_send, small))
         ray_got = swap(ray_send, "slab", owners, 1 << halving_bits(owners)[b])
         if b < parts:
             by_part += part_by_sample(b, later_cots)
+        if b == 1:
+            brick_keep, brick_send = call(
+                functools.partial(brick_kernel, shares=shares),
+                (shaped(bricks // 2, width), shaped(bricks // 2, width)),
+                "bricks",
+                flops=1 << 20,
+            )(packed, moved)
+            w_grad, brick_send = lax.optimization_barrier((w_grad, brick_send))
         if b + 1 < bits:
-            held = (ray_got, later_cots, moved)
-            ray_got, later_cots, moved = lax.optimization_barrier(held)
+            held = (ray_got, later_cots, moved, by_part)
+            ray_got, later_cots, moved, by_part = lax.optimization_barrier(held)
             ray_keep, ray_send = merged(ray_keep, ray_got)
 
     brick = brick_keep

time: 47.6 us -> 46.9 us (0.985)
  Pallas kernels: 19.1 us -> 18.6 us
    pallas_call x18, Pallas kernels: 19.1 us -> 18.6 us  [run(): pl.pallas_call(kernel, out_shape=out_shape, in_specs=[pl.BlockSpec(memory...]
  transfers between devices with their start and end apart: 11 -> 11, of which waited for: 8 -> 7; matrix products, arithmetic and copies ran while one was open for 0% -> 0% of each run, Pallas kernels for 31% -> 32%
where the time goes in v5:
time: 46.9 us; the launch traced here: 46.8 us
  starting transfers between devices  21.9 us (47%)
  Pallas kernels  18.6 us (40%)
  waiting for transfers between devices  4.94 us (11%)
  between operations  1.05 us (2%)
    ppermute x11, starting transfers between devices, swap(): return lax.ppermute(array, axis, [(i, i ^ distance) for i in range(size)])  21.9 us
    pallas_call x18, Pallas kernels, run(): pl.pallas_call(kernel, out_shape=out_shape, in_specs=[pl.BlockSpec(memory...  18.6 us
    ppermute x11, waiting for transfers between devices, swap(): return lax.ppermute(array, axis, [(i, i ^ distance) for i in range(size)])  4.94 us
  transfers between devices with their start and end apart: 11, of which 7 were waited for; matrix products, arithmetic and copies ran while one was open for 0% of the time, Pallas kernels for 32%

profile of v5, /device:TPU:0, one launch (start us, length us, event | category | flops | bytes accessed | tf_op | source)
XLA Modules:
  0.0 46.8 jit_solution(8321239956148686625)
XLA Ops:
  0.7 4.1 %collective-permute-start = (bf16[64,128]{1,0:T(8,128)(2,1)}, bf16[64,128]{1,0:T(8,128)(2,1)S(1)}, u32[]{:S(2)}, u32[]{:S(2)}) collective-permute-start(bf16[64,128]{1,0:T(8,128)(2,1)} %ray_ref.1), channel_id=1, source_target_pairs={{0,16},{4,20},{8,24},{12,28},{16,0},{20,4},{24,8},{28,12},{1,17},{... | collective-permute-start | bytes 49160 | tf_op jit(solution)/shard_map/ppermute | solution.py:64
  5.0 1.0 %prepare.1 = (bf16[64,128]{1,0:T(8,128)(2,1)S(1)}, bf16[208,128]{1,0:T(8,128)(2,1)S(1)}, f32[8,512]{1,0:T(8,128)S(1)}, bf16[128,128]{1,0:T(8,128)(2,1)S(1)}, f32...) custom-call(bf16[64,128]{1,0:T(8,128)(2,1)S(1)} %copy-done.3, ...), custom_call_target="tpu_custom_call" | custom-call | flops 2147483648 | bytes 1024 | tf_op jit(solution)/shard_map/prepare/pallas_call | solution.py:75
  6.0 0.8 %collective-permute-done = bf16[64,128]{1,0:T(8,128)(2,1)S(1)} collective-permute-done((bf16[64,128]{1,0:T(8,128)(2,1)}, bf16[64,128]{1,0:T(8,128)(2,1)S(1)}, u32[]{:S(2)}, u32[]{:S(2)}) %collective-permute-start) | collective-permute-done | bytes 16416 | tf_op jit(solution)/shard_map/ppermute | solution.py:64
  6.8 1.9 %collective-permute-start.1 = (bf16[128,128]{1,0:T(8,128)(2,1)S(1)}, bf16[128,128]{1,0:T(8,128)(2,1)S(1)}, u32[]{:S(2)}, u32[]{:S(2)}) collective-permute-start(bf16[128,128]{1,0:T(8,128)(2,1)S(1)} %pad_maximum_fusion.2), channel_id=1, source_target_pairs={{0,4},{4,0},{8,12},{12,8},{16,20},{20,16},{24,28},{28,24},{1,5},{5... | collective-permute-start | bytes 98312 | tf_op jit(solution)/shard_map/ppermute | solution.py:64
  8.7 0.8 %chosen.1 = (bf16[128,1024]{1,0:T(8,128)(2,1)S(1)}, f32[128,1024]{1,0:T(8,128)S(1)}) custom-call(f32[8,512]{1,0:T(8,128)S(1)} %get-tuple-element.91.lines_ref.refs_5_.refs_7_, bf16[1024,128]{1,0:T(8,128)(2,1)S(1)} %bitcast.14, bf16[128,128]{1,0:T(8,128)(2,1)S(1)} %get-tuple-element.92.w_t_ref.refs_2_), custom_call_target="tpu_custom_call" | custom-call | flops 536870912 | bytes 1024 | tf_op jit(solution)/shard_map/chosen/pallas_call | solution.py:75
  9.5 1.2 %collective-permute-done.1 = bf16[128,128]{1,0:T(8,128)(2,1)S(1)} collective-permute-done((bf16[128,128]{1,0:T(8,128)(2,1)S(1)}, bf16[128,128]{1,0:T(8,128)(2,1)S(1)}, u32[]{:S(2)}, u32[]{:S(2)}) %collective-permute-start.1) | collective-permute-done | bytes 32800 | tf_op jit(solution)/shard_map/ppermute | solution.py:64
  10.7 1.9 %collective-permute-start.2 = (bf16[256,128]{1,0:T(8,128)(2,1)S(1)}, bf16[256,128]{1,0:T(8,128)(2,1)S(1)}, u32[]{:S(2)}, u32[]{:S(2)}) collective-permute-start(bf16[256,128]{1,0:T(8,128)(2,1)S(1)} %constant_dynamic-update-slice_fusion.refs_0_), channel_id=1, source_target_pairs={{0,8},{4,12},{8,0},{12,4},{16,24},{20,28},{24,16},{28,20},{1,9},{5... | collective-permute-start | bytes 196616 | tf_op jit(solution)/shard_map/ppermute | solution.py:64
  12.6 2.0 %forward.2 = (f32[4,256]{1,0:T(4,128)S(1)}, f32[8,64,512]{2,1,0:T(8,128)S(1)}, bf16[512,128]{1,0:T(8,128)(2,1)S(1)}, bf16[256,128]{1,0:T(8,128)(2,1)S(1)}) custom-call(bf16[256,128]{1,0:T(8,128)(2,1)S(1)} %constant_dynamic-update-slice_fusion.refs_0_, f32[128,1024]{1,0:T(8,128)S(1)} %get-tuple-element.93.refs_1_, ...), custom_call_target="tpu_custom_call" | custom-call | flops 1073741824 | bytes 1024 | tf_op jit(solution)/shard_map/forward/pallas_call | solution.py:75
  15.0 2.0 %forward.3 = (f32[4,512]{1,0:T(4,128)S(1)}, f32[8,64,512]{2,1,0:T(8,128)S(1)}, bf16[1024,128]{1,0:T(8,128)(2,1)S(1)}, bf16[512,128]{1,0:T(8,128)(2,1)S(1)}) custom-call(bf16[256,128]{1,0:T(8,128)(2,1)S(1)} %collective-permute-done.2.refs_0_, f32[128,1024]{1,0:T(8,128)S(1)} %get-tuple-element.93.refs_1_, ...), custom_call_target="tpu_custom_call" | custom-call | flops 1073741824 | bytes 1024 | tf_op jit(solution)/shard_map/forward/pallas_call | solution.py:75
  17.0 2.0 %collective-permute-start.3 = (f32[4,512]{1,0:T(4,128)S(1)}, f32[4,512]{1,0:T(4,128)S(1)}, u32[]{:S(2)}, u32[]{:S(2)}) collective-permute-start(f32[4,512]{1,0:T(4,128)S(1)} %get-tuple-element.100.seg_ref.refs_0_), channel_id=1, source_target_pairs={{0,4},{4,0},{8,12},{12,8},{16,20},{20,16},{24,28},{28,24},{1,5},{5... | collective-permute-start | bytes 24584 | tf_op jit(solution)/shard_map/ppermute | solution.py:64
  19.0 1.3 %coefficients.1 = (f32[7,64,1024]{2,1,0:T(8,128)S(1)}, f32[7,1024,128]{2,1,0:T(8,128)S(1)}) custom-call(f32[4,512]{1,0:T(4,128)S(1)} %get-tuple-element.100.seg_ref.refs_0_, f32[8,64,512]{2,1,0:T(8,128)S(1)} %get-tuple-element.101.first_ref, f32[8,64,512]{2,1,0:T(8,128)S(1)} %get-tuple-element.102.second_ref, bf16[64,64]{1,0:T(8,128)(2,1)S(1)} %get-tuple-element.103.later_ref), custom_call_target="tpu_custom_call" | custom-call | flops 1073741824 | bytes 1024 | tf_op jit(solution)/shard_map/coefficients/pallas_call | solution.py:75
  20.9 1.8 %collective-permute-start.4 = (f32[4,512]{1,0:T(4,128)S(1)}, f32[4,512]{1,0:T(4,128)S(1)}, u32[]{:S(2)}, u32[]{:S(2)}) collective-permute-start(f32[4,512]{1,0:T(4,128)S(1)} %pad_maximum_fusion.3), channel_id=1, source_target_pairs={{0,8},{4,12},{8,0},{12,4},{16,24},{20,28},{24,16},{28,20},{1,9},{5... | collective-permute-start | bytes 24584 | tf_op jit(solution)/shard_map/ppermute | solution.py:64
  22.7 2.1 %basis.4 = (f32[7,512,128]{2,1,0:T(8,128)S(1)}, f32[4,512,128]{2,1,0:T(8,128)S(1)}) custom-call(f32[7,1024,128]{2,1,0:T(8,128)S(1)} %get-tuple-element.113.turned_ref, bf16[1024,128]{1,0:T(8,128)(2,1)S(1)} %get-tuple-element.115.u_ref.refs_7_, f32[64,128]{1,0:T(8,128)S(1)} %get-tuple-element.116.s_ref, ...), custom_call_target="tpu_custom_call" | custom-call | flops 536870912 | bytes 1024 | tf_op jit(solution)/shard_map/basis/pallas_call | solution.py:75
  24.9 2.7 %collective-permute-start.5 = (f32[4,512]{1,0:T(4,128)S(1)}, f32[4,512]{1,0:T(4,128)S(1)}, u32[]{:S(2)}, u32[]{:S(2)}) collective-permute-start(f32[4,512]{1,0:T(4,128)S(1)} %pad_maximum_fusion.4), channel_id=1, source_target_pairs={{0,16},{4,20},{8,24},{12,28},{16,0},{20,4},{24,8},{28,12},{1,17},{... | collective-permute-start | bytes 24584 | tf_op jit(solution)/shard_map/ppermute | solution.py:64
  27.6 1.6 %basis.5 = (f32[7,384,128]{2,1,0:T(8,128)S(1)}, f32[4,384,128]{2,1,0:T(8,128)S(1)}) custom-call(f32[7,1024,128]{2,1,0:T(8,128)S(1)} %get-tuple-element.113.turned_ref, bf16[1024,128]{1,0:T(8,128)(2,1)S(1)} %get-tuple-element.115.u_ref.refs_7_, f32[64,128]{1,0:T(8,128)S(1)} %get-tuple-element.116.s_ref, ...), custom_call_target="tpu_custom_call" | custom-call | flops 536870912 | bytes 1024 | tf_op jit(solution)/shard_map/basis/pallas_call | solution.py:75
  29.9 1.6 %collective-permute-start.6 = (bf16[256,128]{1,0:T(8,128)(2,1)S(1)}, bf16[256,128]{1,0:T(8,128)(2,1)S(1)}, u32[]{:S(2)}, u32[]{:S(2)}) collective-permute-start(bf16[256,128]{1,0:T(8,128)(2,1)S(1)} %get-tuple-element.122), channel_id=1, source_target_pairs={{0,8},{4,12},{8,0},{12,4},{16,24},{20,28},{24,16},{28,20},{1,9},{5... | collective-permute-start | bytes 196616 | tf_op jit(solution)/shard_map/ppermute | solution.py:64
  31.6 1.9 %by_sample.2 = (f32[32,128]{1,0:T(8,128)S(1)}, f32[4,8,128]{2,1,0:T(8,128)S(1)}, f32[4,128]{1,0:T(4,128)S(1)}) custom-call(f32[8,512]{1,0:T(8,128)S(1)} %get-tuple-element.135.cot_ref, f32[7,64,1024]{2,1,0:T(8,128)S(1)} %get-tuple-element.130.coef_ref, bf16[1024,128]{1,0:T(8,128)(2,1)S(1)} %get-tuple-element.115.u_ref.refs_7_, ...), custom_call_target="tpu_custom_call" | custom-call | flops 1048576 | bytes 1024 | tf_op jit(solution)/shard_map/by_sample/pallas_call | solution.py:75
  33.5 0.9 %slots.1 = (bf16[1024,128]{1,0:T(8,128)(2,1)S(1)}, f32[128,128]{1,0:T(8,128)S(1)}, f32[4,8,128]{2,1,0:T(8,128)S(1)}) custom-call(f32[7,128,128]{2,1,0:T(8,128)S(1)} %get-tuple-element.124.refs_0_, f32[7,512,128]{2,1,0:T(8,128)S(1)} %get-tuple-element.125.refs_1_, f32[7,384,128]{2,1,0:T(8,128)S(1)} %get-tuple-element.126.refs_2_, ...), custom_call_target="tpu_custom_call" | custom-call | flops 1048576 | bytes 1024 | tf_op jit(solution)/shard_map/slots/pallas_call | solution.py:75
  34.4 1.6 %collective-permute-start.7 = (bf16[128,128]{1,0:T(8,128)(2,1)S(1)}, bf16[128,128]{1,0:T(8,128)(2,1)S(1)}, u32[]{:S(2)}, u32[]{:S(2)}) collective-permute-start(bf16[128,128]{1,0:T(8,128)(2,1)S(1)} %get-tuple-element.176), channel_id=1, source_target_pairs={{0,4},{4,0},{8,12},{12,8},{16,20},{20,16},{24,28},{28,24},{1,5},{5... | collective-permute-start | bytes 98312 | tf_op jit(solution)/shard_map/ppermute | solution.py:64
  36.7 1.9 %by_sample.3 = (f32[32,128]{1,0:T(8,128)S(1)}, f32[4,8,128]{2,1,0:T(8,128)S(1)}, f32[4,128]{1,0:T(4,128)S(1)}) custom-call(f32[8,512]{1,0:T(8,128)S(1)} %get-tuple-element.135.cot_ref, f32[7,64,1024]{2,1,0:T(8,128)S(1)} %get-tuple-element.130.coef_ref, bf16[1024,128]{1,0:T(8,128)(2,1)S(1)} %get-tuple-element.115.u_ref.refs_7_, ...), custom_call_target="tpu_custom_call" | custom-call | flops 1048576 | bytes 1024 | tf_op jit(solution)/shard_map/by_sample/pallas_call | solution.py:75
  39.0 1.6 %collective-permute-start.9 = (bf16[720,128]{1,0:T(8,128)(2,1)S(1)}, bf16[720,128]{1,0:T(8,128)(2,1)S(1)}, u32[]{:S(2)}, u32[]{:S(2)}) collective-permute-start(bf16[720,128]{1,0:T(8,128)(2,1)S(1)} %pad_maximum_fusion), channel_id=1, source_target_pairs={{0,2},{1,3},{2,0},{3,1},{4,6},{5,7},{6,4},{7,5},{8,10},{9,11},{10,... | collective-permute-start | bytes 552968 | tf_op jit(solution)/shard_map/ppermute | solution.py:64
  40.5 2.7 %collective-permute-start.8 = (bf16[64,128]{1,0:T(8,128)(2,1)S(1)}, bf16[64,128]{1,0:T(8,128)(2,1)S(1)}, u32[]{:S(2)}, u32[]{:S(2)}) collective-permute-start(bf16[64,128]{1,0:T(8,128)(2,1)S(1)} %get-tuple-element.154), channel_id=1, source_target_pairs={{0,16},{4,20},{8,24},{12,28},{16,0},{20,4},{24,8},{28,12},{1,17},{... | collective-permute-start | bytes 49160 | tf_op jit(solution)/shard_map/ppermute | solution.py:64
  43.2 1.4 %collective-permute-done.9 = bf16[720,128]{1,0:T(8,128)(2,1)S(1)} collective-permute-done((bf16[720,128]{1,0:T(8,128)(2,1)S(1)}, bf16[720,128]{1,0:T(8,128)(2,1)S(1)}, u32[]{:S(2)}, u32[]{:S(2)}) %collective-permute-start.9) | collective-permute-done | bytes 184352 | tf_op jit(solution)/shard_map/ppermute | solution.py:64
  46.0 0.7 %finish.1 = (f32[3,64]{1,0:T(4,128)}, f32[64,128]{1,0:T(8,128)}, f32[256,128]{1,0:T(8,128)}, f32[64,128]{1,0:T(8,128)}, f32[128,128]{1,0:T(8,128)}, /*index=5*/f...) custom-call(f32[64,128]{1,0:T(8,128)S(1)} %get-tuple-element.155.ray_ref, f32[3,64]{1,0:T(4,128)S(1)} %get-tuple-element.156.color_ref, ...), custom_call_target="tpu_custom_call" | custom-call | bytes 1024 | tf_op jit(solution)/shard_map/finish/pallas_call | solution.py:75
  (57 shorter events, 4.2 us)
Async XLA Ops:
  0.6 4.2 %copy-start.3 = (bf16[64,128]{1,0:T(8,128)(2,1)S(1)}, bf16[64,128]{1,0:T(8,128)(2,1)}, u32[]{:S(2)}) copy-start(bf16[64,128]{1,0:T(8,128)(2,1)} %ray_ref.1) | copy-start | bytes 49156
  0.6 4.2 %copy-start.6 = (s32[1,512]{1,0:T(1,128)S(1)}, s32[1,512]{1,0:T(1,128)}, u32[]{:S(2)}) copy-start(s32[1,512]{1,0:T(1,128)} %occ_ref.1) | copy-start | bytes 6148
  0.7 4.2 %copy-start.5 = (s32[1,2,512]{2,1,0:T(2,128)S(1)}, s32[1,2,512]{2,1,0:T(2,128)}, u32[]{:S(2)}) copy-start(s32[1,2,512]{2,1,0:T(2,128)} %param.20) | copy-start | bytes 12292
  0.7 4.2 %copy-start.10 = (f32[1,4]{1,0:T(1,128)S(1)}, f32[1,4]{1,0:T(1,128)}, u32[]{:S(2)}) copy-start(f32[1,4]{1,0:T(1,128)} %b_out_ref.1) | copy-start | bytes 52
  0.7 4.2 %copy-start.8 = (bf16[1,4,128]{2,1,0:T(4,128)(2,1)S(1)}, bf16[1,4,128]{2,1,0:T(4,128)(2,1)}, u32[]{:S(2)}) copy-start(bf16[1,4,128]{2,1,0:T(4,128)(2,1)} %param.18) | copy-start | bytes 3076
  0.7 4.2 %copy-start.9 = (f32[1,128]{1,0:T(1,128)S(1)}, f32[1,128]{1,0:T(1,128)}, u32[]{:S(2)}) copy-start(f32[1,128]{1,0:T(1,128)} %b_ref.1) | copy-start | bytes 1540
  0.7 4.2 %copy-start.1 = (bf16[1,128,128]{2,1,0:T(8,128)(2,1)S(1)}, bf16[1,128,128]{2,1,0:T(8,128)(2,1)}, u32[]{:S(2)}) copy-start(bf16[1,128,128]{2,1,0:T(8,128)(2,1)} %param.16) | copy-start | bytes 98308
  0.7 4.2 %copy-start.2 = (bf16[1,64,128]{2,1,0:T(8,128)(2,1)S(1)}, bf16[1,64,128]{2,1,0:T(8,128)(2,1)}, u32[]{:S(2)}) copy-start(bf16[1,64,128]{2,1,0:T(8,128)(2,1)} %param.15) | copy-start | bytes 49156
  0.7 4.2 %copy-start.4 = (f32[3,512]{1,0:T(4,128)S(1)}, f32[3,512]{1,0:T(4,128)}, u32[]{:S(2)}) copy-start(f32[3,512]{1,0:T(4,128)} %target_ref.1) | copy-start | bytes 18436
  0.7 4.2 %copy-start.7 = (s32[512]{0:T(512)S(1)}, s32[512]{0:T(512)}, u32[]{:S(2)}) copy-start(s32[512]{0:T(512)} %param.12) | copy-start | bytes 6148
  0.7 6.0 %collective-permute-start = (bf16[64,128]{1,0:T(8,128)(2,1)}, bf16[64,128]{1,0:T(8,128)(2,1)S(1)}, u32[]{:S(2)}, u32[]{:S(2)}) collective-permute-start(bf16[64,128]{1,0:T(8,128)(2,1)} %ray_ref.1), channel_id=1, source_target_pairs={{0,16},{4,20},{8,24},{12,28},{16,0},{20,4},{24,8},{28,12},{1,17},{... | collective-permute-start | bytes 49160 | tf_op jit(solution)/shard_map/ppermute | solution.py:64
  5.0 3.7 %copy-start = (bf16[1,1024,128]{2,1,0:T(8,128)(2,1)S(1)}, bf16[1,1024,128]{2,1,0:T(8,128)(2,1)}, u32[]{:S(2)}) copy-start(bf16[1,1024,128]{2,1,0:T(8,128)(2,1)} %param.14) | copy-start | bytes 786436
  6.8 3.9 %collective-permute-start.1 = (bf16[128,128]{1,0:T(8,128)(2,1)S(1)}, bf16[128,128]{1,0:T(8,128)(2,1)S(1)}, u32[]{:S(2)}, u32[]{:S(2)}) collective-permute-start(bf16[128,128]{1,0:T(8,128)(2,1)S(1)} %pad_maximum_fusion.2), channel_id=1, source_target_pairs={{0,4},{4,0},{8,12},{12,8},{16,20},{20,16},{24,28},{28,24},{1,5},{5... | collective-permute-start | bytes 98312 | tf_op jit(solution)/shard_map/ppermute | solution.py:64
  10.7 4.3 %collective-permute-start.2 = (bf16[256,128]{1,0:T(8,128)(2,1)S(1)}, bf16[256,128]{1,0:T(8,128)(2,1)S(1)}, u32[]{:S(2)}, u32[]{:S(2)}) collective-permute-start(bf16[256,128]{1,0:T(8,128)(2,1)S(1)} %constant_dynamic-update-slice_fusion.refs_0_), channel_id=1, source_target_pairs={{0,8},{4,12},{8,0},{12,4},{16,24},{20,28},{24,16},{28,20},{1,9},{5... | collective-permute-start | bytes 196616 | tf_op jit(solution)/shard_map/ppermute | solution.py:64
  17.0 3.9 %collective-permute-start.3 = (f32[4,512]{1,0:T(4,128)S(1)}, f32[4,512]{1,0:T(4,128)S(1)}, u32[]{:S(2)}, u32[]{:S(2)}) collective-permute-start(f32[4,512]{1,0:T(4,128)S(1)} %get-tuple-element.100.seg_ref.refs_0_), channel_id=1, source_target_pairs={{0,4},{4,0},{8,12},{12,8},{16,20},{20,16},{24,28},{28,24},{1,5},{5... | collective-permute-start | bytes 24584 | tf_op jit(solution)/shard_map/ppermute | solution.py:64
  20.9 3.9 %collective-permute-start.4 = (f32[4,512]{1,0:T(4,128)S(1)}, f32[4,512]{1,0:T(4,128)S(1)}, u32[]{:S(2)}, u32[]{:S(2)}) collective-permute-start(f32[4,512]{1,0:T(4,128)S(1)} %pad_maximum_fusion.3), channel_id=1, source_target_pairs={{0,8},{4,12},{8,0},{12,4},{16,24},{20,28},{24,16},{28,20},{1,9},{5... | collective-permute-start | bytes 24584 | tf_op jit(solution)/shard_map/ppermute | solution.py:64
  24.9 4.6 %collective-permute-start.5 = (f32[4,512]{1,0:T(4,128)S(1)}, f32[4,512]{1,0:T(4,128)S(1)}, u32[]{:S(2)}, u32[]{:S(2)}) collective-permute-start(f32[4,512]{1,0:T(4,128)S(1)} %pad_maximum_fusion.4), channel_id=1, source_target_pairs={{0,16},{4,20},{8,24},{12,28},{16,0},{20,4},{24,8},{28,12},{1,17},{... | collective-permute-start | bytes 24584 | tf_op jit(solution)/shard_map/ppermute | solution.py:64
  29.9 4.4 %collective-permute-start.6 = (bf16[256,128]{1,0:T(8,128)(2,1)S(1)}, bf16[256,128]{1,0:T(8,128)(2,1)S(1)}, u32[]{:S(2)}, u32[]{:S(2)}) collective-permute-start(bf16[256,128]{1,0:T(8,128)(2,1)S(1)} %get-tuple-element.122), channel_id=1, source_target_pairs={{0,8},{4,12},{8,0},{12,4},{16,24},{20,28},{24,16},{28,20},{1,9},{5... | collective-permute-start | bytes 196616 | tf_op jit(solution)/shard_map/ppermute | solution.py:64
  34.4 4.2 %collective-permute-start.7 = (bf16[128,128]{1,0:T(8,128)(2,1)S(1)}, bf16[128,128]{1,0:T(8,128)(2,1)S(1)}, u32[]{:S(2)}, u32[]{:S(2)}) collective-permute-start(bf16[128,128]{1,0:T(8,128)(2,1)S(1)} %get-tuple-element.176), channel_id=1, source_target_pairs={{0,4},{4,0},{8,12},{12,8},{16,20},{20,16},{24,28},{28,24},{1,5},{5... | collective-permute-start | bytes 98312 | tf_op jit(solution)/shard_map/ppermute | solution.py:64
  39.0 5.6 %collective-permute-start.9 = (bf16[720,128]{1,0:T(8,128)(2,1)S(1)}, bf16[720,128]{1,0:T(8,128)(2,1)S(1)}, u32[]{:S(2)}, u32[]{:S(2)}) collective-permute-start(bf16[720,128]{1,0:T(8,128)(2,1)S(1)} %pad_maximum_fusion), channel_id=1, source_target_pairs={{0,2},{1,3},{2,0},{3,1},{4,6},{5,7},{6,4},{7,5},{8,10},{9,11},{10,... | collective-permute-start | bytes 552968 | tf_op jit(solution)/shard_map/ppermute | solution.py:64
  40.5 4.6 %collective-permute-start.8 = (bf16[64,128]{1,0:T(8,128)(2,1)S(1)}, bf16[64,128]{1,0:T(8,128)(2,1)S(1)}, u32[]{:S(2)}, u32[]{:S(2)}) collective-permute-start(bf16[64,128]{1,0:T(8,128)(2,1)S(1)} %get-tuple-element.154), channel_id=1, source_target_pairs={{0,16},{4,20},{8,24},{12,28},{16,0},{20,4},{24,8},{28,12},{1,17},{... | collective-permute-start | bytes 49160 | tf_op jit(solution)/shard_map/ppermute | solution.py:64
  44.6 1.4 %collective-permute-start.10 = (bf16[464,128]{1,0:T(8,128)(2,1)S(1)}, bf16[464,128]{1,0:T(8,128)(2,1)S(1)}, u32[]{:S(2)}, u32[]{:S(2)}) collective-permute-start(bf16[464,128]{1,0:T(8,128)(2,1)S(1)} %pad_maximum_fusion.1.sent_ref), channel_id=1, source_target_pairs={{0,1},{1,0},{2,3},{3,2},{4,5},{5,4},{6,7},{7,6},{8,9},{9,8},{10,11... | collective-permute-start | bytes 356360 | tf_op jit(solution)/shard_map/ppermute | solution.py:64

commit v6 on v5

--- a/solution.py
+++ b/solution.py
@@ -181,8 +181,8 @@
 def forward_kernel(*refs, owners, second, lines):
     ray_ref, project_ref, w_t_ref, wide_ref, left_ref, lines_ref, earlier_ref, *refs = refs
     if second:
-        before_refs, refs = refs[:3], refs[3:]
-    seg_ref, kept_ref, u_ref, sorted_ref, order_ref, ut_ref, raw_ref = refs
+        before_refs, refs = refs[:2], refs[2:]
+    seg_ref, kept_ref, ut_ref, sorted_ref, order_ref, raw_ref = refs
     width, total = project_ref.shape
     samples = wide_ref.shape[0]
     outs = seg_ref.shape[0]
@@ -201,9 +201,7 @@
         for n in range(half // chunk):
             part = slice(n * chunk, (n + 1) * chunk)
             seg_ref[:, whole(n)] = before_refs[0][:, part]
-            sorted_ref[whole(n), :] = before_refs[2][part, :]
-            for k in range(slots):
-                u_ref[whole(n, k), :] = before_refs[1][k * half + n * chunk : k * half + (n + 1) * chunk, :]
+            sorted_ref[whole(n), :] = before_refs[1][part, :]
         side = 1 - side
 
     def spot(n, k=0):
@@ -222,9 +220,7 @@
         sorted_ref[spot(n), :] = order_ref[n * chunk : (n + 1) * chunk, :]
         for k in range(slots):
             part = project_ref[:, whole(n, k, side)] + ray_t[:, n * chunk : (n + 1) * chunk]
-            part = part.astype(bf16)
-            ut_ref[:, k * half + n * chunk : k * half + (n + 1) * chunk] = part
-            u_ref[spot(n, k), :] = part.astype(f32).T.astype(bf16)
+            ut_ref[:, k * half + n * chunk : k * half + (n + 1) * chunk] = part.astype(bf16)
     b_out = [lines_ref[lines["b_out"], c] for c in range(outs)]
 
     def shade_block(block, carry):
@@ -276,15 +272,29 @@
                 colors[c] = colors[c] + jnp.sum(light, 0, keepdims=True)
                 kept_ref[c, :, local] = shading
                 kept_ref[outs + c, :, local] = light
-            kept_ref[outs - 1, :, local] = jnp.exp(-(entered + optical))
-            kept_ref[2 * outs - 1, :, local] = step_length * occupied[k] * jax.nn.sigmoid(raws[k])
+            kept_ref[outs - 1, :, local] = entered + optical
+            kept_ref[2 * outs - 1, :, local] = raws[k]
         place = spot(n)
         for c in range(outs - 1):
             seg_ref[c : c + 1, place] = colors[c]
         seg_ref[outs - 1 : outs, place] = jnp.exp(-before)
 
 
-def coefficient_kernel(seg_ref, first_ref, second_ref, later_ref, coef_ref, turned_ref, *, owners):
+def coefficient_kernel(
+    seg_ref,
+    first_ref,
+    second_ref,
+    first_ut_ref,
+    second_ut_ref,
+    later_ref,
+    lines_ref,
+    coef_ref,
+    turned_ref,
+    u_ref,
+    *,
+    owners,
+    lines,
+):
     outs, rays = seg_ref.shape
     samples, local = first_ref.shape[1:]
     half = rays // 2
@@ -296,18 +306,25 @@
 
     def keep(index, lanes, value):
         coef_ref[index, :, lanes] = value
+        value = value.astype(bf16)
         turned_ref[index, lanes, :] = jnp.concatenate([value] * (128 // samples), 0).T
 
-    for kept_ref, where in ((first_ref, side), (second_ref, 1 - side)):
+    for kept_ref, ut_ref, where in (
+        (first_ref, first_ut_ref, side),
+        (second_ref, second_ut_ref, 1 - side),
+    ):
         for n in range(half // chunk):
             base = (2 * n + where) * chunk
             through = seg_ref[outs - 1 : outs, pl.ds(pl.multiple_of(base, chunk), chunk)]
+            occ = lines_ref[lines["occ"] : lines["occ"] + 1, pl.ds(pl.multiple_of(base, chunk), chunk)]
             after = [jnp.zeros((1, chunk), f32)] * (outs - 1)
             for k in reversed(range(slots)):
                 lanes = pl.ds(pl.multiple_of(k * rays + base, chunk), chunk)
                 at = slice(k * half + n * chunk, k * half + (n + 1) * chunk)
-                passed = kept_ref[outs - 1, :, at]
-                density = kept_ref[2 * outs - 1, :, at]
+                u_ref[lanes, :] = ut_ref[:, at].T
+                passed = jnp.exp(-kept_ref[outs - 1, :, at])
+                occupied = (k < occ).astype(f32)
+                density = step_length * occupied * jax.nn.sigmoid(kept_ref[2 * outs - 1, :, at])
                 lights = [kept_ref[outs + c, :, at] for c in range(outs - 1)]
                 behinds = sum_dot(later, jnp.concatenate(lights, 1))
                 for c in range(outs - 1):
@@ -340,12 +357,13 @@
         for h in range(step // 16):
             base = pl.multiple_of(block * step + h * 16, 16)
             u16 = u_ref[pl.ds(first + base, 16), :]
+            rows16 = [turned_ref[c, pl.ds(first + base, 16), :].astype(f32) for c in range(count)]
             for q in range(2):
                 at = pl.multiple_of(block * step + h * 16 + q * 8, 8)
                 left = [
                     jnp.where(
                         block_mask,
-                        jnp.concatenate([turned_ref[c, pl.ds(first + at, 8), :]] * repeat, 1),
+                        jnp.concatenate([rows16[c][q * 8 : q * 8 + 8]] * repeat, 1),
                         0.0,
                     )
                     for c in range(count)
@@ -375,7 +393,7 @@
 
 def basis_cuts(total, bits):
     eighth = total // 8
-    return [0, eighth, 5 * eighth, total] if bits > 2 else [0, total]
+    return [0, 2 * eighth, 5 * eighth, total] if bits > 2 else [0, total]
 
 
 def basis_part(refs, row):
@@ -462,24 +480,21 @@
             send_ref[at : at + own, :] = ray_ref[pl.ds(place, own), :].astype(bf16)
 
 
-def brick_kernel(lines_ref, moved_ref, keep_ref, send_ref, *, shares):
+def brick_kernel(lines_ref, moved_ref, out_ref, *, first, shares):
     share = lax.axis_index("ray")
     rays = lines_ref.shape[1]
     total, width = moved_ref.shape
-    slots = total // rays
-    half = keep_ref.shape[0]
-    part = 2 * half // shares
+    owners = shares // 2
+    part = out_ref.shape[0] // owners
     moved = moved_ref[...]
     row = lax.broadcasted_iota(jnp.int32, (part, rays), 0).astype(f32)
-    for i in range(shares):
-        first = ((share ^ i) * part).astype(f32)
+    for i in range(owners):
+        begin = ((share ^ (first + i)) * part).astype(f32)
         acc = jnp.zeros((part, width), f32)
-        for k in range(slots):
-            one_hot = jnp.where(row + first == lines_ref[k : k + 1, :], 1.0, 0.0).astype(bf16)
-            rows = slice(k * rays, (k + 1) * rays)
-            acc = acc + nn_dot(one_hot, moved[rows])
-        ref, at = (keep_ref, i * part) if i < shares // 2 else (send_ref, i * part - half)
-        ref[at : at + part, :] = acc
+        for k in range(total // rays):
+            one_hot = jnp.where(row + begin == lines_ref[k : k + 1, :], 1.0, 0.0).astype(bf16)
+            acc = acc + nn_dot(one_hot, moved[k * rays : (k + 1) * rays])
+        out_ref[i * part : (i + 1) * part, :] = acc.astype(out_ref.dtype)
 
 
 def sample_kernel(
@@ -736,34 +751,39 @@
     )(lines_later, brick_code[0], w_t)
     passes = ()
     kept = []
+    uts = []
     for second, part in enumerate((gathered, other)):
         wide_rays = rays if second else rays // 2
-        seg, kept_half, *passes = call(
+        seg, kept_half, ut_half, ray_sorted = call(
             functools.partial(forward_kernel, owners=owners, second=second, lines=lines),
             (
                 shaped(outs, wide_rays),
                 shaped(2 * outs, samples, total // 2),
-                shaped16(slots * wide_rays, width),
+                shaped16(width, total // 2),
                 shaped16(wide_rays, width),
             ),
             "forward",
             scratch=(
                 pltpu.VMEM((rays // 2, width), bf16),
-                pltpu.VMEM((width, total // 2), bf16),
                 pltpu.VMEM((outs, samples, total // 2), f32),
             ),
             flops=1 << 30,
         )(part, project, w_t, wide, left, packed, earlier, *passes)
-        passes = (seg, *passes)
+        passes = (seg, ray_sorted)
         kept.append(kept_half)
-    seg, u, ray_sorted = passes
-
-    coef, turned = call(
-        functools.partial(coefficient_kernel, owners=owners),
-        (shaped(count, samples, total), shaped(count, total, 128)),
+        uts.append(ut_half)
+
+    coef, turned, u = call(
+        functools.partial(coefficient_kernel, owners=owners, lines=lines),
+        (
+            shaped(count, samples, total),
+            shaped16(count, total, 128),
+            shaped16(total, width),
+        ),
         "coefficients",
         flops=1 << 30,
-    )(seg, *kept, later)
+    )(seg, *kept, *uts, later, packed)
+
     forward = packed[lines["direction"]][None] == 0.0
     group = (seg[:channels], seg[channels:])
     received = []
@@ -842,6 +862,14 @@
             flops=1 << 20,
         )(cots, coef, u, s, low)
 
+    def by_brick(first, moved, shape):
+        return call(
+            functools.partial(brick_kernel, first=first, shares=shares),
+            shape,
+            "bricks",
+            flops=1 << 20,
+        )(packed, moved)
+
     parts = 2
     by_part = []
     later_cots = cots
@@ -859,26 +887,23 @@
         if b < parts:
             by_part += part_by_sample(b, later_cots)
         if b == 1:
-            brick_keep, brick_send = call(
-                functools.partial(brick_kernel, shares=shares),
-                (shaped(bricks // 2, width), shaped(bricks // 2, width)),
-                "bricks",
-                flops=1 << 20,
-            )(packed, moved)
-            w_grad, brick_send = lax.optimization_barrier((w_grad, brick_send))
+            brick_sent = by_brick(shares // 2, moved, shaped16(bricks // 2, width))
+            w_grad, brick_sent = lax.optimization_barrier((w_grad, brick_sent))
         if b + 1 < bits:
             held = (ray_got, later_cots, moved, by_part)
             ray_got, later_cots, moved, by_part = lax.optimization_barrier(held)
             ray_keep, ray_send = merged(ray_keep, ray_got)
 
-    brick = brick_keep
-    brick_sent = brick_send.astype(bf16)
+    small = small.astype(bf16)
     for b in reversed(range(bits_of(shares))):
-        sent = jnp.concatenate([brick_sent, small.astype(bf16)], 0)
+        sent = jnp.concatenate([brick_sent, small], 0)
+        if 1 << (b + 1) == shares:
+            sent, moved = lax.optimization_barrier((sent, moved))
+            brick = by_brick(0, moved, shaped(bricks // 2, width))
         other = swap(sent, "ray", shares, 1 << b)
         if b > 0:
             half = brick.shape[0]
-            small = sent[half:].astype(f32) + other[half:].astype(f32)
+            small = (sent[half:].astype(f32) + other[half:].astype(f32)).astype(bf16)
             brick_sent = (brick[half // 2 :] + other[half // 2 : half].astype(f32)).astype(bf16)
             brick = brick[: half // 2] + other[: half // 2].astype(f32)
     ray_sum, color_own = call(

time: 46.9 us -> 46.6 us (level)
    pallas_call x18 -> x19, Pallas kernels: 18.6 us -> 18.3 us  [run(): pl.pallas_call(kernel, out_shape=out_shape, in_specs=[pl.BlockSpec(memory...]
  transfers between devices with their start and end apart: 11 -> 11, of which waited for: 7 -> 8; matrix products, arithmetic and copies ran while one was open for 0% -> 0% of each run, Pallas kernels for 32% -> 32%
where the time goes in v6:
time: 46.6 us; the launch traced here: 46.5 us
  starting transfers between devices  21.7 us (47%)
  Pallas kernels  18.3 us (39%)
  waiting for transfers between devices  5.18 us (11%)
  between operations  1.03 us (2%)
    ppermute x11, starting transfers between devices, swap(): return lax.ppermute(array, axis, [(i, i ^ distance) for i in range(size)])  21.7 us
    pallas_call x19, Pallas kernels, run(): pl.pallas_call(kernel, out_shape=out_shape, in_specs=[pl.BlockSpec(memory...  18.3 us
    ppermute x11, waiting for transfers between devices, swap(): return lax.ppermute(array, axis, [(i, i ^ distance) for i in range(size)])  5.18 us
  transfers between devices with their start and end apart: 11, of which 8 were waited for; matrix products, arithmetic and copies ran while one was open for 0% of the time, Pallas kernels for 32%

profile of v6, /device:TPU:0, one launch (start us, length us, event | category | flops | bytes accessed | tf_op | source)
XLA Modules:
  0.0 46.5 jit_solution(17213225128368413221)
XLA Ops:
  0.7 4.1 %collective-permute-start = (bf16[64,128]{1,0:T(8,128)(2,1)}, bf16[64,128]{1,0:T(8,128)(2,1)S(1)}, u32[]{:S(2)}, u32[]{:S(2)}) collective-permute-start(bf16[64,128]{1,0:T(8,128)(2,1)} %ray_ref.1), channel_id=1, source_target_pairs={{0,16},{4,20},{8,24},{12,28},{16,0},{20,4},{24,8},{28,12},{1,17},{... | collective-permute-start | bytes 49160 | tf_op jit(solution)/shard_map/ppermute | solution.py:64
  5.0 1.0 %prepare.1 = (bf16[64,128]{1,0:T(8,128)(2,1)S(1)}, bf16[208,128]{1,0:T(8,128)(2,1)S(1)}, f32[8,512]{1,0:T(8,128)S(1)}, bf16[128,128]{1,0:T(8,128)(2,1)S(1)}, f32...) custom-call(bf16[64,128]{1,0:T(8,128)(2,1)S(1)} %copy-done.3, ...), custom_call_target="tpu_custom_call" | custom-call | flops 2147483648 | bytes 1024 | tf_op jit(solution)/shard_map/prepare/pallas_call | solution.py:75
  6.0 0.8 %collective-permute-done = bf16[64,128]{1,0:T(8,128)(2,1)S(1)} collective-permute-done((bf16[64,128]{1,0:T(8,128)(2,1)}, bf16[64,128]{1,0:T(8,128)(2,1)S(1)}, u32[]{:S(2)}, u32[]{:S(2)}) %collective-permute-start) | collective-permute-done | bytes 16416 | tf_op jit(solution)/shard_map/ppermute | solution.py:64
  6.8 1.9 %collective-permute-start.1 = (bf16[128,128]{1,0:T(8,128)(2,1)S(1)}, bf16[128,128]{1,0:T(8,128)(2,1)S(1)}, u32[]{:S(2)}, u32[]{:S(2)}) collective-permute-start(bf16[128,128]{1,0:T(8,128)(2,1)S(1)} %pad_maximum_fusion.2), channel_id=1, source_target_pairs={{0,4},{4,0},{8,12},{12,8},{16,20},{20,16},{24,28},{28,24},{1,5},{5... | collective-permute-start | bytes 98312 | tf_op jit(solution)/shard_map/ppermute | solution.py:64
  8.7 0.8 %chosen.1 = (bf16[128,1024]{1,0:T(8,128)(2,1)S(1)}, f32[128,1024]{1,0:T(8,128)S(1)}) custom-call(f32[8,512]{1,0:T(8,128)S(1)} %get-tuple-element.93.lines_ref.refs_5_.refs_7_, bf16[1024,128]{1,0:T(8,128)(2,1)S(1)} %bitcast.14, bf16[128,128]{1,0:T(8,128)(2,1)S(1)} %get-tuple-element.94.w_t_ref.refs_2_), custom_call_target="tpu_custom_call" | custom-call | flops 536870912 | bytes 1024 | tf_op jit(solution)/shard_map/chosen/pallas_call | solution.py:75
  9.5 1.2 %collective-permute-done.1 = bf16[128,128]{1,0:T(8,128)(2,1)S(1)} collective-permute-done((bf16[128,128]{1,0:T(8,128)(2,1)S(1)}, bf16[128,128]{1,0:T(8,128)(2,1)S(1)}, u32[]{:S(2)}, u32[]{:S(2)}) %collective-permute-start.1) | collective-permute-done | bytes 32800 | tf_op jit(solution)/shard_map/ppermute | solution.py:64
  10.7 1.9 %collective-permute-start.2 = (bf16[256,128]{1,0:T(8,128)(2,1)S(1)}, bf16[256,128]{1,0:T(8,128)(2,1)S(1)}, u32[]{:S(2)}, u32[]{:S(2)}) collective-permute-start(bf16[256,128]{1,0:T(8,128)(2,1)S(1)} %constant_dynamic-update-slice_fusion.refs_0_), channel_id=1, source_target_pairs={{0,8},{4,12},{8,0},{12,4},{16,24},{20,28},{24,16},{28,20},{1,9},{5... | collective-permute-start | bytes 196616 | tf_op jit(solution)/shard_map/ppermute | solution.py:64
  12.6 2.0 %forward.2 = (f32[4,256]{1,0:T(4,128)S(1)}, f32[8,64,512]{2,1,0:T(8,128)S(1)}, bf16[128,512]{1,0:T(8,128)(2,1)S(1)}, bf16[256,128]{1,0:T(8,128)(2,1)S(1)}) custom-call(bf16[256,128]{1,0:T(8,128)(2,1)S(1)} %constant_dynamic-update-slice_fusion.refs_0_, f32[128,1024]{1,0:T(8,128)S(1)} %get-tuple-element.95.refs_1_, ...), custom_call_target="tpu_custom_call" | custom-call | flops 1073741824 | bytes 1024 | tf_op jit(solution)/shard_map/forward/pallas_call | solution.py:75
  15.0 2.0 %forward.3 = (f32[4,512]{1,0:T(4,128)S(1)}, f32[8,64,512]{2,1,0:T(8,128)S(1)}, bf16[128,512]{1,0:T(8,128)(2,1)S(1)}, bf16[512,128]{1,0:T(8,128)(2,1)S(1)}) custom-call(bf16[256,128]{1,0:T(8,128)(2,1)S(1)} %collective-permute-done.2.refs_0_, f32[128,1024]{1,0:T(8,128)S(1)} %get-tuple-element.95.refs_1_, ...), custom_call_target="tpu_custom_call" | custom-call | flops 1073741824 | bytes 1024 | tf_op jit(solution)/shard_map/forward/pallas_call | solution.py:75
  17.0 2.0 %collective-permute-start.3 = (f32[4,512]{1,0:T(4,128)S(1)}, f32[4,512]{1,0:T(4,128)S(1)}, u32[]{:S(2)}, u32[]{:S(2)}) collective-permute-start(f32[4,512]{1,0:T(4,128)S(1)} %get-tuple-element.101.seg_ref.refs_0_), channel_id=1, source_target_pairs={{0,4},{4,0},{8,12},{12,8},{16,20},{20,16},{24,28},{28,24},{1,5},{5... | collective-permute-start | bytes 24584 | tf_op jit(solution)/shard_map/ppermute | solution.py:64
  18.9 0.8 %coefficients.1 = (f32[7,64,1024]{2,1,0:T(8,128)S(1)}, bf16[7,1024,128]{2,1,0:T(8,128)(2,1)S(1)}, bf16[1024,128]{1,0:T(8,128)(2,1)S(1)}) custom-call(f32[4,512]{1,0:T(4,128)S(1)} %get-tuple-element.101.seg_ref.refs_0_, f32[8,64,512]{2,1,0:T(8,128)S(1)} %get-tuple-element.102.first_ref, f32[8,64,512]{2,1,0:T(8,128)S(1)} %get-tuple-element.103.second_ref, ...), custom_call_target="tpu_custom_call" | custom-call | flops 1073741824 | bytes 1024 | tf_op jit(solution)/shard_map/coefficients/pallas_call | solution.py:75
  19.7 1.3 %basis.3 = (f32[7,256,128]{2,1,0:T(8,128)S(1)}, f32[4,256,128]{2,1,0:T(8,128)S(1)}) custom-call(bf16[7,1024,128]{2,1,0:T(8,128)(2,1)S(1)} %get-tuple-element.116.turned_ref, bf16[1024,128]{1,0:T(8,128)(2,1)S(1)} %get-tuple-element.118.u_ref.refs_7_, f32[64,128]{1,0:T(8,128)S(1)} %get-tuple-element.119.s_ref, ...), custom_call_target="tpu_custom_call" | custom-call | flops 536870912 | bytes 1024 | tf_op jit(solution)/shard_map/basis/pallas_call | solution.py:75
  21.1 1.6 %collective-permute-start.4 = (f32[4,512]{1,0:T(4,128)S(1)}, f32[4,512]{1,0:T(4,128)S(1)}, u32[]{:S(2)}, u32[]{:S(2)}) collective-permute-start(f32[4,512]{1,0:T(4,128)S(1)} %pad_maximum_fusion.3), channel_id=1, source_target_pairs={{0,8},{4,12},{8,0},{12,4},{16,24},{20,28},{24,16},{28,20},{1,9},{5... | collective-permute-start | bytes 24584 | tf_op jit(solution)/shard_map/ppermute | solution.py:64
  22.7 1.6 %basis.4 = (f32[7,384,128]{2,1,0:T(8,128)S(1)}, f32[4,384,128]{2,1,0:T(8,128)S(1)}) custom-call(bf16[7,1024,128]{2,1,0:T(8,128)(2,1)S(1)} %get-tuple-element.116.turned_ref, bf16[1024,128]{1,0:T(8,128)(2,1)S(1)} %get-tuple-element.118.u_ref.refs_7_, f32[64,128]{1,0:T(8,128)S(1)} %get-tuple-element.119.s_ref, ...), custom_call_target="tpu_custom_call" | custom-call | flops 536870912 | bytes 1024 | tf_op jit(solution)/shard_map/basis/pallas_call | solution.py:75
  24.8 2.7 %collective-permute-start.5 = (f32[4,512]{1,0:T(4,128)S(1)}, f32[4,512]{1,0:T(4,128)S(1)}, u32[]{:S(2)}, u32[]{:S(2)}) collective-permute-start(f32[4,512]{1,0:T(4,128)S(1)} %pad_maximum_fusion.4), channel_id=1, source_target_pairs={{0,16},{4,20},{8,24},{12,28},{16,0},{20,4},{24,8},{28,12},{1,17},{... | collective-permute-start | bytes 24584 | tf_op jit(solution)/shard_map/ppermute | solution.py:64
  27.5 1.6 %basis.5 = (f32[7,384,128]{2,1,0:T(8,128)S(1)}, f32[4,384,128]{2,1,0:T(8,128)S(1)}) custom-call(bf16[7,1024,128]{2,1,0:T(8,128)(2,1)S(1)} %get-tuple-element.116.turned_ref, bf16[1024,128]{1,0:T(8,128)(2,1)S(1)} %get-tuple-element.118.u_ref.refs_7_, f32[64,128]{1,0:T(8,128)S(1)} %get-tuple-element.119.s_ref, ...), custom_call_target="tpu_custom_call" | custom-call | flops 536870912 | bytes 1024 | tf_op jit(solution)/shard_map/basis/pallas_call | solution.py:75
  29.9 1.6 %collective-permute-start.6 = (bf16[256,128]{1,0:T(8,128)(2,1)S(1)}, bf16[256,128]{1,0:T(8,128)(2,1)S(1)}, u32[]{:S(2)}, u32[]{:S(2)}) collective-permute-start(bf16[256,128]{1,0:T(8,128)(2,1)S(1)} %get-tuple-element.125), channel_id=1, source_target_pairs={{0,8},{4,12},{8,0},{12,4},{16,24},{20,28},{24,16},{28,20},{1,9},{5... | collective-permute-start | bytes 196616 | tf_op jit(solution)/shard_map/ppermute | solution.py:64
  31.5 1.9 %by_sample.2 = (f32[32,128]{1,0:T(8,128)S(1)}, f32[4,8,128]{2,1,0:T(8,128)S(1)}, f32[4,128]{1,0:T(4,128)S(1)}) custom-call(f32[8,512]{1,0:T(8,128)S(1)} %get-tuple-element.138.cot_ref, f32[7,64,1024]{2,1,0:T(8,128)S(1)} %get-tuple-element.133.coef_ref, bf16[1024,128]{1,0:T(8,128)(2,1)S(1)} %get-tuple-element.118.u_ref.refs_7_, ...), custom_call_target="tpu_custom_call" | custom-call | flops 1048576 | bytes 1024 | tf_op jit(solution)/shard_map/by_sample/pallas_call | solution.py:75
  33.4 0.9 %slots.1 = (bf16[1024,128]{1,0:T(8,128)(2,1)S(1)}, f32[128,128]{1,0:T(8,128)S(1)}, f32[4,8,128]{2,1,0:T(8,128)S(1)}) custom-call(f32[7,256,128]{2,1,0:T(8,128)S(1)} %get-tuple-element.127.refs_0_, f32[7,384,128]{2,1,0:T(8,128)S(1)} %get-tuple-element.128.refs_1_, f32[7,384,128]{2,1,0:T(8,128)S(1)} %get-tuple-element.129.refs_2_, ...), custom_call_target="tpu_custom_call" | custom-call | flops 1048576 | bytes 1024 | tf_op jit(solution)/shard_map/slots/pallas_call | solution.py:75
  34.4 1.6 %collective-permute-start.7 = (bf16[128,128]{1,0:T(8,128)(2,1)S(1)}, bf16[128,128]{1,0:T(8,128)(2,1)S(1)}, u32[]{:S(2)}, u32[]{:S(2)}) collective-permute-start(bf16[128,128]{1,0:T(8,128)(2,1)S(1)} %get-tuple-element.180), channel_id=1, source_target_pairs={{0,4},{4,0},{8,12},{12,8},{16,20},{20,16},{24,28},{28,24},{1,5},{5... | collective-permute-start | bytes 98312 | tf_op jit(solution)/shard_map/ppermute | solution.py:64
  36.4 1.9 %by_sample.3 = (f32[32,128]{1,0:T(8,128)S(1)}, f32[4,8,128]{2,1,0:T(8,128)S(1)}, f32[4,128]{1,0:T(4,128)S(1)}) custom-call(f32[8,512]{1,0:T(8,128)S(1)} %get-tuple-element.138.cot_ref, f32[7,64,1024]{2,1,0:T(8,128)S(1)} %get-tuple-element.133.coef_ref, bf16[1024,128]{1,0:T(8,128)(2,1)S(1)} %get-tuple-element.118.u_ref.refs_7_, ...), custom_call_target="tpu_custom_call" | custom-call | flops 1048576 | bytes 1024 | tf_op jit(solution)/shard_map/by_sample/pallas_call | solution.py:75
  38.7 1.6 %collective-permute-start.9 = (bf16[720,128]{1,0:T(8,128)(2,1)S(1)}, bf16[720,128]{1,0:T(8,128)(2,1)S(1)}, u32[]{:S(2)}, u32[]{:S(2)}) collective-permute-start(bf16[720,128]{1,0:T(8,128)(2,1)S(1)} %pad_maximum_fusion), channel_id=1, source_target_pairs={{0,2},{1,3},{2,0},{3,1},{4,6},{5,7},{6,4},{7,5},{8,10},{9,11},{10,... | collective-permute-start | bytes 552968 | tf_op jit(solution)/shard_map/ppermute | solution.py:64
  40.2 2.6 %collective-permute-start.8 = (bf16[64,128]{1,0:T(8,128)(2,1)S(1)}, bf16[64,128]{1,0:T(8,128)(2,1)S(1)}, u32[]{:S(2)}, u32[]{:S(2)}) collective-permute-start(bf16[64,128]{1,0:T(8,128)(2,1)S(1)} %get-tuple-element.156), channel_id=1, source_target_pairs={{0,16},{4,20},{8,24},{12,28},{16,0},{20,4},{24,8},{28,12},{1,17},{... | collective-permute-start | bytes 49160 | tf_op jit(solution)/shard_map/ppermute | solution.py:64
  43.3 1.0 %collective-permute-done.9 = bf16[720,128]{1,0:T(8,128)(2,1)S(1)} collective-permute-done((bf16[720,128]{1,0:T(8,128)(2,1)S(1)}, bf16[720,128]{1,0:T(8,128)(2,1)S(1)}, u32[]{:S(2)}, u32[]{:S(2)}) %collective-permute-start.9) | collective-permute-done | bytes 184352 | tf_op jit(solution)/shard_map/ppermute | solution.py:64
  (57 shorter events, 5.2 us)
Async XLA Ops:
  0.6 4.2 %copy-start.3 = (bf16[64,128]{1,0:T(8,128)(2,1)S(1)}, bf16[64,128]{1,0:T(8,128)(2,1)}, u32[]{:S(2)}) copy-start(bf16[64,128]{1,0:T(8,128)(2,1)} %ray_ref.1) | copy-start | bytes 49156
  0.6 4.2 %copy-start.6 = (s32[1,512]{1,0:T(1,128)S(1)}, s32[1,512]{1,0:T(1,128)}, u32[]{:S(2)}) copy-start(s32[1,512]{1,0:T(1,128)} %occ_ref.1) | copy-start | bytes 6148
  0.7 4.2 %copy-start.5 = (s32[1,2,512]{2,1,0:T(2,128)S(1)}, s32[1,2,512]{2,1,0:T(2,128)}, u32[]{:S(2)}) copy-start(s32[1,2,512]{2,1,0:T(2,128)} %param.20) | copy-start | bytes 12292
  0.7 4.2 %copy-start.10 = (f32[1,4]{1,0:T(1,128)S(1)}, f32[1,4]{1,0:T(1,128)}, u32[]{:S(2)}) copy-start(f32[1,4]{1,0:T(1,128)} %b_out_ref.1) | copy-start | bytes 52
  0.7 4.2 %copy-start.8 = (bf16[1,4,128]{2,1,0:T(4,128)(2,1)S(1)}, bf16[1,4,128]{2,1,0:T(4,128)(2,1)}, u32[]{:S(2)}) copy-start(bf16[1,4,128]{2,1,0:T(4,128)(2,1)} %param.18) | copy-start | bytes 3076
  0.7 4.2 %copy-start.9 = (f32[1,128]{1,0:T(1,128)S(1)}, f32[1,128]{1,0:T(1,128)}, u32[]{:S(2)}) copy-start(f32[1,128]{1,0:T(1,128)} %b_ref.1) | copy-start | bytes 1540
  0.7 4.2 %copy-start.1 = (bf16[1,128,128]{2,1,0:T(8,128)(2,1)S(1)}, bf16[1,128,128]{2,1,0:T(8,128)(2,1)}, u32[]{:S(2)}) copy-start(bf16[1,128,128]{2,1,0:T(8,128)(2,1)} %param.16) | copy-start | bytes 98308
  0.7 4.2 %copy-start.2 = (bf16[1,64,128]{2,1,0:T(8,128)(2,1)S(1)}, bf16[1,64,128]{2,1,0:T(8,128)(2,1)}, u32[]{:S(2)}) copy-start(bf16[1,64,128]{2,1,0:T(8,128)(2,1)} %param.15) | copy-start | bytes 49156
  0.7 4.2 %copy-start.4 = (f32[3,512]{1,0:T(4,128)S(1)}, f32[3,512]{1,0:T(4,128)}, u32[]{:S(2)}) copy-start(f32[3,512]{1,0:T(4,128)} %target_ref.1) | copy-start | bytes 18436
  0.7 4.2 %copy-start.7 = (s32[512]{0:T(512)S(1)}, s32[512]{0:T(512)}, u32[]{:S(2)}) copy-start(s32[512]{0:T(512)} %param.12) | copy-start | bytes 6148
  0.7 6.0 %collective-permute-start = (bf16[64,128]{1,0:T(8,128)(2,1)}, bf16[64,128]{1,0:T(8,128)(2,1)S(1)}, u32[]{:S(2)}, u32[]{:S(2)}) collective-permute-start(bf16[64,128]{1,0:T(8,128)(2,1)} %ray_ref.1), channel_id=1, source_target_pairs={{0,16},{4,20},{8,24},{12,28},{16,0},{20,4},{24,8},{28,12},{1,17},{... | collective-permute-start | bytes 49160 | tf_op jit(solution)/shard_map/ppermute | solution.py:64
  5.0 3.7 %copy-start = (bf16[1,1024,128]{2,1,0:T(8,128)(2,1)S(1)}, bf16[1,1024,128]{2,1,0:T(8,128)(2,1)}, u32[]{:S(2)}) copy-start(bf16[1,1024,128]{2,1,0:T(8,128)(2,1)} %param.14) | copy-start | bytes 786436
  6.8 3.9 %collective-permute-start.1 = (bf16[128,128]{1,0:T(8,128)(2,1)S(1)}, bf16[128,128]{1,0:T(8,128)(2,1)S(1)}, u32[]{:S(2)}, u32[]{:S(2)}) collective-permute-start(bf16[128,128]{1,0:T(8,128)(2,1)S(1)} %pad_maximum_fusion.2), channel_id=1, source_target_pairs={{0,4},{4,0},{8,12},{12,8},{16,20},{20,16},{24,28},{28,24},{1,5},{5... | collective-permute-start | bytes 98312 | tf_op jit(solution)/shard_map/ppermute | solution.py:64
  10.7 4.3 %collective-permute-start.2 = (bf16[256,128]{1,0:T(8,128)(2,1)S(1)}, bf16[256,128]{1,0:T(8,128)(2,1)S(1)}, u32[]{:S(2)}, u32[]{:S(2)}) collective-permute-start(bf16[256,128]{1,0:T(8,128)(2,1)S(1)} %constant_dynamic-update-slice_fusion.refs_0_), channel_id=1, source_target_pairs={{0,8},{4,12},{8,0},{12,4},{16,24},{20,28},{24,16},{28,20},{1,9},{5... | collective-permute-start | bytes 196616 | tf_op jit(solution)/shard_map/ppermute | solution.py:64
  17.0 4.0 %collective-permute-start.3 = (f32[4,512]{1,0:T(4,128)S(1)}, f32[4,512]{1,0:T(4,128)S(1)}, u32[]{:S(2)}, u32[]{:S(2)}) collective-permute-start(f32[4,512]{1,0:T(4,128)S(1)} %get-tuple-element.101.seg_ref.refs_0_), channel_id=1, source_target_pairs={{0,4},{4,0},{8,12},{12,8},{16,20},{20,16},{24,28},{28,24},{1,5},{5... | collective-permute-start | bytes 24584 | tf_op jit(solution)/shard_map/ppermute | solution.py:64
  21.1 3.7 %collective-permute-start.4 = (f32[4,512]{1,0:T(4,128)S(1)}, f32[4,512]{1,0:T(4,128)S(1)}, u32[]{:S(2)}, u32[]{:S(2)}) collective-permute-start(f32[4,512]{1,0:T(4,128)S(1)} %pad_maximum_fusion.3), channel_id=1, source_target_pairs={{0,8},{4,12},{8,0},{12,4},{16,24},{20,28},{24,16},{28,20},{1,9},{5... | collective-permute-start | bytes 24584 | tf_op jit(solution)/shard_map/ppermute | solution.py:64
  24.8 4.6 %collective-permute-start.5 = (f32[4,512]{1,0:T(4,128)S(1)}, f32[4,512]{1,0:T(4,128)S(1)}, u32[]{:S(2)}, u32[]{:S(2)}) collective-permute-start(f32[4,512]{1,0:T(4,128)S(1)} %pad_maximum_fusion.4), channel_id=1, source_target_pairs={{0,16},{4,20},{8,24},{12,28},{16,0},{20,4},{24,8},{28,12},{1,17},{... | collective-permute-start | bytes 24584 | tf_op jit(solution)/shard_map/ppermute | solution.py:64
  29.9 4.5 %collective-permute-start.6 = (bf16[256,128]{1,0:T(8,128)(2,1)S(1)}, bf16[256,128]{1,0:T(8,128)(2,1)S(1)}, u32[]{:S(2)}, u32[]{:S(2)}) collective-permute-start(bf16[256,128]{1,0:T(8,128)(2,1)S(1)} %get-tuple-element.125), channel_id=1, source_target_pairs={{0,8},{4,12},{8,0},{12,4},{16,24},{20,28},{24,16},{28,20},{1,9},{5... | collective-permute-start | bytes 196616 | tf_op jit(solution)/shard_map/ppermute | solution.py:64
  34.4 4.0 %collective-permute-start.7 = (bf16[128,128]{1,0:T(8,128)(2,1)S(1)}, bf16[128,128]{1,0:T(8,128)(2,1)S(1)}, u32[]{:S(2)}, u32[]{:S(2)}) collective-permute-start(bf16[128,128]{1,0:T(8,128)(2,1)S(1)} %get-tuple-element.180), channel_id=1, source_target_pairs={{0,4},{4,0},{8,12},{12,8},{16,20},{20,16},{24,28},{28,24},{1,5},{5... | collective-permute-start | bytes 98312 | tf_op jit(solution)/shard_map/ppermute | solution.py:64
  38.7 5.6 %collective-permute-start.9 = (bf16[720,128]{1,0:T(8,128)(2,1)S(1)}, bf16[720,128]{1,0:T(8,128)(2,1)S(1)}, u32[]{:S(2)}, u32[]{:S(2)}) collective-permute-start(bf16[720,128]{1,0:T(8,128)(2,1)S(1)} %pad_maximum_fusion), channel_id=1, source_target_pairs={{0,2},{1,3},{2,0},{3,1},{4,6},{5,7},{6,4},{7,5},{8,10},{9,11},{10,... | collective-permute-start | bytes 552968 | tf_op jit(solution)/shard_map/ppermute | solution.py:64
  40.2 4.6 %collective-permute-start.8 = (bf16[64,128]{1,0:T(8,128)(2,1)S(1)}, bf16[64,128]{1,0:T(8,128)(2,1)S(1)}, u32[]{:S(2)}, u32[]{:S(2)}) collective-permute-start(bf16[64,128]{1,0:T(8,128)(2,1)S(1)} %get-tuple-element.156), channel_id=1, source_target_pairs={{0,16},{4,20},{8,24},{12,28},{16,0},{20,4},{24,8},{28,12},{1,17},{... | collective-permute-start | bytes 49160 | tf_op jit(solution)/shard_map/ppermute | solution.py:64
  44.3 1.4 %collective-permute-start.10 = (bf16[464,128]{1,0:T(8,128)(2,1)S(1)}, bf16[464,128]{1,0:T(8,128)(2,1)S(1)}, u32[]{:S(2)}, u32[]{:S(2)}) collective-permute-start(bf16[464,128]{1,0:T(8,128)(2,1)S(1)} %pad_maximum_fusion.1.sent_ref), channel_id=1, source_target_pairs={{0,1},{1,0},{2,3},{3,2},{4,5},{5,4},{6,7},{7,6},{8,9},{9,8},{10,11... | collective-permute-start | bytes 356360 | tf_op jit(solution)/shard_map/ppermute | solution.py:64

commit v7 on v6

--- a/solution.py
+++ b/solution.py
@@ -11,7 +11,6 @@
 f32 = jnp.float32
 bf16 = jnp.bfloat16
 vmem_bytes = 24 * 1024 * 1024
-exact = lax.Precision.HIGHEST
 
 
 def bits_of(count):
@@ -42,12 +41,6 @@
     for b in reversed(halving_bits(owners)):
         order = order + [t ^ (1 << b) for t in order]
     return order
-
-
-def split_dot(a, b, dot):
-    high = a.astype(bf16)
-    low = (a - high.astype(f32)).astype(bf16)
-    return dot(high, b) + dot(low, b)
 
 
 def nt_dot(a, b, precision=None):
@@ -223,33 +216,31 @@
             ut_ref[:, k * half + n * chunk : k * half + (n + 1) * chunk] = part.astype(bf16)
     b_out = [lines_ref[lines["b_out"], c] for c in range(outs)]
 
-    def shade_block(block, carry):
-        for n in range(slots * half // 256):
-            lanes = slice(n * 256, n * 256 + 256)
-            ut = ut_ref[:, lanes]
+    def shade(n):
+        ut = [ut_ref[:, k * half + n * chunk : k * half + (n + 1) * chunk] for k in range(slots)]
+        ut = jnp.concatenate(ut, 1)
+        for block in range(samples // 8):
             acc = None
             for i in range(4):
                 parts = []
                 for h in range(2):
                     column = wide_ref[block * 8 + 2 * i + h]
-                    column = jnp.concatenate([column, column], 1)
+                    column = jnp.concatenate([column] * slots, 1)
                     parts.append(jnp.maximum(ut + column, 0))
                 left = left_ref[:, 2 * i * width : 2 * (i + 1) * width]
                 term = nn_dot(left, jnp.concatenate(parts, 0))
                 acc = term if acc is None else acc + term
             for c in range(outs):
-                raw_ref[c, pl.ds(pl.multiple_of(block * 8, 8), 8), lanes] = (
-                    acc[c * 8 : c * 8 + 8, :] + b_out[c]
-                )
-        return carry
-
-    lax.fori_loop(0, samples // 8, shade_block, 0, unroll=8)
+                raw_ref[c, n, block * 8 : block * 8 + 8, :] = acc[c * 8 : c * 8 + 8, :] + b_out[c]
+
+    for n in range(half // chunk):
+        shade(n)
     earlier = earlier_ref[...]
     occ_row = lines["occ"]
     for n in range(half // chunk):
         occ = lines_ref[occ_row : occ_row + 1, whole(n, 0, side)]
         raws = [
-            raw_ref[0, :, k * half + n * chunk : k * half + (n + 1) * chunk] for k in range(slots)
+            raw_ref[0, n, :, k * chunk : (k + 1) * chunk] for k in range(slots)
         ]
         occupied = [(k < occ).astype(f32) for k in range(slots)]
         opticals = [
@@ -267,7 +258,7 @@
             tanh = jnp.tanh(0.5 * optical)
             weight = jnp.exp(-entered) * (2.0 * tanh / (1.0 + tanh))
             for c in range(outs - 1):
-                shading = jax.nn.sigmoid(raw_ref[c + 1, :, local])
+                shading = jax.nn.sigmoid(raw_ref[c + 1, n, :, k * chunk : (k + 1) * chunk])
                 light = weight * shading
                 colors[c] = colors[c] + jnp.sum(light, 0, keepdims=True)
                 kept_ref[c, :, local] = shading
@@ -596,10 +587,6 @@
     w_grad_ref[...] = nn_dot(inputs_ref[...], slot_ref[...])
 
 
-def flipped(a, b):
-    return nn_dot(b, a)
-
-
 def network_kernel(*refs, parts, rows):
     part_refs, refs = refs[: 3 * parts], refs[3 * parts :]
     w_grad_ref, sums_ref, low_ref, small_ref = refs
@@ -607,12 +594,11 @@
     samples, width = by_sample.shape
     outs = sums_ref.shape[0]
     w = low_ref[rows["w"], :]
-    sample = low_ref[rows["sample"], :].astype(f32)
+    sample = low_ref[rows["sample"], :]
     sample_t = jnp.concatenate([sample] * (128 // samples), 0).T[:, :samples]
-    small_ref[:samples, :] = split_dot(by_sample, w, nt_dot)
-    small_ref[samples : samples + width, :] = w_grad_ref[...] + split_dot(
-        by_sample, sample_t.astype(bf16), flipped
-    )
+    rounded = by_sample.astype(bf16)
+    small_ref[:samples, :] = nt_dot(rounded, w)
+    small_ref[samples : samples + width, :] = w_grad_ref[...] + nn_dot(sample_t, rounded)
     at = samples + width
     small_ref[at : at + 1, :] = jnp.sum(by_sample, 0, keepdims=True)
     lane128 = lax.broadcasted_iota(jnp.int32, (1, 128), 1)
@@ -765,7 +751,7 @@
             "forward",
             scratch=(
                 pltpu.VMEM((rays // 2, width), bf16),
-                pltpu.VMEM((outs, samples, total // 2), f32),
+                pltpu.VMEM((outs, rays // 256, samples, slots * 128), f32),
             ),
             flops=1 << 30,
         )(part, project, w_t, wide, left, packed, earlier, *passes)

time: 46.6 us -> 46.6 us (level)
  no operation moved by 1% of the time
where the time goes in v7:
time: 46.6 us; the launch traced here: 46.4 us
  starting transfers between devices  21.7 us (47%)
  Pallas kernels  18.2 us (39%)
  waiting for transfers between devices  5.24 us (11%)
  between operations  1.03 us (2%)
    ppermute x11, starting transfers between devices, swap(): return lax.ppermute(array, axis, [(i, i ^ distance) for i in range(size)])  21.7 us
    pallas_call x19, Pallas kernels, run(): pl.pallas_call(kernel, out_shape=out_shape, in_specs=[pl.BlockSpec(memory...  18.2 us
    ppermute x11, waiting for transfers between devices, swap(): return lax.ppermute(array, axis, [(i, i ^ distance) for i in range(size)])  5.24 us
  transfers between devices with their start and end apart: 11, of which 8 were waited for; matrix products, arithmetic and copies ran while one was open for 0% of the time, Pallas kernels for 32%

profile of v7, /device:TPU:0, one launch (start us, length us, event | category | flops | bytes accessed | tf_op | source)
XLA Modules:
  0.0 46.4 jit_solution(11297204594516180297)
XLA Ops:
  0.7 4.1 %collective-permute-start = (bf16[64,128]{1,0:T(8,128)(2,1)}, bf16[64,128]{1,0:T(8,128)(2,1)S(1)}, u32[]{:S(2)}, u32[]{:S(2)}) collective-permute-start(bf16[64,128]{1,0:T(8,128)(2,1)} %ray_ref.1), channel_id=1, source_target_pairs={{0,16},{4,20},{8,24},{12,28},{16,0},{20,4},{24,8},{28,12},{1,17},{... | collective-permute-start | bytes 49160 | tf_op jit(solution)/shard_map/ppermute | solution.py:57
  5.0 1.0 %prepare.1 = (bf16[64,128]{1,0:T(8,128)(2,1)S(1)}, bf16[208,128]{1,0:T(8,128)(2,1)S(1)}, f32[8,512]{1,0:T(8,128)S(1)}, bf16[128,128]{1,0:T(8,128)(2,1)S(1)}, f32...) custom-call(bf16[64,128]{1,0:T(8,128)(2,1)S(1)} %copy-done.3, ...), custom_call_target="tpu_custom_call" | custom-call | flops 2147483648 | bytes 1024 | tf_op jit(solution)/shard_map/prepare/pallas_call | solution.py:68
  6.0 0.8 %collective-permute-done = bf16[64,128]{1,0:T(8,128)(2,1)S(1)} collective-permute-done((bf16[64,128]{1,0:T(8,128)(2,1)}, bf16[64,128]{1,0:T(8,128)(2,1)S(1)}, u32[]{:S(2)}, u32[]{:S(2)}) %collective-permute-start) | collective-permute-done | bytes 16416 | tf_op jit(solution)/shard_map/ppermute | solution.py:57
  6.8 1.9 %collective-permute-start.1 = (bf16[128,128]{1,0:T(8,128)(2,1)S(1)}, bf16[128,128]{1,0:T(8,128)(2,1)S(1)}, u32[]{:S(2)}, u32[]{:S(2)}) collective-permute-start(bf16[128,128]{1,0:T(8,128)(2,1)S(1)} %pad_maximum_fusion.2), channel_id=1, source_target_pairs={{0,4},{4,0},{8,12},{12,8},{16,20},{20,16},{24,28},{28,24},{1,5},{5... | collective-permute-start | bytes 98312 | tf_op jit(solution)/shard_map/ppermute | solution.py:57
  8.7 0.8 %chosen.1 = (bf16[128,1024]{1,0:T(8,128)(2,1)S(1)}, f32[128,1024]{1,0:T(8,128)S(1)}) custom-call(f32[8,512]{1,0:T(8,128)S(1)} %get-tuple-element.93.lines_ref.refs_5_.refs_7_, bf16[1024,128]{1,0:T(8,128)(2,1)S(1)} %bitcast.14, bf16[128,128]{1,0:T(8,128)(2,1)S(1)} %get-tuple-element.94.w_t_ref.refs_2_), custom_call_target="tpu_custom_call" | custom-call | flops 536870912 | bytes 1024 | tf_op jit(solution)/shard_map/chosen/pallas_call | solution.py:68
  9.5 1.2 %collective-permute-done.1 = bf16[128,128]{1,0:T(8,128)(2,1)S(1)} collective-permute-done((bf16[128,128]{1,0:T(8,128)(2,1)S(1)}, bf16[128,128]{1,0:T(8,128)(2,1)S(1)}, u32[]{:S(2)}, u32[]{:S(2)}) %collective-permute-start.1) | collective-permute-done | bytes 32800 | tf_op jit(solution)/shard_map/ppermute | solution.py:57
  10.7 1.9 %collective-permute-start.2 = (bf16[256,128]{1,0:T(8,128)(2,1)S(1)}, bf16[256,128]{1,0:T(8,128)(2,1)S(1)}, u32[]{:S(2)}, u32[]{:S(2)}) collective-permute-start(bf16[256,128]{1,0:T(8,128)(2,1)S(1)} %constant_dynamic-update-slice_fusion.refs_0_), channel_id=1, source_target_pairs={{0,8},{4,12},{8,0},{12,4},{16,24},{20,28},{24,16},{28,20},{1,9},{5... | collective-permute-start | bytes 196616 | tf_op jit(solution)/shard_map/ppermute | solution.py:57
  12.6 2.0 %forward.2 = (f32[4,256]{1,0:T(4,128)S(1)}, f32[8,64,512]{2,1,0:T(8,128)S(1)}, bf16[128,512]{1,0:T(8,128)(2,1)S(1)}, bf16[256,128]{1,0:T(8,128)(2,1)S(1)}) custom-call(bf16[256,128]{1,0:T(8,128)(2,1)S(1)} %constant_dynamic-update-slice_fusion.refs_0_, f32[128,1024]{1,0:T(8,128)S(1)} %get-tuple-element.95.refs_1_, ...), custom_call_target="tpu_custom_call" | custom-call | flops 1073741824 | bytes 1024 | tf_op jit(solution)/shard_map/forward/pallas_call | solution.py:68
  15.0 2.0 %forward.3 = (f32[4,512]{1,0:T(4,128)S(1)}, f32[8,64,512]{2,1,0:T(8,128)S(1)}, bf16[128,512]{1,0:T(8,128)(2,1)S(1)}, bf16[512,128]{1,0:T(8,128)(2,1)S(1)}) custom-call(bf16[256,128]{1,0:T(8,128)(2,1)S(1)} %collective-permute-done.2.refs_0_, f32[128,1024]{1,0:T(8,128)S(1)} %get-tuple-element.95.refs_1_, ...), custom_call_target="tpu_custom_call" | custom-call | flops 1073741824 | bytes 1024 | tf_op jit(solution)/shard_map/forward/pallas_call | solution.py:68
  16.9 2.0 %collective-permute-start.3 = (f32[4,512]{1,0:T(4,128)S(1)}, f32[4,512]{1,0:T(4,128)S(1)}, u32[]{:S(2)}, u32[]{:S(2)}) collective-permute-start(f32[4,512]{1,0:T(4,128)S(1)} %get-tuple-element.101.seg_ref.refs_0_), channel_id=1, source_target_pairs={{0,4},{4,0},{8,12},{12,8},{16,20},{20,16},{24,28},{28,24},{1,5},{5... | collective-permute-start | bytes 24584 | tf_op jit(solution)/shard_map/ppermute | solution.py:57
  18.9 0.8 %coefficients.1 = (f32[7,64,1024]{2,1,0:T(8,128)S(1)}, bf16[7,1024,128]{2,1,0:T(8,128)(2,1)S(1)}, bf16[1024,128]{1,0:T(8,128)(2,1)S(1)}) custom-call(f32[4,512]{1,0:T(4,128)S(1)} %get-tuple-element.101.seg_ref.refs_0_, f32[8,64,512]{2,1,0:T(8,128)S(1)} %get-tuple-element.102.first_ref, f32[8,64,512]{2,1,0:T(8,128)S(1)} %get-tuple-element.103.second_ref, ...), custom_call_target="tpu_custom_call" | custom-call | flops 1073741824 | bytes 1024 | tf_op jit(solution)/shard_map/coefficients/pallas_call | solution.py:68
  19.7 1.3 %basis.3 = (f32[7,256,128]{2,1,0:T(8,128)S(1)}, f32[4,256,128]{2,1,0:T(8,128)S(1)}) custom-call(bf16[7,1024,128]{2,1,0:T(8,128)(2,1)S(1)} %get-tuple-element.116.turned_ref, bf16[1024,128]{1,0:T(8,128)(2,1)S(1)} %get-tuple-element.118.u_ref.refs_7_, f32[64,128]{1,0:T(8,128)S(1)} %get-tuple-element.119.s_ref, ...), custom_call_target="tpu_custom_call" | custom-call | flops 536870912 | bytes 1024 | tf_op jit(solution)/shard_map/basis/pallas_call | solution.py:68
  21.0 1.6 %collective-permute-start.4 = (f32[4,512]{1,0:T(4,128)S(1)}, f32[4,512]{1,0:T(4,128)S(1)}, u32[]{:S(2)}, u32[]{:S(2)}) collective-permute-start(f32[4,512]{1,0:T(4,128)S(1)} %pad_maximum_fusion.3), channel_id=1, source_target_pairs={{0,8},{4,12},{8,0},{12,4},{16,24},{20,28},{24,16},{28,20},{1,9},{5... | collective-permute-start | bytes 24584 | tf_op jit(solution)/shard_map/ppermute | solution.py:57
  22.7 1.6 %basis.4 = (f32[7,384,128]{2,1,0:T(8,128)S(1)}, f32[4,384,128]{2,1,0:T(8,128)S(1)}) custom-call(bf16[7,1024,128]{2,1,0:T(8,128)(2,1)S(1)} %get-tuple-element.116.turned_ref, bf16[1024,128]{1,0:T(8,128)(2,1)S(1)} %get-tuple-element.118.u_ref.refs_7_, f32[64,128]{1,0:T(8,128)S(1)} %get-tuple-element.119.s_ref, ...), custom_call_target="tpu_custom_call" | custom-call | flops 536870912 | bytes 1024 | tf_op jit(solution)/shard_map/basis/pallas_call | solution.py:68
  24.8 2.7 %collective-permute-start.5 = (f32[4,512]{1,0:T(4,128)S(1)}, f32[4,512]{1,0:T(4,128)S(1)}, u32[]{:S(2)}, u32[]{:S(2)}) collective-permute-start(f32[4,512]{1,0:T(4,128)S(1)} %pad_maximum_fusion.4), channel_id=1, source_target_pairs={{0,16},{4,20},{8,24},{12,28},{16,0},{20,4},{24,8},{28,12},{1,17},{... | collective-permute-start | bytes 24584 | tf_op jit(solution)/shard_map/ppermute | solution.py:57
  27.5 1.6 %basis.5 = (f32[7,384,128]{2,1,0:T(8,128)S(1)}, f32[4,384,128]{2,1,0:T(8,128)S(1)}) custom-call(bf16[7,1024,128]{2,1,0:T(8,128)(2,1)S(1)} %get-tuple-element.116.turned_ref, bf16[1024,128]{1,0:T(8,128)(2,1)S(1)} %get-tuple-element.118.u_ref.refs_7_, f32[64,128]{1,0:T(8,128)S(1)} %get-tuple-element.119.s_ref, ...), custom_call_target="tpu_custom_call" | custom-call | flops 536870912 | bytes 1024 | tf_op jit(solution)/shard_map/basis/pallas_call | solution.py:68
  29.9 1.6 %collective-permute-start.6 = (bf16[256,128]{1,0:T(8,128)(2,1)S(1)}, bf16[256,128]{1,0:T(8,128)(2,1)S(1)}, u32[]{:S(2)}, u32[]{:S(2)}) collective-permute-start(bf16[256,128]{1,0:T(8,128)(2,1)S(1)} %get-tuple-element.125), channel_id=1, source_target_pairs={{0,8},{4,12},{8,0},{12,4},{16,24},{20,28},{24,16},{28,20},{1,9},{5... | collective-permute-start | bytes 196616 | tf_op jit(solution)/shard_map/ppermute | solution.py:57
  31.5 1.9 %by_sample.2 = (f32[32,128]{1,0:T(8,128)S(1)}, f32[4,8,128]{2,1,0:T(8,128)S(1)}, f32[4,128]{1,0:T(4,128)S(1)}) custom-call(f32[8,512]{1,0:T(8,128)S(1)} %get-tuple-element.138.cot_ref, f32[7,64,1024]{2,1,0:T(8,128)S(1)} %get-tuple-element.133.coef_ref, bf16[1024,128]{1,0:T(8,128)(2,1)S(1)} %get-tuple-element.118.u_ref.refs_7_, ...), custom_call_target="tpu_custom_call" | custom-call | flops 1048576 | bytes 1024 | tf_op jit(solution)/shard_map/by_sample/pallas_call | solution.py:68
  33.4 0.9 %slots.1 = (bf16[1024,128]{1,0:T(8,128)(2,1)S(1)}, f32[128,128]{1,0:T(8,128)S(1)}, f32[4,8,128]{2,1,0:T(8,128)S(1)}) custom-call(f32[7,256,128]{2,1,0:T(8,128)S(1)} %get-tuple-element.127.refs_0_, f32[7,384,128]{2,1,0:T(8,128)S(1)} %get-tuple-element.128.refs_1_, f32[7,384,128]{2,1,0:T(8,128)S(1)} %get-tuple-element.129.refs_2_, ...), custom_call_target="tpu_custom_call" | custom-call | flops 1048576 | bytes 1024 | tf_op jit(solution)/shard_map/slots/pallas_call | solution.py:68
  34.4 1.6 %collective-permute-start.7 = (bf16[128,128]{1,0:T(8,128)(2,1)S(1)}, bf16[128,128]{1,0:T(8,128)(2,1)S(1)}, u32[]{:S(2)}, u32[]{:S(2)}) collective-permute-start(bf16[128,128]{1,0:T(8,128)(2,1)S(1)} %get-tuple-element.180), channel_id=1, source_target_pairs={{0,4},{4,0},{8,12},{12,8},{16,20},{20,16},{24,28},{28,24},{1,5},{5... | collective-permute-start | bytes 98312 | tf_op jit(solution)/shard_map/ppermute | solution.py:57
  36.4 1.9 %by_sample.3 = (f32[32,128]{1,0:T(8,128)S(1)}, f32[4,8,128]{2,1,0:T(8,128)S(1)}, f32[4,128]{1,0:T(4,128)S(1)}) custom-call(f32[8,512]{1,0:T(8,128)S(1)} %get-tuple-element.138.cot_ref, f32[7,64,1024]{2,1,0:T(8,128)S(1)} %get-tuple-element.133.coef_ref, bf16[1024,128]{1,0:T(8,128)(2,1)S(1)} %get-tuple-element.118.u_ref.refs_7_, ...), custom_call_target="tpu_custom_call" | custom-call | flops 1048576 | bytes 1024 | tf_op jit(solution)/shard_map/by_sample/pallas_call | solution.py:68
  38.6 1.6 %collective-permute-start.9 = (bf16[720,128]{1,0:T(8,128)(2,1)S(1)}, bf16[720,128]{1,0:T(8,128)(2,1)S(1)}, u32[]{:S(2)}, u32[]{:S(2)}) collective-permute-start(bf16[720,128]{1,0:T(8,128)(2,1)S(1)} %pad_maximum_fusion), channel_id=1, source_target_pairs={{0,2},{1,3},{2,0},{3,1},{4,6},{5,7},{6,4},{7,5},{8,10},{9,11},{10,... | collective-permute-start | bytes 552968 | tf_op jit(solution)/shard_map/ppermute | solution.py:57
  40.1 2.7 %collective-permute-start.8 = (bf16[64,128]{1,0:T(8,128)(2,1)S(1)}, bf16[64,128]{1,0:T(8,128)(2,1)S(1)}, u32[]{:S(2)}, u32[]{:S(2)}) collective-permute-start(bf16[64,128]{1,0:T(8,128)(2,1)S(1)} %get-tuple-element.156), channel_id=1, source_target_pairs={{0,16},{4,20},{8,24},{12,28},{16,0},{20,4},{24,8},{28,12},{1,17},{... | collective-permute-start | bytes 49160 | tf_op jit(solution)/shard_map/ppermute | solution.py:57
  43.2 1.0 %collective-permute-done.9 = bf16[720,128]{1,0:T(8,128)(2,1)S(1)} collective-permute-done((bf16[720,128]{1,0:T(8,128)(2,1)S(1)}, bf16[720,128]{1,0:T(8,128)(2,1)S(1)}, u32[]{:S(2)}, u32[]{:S(2)}) %collective-permute-start.9) | collective-permute-done | bytes 184352 | tf_op jit(solution)/shard_map/ppermute | solution.py:57
  (57 shorter events, 5.2 us)
Async XLA Ops:
  0.6 4.2 %copy-start.3 = (bf16[64,128]{1,0:T(8,128)(2,1)S(1)}, bf16[64,128]{1,0:T(8,128)(2,1)}, u32[]{:S(2)}) copy-start(bf16[64,128]{1,0:T(8,128)(2,1)} %ray_ref.1) | copy-start | bytes 49156
  0.6 4.2 %copy-start.6 = (s32[1,512]{1,0:T(1,128)S(1)}, s32[1,512]{1,0:T(1,128)}, u32[]{:S(2)}) copy-start(s32[1,512]{1,0:T(1,128)} %occ_ref.1) | copy-start | bytes 6148
  0.7 4.2 %copy-start.5 = (s32[1,2,512]{2,1,0:T(2,128)S(1)}, s32[1,2,512]{2,1,0:T(2,128)}, u32[]{:S(2)}) copy-start(s32[1,2,512]{2,1,0:T(2,128)} %param.20) | copy-start | bytes 12292
  0.7 4.2 %copy-start.10 = (f32[1,4]{1,0:T(1,128)S(1)}, f32[1,4]{1,0:T(1,128)}, u32[]{:S(2)}) copy-start(f32[1,4]{1,0:T(1,128)} %b_out_ref.1) | copy-start | bytes 52
  0.7 4.2 %copy-start.8 = (bf16[1,4,128]{2,1,0:T(4,128)(2,1)S(1)}, bf16[1,4,128]{2,1,0:T(4,128)(2,1)}, u32[]{:S(2)}) copy-start(bf16[1,4,128]{2,1,0:T(4,128)(2,1)} %param.18) | copy-start | bytes 3076
  0.7 4.2 %copy-start.9 = (f32[1,128]{1,0:T(1,128)S(1)}, f32[1,128]{1,0:T(1,128)}, u32[]{:S(2)}) copy-start(f32[1,128]{1,0:T(1,128)} %b_ref.1) | copy-start | bytes 1540
  0.7 4.2 %copy-start.1 = (bf16[1,128,128]{2,1,0:T(8,128)(2,1)S(1)}, bf16[1,128,128]{2,1,0:T(8,128)(2,1)}, u32[]{:S(2)}) copy-start(bf16[1,128,128]{2,1,0:T(8,128)(2,1)} %param.16) | copy-start | bytes 98308
  0.7 4.2 %copy-start.2 = (bf16[1,64,128]{2,1,0:T(8,128)(2,1)S(1)}, bf16[1,64,128]{2,1,0:T(8,128)(2,1)}, u32[]{:S(2)}) copy-start(bf16[1,64,128]{2,1,0:T(8,128)(2,1)} %param.15) | copy-start | bytes 49156
  0.7 4.2 %copy-start.4 = (f32[3,512]{1,0:T(4,128)S(1)}, f32[3,512]{1,0:T(4,128)}, u32[]{:S(2)}) copy-start(f32[3,512]{1,0:T(4,128)} %target_ref.1) | copy-start | bytes 18436
  0.7 4.2 %copy-start.7 = (s32[512]{0:T(512)S(1)}, s32[512]{0:T(512)}, u32[]{:S(2)}) copy-start(s32[512]{0:T(512)} %param.12) | copy-start | bytes 6148
  0.7 6.0 %collective-permute-start = (bf16[64,128]{1,0:T(8,128)(2,1)}, bf16[64,128]{1,0:T(8,128)(2,1)S(1)}, u32[]{:S(2)}, u32[]{:S(2)}) collective-permute-start(bf16[64,128]{1,0:T(8,128)(2,1)} %ray_ref.1), channel_id=1, source_target_pairs={{0,16},{4,20},{8,24},{12,28},{16,0},{20,4},{24,8},{28,12},{1,17},{... | collective-permute-start | bytes 49160 | tf_op jit(solution)/shard_map/ppermute | solution.py:57
  5.0 3.7 %copy-start = (bf16[1,1024,128]{2,1,0:T(8,128)(2,1)S(1)}, bf16[1,1024,128]{2,1,0:T(8,128)(2,1)}, u32[]{:S(2)}) copy-start(bf16[1,1024,128]{2,1,0:T(8,128)(2,1)} %param.14) | copy-start | bytes 786436
  6.8 3.9 %collective-permute-start.1 = (bf16[128,128]{1,0:T(8,128)(2,1)S(1)}, bf16[128,128]{1,0:T(8,128)(2,1)S(1)}, u32[]{:S(2)}, u32[]{:S(2)}) collective-permute-start(bf16[128,128]{1,0:T(8,128)(2,1)S(1)} %pad_maximum_fusion.2), channel_id=1, source_target_pairs={{0,4},{4,0},{8,12},{12,8},{16,20},{20,16},{24,28},{28,24},{1,5},{5... | collective-permute-start | bytes 98312 | tf_op jit(solution)/shard_map/ppermute | solution.py:57
  10.7 4.3 %collective-permute-start.2 = (bf16[256,128]{1,0:T(8,128)(2,1)S(1)}, bf16[256,128]{1,0:T(8,128)(2,1)S(1)}, u32[]{:S(2)}, u32[]{:S(2)}) collective-permute-start(bf16[256,128]{1,0:T(8,128)(2,1)S(1)} %constant_dynamic-update-slice_fusion.refs_0_), channel_id=1, source_target_pairs={{0,8},{4,12},{8,0},{12,4},{16,24},{20,28},{24,16},{28,20},{1,9},{5... | collective-permute-start | bytes 196616 | tf_op jit(solution)/shard_map/ppermute | solution.py:57
  16.9 4.0 %collective-permute-start.3 = (f32[4,512]{1,0:T(4,128)S(1)}, f32[4,512]{1,0:T(4,128)S(1)}, u32[]{:S(2)}, u32[]{:S(2)}) collective-permute-start(f32[4,512]{1,0:T(4,128)S(1)} %get-tuple-element.101.seg_ref.refs_0_), channel_id=1, source_target_pairs={{0,4},{4,0},{8,12},{12,8},{16,20},{20,16},{24,28},{28,24},{1,5},{5... | collective-permute-start | bytes 24584 | tf_op jit(solution)/shard_map/ppermute | solution.py:57
  21.0 3.7 %collective-permute-start.4 = (f32[4,512]{1,0:T(4,128)S(1)}, f32[4,512]{1,0:T(4,128)S(1)}, u32[]{:S(2)}, u32[]{:S(2)}) collective-permute-start(f32[4,512]{1,0:T(4,128)S(1)} %pad_maximum_fusion.3), channel_id=1, source_target_pairs={{0,8},{4,12},{8,0},{12,4},{16,24},{20,28},{24,16},{28,20},{1,9},{5... | collective-permute-start | bytes 24584 | tf_op jit(solution)/shard_map/ppermute | solution.py:57
  24.8 4.6 %collective-permute-start.5 = (f32[4,512]{1,0:T(4,128)S(1)}, f32[4,512]{1,0:T(4,128)S(1)}, u32[]{:S(2)}, u32[]{:S(2)}) collective-permute-start(f32[4,512]{1,0:T(4,128)S(1)} %pad_maximum_fusion.4), channel_id=1, source_target_pairs={{0,16},{4,20},{8,24},{12,28},{16,0},{20,4},{24,8},{28,12},{1,17},{... | collective-permute-start | bytes 24584 | tf_op jit(solution)/shard_map/ppermute | solution.py:57
  29.9 4.5 %collective-permute-start.6 = (bf16[256,128]{1,0:T(8,128)(2,1)S(1)}, bf16[256,128]{1,0:T(8,128)(2,1)S(1)}, u32[]{:S(2)}, u32[]{:S(2)}) collective-permute-start(bf16[256,128]{1,0:T(8,128)(2,1)S(1)} %get-tuple-element.125), channel_id=1, source_target_pairs={{0,8},{4,12},{8,0},{12,4},{16,24},{20,28},{24,16},{28,20},{1,9},{5... | collective-permute-start | bytes 196616 | tf_op jit(solution)/shard_map/ppermute | solution.py:57
  34.4 4.0 %collective-permute-start.7 = (bf16[128,128]{1,0:T(8,128)(2,1)S(1)}, bf16[128,128]{1,0:T(8,128)(2,1)S(1)}, u32[]{:S(2)}, u32[]{:S(2)}) collective-permute-start(bf16[128,128]{1,0:T(8,128)(2,1)S(1)} %get-tuple-element.180), channel_id=1, source_target_pairs={{0,4},{4,0},{8,12},{12,8},{16,20},{20,16},{24,28},{28,24},{1,5},{5... | collective-permute-start | bytes 98312 | tf_op jit(solution)/shard_map/ppermute | solution.py:57
  38.6 5.6 %collective-permute-start.9 = (bf16[720,128]{1,0:T(8,128)(2,1)S(1)}, bf16[720,128]{1,0:T(8,128)(2,1)S(1)}, u32[]{:S(2)}, u32[]{:S(2)}) collective-permute-start(bf16[720,128]{1,0:T(8,128)(2,1)S(1)} %pad_maximum_fusion), channel_id=1, source_target_pairs={{0,2},{1,3},{2,0},{3,1},{4,6},{5,7},{6,4},{7,5},{8,10},{9,11},{10,... | collective-permute-start | bytes 552968 | tf_op jit(solution)/shard_map/ppermute | solution.py:57
  40.1 4.6 %collective-permute-start.8 = (bf16[64,128]{1,0:T(8,128)(2,1)S(1)}, bf16[64,128]{1,0:T(8,128)(2,1)S(1)}, u32[]{:S(2)}, u32[]{:S(2)}) collective-permute-start(bf16[64,128]{1,0:T(8,128)(2,1)S(1)} %get-tuple-element.156), channel_id=1, source_target_pairs={{0,16},{4,20},{8,24},{12,28},{16,0},{20,4},{24,8},{28,12},{1,17},{... | collective-permute-start | bytes 49160 | tf_op jit(solution)/shard_map/ppermute | solution.py:57
  44.3 1.4 %collective-permute-start.10 = (bf16[464,128]{1,0:T(8,128)(2,1)S(1)}, bf16[464,128]{1,0:T(8,128)(2,1)S(1)}, u32[]{:S(2)}, u32[]{:S(2)}) collective-permute-start(bf16[464,128]{1,0:T(8,128)(2,1)S(1)} %pad_maximum_fusion.1.sent_ref), channel_id=1, source_target_pairs={{0,1},{1,0},{2,3},{3,2},{4,5},{5,4},{6,7},{7,6},{8,9},{9,8},{10,11... | collective-permute-start | bytes 356360 | tf_op jit(solution)/shard_map/ppermute | solution.py:57

commit v8 on v7

--- a/solution.py
+++ b/solution.py
@@ -400,18 +400,32 @@
     return jnp.where(forward, fc + ft * sc, sc + st * fc), ft * st
 
 
-def middle_kernel(*refs, owners, pieces, lines):
+def pair_kernel(*refs):
+    basis_refs, out_ref = refs[:-1], refs[-1]
+    outs, rays, width = out_ref.shape
+    total = sum(ref.shape[1] for ref in basis_refs)
+    chunk = 128
+    for n in range(rays // chunk):
+        for c in range(outs):
+            whole = None
+            for k in range(total // rays):
+                ref, at = basis_part(basis_refs, k * rays + n * chunk)
+                part = ref[c, at : at + chunk, :]
+                whole = part if whole is None else whole + part
+            out_ref[c, n * chunk : (n + 1) * chunk, :] = whole
+
+
+def middle_kernel(*refs, owners, lines):
     bits = bits_of(owners)
     seg_ref, refs = refs[0], refs[1:]
     got_refs, refs = refs[:bits], refs[bits:]
-    moved_refs, refs = refs[:pieces], refs[pieces:]
+    paired_ref, refs = refs[0], refs[1:]
     lines_ref, keep_ref, send_ref, cot_ref, spread_ref, ray_ref = refs
     me = lax.axis_index("slab")
     outs = seg_ref.shape[0]
     channels = outs - 1
     rays = lines_ref.shape[1]
-    width = moved_refs[0].shape[2]
-    slots = sum(ref.shape[1] for ref in moved_refs) // rays
+    width = paired_ref.shape[2]
     forward = lines_ref[lines["direction"] : lines["direction"] + 1, :] == 0.0
     target = lines_ref[lines["target"] : lines["target"] + channels, :]
 
@@ -453,11 +467,7 @@
         spread_ref[these, :] = nn_dot(values[:, these].T.astype(bf16), spread)
         grad = None
         for c in range(outs):
-            whole = None
-            for k in range(slots):
-                ref, at = basis_part(moved_refs, k * rays + n * chunk)
-                part = ref[c, at : at + chunk, :]
-                whole = part if whole is None else whole + part
+            whole = paired_ref[c, these, :]
             term = spread_ref[these, c * width : (c + 1) * width] * whole
             grad = term if grad is None else grad + term
         ray_ref[these, :] = grad
@@ -795,7 +805,10 @@
             inputs = call(inputs_kernel, shaped16(width, total), "inputs", flops=1 << 20)(
                 chosen_later, ray_sorted
             )
-            other, inputs = lax.optimization_barrier((other, inputs))
+            paired = call(pair_kernel, shaped(outs, rays, width), "paired", flops=1 << 20)(
+                *[moved for _, moved in basis]
+            )
+            other, inputs, paired = lax.optimization_barrier((other, inputs, paired))
         other, turned_later, chosen_later = lax.optimization_barrier(
             (other, turned_later, chosen_later)
         )
@@ -808,7 +821,7 @@
 
     h1, moved_basis = zip(*basis)
     ray_keep, ray_send, cots, spread = call(
-        functools.partial(middle_kernel, owners=owners, pieces=pieces, lines=lines),
+        functools.partial(middle_kernel, owners=owners, lines=lines),
         (
             shaped(rays // 2, width),
             shaped16(rays // 2, width),
@@ -818,7 +831,7 @@
         "middle",
         scratch=(pltpu.VMEM((rays, width), f32),),
         flops=1 << 29,
-    )(seg, *received, *moved_basis, packed)
+    )(seg, *received, paired, packed)
     moved, w_grad, sums = call(
         functools.partial(slots_kernel, pieces=pieces, rows=rows),
         (

time: 46.6 us -> 46.6 us (level)
    pallas_call x19 -> x20, Pallas kernels: 18.2 us -> 18.3 us  [run(): pl.pallas_call(kernel, out_shape=out_shape, in_specs=[pl.BlockSpec(memory...]
where the time goes in v8:
time: 46.6 us; the launch traced here: 46.4 us
  starting transfers between devices  21.7 us (47%)
  Pallas kernels  18.3 us (39%)
  waiting for transfers between devices  5.09 us (11%)
  between operations  1.03 us (2%)
    ppermute x11, starting transfers between devices, swap(): return lax.ppermute(array, axis, [(i, i ^ distance) for i in range(size)])  21.7 us
    pallas_call x20, Pallas kernels, run(): pl.pallas_call(kernel, out_shape=out_shape, in_specs=[pl.BlockSpec(memory...  18.3 us
    ppermute x11, waiting for transfers between devices, swap(): return lax.ppermute(array, axis, [(i, i ^ distance) for i in range(size)])  5.09 us
  transfers between devices with their start and end apart: 11, of which 8 were waited for; matrix products, arithmetic and copies ran while one was open for 0% of the time, Pallas kernels for 32%

profile of v8, /device:TPU:0, one launch (start us, length us, event | category | flops | bytes accessed | tf_op | source)
XLA Modules:
  0.0 46.4 jit_solution(14910911940349024407)
XLA Ops:
  0.7 4.1 %collective-permute-start = (bf16[64,128]{1,0:T(8,128)(2,1)}, bf16[64,128]{1,0:T(8,128)(2,1)S(1)}, u32[]{:S(2)}, u32[]{:S(2)}) collective-permute-start(bf16[64,128]{1,0:T(8,128)(2,1)} %ray_ref.1), channel_id=1, source_target_pairs={{0,16},{4,20},{8,24},{12,28},{16,0},{20,4},{24,8},{28,12},{1,17},{... | collective-permute-start | bytes 49160 | tf_op jit(solution)/shard_map/ppermute | solution.py:57
  5.0 1.0 %prepare.1 = (bf16[64,128]{1,0:T(8,128)(2,1)S(1)}, bf16[208,128]{1,0:T(8,128)(2,1)S(1)}, f32[8,512]{1,0:T(8,128)S(1)}, bf16[128,128]{1,0:T(8,128)(2,1)S(1)}, f32...) custom-call(bf16[64,128]{1,0:T(8,128)(2,1)S(1)} %copy-done.3, ...), custom_call_target="tpu_custom_call" | custom-call | flops 2147483648 | bytes 1024 | tf_op jit(solution)/shard_map/prepare/pallas_call | solution.py:68
  6.0 0.8 %collective-permute-done = bf16[64,128]{1,0:T(8,128)(2,1)S(1)} collective-permute-done((bf16[64,128]{1,0:T(8,128)(2,1)}, bf16[64,128]{1,0:T(8,128)(2,1)S(1)}, u32[]{:S(2)}, u32[]{:S(2)}) %collective-permute-start) | collective-permute-done | bytes 16416 | tf_op jit(solution)/shard_map/ppermute | solution.py:57
  6.8 1.9 %collective-permute-start.1 = (bf16[128,128]{1,0:T(8,128)(2,1)S(1)}, bf16[128,128]{1,0:T(8,128)(2,1)S(1)}, u32[]{:S(2)}, u32[]{:S(2)}) collective-permute-start(bf16[128,128]{1,0:T(8,128)(2,1)S(1)} %pad_maximum_fusion.2), channel_id=1, source_target_pairs={{0,4},{4,0},{8,12},{12,8},{16,20},{20,16},{24,28},{28,24},{1,5},{5... | collective-permute-start | bytes 98312 | tf_op jit(solution)/shard_map/ppermute | solution.py:57
  8.7 0.8 %chosen.1 = (bf16[128,1024]{1,0:T(8,128)(2,1)S(1)}, f32[128,1024]{1,0:T(8,128)S(1)}) custom-call(f32[8,512]{1,0:T(8,128)S(1)} %get-tuple-element.94.lines_ref.refs_5_, bf16[1024,128]{1,0:T(8,128)(2,1)S(1)} %bitcast.14, bf16[128,128]{1,0:T(8,128)(2,1)S(1)} %get-tuple-element.95.w_t_ref.refs_2_), custom_call_target="tpu_custom_call" | custom-call | flops 536870912 | bytes 1024 | tf_op jit(solution)/shard_map/chosen/pallas_call | solution.py:68
  9.5 1.2 %collective-permute-done.1 = bf16[128,128]{1,0:T(8,128)(2,1)S(1)} collective-permute-done((bf16[128,128]{1,0:T(8,128)(2,1)S(1)}, bf16[128,128]{1,0:T(8,128)(2,1)S(1)}, u32[]{:S(2)}, u32[]{:S(2)}) %collective-permute-start.1) | collective-permute-done | bytes 32800 | tf_op jit(solution)/shard_map/ppermute | solution.py:57
  10.7 1.9 %collective-permute-start.2 = (bf16[256,128]{1,0:T(8,128)(2,1)S(1)}, bf16[256,128]{1,0:T(8,128)(2,1)S(1)}, u32[]{:S(2)}, u32[]{:S(2)}) collective-permute-start(bf16[256,128]{1,0:T(8,128)(2,1)S(1)} %constant_dynamic-update-slice_fusion.refs_0_), channel_id=1, source_target_pairs={{0,8},{4,12},{8,0},{12,4},{16,24},{20,28},{24,16},{28,20},{1,9},{5... | collective-permute-start | bytes 196616 | tf_op jit(solution)/shard_map/ppermute | solution.py:57
  12.6 2.0 %forward.2 = (f32[4,256]{1,0:T(4,128)S(1)}, f32[8,64,512]{2,1,0:T(8,128)S(1)}, bf16[128,512]{1,0:T(8,128)(2,1)S(1)}, bf16[256,128]{1,0:T(8,128)(2,1)S(1)}) custom-call(bf16[256,128]{1,0:T(8,128)(2,1)S(1)} %constant_dynamic-update-slice_fusion.refs_0_, f32[128,1024]{1,0:T(8,128)S(1)} %get-tuple-element.96.refs_1_, ...), custom_call_target="tpu_custom_call" | custom-call | flops 1073741824 | bytes 1024 | tf_op jit(solution)/shard_map/forward/pallas_call | solution.py:68
  15.0 2.0 %forward.3 = (f32[4,512]{1,0:T(4,128)S(1)}, f32[8,64,512]{2,1,0:T(8,128)S(1)}, bf16[128,512]{1,0:T(8,128)(2,1)S(1)}, bf16[512,128]{1,0:T(8,128)(2,1)S(1)}) custom-call(bf16[256,128]{1,0:T(8,128)(2,1)S(1)} %collective-permute-done.2.refs_0_, f32[128,1024]{1,0:T(8,128)S(1)} %get-tuple-element.96.refs_1_, ...), custom_call_target="tpu_custom_call" | custom-call | flops 1073741824 | bytes 1024 | tf_op jit(solution)/shard_map/forward/pallas_call | solution.py:68
  16.9 2.0 %collective-permute-start.3 = (f32[4,512]{1,0:T(4,128)S(1)}, f32[4,512]{1,0:T(4,128)S(1)}, u32[]{:S(2)}, u32[]{:S(2)}) collective-permute-start(f32[4,512]{1,0:T(4,128)S(1)} %get-tuple-element.102.seg_ref.refs_0_), channel_id=1, source_target_pairs={{0,4},{4,0},{8,12},{12,8},{16,20},{20,16},{24,28},{28,24},{1,5},{5... | collective-permute-start | bytes 24584 | tf_op jit(solution)/shard_map/ppermute | solution.py:57
  18.9 0.8 %coefficients.1 = (f32[7,64,1024]{2,1,0:T(8,128)S(1)}, bf16[7,1024,128]{2,1,0:T(8,128)(2,1)S(1)}, bf16[1024,128]{1,0:T(8,128)(2,1)S(1)}) custom-call(f32[4,512]{1,0:T(4,128)S(1)} %get-tuple-element.102.seg_ref.refs_0_, f32[8,64,512]{2,1,0:T(8,128)S(1)} %get-tuple-element.103.first_ref, f32[8,64,512]{2,1,0:T(8,128)S(1)} %get-tuple-element.104.second_ref, ...), custom_call_target="tpu_custom_call" | custom-call | flops 1073741824 | bytes 1024 | tf_op jit(solution)/shard_map/coefficients/pallas_call | solution.py:68
  19.7 1.3 %basis.3 = (f32[7,256,128]{2,1,0:T(8,128)S(1)}, f32[4,256,128]{2,1,0:T(8,128)S(1)}) custom-call(bf16[7,1024,128]{2,1,0:T(8,128)(2,1)S(1)} %get-tuple-element.121.turned_ref, bf16[1024,128]{1,0:T(8,128)(2,1)S(1)} %get-tuple-element.116.u_ref.refs_7_, f32[64,128]{1,0:T(8,128)S(1)} %get-tuple-element.117.s_ref, ...), custom_call_target="tpu_custom_call" | custom-call | flops 536870912 | bytes 1024 | tf_op jit(solution)/shard_map/basis/pallas_call | solution.py:68
  21.0 1.6 %collective-permute-start.4 = (f32[4,512]{1,0:T(4,128)S(1)}, f32[4,512]{1,0:T(4,128)S(1)}, u32[]{:S(2)}, u32[]{:S(2)}) collective-permute-start(f32[4,512]{1,0:T(4,128)S(1)} %pad_maximum_fusion.3), channel_id=1, source_target_pairs={{0,8},{4,12},{8,0},{12,4},{16,24},{20,28},{24,16},{28,20},{1,9},{5... | collective-permute-start | bytes 24584 | tf_op jit(solution)/shard_map/ppermute | solution.py:57
  22.7 1.6 %basis.4 = (f32[7,384,128]{2,1,0:T(8,128)S(1)}, f32[4,384,128]{2,1,0:T(8,128)S(1)}) custom-call(bf16[7,1024,128]{2,1,0:T(8,128)(2,1)S(1)} %get-tuple-element.121.turned_ref, bf16[1024,128]{1,0:T(8,128)(2,1)S(1)} %get-tuple-element.116.u_ref.refs_7_, f32[64,128]{1,0:T(8,128)S(1)} %get-tuple-element.117.s_ref, ...), custom_call_target="tpu_custom_call" | custom-call | flops 536870912 | bytes 1024 | tf_op jit(solution)/shard_map/basis/pallas_call | solution.py:68
  24.8 2.7 %collective-permute-start.5 = (f32[4,512]{1,0:T(4,128)S(1)}, f32[4,512]{1,0:T(4,128)S(1)}, u32[]{:S(2)}, u32[]{:S(2)}) collective-permute-start(f32[4,512]{1,0:T(4,128)S(1)} %pad_maximum_fusion.4), channel_id=1, source_target_pairs={{0,16},{4,20},{8,24},{12,28},{16,0},{20,4},{24,8},{28,12},{1,17},{... | collective-permute-start | bytes 24584 | tf_op jit(solution)/shard_map/ppermute | solution.py:57
  27.5 1.6 %basis.5 = (f32[7,384,128]{2,1,0:T(8,128)S(1)}, f32[4,384,128]{2,1,0:T(8,128)S(1)}) custom-call(bf16[7,1024,128]{2,1,0:T(8,128)(2,1)S(1)} %get-tuple-element.121.turned_ref, bf16[1024,128]{1,0:T(8,128)(2,1)S(1)} %get-tuple-element.116.u_ref.refs_7_, f32[64,128]{1,0:T(8,128)S(1)} %get-tuple-element.117.s_ref, ...), custom_call_target="tpu_custom_call" | custom-call | flops 536870912 | bytes 1024 | tf_op jit(solution)/shard_map/basis/pallas_call | solution.py:68
  29.8 1.6 %collective-permute-start.6 = (bf16[256,128]{1,0:T(8,128)(2,1)S(1)}, bf16[256,128]{1,0:T(8,128)(2,1)S(1)}, u32[]{:S(2)}, u32[]{:S(2)}) collective-permute-start(bf16[256,128]{1,0:T(8,128)(2,1)S(1)} %get-tuple-element.127), channel_id=1, source_target_pairs={{0,8},{4,12},{8,0},{12,4},{16,24},{20,28},{24,16},{28,20},{1,9},{5... | collective-permute-start | bytes 196616 | tf_op jit(solution)/shard_map/ppermute | solution.py:57
  31.5 1.9 %by_sample.2 = (f32[32,128]{1,0:T(8,128)S(1)}, f32[4,8,128]{2,1,0:T(8,128)S(1)}, f32[4,128]{1,0:T(4,128)S(1)}) custom-call(f32[8,512]{1,0:T(8,128)S(1)} %get-tuple-element.140.cot_ref, f32[7,64,1024]{2,1,0:T(8,128)S(1)} %get-tuple-element.135.coef_ref, bf16[1024,128]{1,0:T(8,128)(2,1)S(1)} %get-tuple-element.116.u_ref.refs_7_, ...), custom_call_target="tpu_custom_call" | custom-call | flops 1048576 | bytes 1024 | tf_op jit(solution)/shard_map/by_sample/pallas_call | solution.py:68
  33.4 0.9 %slots.1 = (bf16[1024,128]{1,0:T(8,128)(2,1)S(1)}, f32[128,128]{1,0:T(8,128)S(1)}, f32[4,8,128]{2,1,0:T(8,128)S(1)}) custom-call(f32[7,256,128]{2,1,0:T(8,128)S(1)} %get-tuple-element.129.refs_0_, f32[7,384,128]{2,1,0:T(8,128)S(1)} %get-tuple-element.130.refs_1_, f32[7,384,128]{2,1,0:T(8,128)S(1)} %get-tuple-element.131.refs_2_, ...), custom_call_target="tpu_custom_call" | custom-call | flops 1048576 | bytes 1024 | tf_op jit(solution)/shard_map/slots/pallas_call | solution.py:68
  34.4 1.6 %collective-permute-start.7 = (bf16[128,128]{1,0:T(8,128)(2,1)S(1)}, bf16[128,128]{1,0:T(8,128)(2,1)S(1)}, u32[]{:S(2)}, u32[]{:S(2)}) collective-permute-start(bf16[128,128]{1,0:T(8,128)(2,1)S(1)} %get-tuple-element.182), channel_id=1, source_target_pairs={{0,4},{4,0},{8,12},{12,8},{16,20},{20,16},{24,28},{28,24},{1,5},{5... | collective-permute-start | bytes 98312 | tf_op jit(solution)/shard_map/ppermute | solution.py:57
  36.4 1.9 %by_sample.3 = (f32[32,128]{1,0:T(8,128)S(1)}, f32[4,8,128]{2,1,0:T(8,128)S(1)}, f32[4,128]{1,0:T(4,128)S(1)}) custom-call(f32[8,512]{1,0:T(8,128)S(1)} %get-tuple-element.140.cot_ref, f32[7,64,1024]{2,1,0:T(8,128)S(1)} %get-tuple-element.135.coef_ref, bf16[1024,128]{1,0:T(8,128)(2,1)S(1)} %get-tuple-element.116.u_ref.refs_7_, ...), custom_call_target="tpu_custom_call" | custom-call | flops 1048576 | bytes 1024 | tf_op jit(solution)/shard_map/by_sample/pallas_call | solution.py:68
  38.6 1.6 %collective-permute-start.9 = (bf16[720,128]{1,0:T(8,128)(2,1)S(1)}, bf16[720,128]{1,0:T(8,128)(2,1)S(1)}, u32[]{:S(2)}, u32[]{:S(2)}) collective-permute-start(bf16[720,128]{1,0:T(8,128)(2,1)S(1)} %pad_maximum_fusion), channel_id=1, source_target_pairs={{0,2},{1,3},{2,0},{3,1},{4,6},{5,7},{6,4},{7,5},{8,10},{9,11},{10,... | collective-permute-start | bytes 552968 | tf_op jit(solution)/shard_map/ppermute | solution.py:57
  40.2 2.7 %collective-permute-start.8 = (bf16[64,128]{1,0:T(8,128)(2,1)S(1)}, bf16[64,128]{1,0:T(8,128)(2,1)S(1)}, u32[]{:S(2)}, u32[]{:S(2)}) collective-permute-start(bf16[64,128]{1,0:T(8,128)(2,1)S(1)} %get-tuple-element.158), channel_id=1, source_target_pairs={{0,16},{4,20},{8,24},{12,28},{16,0},{20,4},{24,8},{28,12},{1,17},{... | collective-permute-start | bytes 49160 | tf_op jit(solution)/shard_map/ppermute | solution.py:57
  43.2 1.0 %collective-permute-done.9 = bf16[720,128]{1,0:T(8,128)(2,1)S(1)} collective-permute-done((bf16[720,128]{1,0:T(8,128)(2,1)S(1)}, bf16[720,128]{1,0:T(8,128)(2,1)S(1)}, u32[]{:S(2)}, u32[]{:S(2)}) %collective-permute-start.9) | collective-permute-done | bytes 184352 | tf_op jit(solution)/shard_map/ppermute | solution.py:57
  (58 shorter events, 5.2 us)
Async XLA Ops:
  0.6 4.2 %copy-start.3 = (bf16[64,128]{1,0:T(8,128)(2,1)S(1)}, bf16[64,128]{1,0:T(8,128)(2,1)}, u32[]{:S(2)}) copy-start(bf16[64,128]{1,0:T(8,128)(2,1)} %ray_ref.1) | copy-start | bytes 49156
  0.6 4.2 %copy-start.6 = (s32[1,512]{1,0:T(1,128)S(1)}, s32[1,512]{1,0:T(1,128)}, u32[]{:S(2)}) copy-start(s32[1,512]{1,0:T(1,128)} %occ_ref.1) | copy-start | bytes 6148
  0.7 4.2 %copy-start.5 = (s32[1,2,512]{2,1,0:T(2,128)S(1)}, s32[1,2,512]{2,1,0:T(2,128)}, u32[]{:S(2)}) copy-start(s32[1,2,512]{2,1,0:T(2,128)} %param.20) | copy-start | bytes 12292
  0.7 4.2 %copy-start.10 = (f32[1,4]{1,0:T(1,128)S(1)}, f32[1,4]{1,0:T(1,128)}, u32[]{:S(2)}) copy-start(f32[1,4]{1,0:T(1,128)} %b_out_ref.1) | copy-start | bytes 52
  0.7 4.2 %copy-start.8 = (bf16[1,4,128]{2,1,0:T(4,128)(2,1)S(1)}, bf16[1,4,128]{2,1,0:T(4,128)(2,1)}, u32[]{:S(2)}) copy-start(bf16[1,4,128]{2,1,0:T(4,128)(2,1)} %param.18) | copy-start | bytes 3076
  0.7 4.2 %copy-start.9 = (f32[1,128]{1,0:T(1,128)S(1)}, f32[1,128]{1,0:T(1,128)}, u32[]{:S(2)}) copy-start(f32[1,128]{1,0:T(1,128)} %b_ref.1) | copy-start | bytes 1540
  0.7 4.2 %copy-start.1 = (bf16[1,128,128]{2,1,0:T(8,128)(2,1)S(1)}, bf16[1,128,128]{2,1,0:T(8,128)(2,1)}, u32[]{:S(2)}) copy-start(bf16[1,128,128]{2,1,0:T(8,128)(2,1)} %param.16) | copy-start | bytes 98308
  0.7 4.2 %copy-start.2 = (bf16[1,64,128]{2,1,0:T(8,128)(2,1)S(1)}, bf16[1,64,128]{2,1,0:T(8,128)(2,1)}, u32[]{:S(2)}) copy-start(bf16[1,64,128]{2,1,0:T(8,128)(2,1)} %param.15) | copy-start | bytes 49156
  0.7 4.2 %copy-start.4 = (f32[3,512]{1,0:T(4,128)S(1)}, f32[3,512]{1,0:T(4,128)}, u32[]{:S(2)}) copy-start(f32[3,512]{1,0:T(4,128)} %target_ref.1) | copy-start | bytes 18436
  0.7 4.2 %copy-start.7 = (s32[512]{0:T(512)S(1)}, s32[512]{0:T(512)}, u32[]{:S(2)}) copy-start(s32[512]{0:T(512)} %param.12) | copy-start | bytes 6148
  0.7 6.0 %collective-permute-start = (bf16[64,128]{1,0:T(8,128)(2,1)}, bf16[64,128]{1,0:T(8,128)(2,1)S(1)}, u32[]{:S(2)}, u32[]{:S(2)}) collective-permute-start(bf16[64,128]{1,0:T(8,128)(2,1)} %ray_ref.1), channel_id=1, source_target_pairs={{0,16},{4,20},{8,24},{12,28},{16,0},{20,4},{24,8},{28,12},{1,17},{... | collective-permute-start | bytes 49160 | tf_op jit(solution)/shard_map/ppermute | solution.py:57
  5.0 3.7 %copy-start = (bf16[1,1024,128]{2,1,0:T(8,128)(2,1)S(1)}, bf16[1,1024,128]{2,1,0:T(8,128)(2,1)}, u32[]{:S(2)}) copy-start(bf16[1,1024,128]{2,1,0:T(8,128)(2,1)} %param.14) | copy-start | bytes 786436
  6.8 3.9 %collective-permute-start.1 = (bf16[128,128]{1,0:T(8,128)(2,1)S(1)}, bf16[128,128]{1,0:T(8,128)(2,1)S(1)}, u32[]{:S(2)}, u32[]{:S(2)}) collective-permute-start(bf16[128,128]{1,0:T(8,128)(2,1)S(1)} %pad_maximum_fusion.2), channel_id=1, source_target_pairs={{0,4},{4,0},{8,12},{12,8},{16,20},{20,16},{24,28},{28,24},{1,5},{5... | collective-permute-start | bytes 98312 | tf_op jit(solution)/shard_map/ppermute | solution.py:57
  10.7 4.3 %collective-permute-start.2 = (bf16[256,128]{1,0:T(8,128)(2,1)S(1)}, bf16[256,128]{1,0:T(8,128)(2,1)S(1)}, u32[]{:S(2)}, u32[]{:S(2)}) collective-permute-start(bf16[256,128]{1,0:T(8,128)(2,1)S(1)} %constant_dynamic-update-slice_fusion.refs_0_), channel_id=1, source_target_pairs={{0,8},{4,12},{8,0},{12,4},{16,24},{20,28},{24,16},{28,20},{1,9},{5... | collective-permute-start | bytes 196616 | tf_op jit(solution)/shard_map/ppermute | solution.py:57
  16.9 4.0 %collective-permute-start.3 = (f32[4,512]{1,0:T(4,128)S(1)}, f32[4,512]{1,0:T(4,128)S(1)}, u32[]{:S(2)}, u32[]{:S(2)}) collective-permute-start(f32[4,512]{1,0:T(4,128)S(1)} %get-tuple-element.102.seg_ref.refs_0_), channel_id=1, source_target_pairs={{0,4},{4,0},{8,12},{12,8},{16,20},{20,16},{24,28},{28,24},{1,5},{5... | collective-permute-start | bytes 24584 | tf_op jit(solution)/shard_map/ppermute | solution.py:57
  21.0 3.7 %collective-permute-start.4 = (f32[4,512]{1,0:T(4,128)S(1)}, f32[4,512]{1,0:T(4,128)S(1)}, u32[]{:S(2)}, u32[]{:S(2)}) collective-permute-start(f32[4,512]{1,0:T(4,128)S(1)} %pad_maximum_fusion.3), channel_id=1, source_target_pairs={{0,8},{4,12},{8,0},{12,4},{16,24},{20,28},{24,16},{28,20},{1,9},{5... | collective-permute-start | bytes 24584 | tf_op jit(solution)/shard_map/ppermute | solution.py:57
  24.8 4.6 %collective-permute-start.5 = (f32[4,512]{1,0:T(4,128)S(1)}, f32[4,512]{1,0:T(4,128)S(1)}, u32[]{:S(2)}, u32[]{:S(2)}) collective-permute-start(f32[4,512]{1,0:T(4,128)S(1)} %pad_maximum_fusion.4), channel_id=1, source_target_pairs={{0,16},{4,20},{8,24},{12,28},{16,0},{20,4},{24,8},{28,12},{1,17},{... | collective-permute-start | bytes 24584 | tf_op jit(solution)/shard_map/ppermute | solution.py:57
  29.8 4.5 %collective-permute-start.6 = (bf16[256,128]{1,0:T(8,128)(2,1)S(1)}, bf16[256,128]{1,0:T(8,128)(2,1)S(1)}, u32[]{:S(2)}, u32[]{:S(2)}) collective-permute-start(bf16[256,128]{1,0:T(8,128)(2,1)S(1)} %get-tuple-element.127), channel_id=1, source_target_pairs={{0,8},{4,12},{8,0},{12,4},{16,24},{20,28},{24,16},{28,20},{1,9},{5... | collective-permute-start | bytes 196616 | tf_op jit(solution)/shard_map/ppermute | solution.py:57
  34.4 4.0 %collective-permute-start.7 = (bf16[128,128]{1,0:T(8,128)(2,1)S(1)}, bf16[128,128]{1,0:T(8,128)(2,1)S(1)}, u32[]{:S(2)}, u32[]{:S(2)}) collective-permute-start(bf16[128,128]{1,0:T(8,128)(2,1)S(1)} %get-tuple-element.182), channel_id=1, source_target_pairs={{0,4},{4,0},{8,12},{12,8},{16,20},{20,16},{24,28},{28,24},{1,5},{5... | collective-permute-start | bytes 98312 | tf_op jit(solution)/shard_map/ppermute | solution.py:57
  38.6 5.6 %collective-permute-start.9 = (bf16[720,128]{1,0:T(8,128)(2,1)S(1)}, bf16[720,128]{1,0:T(8,128)(2,1)S(1)}, u32[]{:S(2)}, u32[]{:S(2)}) collective-permute-start(bf16[720,128]{1,0:T(8,128)(2,1)S(1)} %pad_maximum_fusion), channel_id=1, source_target_pairs={{0,2},{1,3},{2,0},{3,1},{4,6},{5,7},{6,4},{7,5},{8,10},{9,11},{10,... | collective-permute-start | bytes 552968 | tf_op jit(solution)/shard_map/ppermute | solution.py:57
  40.2 4.6 %collective-permute-start.8 = (bf16[64,128]{1,0:T(8,128)(2,1)S(1)}, bf16[64,128]{1,0:T(8,128)(2,1)S(1)}, u32[]{:S(2)}, u32[]{:S(2)}) collective-permute-start(bf16[64,128]{1,0:T(8,128)(2,1)S(1)} %get-tuple-element.158), channel_id=1, source_target_pairs={{0,16},{4,20},{8,24},{12,28},{16,0},{20,4},{24,8},{28,12},{1,17},{... | collective-permute-start | bytes 49160 | tf_op jit(solution)/shard_map/ppermute | solution.py:57
  44.3 1.4 %collective-permute-start.10 = (bf16[464,128]{1,0:T(8,128)(2,1)S(1)}, bf16[464,128]{1,0:T(8,128)(2,1)S(1)}, u32[]{:S(2)}, u32[]{:S(2)}) collective-permute-start(bf16[464,128]{1,0:T(8,128)(2,1)S(1)} %pad_maximum_fusion.1.sent_ref), channel_id=1, source_target_pairs={{0,1},{1,0},{2,3},{3,2},{4,5},{5,4},{6,7},{7,6},{8,9},{9,8},{10,11... | collective-permute-start | bytes 356360 | tf_op jit(solution)/shard_map/ppermute | solution.py:57

commit v9 on v7

--- a/solution.py
+++ b/solution.py
@@ -33,7 +33,7 @@
 
 def halving_bits(owners):
     bits = list(range(bits_of(owners)))
-    return bits[1:-1] + bits[:1] + bits[1:][-1:]
+    return bits
 
 
 def halving_order(owners):

time: 46.6 us -> 46.6 us (level)
  no operation moved by 1% of the time
where the time goes in v9:
time: 46.6 us; the launch traced here: 46.4 us
  starting transfers between devices  21.7 us (47%)
  Pallas kernels  18.2 us (39%)
  waiting for transfers between devices  5.26 us (11%)
  between operations  1.03 us (2%)
    ppermute x11, starting transfers between devices, swap(): return lax.ppermute(array, axis, [(i, i ^ distance) for i in range(size)])  21.7 us
    pallas_call x19, Pallas kernels, run(): pl.pallas_call(kernel, out_shape=out_shape, in_specs=[pl.BlockSpec(memory...  18.2 us
    ppermute x11, waiting for transfers between devices, swap(): return lax.ppermute(array, axis, [(i, i ^ distance) for i in range(size)])  5.26 us
  transfers between devices with their start and end apart: 11, of which 8 were waited for; matrix products, arithmetic and copies ran while one was open for 0% of the time, Pallas kernels for 32%

profile of v9, /device:TPU:0, one launch (start us, length us, event | category | flops | bytes accessed | tf_op | source)
XLA Modules:
  0.0 46.4 jit_solution(6640748121433136808)
XLA Ops:
  0.7 4.1 %collective-permute-start = (bf16[64,128]{1,0:T(8,128)(2,1)}, bf16[64,128]{1,0:T(8,128)(2,1)S(1)}, u32[]{:S(2)}, u32[]{:S(2)}) collective-permute-start(bf16[64,128]{1,0:T(8,128)(2,1)} %ray_ref.1), channel_id=1, source_target_pairs={{0,16},{4,20},{8,24},{12,28},{16,0},{20,4},{24,8},{28,12},{1,17},{... | collective-permute-start | bytes 49160 | tf_op jit(solution)/shard_map/ppermute | solution.py:57
  5.0 1.0 %prepare.1 = (bf16[64,128]{1,0:T(8,128)(2,1)S(1)}, bf16[208,128]{1,0:T(8,128)(2,1)S(1)}, f32[8,512]{1,0:T(8,128)S(1)}, bf16[128,128]{1,0:T(8,128)(2,1)S(1)}, f32...) custom-call(bf16[64,128]{1,0:T(8,128)(2,1)S(1)} %copy-done.3, ...), custom_call_target="tpu_custom_call" | custom-call | flops 2147483648 | bytes 1024 | tf_op jit(solution)/shard_map/prepare/pallas_call | solution.py:68
  6.0 0.8 %collective-permute-done = bf16[64,128]{1,0:T(8,128)(2,1)S(1)} collective-permute-done((bf16[64,128]{1,0:T(8,128)(2,1)}, bf16[64,128]{1,0:T(8,128)(2,1)S(1)}, u32[]{:S(2)}, u32[]{:S(2)}) %collective-permute-start) | collective-permute-done | bytes 16416 | tf_op jit(solution)/shard_map/ppermute | solution.py:57
  6.8 1.9 %collective-permute-start.1 = (bf16[128,128]{1,0:T(8,128)(2,1)S(1)}, bf16[128,128]{1,0:T(8,128)(2,1)S(1)}, u32[]{:S(2)}, u32[]{:S(2)}) collective-permute-start(bf16[128,128]{1,0:T(8,128)(2,1)S(1)} %pad_maximum_fusion.2), channel_id=1, source_target_pairs={{0,4},{4,0},{8,12},{12,8},{16,20},{20,16},{24,28},{28,24},{1,5},{5... | collective-permute-start | bytes 98312 | tf_op jit(solution)/shard_map/ppermute | solution.py:57
  8.7 0.8 %chosen.1 = (bf16[128,1024]{1,0:T(8,128)(2,1)S(1)}, f32[128,1024]{1,0:T(8,128)S(1)}) custom-call(f32[8,512]{1,0:T(8,128)S(1)} %get-tuple-element.93.lines_ref.refs_5_.refs_7_, bf16[1024,128]{1,0:T(8,128)(2,1)S(1)} %bitcast.14, bf16[128,128]{1,0:T(8,128)(2,1)S(1)} %get-tuple-element.94.w_t_ref.refs_2_), custom_call_target="tpu_custom_call" | custom-call | flops 536870912 | bytes 1024 | tf_op jit(solution)/shard_map/chosen/pallas_call | solution.py:68
  9.5 1.2 %collective-permute-done.1 = bf16[128,128]{1,0:T(8,128)(2,1)S(1)} collective-permute-done((bf16[128,128]{1,0:T(8,128)(2,1)S(1)}, bf16[128,128]{1,0:T(8,128)(2,1)S(1)}, u32[]{:S(2)}, u32[]{:S(2)}) %collective-permute-start.1) | collective-permute-done | bytes 32800 | tf_op jit(solution)/shard_map/ppermute | solution.py:57
  10.7 1.9 %collective-permute-start.2 = (bf16[256,128]{1,0:T(8,128)(2,1)S(1)}, bf16[256,128]{1,0:T(8,128)(2,1)S(1)}, u32[]{:S(2)}, u32[]{:S(2)}) collective-permute-start(bf16[256,128]{1,0:T(8,128)(2,1)S(1)} %constant_dynamic-update-slice_fusion.refs_0_), channel_id=1, source_target_pairs={{0,8},{4,12},{8,0},{12,4},{16,24},{20,28},{24,16},{28,20},{1,9},{5... | collective-permute-start | bytes 196616 | tf_op jit(solution)/shard_map/ppermute | solution.py:57
  12.6 2.0 %forward.2 = (f32[4,256]{1,0:T(4,128)S(1)}, f32[8,64,512]{2,1,0:T(8,128)S(1)}, bf16[128,512]{1,0:T(8,128)(2,1)S(1)}, bf16[256,128]{1,0:T(8,128)(2,1)S(1)}) custom-call(bf16[256,128]{1,0:T(8,128)(2,1)S(1)} %constant_dynamic-update-slice_fusion.refs_0_, f32[128,1024]{1,0:T(8,128)S(1)} %get-tuple-element.95.refs_1_, ...), custom_call_target="tpu_custom_call" | custom-call | flops 1073741824 | bytes 1024 | tf_op jit(solution)/shard_map/forward/pallas_call | solution.py:68
  15.0 2.0 %forward.3 = (f32[4,512]{1,0:T(4,128)S(1)}, f32[8,64,512]{2,1,0:T(8,128)S(1)}, bf16[128,512]{1,0:T(8,128)(2,1)S(1)}, bf16[512,128]{1,0:T(8,128)(2,1)S(1)}) custom-call(bf16[256,128]{1,0:T(8,128)(2,1)S(1)} %collective-permute-done.2.refs_0_, f32[128,1024]{1,0:T(8,128)S(1)} %get-tuple-element.95.refs_1_, ...), custom_call_target="tpu_custom_call" | custom-call | flops 1073741824 | bytes 1024 | tf_op jit(solution)/shard_map/forward/pallas_call | solution.py:68
  16.9 2.0 %collective-permute-start.3 = (f32[4,512]{1,0:T(4,128)S(1)}, f32[4,512]{1,0:T(4,128)S(1)}, u32[]{:S(2)}, u32[]{:S(2)}) collective-permute-start(f32[4,512]{1,0:T(4,128)S(1)} %get-tuple-element.101.seg_ref.refs_0_), channel_id=1, source_target_pairs={{0,4},{4,0},{8,12},{12,8},{16,20},{20,16},{24,28},{28,24},{1,5},{5... | collective-permute-start | bytes 24584 | tf_op jit(solution)/shard_map/ppermute | solution.py:57
  18.9 0.8 %coefficients.1 = (f32[7,64,1024]{2,1,0:T(8,128)S(1)}, bf16[7,1024,128]{2,1,0:T(8,128)(2,1)S(1)}, bf16[1024,128]{1,0:T(8,128)(2,1)S(1)}) custom-call(f32[4,512]{1,0:T(4,128)S(1)} %get-tuple-element.101.seg_ref.refs_0_, f32[8,64,512]{2,1,0:T(8,128)S(1)} %get-tuple-element.102.first_ref, f32[8,64,512]{2,1,0:T(8,128)S(1)} %get-tuple-element.103.second_ref, ...), custom_call_target="tpu_custom_call" | custom-call | flops 1073741824 | bytes 1024 | tf_op jit(solution)/shard_map/coefficients/pallas_call | solution.py:68
  19.7 1.3 %basis.3 = (f32[7,256,128]{2,1,0:T(8,128)S(1)}, f32[4,256,128]{2,1,0:T(8,128)S(1)}) custom-call(bf16[7,1024,128]{2,1,0:T(8,128)(2,1)S(1)} %get-tuple-element.116.turned_ref, bf16[1024,128]{1,0:T(8,128)(2,1)S(1)} %get-tuple-element.118.u_ref.refs_7_, f32[64,128]{1,0:T(8,128)S(1)} %get-tuple-element.119.s_ref, ...), custom_call_target="tpu_custom_call" | custom-call | flops 536870912 | bytes 1024 | tf_op jit(solution)/shard_map/basis/pallas_call | solution.py:68
  21.0 1.6 %collective-permute-start.4 = (f32[4,512]{1,0:T(4,128)S(1)}, f32[4,512]{1,0:T(4,128)S(1)}, u32[]{:S(2)}, u32[]{:S(2)}) collective-permute-start(f32[4,512]{1,0:T(4,128)S(1)} %pad_maximum_fusion.3), channel_id=1, source_target_pairs={{0,8},{4,12},{8,0},{12,4},{16,24},{20,28},{24,16},{28,20},{1,9},{5... | collective-permute-start | bytes 24584 | tf_op jit(solution)/shard_map/ppermute | solution.py:57
  22.7 1.6 %basis.4 = (f32[7,384,128]{2,1,0:T(8,128)S(1)}, f32[4,384,128]{2,1,0:T(8,128)S(1)}) custom-call(bf16[7,1024,128]{2,1,0:T(8,128)(2,1)S(1)} %get-tuple-element.116.turned_ref, bf16[1024,128]{1,0:T(8,128)(2,1)S(1)} %get-tuple-element.118.u_ref.refs_7_, f32[64,128]{1,0:T(8,128)S(1)} %get-tuple-element.119.s_ref, ...), custom_call_target="tpu_custom_call" | custom-call | flops 536870912 | bytes 1024 | tf_op jit(solution)/shard_map/basis/pallas_call | solution.py:68
  24.8 2.7 %collective-permute-start.5 = (f32[4,512]{1,0:T(4,128)S(1)}, f32[4,512]{1,0:T(4,128)S(1)}, u32[]{:S(2)}, u32[]{:S(2)}) collective-permute-start(f32[4,512]{1,0:T(4,128)S(1)} %pad_maximum_fusion.4), channel_id=1, source_target_pairs={{0,16},{4,20},{8,24},{12,28},{16,0},{20,4},{24,8},{28,12},{1,17},{... | collective-permute-start | bytes 24584 | tf_op jit(solution)/shard_map/ppermute | solution.py:57
  27.5 1.6 %basis.5 = (f32[7,384,128]{2,1,0:T(8,128)S(1)}, f32[4,384,128]{2,1,0:T(8,128)S(1)}) custom-call(bf16[7,1024,128]{2,1,0:T(8,128)(2,1)S(1)} %get-tuple-element.116.turned_ref, bf16[1024,128]{1,0:T(8,128)(2,1)S(1)} %get-tuple-element.118.u_ref.refs_7_, f32[64,128]{1,0:T(8,128)S(1)} %get-tuple-element.119.s_ref, ...), custom_call_target="tpu_custom_call" | custom-call | flops 536870912 | bytes 1024 | tf_op jit(solution)/shard_map/basis/pallas_call | solution.py:68
  29.9 1.6 %collective-permute-start.6 = (bf16[256,128]{1,0:T(8,128)(2,1)S(1)}, bf16[256,128]{1,0:T(8,128)(2,1)S(1)}, u32[]{:S(2)}, u32[]{:S(2)}) collective-permute-start(bf16[256,128]{1,0:T(8,128)(2,1)S(1)} %get-tuple-element.125), channel_id=1, source_target_pairs={{0,4},{4,0},{8,12},{12,8},{16,20},{20,16},{24,28},{28,24},{1,5},{5... | collective-permute-start | bytes 196616 | tf_op jit(solution)/shard_map/ppermute | solution.py:57
  31.5 1.9 %by_sample.2 = (f32[32,128]{1,0:T(8,128)S(1)}, f32[4,8,128]{2,1,0:T(8,128)S(1)}, f32[4,128]{1,0:T(4,128)S(1)}) custom-call(f32[8,512]{1,0:T(8,128)S(1)} %get-tuple-element.138.cot_ref, f32[7,64,1024]{2,1,0:T(8,128)S(1)} %get-tuple-element.133.coef_ref, bf16[1024,128]{1,0:T(8,128)(2,1)S(1)} %get-tuple-element.118.u_ref.refs_7_, ...), custom_call_target="tpu_custom_call" | custom-call | flops 1048576 | bytes 1024 | tf_op jit(solution)/shard_map/by_sample/pallas_call | solution.py:68
  33.4 0.9 %slots.1 = (bf16[1024,128]{1,0:T(8,128)(2,1)S(1)}, f32[128,128]{1,0:T(8,128)S(1)}, f32[4,8,128]{2,1,0:T(8,128)S(1)}) custom-call(f32[7,256,128]{2,1,0:T(8,128)S(1)} %get-tuple-element.127.refs_0_, f32[7,384,128]{2,1,0:T(8,128)S(1)} %get-tuple-element.128.refs_1_, f32[7,384,128]{2,1,0:T(8,128)S(1)} %get-tuple-element.129.refs_2_, ...), custom_call_target="tpu_custom_call" | custom-call | flops 1048576 | bytes 1024 | tf_op jit(solution)/shard_map/slots/pallas_call | solution.py:68
  34.4 1.6 %collective-permute-start.7 = (bf16[128,128]{1,0:T(8,128)(2,1)S(1)}, bf16[128,128]{1,0:T(8,128)(2,1)S(1)}, u32[]{:S(2)}, u32[]{:S(2)}) collective-permute-start(bf16[128,128]{1,0:T(8,128)(2,1)S(1)} %get-tuple-element.180), channel_id=1, source_target_pairs={{0,8},{4,12},{8,0},{12,4},{16,24},{20,28},{24,16},{28,20},{1,9},{5... | collective-permute-start | bytes 98312 | tf_op jit(solution)/shard_map/ppermute | solution.py:57
  36.4 1.9 %by_sample.3 = (f32[32,128]{1,0:T(8,128)S(1)}, f32[4,8,128]{2,1,0:T(8,128)S(1)}, f32[4,128]{1,0:T(4,128)S(1)}) custom-call(f32[8,512]{1,0:T(8,128)S(1)} %get-tuple-element.138.cot_ref, f32[7,64,1024]{2,1,0:T(8,128)S(1)} %get-tuple-element.133.coef_ref, bf16[1024,128]{1,0:T(8,128)(2,1)S(1)} %get-tuple-element.118.u_ref.refs_7_, ...), custom_call_target="tpu_custom_call" | custom-call | flops 1048576 | bytes 1024 | tf_op jit(solution)/shard_map/by_sample/pallas_call | solution.py:68
  38.6 1.6 %collective-permute-start.9 = (bf16[720,128]{1,0:T(8,128)(2,1)S(1)}, bf16[720,128]{1,0:T(8,128)(2,1)S(1)}, u32[]{:S(2)}, u32[]{:S(2)}) collective-permute-start(bf16[720,128]{1,0:T(8,128)(2,1)S(1)} %pad_maximum_fusion), channel_id=1, source_target_pairs={{0,2},{1,3},{2,0},{3,1},{4,6},{5,7},{6,4},{7,5},{8,10},{9,11},{10,... | collective-permute-start | bytes 552968 | tf_op jit(solution)/shard_map/ppermute | solution.py:57
  40.1 2.6 %collective-permute-start.8 = (bf16[64,128]{1,0:T(8,128)(2,1)S(1)}, bf16[64,128]{1,0:T(8,128)(2,1)S(1)}, u32[]{:S(2)}, u32[]{:S(2)}) collective-permute-start(bf16[64,128]{1,0:T(8,128)(2,1)S(1)} %get-tuple-element.156), channel_id=1, source_target_pairs={{0,16},{4,20},{8,24},{12,28},{16,0},{20,4},{24,8},{28,12},{1,17},{... | collective-permute-start | bytes 49160 | tf_op jit(solution)/shard_map/ppermute | solution.py:57
  43.2 1.0 %collective-permute-done.9 = bf16[720,128]{1,0:T(8,128)(2,1)S(1)} collective-permute-done((bf16[720,128]{1,0:T(8,128)(2,1)S(1)}, bf16[720,128]{1,0:T(8,128)(2,1)S(1)}, u32[]{:S(2)}, u32[]{:S(2)}) %collective-permute-start.9) | collective-permute-done | bytes 184352 | tf_op jit(solution)/shard_map/ppermute | solution.py:57
  (57 shorter events, 5.2 us)
Async XLA Ops:
  0.6 4.2 %copy-start.3 = (bf16[64,128]{1,0:T(8,128)(2,1)S(1)}, bf16[64,128]{1,0:T(8,128)(2,1)}, u32[]{:S(2)}) copy-start(bf16[64,128]{1,0:T(8,128)(2,1)} %ray_ref.1) | copy-start | bytes 49156
  0.6 4.2 %copy-start.6 = (s32[1,512]{1,0:T(1,128)S(1)}, s32[1,512]{1,0:T(1,128)}, u32[]{:S(2)}) copy-start(s32[1,512]{1,0:T(1,128)} %occ_ref.1) | copy-start | bytes 6148
  0.7 4.2 %copy-start.5 = (s32[1,2,512]{2,1,0:T(2,128)S(1)}, s32[1,2,512]{2,1,0:T(2,128)}, u32[]{:S(2)}) copy-start(s32[1,2,512]{2,1,0:T(2,128)} %param.20) | copy-start | bytes 12292
  0.7 4.2 %copy-start.10 = (f32[1,4]{1,0:T(1,128)S(1)}, f32[1,4]{1,0:T(1,128)}, u32[]{:S(2)}) copy-start(f32[1,4]{1,0:T(1,128)} %b_out_ref.1) | copy-start | bytes 52
  0.7 4.2 %copy-start.8 = (bf16[1,4,128]{2,1,0:T(4,128)(2,1)S(1)}, bf16[1,4,128]{2,1,0:T(4,128)(2,1)}, u32[]{:S(2)}) copy-start(bf16[1,4,128]{2,1,0:T(4,128)(2,1)} %param.18) | copy-start | bytes 3076
  0.7 4.2 %copy-start.9 = (f32[1,128]{1,0:T(1,128)S(1)}, f32[1,128]{1,0:T(1,128)}, u32[]{:S(2)}) copy-start(f32[1,128]{1,0:T(1,128)} %b_ref.1) | copy-start | bytes 1540
  0.7 4.2 %copy-start.1 = (bf16[1,128,128]{2,1,0:T(8,128)(2,1)S(1)}, bf16[1,128,128]{2,1,0:T(8,128)(2,1)}, u32[]{:S(2)}) copy-start(bf16[1,128,128]{2,1,0:T(8,128)(2,1)} %param.16) | copy-start | bytes 98308
  0.7 4.2 %copy-start.2 = (bf16[1,64,128]{2,1,0:T(8,128)(2,1)S(1)}, bf16[1,64,128]{2,1,0:T(8,128)(2,1)}, u32[]{:S(2)}) copy-start(bf16[1,64,128]{2,1,0:T(8,128)(2,1)} %param.15) | copy-start | bytes 49156
  0.7 4.2 %copy-start.4 = (f32[3,512]{1,0:T(4,128)S(1)}, f32[3,512]{1,0:T(4,128)}, u32[]{:S(2)}) copy-start(f32[3,512]{1,0:T(4,128)} %target_ref.1) | copy-start | bytes 18436
  0.7 4.2 %copy-start.7 = (s32[512]{0:T(512)S(1)}, s32[512]{0:T(512)}, u32[]{:S(2)}) copy-start(s32[512]{0:T(512)} %param.12) | copy-start | bytes 6148
  0.7 6.0 %collective-permute-start = (bf16[64,128]{1,0:T(8,128)(2,1)}, bf16[64,128]{1,0:T(8,128)(2,1)S(1)}, u32[]{:S(2)}, u32[]{:S(2)}) collective-permute-start(bf16[64,128]{1,0:T(8,128)(2,1)} %ray_ref.1), channel_id=1, source_target_pairs={{0,16},{4,20},{8,24},{12,28},{16,0},{20,4},{24,8},{28,12},{1,17},{... | collective-permute-start | bytes 49160 | tf_op jit(solution)/shard_map/ppermute | solution.py:57
  5.0 3.7 %copy-start = (bf16[1,1024,128]{2,1,0:T(8,128)(2,1)S(1)}, bf16[1,1024,128]{2,1,0:T(8,128)(2,1)}, u32[]{:S(2)}) copy-start(bf16[1,1024,128]{2,1,0:T(8,128)(2,1)} %param.14) | copy-start | bytes 786436
  6.8 3.9 %collective-permute-start.1 = (bf16[128,128]{1,0:T(8,128)(2,1)S(1)}, bf16[128,128]{1,0:T(8,128)(2,1)S(1)}, u32[]{:S(2)}, u32[]{:S(2)}) collective-permute-start(bf16[128,128]{1,0:T(8,128)(2,1)S(1)} %pad_maximum_fusion.2), channel_id=1, source_target_pairs={{0,4},{4,0},{8,12},{12,8},{16,20},{20,16},{24,28},{28,24},{1,5},{5... | collective-permute-start | bytes 98312 | tf_op jit(solution)/shard_map/ppermute | solution.py:57
  10.7 4.3 %collective-permute-start.2 = (bf16[256,128]{1,0:T(8,128)(2,1)S(1)}, bf16[256,128]{1,0:T(8,128)(2,1)S(1)}, u32[]{:S(2)}, u32[]{:S(2)}) collective-permute-start(bf16[256,128]{1,0:T(8,128)(2,1)S(1)} %constant_dynamic-update-slice_fusion.refs_0_), channel_id=1, source_target_pairs={{0,8},{4,12},{8,0},{12,4},{16,24},{20,28},{24,16},{28,20},{1,9},{5... | collective-permute-start | bytes 196616 | tf_op jit(solution)/shard_map/ppermute | solution.py:57
  16.9 4.0 %collective-permute-start.3 = (f32[4,512]{1,0:T(4,128)S(1)}, f32[4,512]{1,0:T(4,128)S(1)}, u32[]{:S(2)}, u32[]{:S(2)}) collective-permute-start(f32[4,512]{1,0:T(4,128)S(1)} %get-tuple-element.101.seg_ref.refs_0_), channel_id=1, source_target_pairs={{0,4},{4,0},{8,12},{12,8},{16,20},{20,16},{24,28},{28,24},{1,5},{5... | collective-permute-start | bytes 24584 | tf_op jit(solution)/shard_map/ppermute | solution.py:57
  21.0 3.7 %collective-permute-start.4 = (f32[4,512]{1,0:T(4,128)S(1)}, f32[4,512]{1,0:T(4,128)S(1)}, u32[]{:S(2)}, u32[]{:S(2)}) collective-permute-start(f32[4,512]{1,0:T(4,128)S(1)} %pad_maximum_fusion.3), channel_id=1, source_target_pairs={{0,8},{4,12},{8,0},{12,4},{16,24},{20,28},{24,16},{28,20},{1,9},{5... | collective-permute-start | bytes 24584 | tf_op jit(solution)/shard_map/ppermute | solution.py:57
  24.8 4.6 %collective-permute-start.5 = (f32[4,512]{1,0:T(4,128)S(1)}, f32[4,512]{1,0:T(4,128)S(1)}, u32[]{:S(2)}, u32[]{:S(2)}) collective-permute-start(f32[4,512]{1,0:T(4,128)S(1)} %pad_maximum_fusion.4), channel_id=1, source_target_pairs={{0,16},{4,20},{8,24},{12,28},{16,0},{20,4},{24,8},{28,12},{1,17},{... | collective-permute-start | bytes 24584 | tf_op jit(solution)/shard_map/ppermute | solution.py:57
  29.9 4.5 %collective-permute-start.6 = (bf16[256,128]{1,0:T(8,128)(2,1)S(1)}, bf16[256,128]{1,0:T(8,128)(2,1)S(1)}, u32[]{:S(2)}, u32[]{:S(2)}) collective-permute-start(bf16[256,128]{1,0:T(8,128)(2,1)S(1)} %get-tuple-element.125), channel_id=1, source_target_pairs={{0,4},{4,0},{8,12},{12,8},{16,20},{20,16},{24,28},{28,24},{1,5},{5... | collective-permute-start | bytes 196616 | tf_op jit(solution)/shard_map/ppermute | solution.py:57
  34.4 4.0 %collective-permute-start.7 = (bf16[128,128]{1,0:T(8,128)(2,1)S(1)}, bf16[128,128]{1,0:T(8,128)(2,1)S(1)}, u32[]{:S(2)}, u32[]{:S(2)}) collective-permute-start(bf16[128,128]{1,0:T(8,128)(2,1)S(1)} %get-tuple-element.180), channel_id=1, source_target_pairs={{0,8},{4,12},{8,0},{12,4},{16,24},{20,28},{24,16},{28,20},{1,9},{5... | collective-permute-start | bytes 98312 | tf_op jit(solution)/shard_map/ppermute | solution.py:57
  38.6 5.6 %collective-permute-start.9 = (bf16[720,128]{1,0:T(8,128)(2,1)S(1)}, bf16[720,128]{1,0:T(8,128)(2,1)S(1)}, u32[]{:S(2)}, u32[]{:S(2)}) collective-permute-start(bf16[720,128]{1,0:T(8,128)(2,1)S(1)} %pad_maximum_fusion), channel_id=1, source_target_pairs={{0,2},{1,3},{2,0},{3,1},{4,6},{5,7},{6,4},{7,5},{8,10},{9,11},{10,... | collective-permute-start | bytes 552968 | tf_op jit(solution)/shard_map/ppermute | solution.py:57
  40.1 4.6 %collective-permute-start.8 = (bf16[64,128]{1,0:T(8,128)(2,1)S(1)}, bf16[64,128]{1,0:T(8,128)(2,1)S(1)}, u32[]{:S(2)}, u32[]{:S(2)}) collective-permute-start(bf16[64,128]{1,0:T(8,128)(2,1)S(1)} %get-tuple-element.156), channel_id=1, source_target_pairs={{0,16},{4,20},{8,24},{12,28},{16,0},{20,4},{24,8},{28,12},{1,17},{... | collective-permute-start | bytes 49160 | tf_op jit(solution)/shard_map/ppermute | solution.py:57
  44.3 1.4 %collective-permute-start.10 = (bf16[464,128]{1,0:T(8,128)(2,1)S(1)}, bf16[464,128]{1,0:T(8,128)(2,1)S(1)}, u32[]{:S(2)}, u32[]{:S(2)}) collective-permute-start(bf16[464,128]{1,0:T(8,128)(2,1)S(1)} %pad_maximum_fusion.1.sent_ref), channel_id=1, source_target_pairs={{0,1},{1,0},{2,3},{3,2},{4,5},{5,4},{6,7},{7,6},{8,9},{9,8},{10,11... | collective-permute-start | bytes 356360 | tf_op jit(solution)/shard_map/ppermute | solution.py:57
